TPU v7x, 32 devices: a whole 2x2x4 slice. The times are simulated.
32 devices in a mesh: tm: 4 (over y, x), space: 8 (over z, core).
Axes of the slice: x: 2, y: 2, z: 4, core: 2. Of those that a mesh axis runs over, the one named last changes fastest.
Arguments:
- residual: float32 [256, 16, 32, 256], P('tm', 'space'), may hold values from -8 to 8
- step_ratio: int32 [256], P('tm'), may hold values from 4 to 12
- forward_map: float32 [2, 256, 256], replicated, may hold values from -1 to 2
- back_map: float32 [2, 256, 256], replicated, may hold values from -1 to 2
- eigen_values: float32 [2, 256], replicated, may hold values from -3 to 4, as said below
Outputs:
- correction: float32 [2, 256, 16, 32, 256], P(None, 'tm', 'space')
Inputs may be any that keep to these rules, and one draw needn't show every extreme that they name: `eigen_values`: real parts of the shifts are positive, from 0.2 to 4; imaginary parts lie in -3 to 3.
All inputs are finite; a program needn't handle non-finite values.
Results may differ from a plain program's by a relative error of at most 0.000098.
Values sent between devices are 32-bit elements; how exact they have to be, the bound alone decides.
No kernel may reach another device: no remote copies, remote signals or barrier semaphores. Data moves between devices by JAX's collectives and lax.ppermute only.
A program may use at most 128 MiB of HBM per device.

v0:
```python
import jax
import jax.numpy as jnp
from jax import lax
from jax.sharding import PartitionSpec as P


def extended(cells, sides, width):
    for axis, dim in sides:
        count = lax.axis_size(axis)
        ends = count - 1
        head = lax.slice_in_dim(cells, 0, width, axis=dim)
        tail = lax.slice_in_dim(cells, cells.shape[dim] - width, cells.shape[dim], axis=dim)
        cells = jnp.concatenate(
            [
                lax.ppermute(tail, axis, [(i, (i + 1) % count) for i in range(ends)]),
                cells,
                lax.ppermute(head, axis, [((i + 1) % count, i) for i in range(ends)]),
            ],
            axis=dim,
        )
    return cells


def combine(prod, count):
    if count == 1:
        return prod[:, 0]
    return jnp.stack([prod[0, 0] - prod[1, 1], prod[0, 1] + prod[1, 0]])


def transform(data, matrix):
    count, local_steps, cells = data.shape
    highest = lax.Precision.HIGHEST
    moved = lax.all_to_all(data, "tm", split_axis=2, concat_axis=1, tiled=True)
    prod = jnp.einsum("pjn,qnc->pqjc", matrix, moved, precision=highest)
    mixed = combine(prod, count)
    back = lax.all_to_all(mixed, "tm", split_axis=1, concat_axis=2, tiled=True)
    return back


def plane_sum(field, padded):
    total = padded[:, :, 2:] + padded[:, :, :-2]
    flat_pad = jnp.pad(field, ((0, 0), (0, 0), (0, 0), (1, 1), (1, 1)))
    total = total + flat_pad[:, :, :, 2:, 1:-1] + flat_pad[:, :, :, :-2, 1:-1]
    return total + flat_pad[:, :, :, 1:-1, 2:] + flat_pad[:, :, :, 1:-1, :-2]


def make_divide(eigen_block):
    real_part = 6.0 + eigen_block[0]
    imag_part = eigen_block[1]
    denom = real_part * real_part + imag_part * imag_part
    coef_re = (real_part / denom)[:, None, None, None]
    coef_im = (-imag_part / denom)[:, None, None, None]

    def divide(total):
        return jnp.stack(
            [total[0] * coef_re - total[1] * coef_im, total[0] * coef_im + total[1] * coef_re]
        )

    return divide


def local(residual, step_ratio, forward_map, back_map, eigen_values):
    local_steps, planes, rows_x, rows_y = residual.shape
    cells = planes * rows_x * rows_y
    ratio = step_ratio.astype(jnp.float32) / 8.0
    scaled = residual * ratio[:, None, None, None]
    start = lax.axis_index("tm") * local_steps
    eigen_block = lax.dynamic_slice_in_dim(eigen_values, start, local_steps, 1)
    divide = make_divide(eigen_block)
    source = transform(scaled.reshape(1, local_steps, cells), forward_map)
    source = source.reshape(2, local_steps, planes, rows_x, rows_y)
    field = divide(source)
    padded = extended(field, (("space", 2),), 1)
    field = divide(source + plane_sum(field, padded))
    result = transform(field.reshape(2, local_steps, cells), back_map)
    return result.reshape(2, local_steps, planes, rows_x, rows_y)


def solution(mesh):
    in_specs = (P("tm", "space", None, None), P("tm"), P(), P(), P())
    out_specs = P(None, "tm", "space", None, None)
    return jax.shard_map(local, mesh=mesh, in_specs=in_specs, out_specs=out_specs, check_vma=False)
```

profile of v0, /device:TPU:8, one launch (start us, length us, event | category | flops | bytes accessed | tf_op | source)
XLA Modules:
  0.0 874.8 jit_solution(10125297887611244133)
XLA Ops:
  0.0 0.0 copy-start
  0.0 0.7 convert_multiply_fusion
  0.7 4.5 broadcast_multiply_fusion
  5.2 6.9 copy.32
  12.1 0.5 broadcast.45
  12.6 74.4 %reduce = f32[16384,64]{1,0:T(8,128)} reduce(f32[16384,1,64]{2,1,0:T(1,128)} %bitcast.68, f32[]{:T(128)} %broadcast.45), dimensions={1}, to_apply=%bitcast.55.reduce_sub_computation | reduce | bytes 8388612
  87.0 8.6 reshape.141
  95.6 53.8 %all_to_all.63 = f32[4,1,262144]{2,1,0:T(1,128)} all-to-all(f32[4,1,262144]{2,1,0:T(1,128)} %reshape.141), channel_id=1, replica_groups=mesh['tm'=4,'space'=8] {'tm'}, dimensions={0} | all-to-all | bytes 8388608 | tf_op jit(solution)/shard_map/all_to_all | solution.py:33
  149.4 15.3 %reduce.1 = f32[4,262144]{1,0:T(4,128)} reduce(f32[4,1,262144]{2,1,0:T(1,128)} %all_to_all.63, f32[]{:T(128)} %broadcast.45), dimensions={1}, to_apply=%all_to_all.46.reduce_sub_computation | reduce | bytes 8388612 | tf_op jit(solution)/shard_map/all_to_all | solution.py:33
  164.7 19.9 %reshape.142 = f32[16384,1,64]{2,1,0:T(1,128)} reshape(f32[4,262144]{1,0:T(4,128)} %reduce.1) | data formatting | bytes 8388608
  184.7 0.0 copy-start.5
  184.7 8.1 copy.53
  192.7 4.6 copy.34
  197.3 0.0 copy-done.5
  197.4 15.5 %convolution_bitcast_fusion.1 = f32[2,256,4096]{1,2,0:T(8,128)} fusion(f32[256,4096,1]{1,0,2:T(8,128)S(1)} %bitcast.76, f32[2,256,256]{2,1,0:T(8,128)S(1)} %copy-done.5), kind=kOutput, calls=%fused_computation.22 | convolution fusion | flops 6442450944 | bytes 13107200 | tf_op jit(solution)/shard_map/pjn,qnc->pqjc/dot_general | solution.py:34
  212.8 13.4 %copy.36 = f32[2,256,4096]{2,0,1:T(2,128)} copy(f32[2,256,4096]{1,2,0:T(8,128)} %convolution_bitcast_fusion.1) | data formatting | bytes 16777216 | tf_op jit(solution)/shard_map/squeeze | solution.py:26
  226.2 0.0 copy-start.6
  226.2 6.2 all-to-all-start.1
  232.4 0.0 copy-done.6
  232.4 0.1 constant_dynamic-slice_fusion
  232.5 91.1 %all-to-all-done.1 = f32[2,256,4096]{2,0,1:T(2,128)} async-done(((f32[2,256,4096]{2,0,1:T(2,128)}), f32[2,256,4096]{2,0,1:T(2,128)}, u32[]{:S(2)}, u32[]{:S(2)}) %all-to-all-start.1) | async-done | bytes 8388640 | tf_op jit(solution)/shard_map/all_to_all | solution.py:36
  323.6 8.3 copy.37
  331.9 0.0 copy-start.1
  331.9 3.2 fusion.12
  335.1 1.5 copy-done.1
  336.6 4.7 copy.39
  341.2 6.2 squeeze.7
  347.4 6.8 copy.40
  354.3 6.1 squeeze.8
  360.4 4.8 multiply_subtract_fusion.1
  365.2 0.0 copy-start.2
  365.2 0.0 copy-start.4
  365.2 3.8 fusion.6
  369.0 1.0 copy-done.2
  370.1 0.9 copy-done.4
  370.9 1.9 collective-permute-start
  372.8 2.4 collective-permute-start.1
  375.2 12.0 %copy.38 = f32[2,64,4,4096]{3,2,1,0:T(4,128)} copy(f32[2,64,4,4096]{3,1,2,0:T(8,128)} %bitcast.66) | data formatting | bytes 16777216 | tf_op jit(solution)/shard_map/all_to_all | solution.py:36
  387.3 11.2 %reshape.136 = f32[2,64,2,32,256]{4,3,2,1,0:T(8,128)} reshape(f32[2,64,4,4096]{3,2,1,0:T(4,128)} %copy.38) | data formatting | bytes 16777216 | tf_op jit(solution)/shard_map/reshape | solution.py:71
  398.5 8.5 pad_maximum_fusion.1
  407.0 12.1 %collective-permute-done = f32[2,64,1,32,256]{4,3,2,1,0:T(8,128)} collective-permute-done((f32[2,64,1,32,256]{4,3,2,1,0:T(8,128)}, f32[2,64,1,32,256]{4,3,2,1,0:T(8,128)}, u32[]{:S(2)}, u32[]{:S(2)}) %collective-permute-start) | collective-permute-done | bytes 4194336 | tf_op jit(solution)/shard_map/ppermute | solution.py:17
  419.2 3.8 collective-permute-done.1
  423.0 0.0 copy-done.3
  423.0 21.6 %fusion.4 = f32[2,64,2,32,256]{4,3,2,1,0:T(8,128)} fusion(f32[2,64,2,32,256]{4,3,2,1,0:T(8,128)} %reshape.136, f32[2,64,2,32,256]{4,3,2,1,0:T(8,128)} %pad_maximum_fusion.1, f32[2,64,1,32,256]{4,3,2,1,0:T(8,128)} %collective-permute-done.1, f32[1,64,2,32,256]{4,3,2,1,0:T(8,128)} %copy-done.4, f32[1,64,2,32,256]{4,3,2,1,0:T(8,128)S(1)} %copy-done.3, ...), kind=kLoop, calls=%fused_computation.15 | loop fusion | flops 20971520 | bytes 41943040 | tf_op jit(solution)/shard_map/add | solution.py:74
  444.6 6.5 multiply_subtract_fusion
  451.0 7.0 copy.55
  458.0 6.9 copy.56
  465.0 21.3 %fusion.13 = f32[16384,2,64]{2,1,0:T(2,128)} fusion(f32[1,64,16384]{1,0,2:T(1,128)} %bitcast.74, f32[1,64,16384]{1,0,2:T(1,128)} %bitcast.73), kind=kLoop, calls=%fused_computation.45 | loop fusion | flops 2097152 | bytes 16777216
  486.3 21.0 %reshape.143 = f32[4,1,524288]{2,1,0:T(1,128)} reshape(f32[16384,2,64]{2,1,0:T(2,128)} %fusion.13) | data formatting | bytes 16777216
  507.3 100.0 %all_to_all.64 = f32[4,1,524288]{2,1,0:T(1,128)} all-to-all(f32[4,1,524288]{2,1,0:T(1,128)} %reshape.143), channel_id=1, replica_groups=mesh['tm'=4,'space'=8] {'tm'}, dimensions={0} | all-to-all | bytes 16777216 | tf_op jit(solution)/shard_map/all_to_all | solution.py:33
  607.2 28.5 %reduce.2 = f32[4,524288]{1,0:T(4,128)} reduce(f32[4,1,524288]{2,1,0:T(1,128)} %all_to_all.64, f32[]{:T(128)} %broadcast.45), dimensions={1}, to_apply=%all_to_all.52.reduce_sub_computation | reduce | bytes 16777220 | tf_op jit(solution)/shard_map/all_to_all | solution.py:33
  635.7 34.4 %reshape.144 = f32[16384,2,64]{2,1,0:T(2,128)} reshape(f32[4,524288]{1,0:T(4,128)} %reduce.2) | data formatting | bytes 16777216
  670.1 23.2 %copy.57 = f32[2,64,4,4096]{3,2,1,0:T(4,128)} copy(f32[2,64,4,4096]{1,0,3,2:T(2,128)} %bitcast.67) | data formatting | bytes 16777216 | tf_op jit(solution)/shard_map/all_to_all | solution.py:33
  693.2 8.2 copy.44
  701.5 0.0 copy-done
  701.5 28.4 %convolution_bitcast_fusion = f32[2,2,256,4096]{2,3,0,1:T(8,128)S(1)} fusion(f32[2,256,4096,1]{2,1,3,0:T(8,128)S(1)} %bitcast.70, f32[2,256,256]{2,1,0:T(8,128)S(1)} %copy-done), kind=kOutput, calls=%fused_computation.10 | convolution fusion | flops 12884901888 | bytes 25690112 | tf_op jit(solution)/shard_map/pjn,qnc->pqjc/dot_general | solution.py:34
  729.9 0.5 fusion.8
  730.4 0.5 fusion.10
  731.0 3.9 pad_maximum_fusion.6
  734.9 13.4 %copy.48 = f32[2,256,4096]{2,0,1:T(2,128)} copy(f32[2,256,4096]{1,2,0:T(8,128)} %pad_maximum_fusion.6) | data formatting | bytes 16777216 | tf_op jit(solution)/shard_map/stack | solution.py:27
  748.3 95.1 %all_to_all.65 = f32[2,256,4096]{2,0,1:T(2,128)S(1)} all-to-all(f32[2,256,4096]{2,0,1:T(2,128)} %copy.48), channel_id=1, replica_groups=mesh['tm'=4,'space'=8] {'tm'}, dimensions={1} | all-to-all | bytes 16777216 | tf_op jit(solution)/shard_map/all_to_all | solution.py:36
  843.4 8.3 copy.49
  851.7 12.0 %copy.50 = f32[2,64,4,4096]{3,2,1,0:T(4,128)} copy(f32[2,64,4,4096]{3,1,2,0:T(8,128)} %bitcast.72) | data formatting | bytes 16777216 | tf_op jit(solution)/shard_map/all_to_all | solution.py:36
  863.7 10.9 %reshape.137 = f32[2,64,2,32,256]{4,3,2,1,0:T(8,128)} reshape(f32[2,64,4,4096]{3,2,1,0:T(4,128)} %copy.50) | data formatting | bytes 16777216 | tf_op jit(solution)/shard_map/reshape | solution.py:76
  (3 shorter events, 0.0 us)
Async XLA Ops:
  0.0 701.5 %copy-start = (f32[2,256,256]{2,1,0:T(8,128)S(1)}, f32[2,256,256]{2,1,0:T(8,128)}, u32[]{:S(2)}) copy-start(f32[2,256,256]{2,1,0:T(8,128)} %param.8) | copy-start | bytes 1572868
  184.7 12.7 %copy-start.5 = (f32[2,256,256]{2,1,0:T(8,128)S(1)}, f32[2,256,256]{2,1,0:T(8,128)}, u32[]{:S(2)}) copy-start(f32[2,256,256]{2,1,0:T(8,128)} %param.7) | copy-start | bytes 1572868
  226.2 6.2 copy-start.6
  226.2 97.4 %all-to-all-start.1 = ((f32[2,256,4096]{2,0,1:T(2,128)}), f32[2,256,4096]{2,0,1:T(2,128)}, u32[]{:S(2)}, u32[]{:S(2)}) async-start(f32[2,256,4096]{2,0,1:T(2,128)} %copy.36), calls=%async_computation.1 | async-start | bytes 16777216 | tf_op jit(solution)/shard_map/all_to_all | solution.py:36
  331.9 4.7 copy-start.1
  365.2 4.9 copy-start.2
  365.2 5.7 copy-start.4
  370.9 48.2 %collective-permute-start = (f32[2,64,1,32,256]{4,3,2,1,0:T(8,128)}, f32[2,64,1,32,256]{4,3,2,1,0:T(8,128)}, u32[]{:S(2)}, u32[]{:S(2)}) collective-permute-start(f32[2,64,1,32,256]{4,3,2,1,0:T(8,128)} %get-tuple-element.11), channel_id=1, source_target_pairs={{1,0},{2,1},{3,2},{4,3},{5,4},{6,5},{7,6},{9,8},{10,9},{11,10},{12... | collective-permute-start | bytes 12582920 | tf_op jit(solution)/shard_map/ppermute | solution.py:17
  372.8 50.1 %collective-permute-start.1 = (f32[2,64,1,32,256]{4,3,2,1,0:T(8,128)}, f32[2,64,1,32,256]{4,3,2,1,0:T(8,128)}, u32[]{:S(2)}, u32[]{:S(2)}) collective-permute-start(f32[2,64,1,32,256]{4,3,2,1,0:T(8,128)} %get-tuple-element.12), channel_id=1, source_target_pairs={{0,1},{1,2},{2,3},{3,4},{4,5},{5,6},{6,7},{8,9},{9,10},{10,11},{11... | collective-permute-start | bytes 12582920 | tf_op jit(solution)/shard_map/ppermute | solution.py:15
  398.5 24.5 %copy-start.3 = (f32[1,64,2,32,256]{4,3,2,1,0:T(8,128)S(1)}, f32[1,64,2,32,256]{4,3,2,1,0:T(8,128)}, u32[]{:S(2)}) copy-start(f32[1,64,2,32,256]{4,3,2,1,0:T(8,128)} %copy-done.2) | copy-start | bytes 12582916
where the time goes:
time: 884 us; the launch traced here: 875 us
  local copies, waits for them, and re-layouts  269 us (30%)
  blocking collectives  249 us (28%)
  other arithmetic  195 us (22%)
  waiting for transfers between devices  107 us (12%)
  matrix products  43.8 us (5%)
  starting transfers between devices  10.5 us (1%)
    all_to_all x2, blocking collectives, transform(): moved = lax.all_to_all(data, 'tm', split_axis=2, concat_axis=1, tiled=True)  154 us
    unnamed x2, other arithmetic  95.7 us
    all_to_all x1, blocking collectives, transform(): back = lax.all_to_all(mixed, 'tm', split_axis=1, concat_axis=2, tiled=True)  95.1 us
    all_to_all x1, waiting for transfers between devices, transform(): back = lax.all_to_all(mixed, 'tm', split_axis=1, concat_axis=2, tiled=True)  91.1 us
    unnamed x19, local copies, waits for them, and re-layouts  87.8 us
    all_to_all x4, local copies, waits for them, and re-layouts, transform(): moved = lax.all_to_all(data, 'tm', split_axis=2, concat_axis=1, tiled=True)  44.1 us
    dot_general x2, matrix products, transform(): prod = jnp.einsum('pjn,qnc->pqjc', matrix, moved, precision=highest)  43.8 us
    all_to_all x2, other arithmetic, transform(): moved = lax.all_to_all(data, 'tm', split_axis=2, concat_axis=1, tiled=True)  43.8 us
  transfers between devices with their start and end apart: 3, of which 3 were waited for; matrix products, arithmetic and copies ran while one was open for 4% of the time, Pallas kernels for 0%

commit v1 on v0

v1 whole, which is shorter than its diff:
```python
import functools

import jax
import jax.numpy as jnp
from jax import lax
from jax.experimental import pallas as pl
from jax.experimental.pallas import tpu as pltpu
from jax.sharding import PartitionSpec as P


CUTS = 2


def block_row(stream, side, row, depth, rows_x):
    if stream == 0:
        return row + side * (rows_x - 1 - 2 * row)
    return depth * (1 + side) + row


def chunk_rows(stream, chunk, depth):
    high = depth // CUTS
    first = chunk * high + 1 if chunk else (0 if stream == 0 else -1)
    return list(range(first, (chunk + 1) * high + 1))


def spread_kernel(depth, planes, sides_ref, ratio_ref, in_ref, *outs):
    steps, _, rows_x, _ = in_ref.shape
    flat = in_ref.reshape(steps * planes * rows_x, in_ref.shape[3])
    ratio = ratio_ref[...]
    place = 0
    for stream in range(2):
        for other in range(2):
            side = sides_ref[stream] if other == 0 else 1 - sides_ref[stream]
            for chunk in range(CUTS):
                out = outs[place]
                place += 1
                for at, row in enumerate(chunk_rows(stream, chunk, depth)):
                    x = block_row(stream, side, row, depth, rows_x)
                    for z in range(planes):
                        part = flat[pl.ds(z * rows_x + x, steps, stride=planes * rows_x), :]
                        out[at, z] = part * ratio


def spread(residual, ratio, sides, depth):
    steps, planes, rows_x, rows_y = residual.shape
    lanes = 128
    block = min(steps, 32)
    shapes, specs = [], []
    for stream in range(2):
        for _ in range(2):
            for chunk in range(CUTS):
                count = len(chunk_rows(stream, chunk, depth))
                shapes.append(jax.ShapeDtypeStruct((count, planes, steps, rows_y), jnp.float32))
                specs.append(pl.BlockSpec((count, planes, block, lanes), lambda i, j: (0, 0, i, j)))
    outs = pl.pallas_call(
        functools.partial(spread_kernel, depth, planes),
        out_shape=shapes,
        grid=(steps // block, rows_y // lanes),
        in_specs=[
            pl.BlockSpec(memory_space=pltpu.SMEM),
            pl.BlockSpec((block, 1), lambda i, j: (i, 0)),
            pl.BlockSpec((block, planes, rows_x, lanes), lambda i, j: (i, 0, 0, j)),
        ],
        out_specs=specs,
        compiler_params=pltpu.CompilerParams(vmem_limit_bytes=48 * 2**20),
        cost_estimate=pl.CostEstimate(flops=residual.size * 2, bytes_accessed=residual.size * 10, transcendentals=0),
        name="spread",
    )(sides, ratio, residual)
    outs = list(outs)
    return [[outs[(2 * s + o) * CUTS : (2 * s + o + 1) * CUTS] for o in range(2)] for s in range(2)]


def halves(value):
    high = value.astype(jnp.bfloat16)
    return high, (value - high.astype(jnp.float32)).astype(jnp.bfloat16)


def apply_kernel(stream, chunk, depth, planes, groups, near_ref, far_ref, *refs):
    outs = refs[-4:]
    raws = refs[:-4]
    count = len(raws) // groups
    own_ref, send_ref, down_ref, up_ref = outs
    rows_y = own_ref.shape[-1]
    where = {}
    for c in range(count):
        for at, row in enumerate(chunk_rows(stream, chunk - count + 1 + c, depth)):
            where[row] = (c, at)

    def load(row, z):
        if row not in where:
            return None
        c, at = where[row]
        return jnp.concatenate([raws[c * groups + g][at, z] for g in range(groups)], axis=0)

    near, far = near_ref[...], far_ref[...]
    half = near.shape[0] // 2
    high = depth // CUTS
    for at in range(high):
        row = chunk * high + at
        across = []
        for z in range(planes):
            mid = load(row, z)
            lane = lax.broadcasted_iota(jnp.int32, mid.shape, 1)
            total = jnp.where(lane == 0, 0.0, pltpu.roll(mid, 1, 1))
            total = total + jnp.where(lane == rows_y - 1, 0.0, pltpu.roll(mid, rows_y - 1, 1))
            for beside in (load(row - 1, z), load(row + 1, z)):
                if beside is not None:
                    total = total + beside
            mid_h, mid_l = halves(mid)
            sum_h, sum_l = halves(total)
            thick = jnp.concatenate([mid_h, mid_h, mid_l, sum_h, sum_h, sum_l], axis=0)
            thin = jnp.concatenate([mid_h, mid_h, mid_l], axis=0)
            value = jnp.dot(near, thick, preferred_element_type=jnp.float32)
            own_ref[at, z] = value[:half]
            send_ref[at, z] = value[half:]
            across.append(jnp.dot(far, thin, preferred_element_type=jnp.float32))
        down_ref[0, at] = across[0][:half]
        down_ref[1, at] = across[0][half:]
        up_ref[0, at] = across[-1][:half]
        up_ref[1, at] = across[-1][half:]
        for z in range(planes):
            for beside in across[max(z - 1, 0) : z] + across[z + 1 : z + 2]:
                own_ref[at, z] += beside[:half]
                send_ref[at, z] += beside[half:]


def apply(stream, chunk, depth, near, far, raws):
    groups = len(raws[0])
    _, planes, steps, rows_y = raws[0][0].shape
    high = depth // CUTS
    half = near.shape[0] // 2
    flat = [r for chunk_raws in raws for r in chunk_raws]
    shapes = [jax.ShapeDtypeStruct((high, planes, half, rows_y), jnp.float32)] * 2
    shapes += [jax.ShapeDtypeStruct((2, high, half, rows_y), jnp.float32)] * 2
    flops = 2 * high * planes * rows_y * (near.size + far.size)
    return pl.pallas_call(
        functools.partial(apply_kernel, stream, chunk, depth, planes, groups),
        out_shape=shapes,
        in_specs=[pl.BlockSpec(memory_space=pltpu.VMEM)] * (2 + len(flat)),
        out_specs=[pl.BlockSpec(memory_space=pltpu.VMEM)] * 4,
        compiler_params=pltpu.CompilerParams(vmem_limit_bytes=48 * 2**20),
        cost_estimate=pl.CostEstimate(flops=flops, bytes_accessed=12 * 2**20, transcendentals=0),
        name="apply",
    )(near, far, *flat)


def add_kernel(send_ref, low_ref, high_ref, out_ref):
    planes = out_ref.shape[1]
    for z in range(planes):
        value = send_ref[:, z]
        if z == 0:
            value = value + low_ref[0]
        if z == planes - 1:
            value = value + high_ref[0]
        out_ref[:, z] = value


def add_far(send, low, high):
    count, planes, half, rows_y = send.shape
    return pl.pallas_call(
        add_kernel,
        out_shape=jax.ShapeDtypeStruct(send.shape, jnp.float32),
        grid=(count,),
        in_specs=[
            pl.BlockSpec((1, planes, half, rows_y), lambda i: (i, 0, 0, 0)),
            pl.BlockSpec((1, 1, half, rows_y), lambda i: (1, i, 0, 0)),
            pl.BlockSpec((1, 1, half, rows_y), lambda i: (1, i, 0, 0)),
        ],
        out_specs=pl.BlockSpec((1, planes, half, rows_y), lambda i: (i, 0, 0, 0)),
        cost_estimate=pl.CostEstimate(flops=send.size, bytes_accessed=send.size * 12, transcendentals=0),
        name="add_far",
    )(send, low, high)


def gather_kernel(depth, sides_ref, *refs):
    out_ref = refs[-1]
    place = 0
    count, planes, rows_x, lanes = out_ref.shape
    flat = out_ref.reshape(count * planes * rows_x, lanes)
    high = depth // CUTS
    for stream in range(2):
        side = sides_ref[stream]
        for chunk in range(CUTS):
            own, low, up, got = refs[place : place + 4]
            place += 4
            for at in range(high):
                row = chunk * high + at
                x = block_row(stream, side, row, depth, rows_x)
                y = block_row(stream, 1 - side, row, depth, rows_x)
                for z in range(planes):
                    value = own[at, z]
                    if z == 0:
                        value = value + low[0, at]
                    if z == planes - 1:
                        value = value + up[0, at]
                    flat[pl.ds(z * rows_x + x, count, stride=planes * rows_x), :] = value
                    flat[pl.ds(z * rows_x + y, count, stride=planes * rows_x), :] = got[at, z]


def collect(parts, sides, depth, rows_x):
    high, planes, half, rows_y = parts[0][0].shape
    lanes = 128
    block = min(half, 32)
    cells = pl.BlockSpec((high, planes, block, lanes), lambda i, j: (0, 0, i, j))
    edge = pl.BlockSpec((1, high, block, lanes), lambda i, j: (0, 0, i, j))
    flat = [a for part in parts for a in part]
    return pl.pallas_call(
        functools.partial(gather_kernel, depth),
        out_shape=jax.ShapeDtypeStruct((half, planes, rows_x, rows_y), jnp.float32),
        grid=(half // block, rows_y // lanes),
        in_specs=[pl.BlockSpec(memory_space=pltpu.SMEM)] + [cells, edge, edge, cells] * len(parts),
        out_specs=pl.BlockSpec((block, planes, rows_x, lanes), lambda i, j: (i, 0, 0, j)),
        compiler_params=pltpu.CompilerParams(vmem_limit_bytes=48 * 2**20),
        name="collect",
    )(sides, *flat)


def make_maps(forward_map, back_map, eigen_values, me, count, bits):
    steps = forward_map.shape[1]
    local_steps = steps // count
    highest = lax.Precision.HIGHEST
    real_part = 6.0 + eigen_values[0]
    imag_part = eigen_values[1]
    denom = real_part * real_part + imag_part * imag_part
    coef_re = (real_part / denom)[:, None]
    coef_im = (-imag_part / denom)[:, None]
    order = jnp.bitwise_xor(me, jnp.arange(count))
    ahead = forward_map.reshape(2, steps, count, local_steps)
    ahead = jnp.take(ahead, order, axis=2).reshape(2, steps, steps)
    once_re = coef_re * ahead[0] - coef_im * ahead[1]
    once_im = coef_re * ahead[1] + coef_im * ahead[0]
    twice_re = coef_re * once_re - coef_im * once_im
    twice_im = coef_re * once_im + coef_im * once_re
    right = jnp.concatenate(
        [jnp.concatenate([once_re, twice_re], axis=1), jnp.concatenate([once_im, twice_im], axis=1)], axis=0
    )
    blocks = jnp.stack([me, jnp.bitwise_xor(me, bits[0]), jnp.bitwise_xor(me, bits[1])])
    back = jnp.take(back_map.reshape(2, count, local_steps, steps), blocks, axis=1)
    left_re = jnp.concatenate([back[0], -back[1]], axis=2)
    left_im = jnp.concatenate([back[1], back[0]], axis=2)
    left = jnp.stack([left_re, left_im], axis=1).reshape(3, 2 * local_steps, 2 * steps)
    maps = jnp.einsum("bmk,kn->bmn", left, right, precision=highest)
    maps = [jnp.concatenate([maps[0], maps[1 + s]], axis=0) for s in range(2)]
    result = []
    for both in maps:
        one_h, one_l = halves(both[:, :steps])
        two_h, two_l = halves(both[:, steps:])
        near = jnp.concatenate([one_h, one_l, one_h, two_h, two_l, two_h], axis=1)
        far = jnp.concatenate([two_h, two_l, two_h], axis=1)
        result.append((near, far))
    return result


def local(residual, step_ratio, forward_map, back_map, eigen_values):
    local_steps, planes, rows_x, rows_y = residual.shape
    depth = rows_x // 4
    count = lax.axis_size("tm")
    bits = (1, count // 2)
    all_bits = [1 << k for k in range(count.bit_length() - 1)]
    me = lax.axis_index("tm")
    sides = jnp.stack([jnp.where(jnp.bitwise_and(me, b) > 0, 1, 0) for b in bits]).astype(jnp.int32)
    ratio = (step_ratio.astype(jnp.float32) / 8.0)[:, None]

    def swap(data, bit):
        return lax.ppermute(data, "tm", [(i, i ^ bit) for i in range(count)])

    spaces = lax.axis_size("space")
    upward = [(i, i + 1) for i in range(spaces - 1)]
    downward = [(i + 1, i) for i in range(spaces - 1)]

    raws = spread(residual, ratio, sides, depth)
    maps = make_maps(forward_map, back_map, eigen_values, me, count, bits)

    held = [[None] * CUTS for _ in range(2)]
    for chunk in range(CUTS):
        for stream in range(2):
            keep, send = raws[stream][0][chunk], raws[stream][1][chunk]
            have = {0: keep, bits[stream]: swap(send, bits[stream])}
            for bit in all_bits:
                if bit != bits[stream]:
                    have.update({mask | bit: swap(have[mask], bit) for mask in list(have)})
            held[stream][chunk] = [have[mask] for mask in range(count)]

    parts = [[None] * CUTS for _ in range(2)]
    for chunk in range(CUTS):
        for stream in range(2):
            near, far = maps[stream]
            used = held[stream][max(chunk - 1, 0) : chunk + 1]
            own, send, down, up = apply(stream, chunk, depth, near, far, used)
            low = lax.ppermute(up, "space", upward)
            high = lax.ppermute(down, "space", downward)
            got = swap(add_far(send, low, high), bits[stream])
            parts[stream][chunk] = (own, low, high, got)

    flat = [parts[s][c] for s in range(2) for c in range(CUTS)]
    result = collect(flat, sides, depth, rows_x)
    return result.reshape(2, local_steps, planes, rows_x, rows_y)


def solution(mesh):
    in_specs = (P("tm", "space", None, None), P("tm"), P(), P(), P())
    out_specs = P(None, "tm", "space", None, None)
    return jax.shard_map(local, mesh=mesh, in_specs=in_specs, out_specs=out_specs, check_vma=False)
```

time: 884 us -> 217 us (0.25)
  local copies, waits for them, and re-layouts: 269 us -> 17.7 us
  blocking collectives: 249 us -> 0 us
  other arithmetic: 195 us -> 5.79 us
  Pallas kernels: 0 us -> 55.6 us
  matrix products: 43.8 us -> 2.57 us
  starting transfers between devices: 10.5 us -> 38.6 us
  waiting for transfers between devices: 107 us -> 92.8 us
    all_to_all x3 -> x0, blocking collectives: 249 us -> none  [the longest x2 154 us: transform(): moved = lax.all_to_all(data, 'tm', split_axis=2, concat_axis=1, tiled=True)]
    unnamed x2 -> x6, other arithmetic: 95.7 us -> 0.22 us
    all_to_all x1 -> x0, waiting for transfers between devices: 91.1 us -> none  [transform(): back = lax.all_to_all(mixed, 'tm', split_axis=1, concat_axis=2, tiled=True)]
    all_to_all x8 -> x0, local copies, waits for them, and re-layouts: 84.7 us -> none  [the longest x4 44.1 us: transform(): moved = lax.all_to_all(data, 'tm', split_axis=2, concat_axis=1, tiled=True)]
    unnamed x19 -> x39, local copies, waits for them, and re-layouts: 87.8 us -> 10.5 us
    ppermute x2 -> x24, waiting for transfers between devices: 16 us -> 92.8 us  [the longest x16 88.9 us: swap(): return lax.ppermute(data, 'tm', [(i, i ^ bit) for i in range(count)])]
    pallas_call x0 -> x10, Pallas kernels: none -> 55.6 us  [the longest x4 22.6 us: apply(): pl.pallas_call(functools.partial(apply_kernel, stream, chunk, depth, plan...]
    all_to_all x2 -> x0, other arithmetic: 43.8 us -> none  [transform(): moved = lax.all_to_all(data, 'tm', split_axis=2, concat_axis=1, tiled=True)]
  transfers between devices with their start and end apart: 3 -> 24, of which waited for: 3 -> 9; matrix products, arithmetic and copies ran while one was open for 4% -> 7% of each run, Pallas kernels for 0% -> 17%
where the time goes in v1:
time: 217 us; the launch traced here: 214 us
  waiting for transfers between devices  92.8 us (43%)
  Pallas kernels  55.6 us (26%)
  starting transfers between devices  38.6 us (18%)
  local copies, waits for them, and re-layouts  17.7 us (8%)
  other arithmetic  5.79 us (3%)
  matrix products  2.57 us (1%)
    ppermute x16, waiting for transfers between devices, swap(): return lax.ppermute(data, 'tm', [(i, i ^ bit) for i in range(count)])  88.9 us
    pallas_call x4, Pallas kernels, apply(): pl.pallas_call(functools.partial(apply_kernel, stream, chunk, depth, plan...  22.6 us
    ppermute x16, starting transfers between devices, swap(): return lax.ppermute(data, 'tm', [(i, i ^ bit) for i in range(count)])  18.5 us
    pallas_call x4, Pallas kernels, add_far(): pl.pallas_call(add_kernel, out_shape=jax.ShapeDtypeStruct(send.shape, jnp...  14.3 us
    pallas_call x1, Pallas kernels, collect(): pl.pallas_call(functools.partial(gather_kernel, depth), out_shape=jax.Sha...  12.8 us
    ppermute x4, starting transfers between devices, local(): high = lax.ppermute(down, 'space', downward)  12.2 us
    unnamed x39, local copies, waits for them, and re-layouts  10.5 us
    ppermute x4, starting transfers between devices, local(): low = lax.ppermute(up, 'space', upward)  7.91 us
  transfers between devices with their start and end apart: 24, of which 9 were waited for; matrix products, arithmetic and copies ran while one was open for 7% of the time, Pallas kernels for 17%

profile of v1, /device:TPU:8, one launch (start us, length us, event | category | flops | bytes accessed | tf_op | source)
XLA Modules:
  0.0 213.5 jit_solution(11089748109067461520)
XLA Ops:
  0.0 0.7 multiply_bitcast_fusion
  0.9 5.9 %spread.1 = (f32[5,2,64,256]{3,2,1,0:T(8,128)S(1)}, f32[4,2,64,256]{3,2,1,0:T(8,128)}, f32[5,2,64,256]{3,2,1,0:T(8,128)}, f32[4,2,64,256]{3,2,1,0:T(8,128)}, f32...) custom-call(s32[2]{0:T(128)S(1)} %pad_add_fusion.sides_ref, ...), custom_call_target="tpu_custom_call" | custom-call | flops 2097152 | bytes 10485760 | tf_op jit(solution)/shard_map/spread/pallas_call | solution.py:55
  6.8 0.8 copy-done.13
  7.6 1.5 collective-permute-start.6
  9.1 1.5 collective-permute-start.7
  10.6 0.5 collective-permute-start
  11.6 1.5 collective-permute-start.13
  13.3 1.3 gather_fusion
  14.7 1.1 select_bitcast_fusion.1
  15.8 0.8 slice_add_fusion
  16.7 0.9 copy.9
  17.7 1.2 copy.10
  18.9 1.4 gather_fusion.1
  20.3 1.2 select_bitcast_fusion
  21.5 0.7 fusion.25
  22.2 1.8 copy.12
  24.0 0.8 copy.11
  24.9 1.2 multiply_subtract_fusion
  26.2 2.6 %fusion = f32[3,128,512]{2,1,0:T(8,128)S(1)} fusion(f32[3,128,512]{2,1,0:T(8,128)} %bitcast.51, f32[256,256]{1,0:T(8,128)S(1)} %multiply_add_fusion, f32[256,256]{1,0:T(8,128)S(1)} %get-tuple-element.66, f32[256,256]{1,0:T(8,128)S(1)} %get-tuple-element.65, f32[256,256]{1,0:T(8,128)S(1)} %get-tuple-element.67), kind=kOutput, calls=%fused_computation.3 | convolution fusion | flops 1208745984 | bytes 2621440 | tf_op jit(solution)/shard_map/bmk,kn->bmn/dot_general | solution.py:242
  29.0 6.6 %collective-permute-done.refs_1_ = f32[5,2,64,256]{3,2,1,0:T(8,128)} collective-permute-done((f32[5,2,64,256]{3,2,1,0:T(8,128)}, f32[5,2,64,256]{3,2,1,0:T(8,128)}, u32[]{:S(2)}, u32[]{:S(2)}) %collective-permute-start) | collective-permute-done | bytes 655392 | tf_op jit(solution)/shard_map/ppermute | solution.py:265
  35.6 1.5 collective-permute-start.2
  37.2 1.6 collective-permute-start.12
  38.8 0.5 collective-permute-start.8
  39.4 1.6 collective-permute-start.19
  41.0 28.1 %collective-permute-done.2.refs_3_ = f32[5,2,64,256]{3,2,1,0:T(8,128)S(1)} collective-permute-done((f32[5,2,64,256]{3,2,1,0:T(8,128)}, f32[5,2,64,256]{3,2,1,0:T(8,128)S(1)}, u32[]{:S(2)}, u32[]{:S(2)}) %collective-permute-start.2) | collective-permute-done | bytes 655392 | tf_op jit(solution)/shard_map/ppermute | solution.py:265
  69.1 0.5 collective-permute-start.18
  69.6 5.0 %apply.4 = (f32[4,2,128,256]{3,2,1,0:T(8,128)S(1)}, f32[4,2,128,256]{3,2,1,0:T(8,128)S(1)}, f32[2,4,128,256]{3,2,1,0:T(8,128)}, f32[2,4,128,256]{3,2,1,0:T(8,128)}) custom-call(bf16[256,1536]{1,0:T(8,128)(2,1)S(1)} %constant_dynamic-update-slice_fusion.near_ref, bf16[256,768]{1,0:T(8,128)(2,1)S(1)} %pad_maximum_fusion.1.far_ref, ...), custom_call_target="tpu_custom_call" | custom-call | flops 2415919104 | bytes 12582912 | tf_op jit(solution)/shard_map/apply/pallas_call | solution.py:136
  74.7 1.0 copy-done.6
  75.7 1.0 copy-done.10
  76.7 1.5 collective-permute-start.14
  78.2 2.1 collective-permute-done.8.refs_7_
  80.3 1.9 collective-permute-start.3
  82.2 6.4 %apply.5 = (f32[4,2,128,256]{3,2,1,0:T(8,128)}, f32[4,2,128,256]{3,2,1,0:T(8,128)}, f32[2,4,128,256]{3,2,1,0:T(8,128)}, f32[2,4,128,256]{3,2,1,0:T(8,128)}) custom-call(bf16[256,1536]{1,0:T(8,128)(2,1)S(1)} %constant_dynamic-update-slice_fusion.near_ref, bf16[256,768]{1,0:T(8,128)(2,1)S(1)} %pad_maximum_fusion.1.far_ref, ...), custom_call_target="tpu_custom_call" | custom-call | flops 2415919104 | bytes 12582912 | tf_op jit(solution)/shard_map/apply/pallas_call | solution.py:136
  88.6 1.5 collective-permute-done.19.refs_6_
  90.1 2.1 %collective-permute-start.4 = (f32[2,4,128,256]{3,2,1,0:T(8,128)S(1)}, f32[2,4,128,256]{3,2,1,0:T(8,128)S(1)}, u32[]{:S(2)}, u32[]{:S(2)}) collective-permute-start(f32[2,4,128,256]{3,2,1,0:T(8,128)S(1)} %copy-done.17), channel_id=1, source_target_pairs={{1,0},{2,1},{3,2},{4,3},{5,4},{6,5},{7,6},{9,8},{10,9},{11,10},{12... | collective-permute-start | bytes 3145736 | tf_op jit(solution)/shard_map/ppermute | solution.py:291
  92.2 2.2 %collective-permute-start.9 = (f32[2,4,128,256]{3,2,1,0:T(8,128)}, f32[2,4,128,256]{3,2,1,0:T(8,128)}, u32[]{:S(2)}, u32[]{:S(2)}) collective-permute-start(f32[2,4,128,256]{3,2,1,0:T(8,128)} %get-tuple-element.38), channel_id=1, source_target_pairs={{0,1},{1,2},{2,3},{3,4},{4,5},{5,6},{6,7},{8,9},{9,10},{10,11},{11... | collective-permute-start | bytes 3145736 | tf_op jit(solution)/shard_map/ppermute | solution.py:290
  94.4 0.6 collective-permute-start.20
  95.1 13.8 %collective-permute-done.20.refs_7_ = f32[4,2,64,256]{3,2,1,0:T(8,128)S(1)} collective-permute-done((f32[4,2,64,256]{3,2,1,0:T(8,128)S(1)}, f32[4,2,64,256]{3,2,1,0:T(8,128)S(1)}, u32[]{:S(2)}, u32[]{:S(2)}) %collective-permute-start.20) | collective-permute-done | bytes 524320 | tf_op jit(solution)/shard_map/ppermute | solution.py:265
  108.9 2.7 %collective-permute-start.10 = (f32[2,4,128,256]{3,2,1,0:T(8,128)}, f32[2,4,128,256]{3,2,1,0:T(8,128)}, u32[]{:S(2)}, u32[]{:S(2)}) collective-permute-start(f32[2,4,128,256]{3,2,1,0:T(8,128)} %get-tuple-element.39), channel_id=1, source_target_pairs={{1,0},{2,1},{3,2},{4,3},{5,4},{6,5},{7,6},{9,8},{10,9},{11,10},{12... | collective-permute-start | bytes 3145736 | tf_op jit(solution)/shard_map/ppermute | solution.py:291
  111.7 0.9 copy-done.11
  112.5 6.0 %apply.7 = (f32[4,2,128,256]{3,2,1,0:T(8,128)}, f32[4,2,128,256]{3,2,1,0:T(8,128)}, f32[2,4,128,256]{3,2,1,0:T(8,128)}, f32[2,4,128,256]{3,2,1,0:T(8,128)}) custom-call(bf16[256,1536]{1,0:T(8,128)(2,1)S(1)} %constant_dynamic-update-slice_fusion.5.near_ref, bf16[256,768]{1,0:T(8,128)(2,1)S(1)} %pad_maximum_fusion.2.far_ref, ...), custom_call_target="tpu_custom_call" | custom-call | flops 2415919104 | bytes 12582912 | tf_op jit(solution)/shard_map/apply/pallas_call | solution.py:136
  118.5 1.9 collective-permute-start.21
  120.5 1.1 copy-done.12
  121.6 5.3 %apply.6 = (f32[4,2,128,256]{3,2,1,0:T(8,128)S(1)}, f32[4,2,128,256]{3,2,1,0:T(8,128)}, f32[2,4,128,256]{3,2,1,0:T(8,128)}, f32[2,4,128,256]{3,2,1,0:T(8,128)}) custom-call(bf16[256,1536]{1,0:T(8,128)(2,1)S(1)} %constant_dynamic-update-slice_fusion.5.near_ref, bf16[256,768]{1,0:T(8,128)(2,1)S(1)} %pad_maximum_fusion.2.far_ref, ...), custom_call_target="tpu_custom_call" | custom-call | flops 2415919104 | bytes 12582912 | tf_op jit(solution)/shard_map/apply/pallas_call | solution.py:136
  126.8 1.0 copy-done.9
  127.8 3.6 %collective-permute-start.22 = (f32[2,4,128,256]{3,2,1,0:T(8,128)}, f32[2,4,128,256]{3,2,1,0:T(8,128)}, u32[]{:S(2)}, u32[]{:S(2)}) collective-permute-start(f32[2,4,128,256]{3,2,1,0:T(8,128)} %get-tuple-element.51), channel_id=1, source_target_pairs={{1,0},{2,1},{3,2},{4,3},{5,4},{6,5},{7,6},{9,8},{10,9},{11,10},{12... | collective-permute-start | bytes 3145736 | tf_op jit(solution)/shard_map/ppermute | solution.py:291
  131.5 1.9 collective-permute-start.15
  133.4 3.6 %collective-permute-start.16 = (f32[2,4,128,256]{3,2,1,0:T(8,128)}, f32[2,4,128,256]{3,2,1,0:T(8,128)}, u32[]{:S(2)}, u32[]{:S(2)}) collective-permute-start(f32[2,4,128,256]{3,2,1,0:T(8,128)} %get-tuple-element.45), channel_id=1, source_target_pairs={{1,0},{2,1},{3,2},{4,3},{5,4},{6,5},{7,6},{9,8},{10,9},{11,10},{12... | collective-permute-start | bytes 3145736 | tf_op jit(solution)/shard_map/ppermute | solution.py:291
  137.1 3.6 %add_far.4 = f32[4,2,128,256]{3,2,1,0:T(8,128)} custom-call(f32[4,2,128,256]{3,2,1,0:T(8,128)} %copy-done.10, f32[2,4,128,256]{3,2,1,0:T(8,128)} %copy-done.2, f32[2,4,128,256]{3,2,1,0:T(8,128)} %copy-done.4), custom_call_target="tpu_custom_call" | custom-call | flops 262144 | bytes 3145728 | tf_op jit(solution)/shard_map/add_far/pallas_call | solution.py:160
  140.7 0.8 collective-permute-start.5
  141.4 3.6 %add_far.5 = f32[4,2,128,256]{3,2,1,0:T(8,128)} custom-call(f32[4,2,128,256]{3,2,1,0:T(8,128)} %get-tuple-element.40.send_ref, f32[2,4,128,256]{3,2,1,0:T(8,128)} %collective-permute-done.9.low_ref.refs_5_, f32[2,4,128,256]{3,2,1,0:T(8,128)} %collective-permute-done.10.high_ref.refs_6_), custom_call_target="tpu_custom_call" | custom-call | flops 262144 | bytes 3145728 | tf_op jit(solution)/shard_map/add_far/pallas_call | solution.py:160
  145.0 1.3 collective-permute-start.11
  146.3 3.6 %add_far.7 = f32[4,2,128,256]{3,2,1,0:T(8,128)} custom-call(f32[4,2,128,256]{3,2,1,0:T(8,128)} %get-tuple-element.52.send_ref, f32[2,4,128,256]{3,2,1,0:T(8,128)} %collective-permute-done.21.low_ref.refs_13_, f32[2,4,128,256]{3,2,1,0:T(8,128)} %collective-permute-done.22.high_ref.refs_14_), custom_call_target="tpu_custom_call" | custom-call | flops 262144 | bytes 3145728 | tf_op jit(solution)/shard_map/add_far/pallas_call | solution.py:160
  149.9 1.5 collective-permute-start.23
  151.4 3.9 %collective-permute-done.16.high_ref.refs_10_ = f32[2,4,128,256]{3,2,1,0:T(8,128)} collective-permute-done((f32[2,4,128,256]{3,2,1,0:T(8,128)}, f32[2,4,128,256]{3,2,1,0:T(8,128)}, u32[]{:S(2)}, u32[]{:S(2)}) %collective-permute-start.16) | collective-permute-done | bytes 1048608 | tf_op jit(solution)/shard_map/ppermute | solution.py:291
  155.3 3.6 %add_far.6 = f32[4,2,128,256]{3,2,1,0:T(8,128)} custom-call(f32[4,2,128,256]{3,2,1,0:T(8,128)} %get-tuple-element.46.send_ref, f32[2,4,128,256]{3,2,1,0:T(8,128)} %collective-permute-done.15.low_ref.refs_9_, f32[2,4,128,256]{3,2,1,0:T(8,128)} %collective-permute-done.16.high_ref.refs_10_), custom_call_target="tpu_custom_call" | custom-call | flops 262144 | bytes 3145728 | tf_op jit(solution)/shard_map/add_far/pallas_call | solution.py:160
  158.9 1.5 collective-permute-start.17
  160.4 6.8 %collective-permute-done.5.refs_3_ = f32[4,2,128,256]{3,2,1,0:T(8,128)} collective-permute-done((f32[4,2,128,256]{3,2,1,0:T(8,128)}, f32[4,2,128,256]{3,2,1,0:T(8,128)}, u32[]{:S(2)}, u32[]{:S(2)}) %collective-permute-start.5) | collective-permute-done | bytes 1048608 | tf_op jit(solution)/shard_map/ppermute | solution.py:265
  167.1 21.0 %collective-permute-done.11.refs_7_ = f32[4,2,128,256]{3,2,1,0:T(8,128)} collective-permute-done((f32[4,2,128,256]{3,2,1,0:T(8,128)}, f32[4,2,128,256]{3,2,1,0:T(8,128)}, u32[]{:S(2)}, u32[]{:S(2)}) %collective-permute-start.11) | collective-permute-done | bytes 1048608 | tf_op jit(solution)/shard_map/ppermute | solution.py:265
  188.1 9.0 %collective-permute-done.17.refs_11_ = f32[4,2,128,256]{3,2,1,0:T(8,128)S(1)} collective-permute-done((f32[4,2,128,256]{3,2,1,0:T(8,128)}, f32[4,2,128,256]{3,2,1,0:T(8,128)S(1)}, u32[]{:S(2)}, u32[]{:S(2)}) %collective-permute-start.17) | collective-permute-done | bytes 1048608 | tf_op jit(solution)/shard_map/ppermute | solution.py:265
  197.1 1.0 copy-done.16
  198.2 1.2 copy-done.7
  199.4 1.2 copy-done.8
  200.6 12.8 %collect.1 = f32[128,2,32,256]{3,2,1,0:T(8,128)} custom-call(s32[2]{0:T(128)S(1)} %pad_add_fusion.sides_ref, f32[4,2,128,256]{3,2,1,0:T(8,128)S(1)} %copy-done.7, f32[2,4,128,256]{3,2,1,0:T(8,128)S(1)} %copy-done.3, f32[2,4,128,256]{3,2,1,0:T(8,128)S(1)} %copy-done.5, f32[4,2,128,256]{3,2,1,0:T(8,128)} %collective-permute-done.5.refs_3_, ...), custom_call_target="tpu_custom_call" | custom-call | tf_op jit(solution)/shard_map/collect/pallas_call | solution.py:207
  (69 shorter events, 1.6 us)
Async XLA Ops:
  0.0 13.3 %copy-start = (f32[2,256,256]{2,1,0:T(8,128)S(1)}, f32[2,256,256]{2,1,0:T(8,128)}, u32[]{:S(2)}) copy-start(f32[2,256,256]{2,1,0:T(8,128)} %param.8) | copy-start | bytes 1572868
  6.8 0.8 copy-start.13
  7.6 4.1 %copy-start.15 = (f32[4,2,64,256]{3,2,1,0:T(8,128)}, f32[4,2,64,256]{3,2,1,0:T(8,128)S(1)}, u32[]{:S(2)}) copy-start(f32[4,2,64,256]{3,2,1,0:T(8,128)S(1)} %get-tuple-element.48) | copy-start | bytes 1572868
  7.6 29.7 %collective-permute-start.6 = (f32[4,2,64,256]{3,2,1,0:T(8,128)}, f32[4,2,64,256]{3,2,1,0:T(8,128)}, u32[]{:S(2)}, u32[]{:S(2)}) collective-permute-start(f32[4,2,64,256]{3,2,1,0:T(8,128)} %get-tuple-element.36), channel_id=1, source_target_pairs={{0,8},{8,0},{16,24},{24,16},{1,9},{9,1},{17,25},{25,17},{2,10},{10... | collective-permute-start | bytes 1572872 | tf_op jit(solution)/shard_map/ppermute | solution.py:265
  9.1 29.7 %collective-permute-start.7 = (f32[4,2,64,256]{3,2,1,0:T(8,128)}, f32[4,2,64,256]{3,2,1,0:T(8,128)}, u32[]{:S(2)}, u32[]{:S(2)}) collective-permute-start(f32[4,2,64,256]{3,2,1,0:T(8,128)} %get-tuple-element.35.refs_4_), channel_id=1, source_target_pairs={{0,16},{8,24},{16,0},{24,8},{1,17},{9,25},{17,1},{25,9},{2,18},{10... | collective-permute-start | bytes 1572872 | tf_op jit(solution)/shard_map/ppermute | solution.py:265
  10.6 25.0 %collective-permute-start = (f32[5,2,64,256]{3,2,1,0:T(8,128)}, f32[5,2,64,256]{3,2,1,0:T(8,128)}, u32[]{:S(2)}, u32[]{:S(2)}) collective-permute-start(f32[5,2,64,256]{3,2,1,0:T(8,128)} %get-tuple-element.30), channel_id=1, source_target_pairs={{0,8},{8,0},{16,24},{24,16},{1,9},{9,1},{17,25},{25,17},{2,10},{10... | collective-permute-start | bytes 1966088 | tf_op jit(solution)/shard_map/ppermute | solution.py:265
  11.1 28.3 %collective-permute-start.1 = (f32[5,2,64,256]{3,2,1,0:T(8,128)S(1)}, f32[5,2,64,256]{3,2,1,0:T(8,128)}, u32[]{:S(2)}, u32[]{:S(2)}) collective-permute-start(f32[5,2,64,256]{3,2,1,0:T(8,128)S(1)} %get-tuple-element.29.refs_0_), channel_id=1, source_target_pairs={{0,16},{8,24},{16,0},{24,8},{1,17},{9,25},{17,1},{25,9},{2,18},{10... | collective-permute-start | bytes 1966088 | tf_op jit(solution)/shard_map/ppermute | solution.py:265
  11.6 65.1 %collective-permute-start.13 = (f32[6,2,64,256]{3,2,1,0:T(8,128)S(1)}, f32[6,2,64,256]{3,2,1,0:T(8,128)}, u32[]{:S(2)}, u32[]{:S(2)}) collective-permute-start(f32[6,2,64,256]{3,2,1,0:T(8,128)S(1)} %get-tuple-element.42), channel_id=1, source_target_pairs={{0,16},{8,24},{16,0},{24,8},{1,17},{9,25},{17,1},{25,9},{2,18},{10... | collective-permute-start | bytes 2359304 | tf_op jit(solution)/shard_map/ppermute | solution.py:265
  20.3 48.8 %copy-start.14 = (f32[4,2,64,256]{3,2,1,0:T(8,128)S(1)}, f32[4,2,64,256]{3,2,1,0:T(8,128)}, u32[]{:S(2)}) copy-start(f32[4,2,64,256]{3,2,1,0:T(8,128)} %copy-done.13) | copy-start | bytes 1572868
  35.6 33.5 %collective-permute-start.2 = (f32[5,2,64,256]{3,2,1,0:T(8,128)}, f32[5,2,64,256]{3,2,1,0:T(8,128)S(1)}, u32[]{:S(2)}, u32[]{:S(2)}) collective-permute-start(f32[5,2,64,256]{3,2,1,0:T(8,128)} %collective-permute-done.refs_1_), channel_id=1, source_target_pairs={{0,16},{8,24},{16,0},{24,8},{1,17},{9,25},{17,1},{25,9},{2,18},{10... | collective-permute-start | bytes 1966088 | tf_op jit(solution)/shard_map/ppermute | solution.py:265
  37.2 57.2 %collective-permute-start.12 = (f32[6,2,64,256]{3,2,1,0:T(8,128)S(1)}, f32[6,2,64,256]{3,2,1,0:T(8,128)S(1)}, u32[]{:S(2)}, u32[]{:S(2)}) collective-permute-start(f32[6,2,64,256]{3,2,1,0:T(8,128)S(1)} %get-tuple-element.41.refs_0_), channel_id=1, source_target_pairs={{0,8},{8,0},{16,24},{24,16},{1,9},{9,1},{17,25},{25,17},{2,10},{10... | collective-permute-start | bytes 2359304 | tf_op jit(solution)/shard_map/ppermute | solution.py:265
  38.8 41.5 %collective-permute-start.8 = (f32[4,2,64,256]{3,2,1,0:T(8,128)}, f32[4,2,64,256]{3,2,1,0:T(8,128)S(1)}, u32[]{:S(2)}, u32[]{:S(2)}) collective-permute-start(f32[4,2,64,256]{3,2,1,0:T(8,128)} %collective-permute-done.6.refs_5_), channel_id=1, source_target_pairs={{0,16},{8,24},{16,0},{24,8},{1,17},{9,25},{17,1},{25,9},{2,18},{10... | collective-permute-start | bytes 1572872 | tf_op jit(solution)/shard_map/ppermute | solution.py:265
  39.4 50.7 %collective-permute-start.19 = (f32[4,2,64,256]{3,2,1,0:T(8,128)}, f32[4,2,64,256]{3,2,1,0:T(8,128)S(1)}, u32[]{:S(2)}, u32[]{:S(2)}) collective-permute-start(f32[4,2,64,256]{3,2,1,0:T(8,128)} %copy-done.15), channel_id=1, source_target_pairs={{0,16},{8,24},{16,0},{24,8},{1,17},{9,25},{17,1},{25,9},{2,18},{10... | collective-permute-start | bytes 1572872 | tf_op jit(solution)/shard_map/ppermute | solution.py:265
  69.1 23.2 %collective-permute-start.18 = (f32[4,2,64,256]{3,2,1,0:T(8,128)S(1)}, f32[4,2,64,256]{3,2,1,0:T(8,128)S(1)}, u32[]{:S(2)}, u32[]{:S(2)}) collective-permute-start(f32[4,2,64,256]{3,2,1,0:T(8,128)S(1)} %copy-done.14), channel_id=1, source_target_pairs={{0,8},{8,0},{16,24},{24,16},{1,9},{9,1},{17,25},{25,17},{2,10},{10... | collective-permute-start | bytes 1572872 | tf_op jit(solution)/shard_map/ppermute | solution.py:265
  74.7 1.0 copy-start.6
  75.7 1.0 copy-start.10
  76.7 13.4 %copy-start.17 = (f32[2,4,128,256]{3,2,1,0:T(8,128)S(1)}, f32[2,4,128,256]{3,2,1,0:T(8,128)}, u32[]{:S(2)}) copy-start(f32[2,4,128,256]{3,2,1,0:T(8,128)} %get-tuple-element.33) | copy-start | bytes 3145732
  76.7 34.9 %collective-permute-start.14 = (f32[6,2,64,256]{3,2,1,0:T(8,128)}, f32[6,2,64,256]{3,2,1,0:T(8,128)S(1)}, u32[]{:S(2)}, u32[]{:S(2)}) collective-permute-start(f32[6,2,64,256]{3,2,1,0:T(8,128)} %collective-permute-done.13.refs_2_), channel_id=1, source_target_pairs={{0,8},{8,0},{16,24},{24,16},{1,9},{9,1},{17,25},{25,17},{2,10},{10... | collective-permute-start | bytes 2359304 | tf_op jit(solution)/shard_map/ppermute | solution.py:265
  80.3 47.5 %collective-permute-start.3 = (f32[2,4,128,256]{3,2,1,0:T(8,128)}, f32[2,4,128,256]{3,2,1,0:T(8,128)S(1)}, u32[]{:S(2)}, u32[]{:S(2)}) collective-permute-start(f32[2,4,128,256]{3,2,1,0:T(8,128)} %get-tuple-element.32), channel_id=1, source_target_pairs={{0,1},{1,2},{2,3},{3,4},{4,5},{5,6},{6,7},{8,9},{9,10},{10,11},{11... | collective-permute-start | bytes 3145736 | tf_op jit(solution)/shard_map/ppermute | solution.py:290
  90.1 41.4 %collective-permute-start.4 = (f32[2,4,128,256]{3,2,1,0:T(8,128)S(1)}, f32[2,4,128,256]{3,2,1,0:T(8,128)S(1)}, u32[]{:S(2)}, u32[]{:S(2)}) collective-permute-start(f32[2,4,128,256]{3,2,1,0:T(8,128)S(1)} %copy-done.17), channel_id=1, source_target_pairs={{1,0},{2,1},{3,2},{4,3},{5,4},{6,5},{7,6},{9,8},{10,9},{11,10},{12... | collective-permute-start | bytes 3145736 | tf_op jit(solution)/shard_map/ppermute | solution.py:291
  92.2 41.2 %collective-permute-start.9 = (f32[2,4,128,256]{3,2,1,0:T(8,128)}, f32[2,4,128,256]{3,2,1,0:T(8,128)}, u32[]{:S(2)}, u32[]{:S(2)}) collective-permute-start(f32[2,4,128,256]{3,2,1,0:T(8,128)} %get-tuple-element.38), channel_id=1, source_target_pairs={{0,1},{1,2},{2,3},{3,4},{4,5},{5,6},{6,7},{8,9},{9,10},{10,11},{11... | collective-permute-start | bytes 3145736 | tf_op jit(solution)/shard_map/ppermute | solution.py:290
  94.4 14.5 %collective-permute-start.20 = (f32[4,2,64,256]{3,2,1,0:T(8,128)S(1)}, f32[4,2,64,256]{3,2,1,0:T(8,128)S(1)}, u32[]{:S(2)}, u32[]{:S(2)}) collective-permute-start(f32[4,2,64,256]{3,2,1,0:T(8,128)S(1)} %collective-permute-done.19.refs_6_), channel_id=1, source_target_pairs={{0,8},{8,0},{16,24},{24,16},{1,9},{9,1},{17,25},{25,17},{2,10},{10... | collective-permute-start | bytes 1572872 | tf_op jit(solution)/shard_map/ppermute | solution.py:265
  108.9 31.8 %collective-permute-start.10 = (f32[2,4,128,256]{3,2,1,0:T(8,128)}, f32[2,4,128,256]{3,2,1,0:T(8,128)}, u32[]{:S(2)}, u32[]{:S(2)}) collective-permute-start(f32[2,4,128,256]{3,2,1,0:T(8,128)} %get-tuple-element.39), channel_id=1, source_target_pairs={{1,0},{2,1},{3,2},{4,3},{5,4},{6,5},{7,6},{9,8},{10,9},{11,10},{12... | collective-permute-start | bytes 3145736 | tf_op jit(solution)/shard_map/ppermute | solution.py:291
  111.7 0.9 copy-start.11
  118.5 26.5 %collective-permute-start.21 = (f32[2,4,128,256]{3,2,1,0:T(8,128)}, f32[2,4,128,256]{3,2,1,0:T(8,128)}, u32[]{:S(2)}, u32[]{:S(2)}) collective-permute-start(f32[2,4,128,256]{3,2,1,0:T(8,128)} %get-tuple-element.50), channel_id=1, source_target_pairs={{0,1},{1,2},{2,3},{3,4},{4,5},{5,6},{6,7},{8,9},{9,10},{10,11},{11... | collective-permute-start | bytes 3145736 | tf_op jit(solution)/shard_map/ppermute | solution.py:290
  120.5 1.1 copy-start.12
  126.8 1.0 copy-start.9
  127.8 9.3 %copy-start.2 = (f32[2,4,128,256]{3,2,1,0:T(8,128)}, f32[2,4,128,256]{3,2,1,0:T(8,128)S(1)}, u32[]{:S(2)}) copy-start(f32[2,4,128,256]{3,2,1,0:T(8,128)S(1)} %collective-permute-done.3.low_ref.refs_1_) | copy-start | bytes 3145732
  127.8 18.5 %collective-permute-start.22 = (f32[2,4,128,256]{3,2,1,0:T(8,128)}, f32[2,4,128,256]{3,2,1,0:T(8,128)}, u32[]{:S(2)}, u32[]{:S(2)}) collective-permute-start(f32[2,4,128,256]{3,2,1,0:T(8,128)} %get-tuple-element.51), channel_id=1, source_target_pairs={{1,0},{2,1},{3,2},{4,3},{5,4},{6,5},{7,6},{9,8},{10,9},{11,10},{12... | collective-permute-start | bytes 3145736 | tf_op jit(solution)/shard_map/ppermute | solution.py:291
  131.5 5.6 %copy-start.4 = (f32[2,4,128,256]{3,2,1,0:T(8,128)}, f32[2,4,128,256]{3,2,1,0:T(8,128)S(1)}, u32[]{:S(2)}) copy-start(f32[2,4,128,256]{3,2,1,0:T(8,128)S(1)} %collective-permute-done.4.high_ref.refs_2_) | copy-start | bytes 3145732
  131.5 20.0 %collective-permute-start.15 = (f32[2,4,128,256]{3,2,1,0:T(8,128)}, f32[2,4,128,256]{3,2,1,0:T(8,128)}, u32[]{:S(2)}, u32[]{:S(2)}) collective-permute-start(f32[2,4,128,256]{3,2,1,0:T(8,128)} %get-tuple-element.44), channel_id=1, source_target_pairs={{0,1},{1,2},{2,3},{3,4},{4,5},{5,6},{6,7},{8,9},{9,10},{10,11},{11... | collective-permute-start | bytes 3145736 | tf_op jit(solution)/shard_map/ppermute | solution.py:290
  133.4 21.9 %collective-permute-start.16 = (f32[2,4,128,256]{3,2,1,0:T(8,128)}, f32[2,4,128,256]{3,2,1,0:T(8,128)}, u32[]{:S(2)}, u32[]{:S(2)}) collective-permute-start(f32[2,4,128,256]{3,2,1,0:T(8,128)} %get-tuple-element.45), channel_id=1, source_target_pairs={{1,0},{2,1},{3,2},{4,3},{5,4},{6,5},{7,6},{9,8},{10,9},{11,10},{12... | collective-permute-start | bytes 3145736 | tf_op jit(solution)/shard_map/ppermute | solution.py:291
  140.7 57.5 %copy-start.3 = (f32[2,4,128,256]{3,2,1,0:T(8,128)S(1)}, f32[2,4,128,256]{3,2,1,0:T(8,128)}, u32[]{:S(2)}) copy-start(f32[2,4,128,256]{3,2,1,0:T(8,128)} %copy-done.2) | copy-start | bytes 3145732
  140.7 57.5 %copy-start.5 = (f32[2,4,128,256]{3,2,1,0:T(8,128)S(1)}, f32[2,4,128,256]{3,2,1,0:T(8,128)}, u32[]{:S(2)}) copy-start(f32[2,4,128,256]{3,2,1,0:T(8,128)} %copy-done.4) | copy-start | bytes 3145732
  140.7 26.5 %collective-permute-start.5 = (f32[4,2,128,256]{3,2,1,0:T(8,128)}, f32[4,2,128,256]{3,2,1,0:T(8,128)}, u32[]{:S(2)}, u32[]{:S(2)}) collective-permute-start(f32[4,2,128,256]{3,2,1,0:T(8,128)} %add_far.4), channel_id=1, source_target_pairs={{0,8},{8,0},{16,24},{24,16},{1,9},{9,1},{17,25},{25,17},{2,10},{10... | collective-permute-start | bytes 3145736 | tf_op jit(solution)/shard_map/ppermute | solution.py:265
  145.0 43.1 %collective-permute-start.11 = (f32[4,2,128,256]{3,2,1,0:T(8,128)}, f32[4,2,128,256]{3,2,1,0:T(8,128)}, u32[]{:S(2)}, u32[]{:S(2)}) collective-permute-start(f32[4,2,128,256]{3,2,1,0:T(8,128)} %add_far.5), channel_id=1, source_target_pairs={{0,8},{8,0},{16,24},{24,16},{1,9},{9,1},{17,25},{25,17},{2,10},{10... | collective-permute-start | bytes 3145736 | tf_op jit(solution)/shard_map/ppermute | solution.py:265
  149.9 38.2 %collective-permute-start.23 = (f32[4,2,128,256]{3,2,1,0:T(8,128)}, f32[4,2,128,256]{3,2,1,0:T(8,128)}, u32[]{:S(2)}, u32[]{:S(2)}) collective-permute-start(f32[4,2,128,256]{3,2,1,0:T(8,128)} %add_far.7), channel_id=1, source_target_pairs={{0,16},{8,24},{16,0},{24,8},{1,17},{9,25},{17,1},{25,9},{2,18},{10... | collective-permute-start | bytes 3145736 | tf_op jit(solution)/shard_map/ppermute | solution.py:265
  158.9 38.3 %collective-permute-start.17 = (f32[4,2,128,256]{3,2,1,0:T(8,128)}, f32[4,2,128,256]{3,2,1,0:T(8,128)S(1)}, u32[]{:S(2)}, u32[]{:S(2)}) collective-permute-start(f32[4,2,128,256]{3,2,1,0:T(8,128)} %add_far.6), channel_id=1, source_target_pairs={{0,16},{8,24},{16,0},{24,8},{1,17},{9,25},{17,1},{25,9},{2,18},{10... | collective-permute-start | bytes 3145736 | tf_op jit(solution)/shard_map/ppermute | solution.py:265
  197.1 1.0 copy-start.16
  197.1 16.2 %copy-start.1 = (f32[2,256,256]{2,1,0:T(8,128)S(1)}, f32[2,256,256]{2,1,0:T(8,128)}, u32[]{:S(2)}) copy-start(f32[2,256,256]{2,1,0:T(8,128)} %param.8) | copy-start | bytes 1572868
  198.1 1.2 copy-start.7
  199.4 1.2 copy-start.8

commit v2 on v1

--- a/solution.py
+++ b/solution.py
@@ -9,6 +9,7 @@
 
 
 CUTS = 2
+VMEM_LIMIT = 60 * 2**20
 
 
 def block_row(stream, side, row, depth, rows_x):
@@ -23,7 +24,7 @@
     return list(range(first, (chunk + 1) * high + 1))
 
 
-def spread_kernel(depth, planes, sides_ref, ratio_ref, in_ref, *outs):
+def spread_kernel(chunk, depth, planes, sides_ref, ratio_ref, in_ref, *outs):
     steps, _, rows_x, _ = in_ref.shape
     flat = in_ref.reshape(steps * planes * rows_x, in_ref.shape[3])
     ratio = ratio_ref[...]
@@ -31,29 +32,27 @@
     for stream in range(2):
         for other in range(2):
             side = sides_ref[stream] if other == 0 else 1 - sides_ref[stream]
-            for chunk in range(CUTS):
-                out = outs[place]
-                place += 1
-                for at, row in enumerate(chunk_rows(stream, chunk, depth)):
-                    x = block_row(stream, side, row, depth, rows_x)
-                    for z in range(planes):
-                        part = flat[pl.ds(z * rows_x + x, steps, stride=planes * rows_x), :]
-                        out[at, z] = part * ratio
-
-
-def spread(residual, ratio, sides, depth):
+            out = outs[place]
+            place += 1
+            for at, row in enumerate(chunk_rows(stream, chunk, depth)):
+                x = block_row(stream, side, row, depth, rows_x)
+                for z in range(planes):
+                    part = flat[pl.ds(z * rows_x + x, steps, stride=planes * rows_x), :]
+                    out[at, z] = part * ratio
+
+
+def spread(chunk, residual, ratio, sides, depth):
     steps, planes, rows_x, rows_y = residual.shape
     lanes = 128
     block = min(steps, 32)
     shapes, specs = [], []
     for stream in range(2):
         for _ in range(2):
-            for chunk in range(CUTS):
-                count = len(chunk_rows(stream, chunk, depth))
-                shapes.append(jax.ShapeDtypeStruct((count, planes, steps, rows_y), jnp.float32))
-                specs.append(pl.BlockSpec((count, planes, block, lanes), lambda i, j: (0, 0, i, j)))
+            count = len(chunk_rows(stream, chunk, depth))
+            shapes.append(jax.ShapeDtypeStruct((count, planes, steps, rows_y), jnp.float32))
+            specs.append(pl.BlockSpec((count, planes, block, lanes), lambda i, j: (0, 0, i, j)))
     outs = pl.pallas_call(
-        functools.partial(spread_kernel, depth, planes),
+        functools.partial(spread_kernel, chunk, depth, planes),
         out_shape=shapes,
         grid=(steps // block, rows_y // lanes),
         in_specs=[
@@ -62,12 +61,11 @@
             pl.BlockSpec((block, planes, rows_x, lanes), lambda i, j: (i, 0, 0, j)),
         ],
         out_specs=specs,
-        compiler_params=pltpu.CompilerParams(vmem_limit_bytes=48 * 2**20),
+        compiler_params=pltpu.CompilerParams(vmem_limit_bytes=VMEM_LIMIT),
         cost_estimate=pl.CostEstimate(flops=residual.size * 2, bytes_accessed=residual.size * 10, transcendentals=0),
         name="spread",
     )(sides, ratio, residual)
-    outs = list(outs)
-    return [[outs[(2 * s + o) * CUTS : (2 * s + o + 1) * CUTS] for o in range(2)] for s in range(2)]
+    return [outs[0:2], outs[2:4]]
 
 
 def halves(value):
@@ -138,7 +136,7 @@
         out_shape=shapes,
         in_specs=[pl.BlockSpec(memory_space=pltpu.VMEM)] * (2 + len(flat)),
         out_specs=[pl.BlockSpec(memory_space=pltpu.VMEM)] * 4,
-        compiler_params=pltpu.CompilerParams(vmem_limit_bytes=48 * 2**20),
+        compiler_params=pltpu.CompilerParams(vmem_limit_bytes=VMEM_LIMIT),
         cost_estimate=pl.CostEstimate(flops=flops, bytes_accessed=12 * 2**20, transcendentals=0),
         name="apply",
     )(near, far, *flat)
@@ -167,52 +165,89 @@
             pl.BlockSpec((1, 1, half, rows_y), lambda i: (1, i, 0, 0)),
         ],
         out_specs=pl.BlockSpec((1, planes, half, rows_y), lambda i: (i, 0, 0, 0)),
+        compiler_params=pltpu.CompilerParams(vmem_limit_bytes=VMEM_LIMIT),
         cost_estimate=pl.CostEstimate(flops=send.size, bytes_accessed=send.size * 12, transcendentals=0),
         name="add_far",
     )(send, low, high)
 
 
-def gather_kernel(depth, sides_ref, *refs):
+def place_kernel(depth, other, sides_ref, *refs):
     out_ref = refs[-1]
-    place = 0
-    count, planes, rows_x, lanes = out_ref.shape
-    flat = out_ref.reshape(count * planes * rows_x, lanes)
+    refs = refs[other:-1]
+    each = 1 if other else 3
+    count, planes, _, lanes = out_ref.shape
+    flat = out_ref.reshape(count * planes * depth, lanes)
     high = depth // CUTS
-    for stream in range(2):
-        side = sides_ref[stream]
-        for chunk in range(CUTS):
-            own, low, up, got = refs[place : place + 4]
-            place += 4
-            for at in range(high):
-                row = chunk * high + at
-                x = block_row(stream, side, row, depth, rows_x)
-                y = block_row(stream, 1 - side, row, depth, rows_x)
-                for z in range(planes):
-                    value = own[at, z]
-                    if z == 0:
-                        value = value + low[0, at]
-                    if z == planes - 1:
-                        value = value + up[0, at]
-                    flat[pl.ds(z * rows_x + x, count, stride=planes * rows_x), :] = value
-                    flat[pl.ds(z * rows_x + y, count, stride=planes * rows_x), :] = got[at, z]
-
-
-def collect(parts, sides, depth, rows_x):
+    stream = pl.program_id(0)
+    for which in range(2):
+
+        @pl.when(stream == which)
+        def _():
+            side = 1 - sides_ref[which] if other else sides_ref[which]
+            for chunk in range(CUTS):
+                part = refs[(which * CUTS + chunk) * each : (which * CUTS + chunk + 1) * each]
+                for at in range(high):
+                    row = chunk * high + at
+                    at_x = row if which else row + side * (depth - 1 - 2 * row)
+                    for z in range(planes):
+                        value = part[0][at, z]
+                        if not other and z == 0:
+                            value = value + part[1][0, at]
+                        if not other and z == planes - 1:
+                            value = value + part[2][0, at]
+                        flat[pl.ds(z * depth + at_x, count, stride=planes * depth), :] = value
+
+
+def place(parts, sides, depth, rows_x, result=None):
     high, planes, half, rows_y = parts[0][0].shape
     lanes = 128
-    block = min(half, 32)
-    cells = pl.BlockSpec((high, planes, block, lanes), lambda i, j: (0, 0, i, j))
-    edge = pl.BlockSpec((1, high, block, lanes), lambda i, j: (0, 0, i, j))
-    flat = [a for part in parts for a in part]
+    block = min(half, 64)
+    other = int(result is not None)
+
+    def cells(which):
+        def index(s, i, j, sides):
+            mine = (s == which).astype(jnp.int32)
+            last_i, last_j = half // block - 1, rows_y // lanes - 1
+            stay_i, stay_j = (last_i, last_j) if which == 0 else (0, 0)
+            return (0, 0, mine * i + (1 - mine) * stay_i, mine * j + (1 - mine) * stay_j)
+
+        return pl.BlockSpec((high, planes, block, lanes), index)
+
+    def edge(which):
+        def index(s, i, j, sides):
+            return cells(which).index_map(s, i, j, sides)
+
+        return pl.BlockSpec((1, high, block, lanes), index)
+
+    def out_index(s, i, j, sides):
+        side = 1 - sides[s] if other else sides[s]
+        tile = s * (1 + side) + (1 - s) * 3 * side
+        return (i, 0, tile, j)
+
+    specs, flat = [], []
+    for place_of, part in enumerate(parts):
+        which = place_of // CUTS
+        specs += [cells(which)] if other else [cells(which), edge(which), edge(which)]
+        flat += list(part)
+    first = [result] if other else []
     return pl.pallas_call(
-        functools.partial(gather_kernel, depth),
+        functools.partial(place_kernel, depth, other),
         out_shape=jax.ShapeDtypeStruct((half, planes, rows_x, rows_y), jnp.float32),
-        grid=(half // block, rows_y // lanes),
-        in_specs=[pl.BlockSpec(memory_space=pltpu.SMEM)] + [cells, edge, edge, cells] * len(parts),
-        out_specs=pl.BlockSpec((block, planes, rows_x, lanes), lambda i, j: (i, 0, 0, j)),
-        compiler_params=pltpu.CompilerParams(vmem_limit_bytes=48 * 2**20),
-        name="collect",
-    )(sides, *flat)
+        grid_spec=pltpu.PrefetchScalarGridSpec(
+            num_scalar_prefetch=1,
+            grid=(2, half // block, rows_y // lanes),
+            in_specs=[pl.BlockSpec(memory_space=pl.ANY)] * other + specs,
+            out_specs=pl.BlockSpec((block, planes, depth, lanes), out_index),
+        ),
+        input_output_aliases={1: 0} if other else {},
+        compiler_params=pltpu.CompilerParams(vmem_limit_bytes=VMEM_LIMIT),
+        cost_estimate=pl.CostEstimate(flops=0, bytes_accessed=16 * 2**20, transcendentals=0),
+        name="place_got" if other else "place_own",
+    )(sides, *first, *flat)
+
+
+def after(value, *others):
+    return lax.optimization_barrier((value, *others))[0]
 
 
 def make_maps(forward_map, back_map, eigen_values, me, count, bits):
@@ -268,32 +303,56 @@
     upward = [(i, i + 1) for i in range(spaces - 1)]
     downward = [(i + 1, i) for i in range(spaces - 1)]
 
-    raws = spread(residual, ratio, sides, depth)
     maps = make_maps(forward_map, back_map, eigen_values, me, count, bits)
 
+    queues = [[], []]
+
+    def swap_in_turn(data, bit):
+        queue = queues[0 if bit == bits[0] else 1]
+        if len(queue) > 1:
+            data = after(data, queue[-2])
+        got = swap(data, bit)
+        queue.append(got)
+        return got
+
     held = [[None] * CUTS for _ in range(2)]
-    for chunk in range(CUTS):
+    parts = [[None] * CUTS for _ in range(2)]
+
+    def raw(chunk):
+        raws = spread(chunk, residual, ratio, sides, depth)
+        have = [{0: raws[s][0], bits[s]: swap_in_turn(raws[s][1], bits[s])} for s in range(2)]
+        for bit in all_bits:
+            for mask in range(count):
+                for stream in (1, 0):
+                    now = have[stream]
+                    free = bit != bits[stream] and not mask & bit
+                    if free and mask in now and (mask | bit) not in now:
+                        now[mask | bit] = swap_in_turn(now[mask], bit)
         for stream in range(2):
-            keep, send = raws[stream][0][chunk], raws[stream][1][chunk]
-            have = {0: keep, bits[stream]: swap(send, bits[stream])}
-            for bit in all_bits:
-                if bit != bits[stream]:
-                    have.update({mask | bit: swap(have[mask], bit) for mask in list(have)})
-            held[stream][chunk] = [have[mask] for mask in range(count)]
-
-    parts = [[None] * CUTS for _ in range(2)]
-    for chunk in range(CUTS):
+            held[stream][chunk] = [have[stream][mask] for mask in range(count)]
+
+    def products(chunk):
         for stream in range(2):
             near, far = maps[stream]
             used = held[stream][max(chunk - 1, 0) : chunk + 1]
             own, send, down, up = apply(stream, chunk, depth, near, far, used)
             low = lax.ppermute(up, "space", upward)
             high = lax.ppermute(down, "space", downward)
-            got = swap(add_far(send, low, high), bits[stream])
-            parts[stream][chunk] = (own, low, high, got)
+            parts[stream][chunk] = [own, low, high, add_far(send, low, high)]
+
+    def give(chunk):
+        for stream in range(2):
+            parts[stream][chunk][3] = swap_in_turn(parts[stream][chunk][3], bits[stream])
+
+    for chunk in range(CUTS):
+        raw(chunk)
+        products(chunk)
+    for chunk in range(CUTS):
+        give(chunk)
 
     flat = [parts[s][c] for s in range(2) for c in range(CUTS)]
-    result = collect(flat, sides, depth, rows_x)
+    result = place([p[:3] for p in flat], sides, depth, rows_x)
+    result = place([p[3:] for p in flat], sides, depth, rows_x, result)
     return result.reshape(2, local_steps, planes, rows_x, rows_y)
 
 

time: 217 us -> 203 us (0.935)
  Pallas kernels: 55.6 us -> 70.6 us
  local copies, waits for them, and re-layouts: 17.7 us -> 2.71 us
  waiting for transfers between devices: 92.8 us -> 82.1 us
    unnamed x39 -> x33, local copies, waits for them, and re-layouts: 10.5 us -> 0.38 us
    pallas_call x2 -> x4, Pallas kernels: 18.7 us -> 28 us  [the longest x2 17.9 us: place(): pl.pallas_call(functools.partial(place_kernel, depth, other), out_shape=j...]
    ppermute x16, waiting for transfers between devices: 88.9 us -> 82.1 us  [swap(): return lax.ppermute(data, 'tm', [(i, i ^ bit) for i in range(count)])]
    pallas_call x4, Pallas kernels: 22.6 us -> 28.3 us  [apply(): pl.pallas_call(functools.partial(apply_kernel, stream, chunk, depth, plan...]
    ppermute x8, waiting for transfers between devices: 3.88 us -> 0.02 us  [the longest x4 0.01 us: products(): low = lax.ppermute(up, 'space', upward)]
    squeeze x2, local copies, waits for them, and re-layouts: 2.63 us -> 0.26 us  [make_maps(): once_re = coef_re * ahead[0] - coef_im * ahead[1]]
    ppermute x8, starting transfers between devices: 20.1 us -> 22.3 us  [the longest x4 14 us: products(): high = lax.ppermute(down, 'space', downward)]
  transfers between devices with their start and end apart: 24 -> 24, of which waited for: 9 -> 9; matrix products, arithmetic and copies ran while one was open for 7% -> 3% of each run, Pallas kernels for 17% -> 29%
where the time goes in v2:
time: 203 us; the launch traced here: 200 us
  waiting for transfers between devices  82.1 us (40%)
  Pallas kernels  70.6 us (35%)
  starting transfers between devices  38.9 us (19%)
  other arithmetic  4.14 us (2%)
  local copies, waits for them, and re-layouts  2.71 us (1%)
    ppermute x16, waiting for transfers between devices, swap(): return lax.ppermute(data, 'tm', [(i, i ^ bit) for i in range(count)])  82.1 us
    pallas_call x4, Pallas kernels, apply(): pl.pallas_call(functools.partial(apply_kernel, stream, chunk, depth, plan...  28.3 us
    pallas_call x2, Pallas kernels, place(): pl.pallas_call(functools.partial(place_kernel, depth, other), out_shape=j...  17.9 us
    ppermute x16, starting transfers between devices, swap(): return lax.ppermute(data, 'tm', [(i, i ^ bit) for i in range(count)])  16.6 us
    pallas_call x4, Pallas kernels, add_far(): pl.pallas_call(add_kernel, out_shape=jax.ShapeDtypeStruct(send.shape, jnp...  14.3 us
    ppermute x4, starting transfers between devices, products(): high = lax.ppermute(down, 'space', downward)  14 us
    pallas_call x2, Pallas kernels, spread(): pl.pallas_call(functools.partial(spread_kernel, chunk, depth, planes), ou...  10.2 us
    ppermute x4, starting transfers between devices, products(): low = lax.ppermute(up, 'space', upward)  8.31 us
  transfers between devices with their start and end apart: 24, of which 9 were waited for; matrix products, arithmetic and copies ran while one was open for 3% of the time, Pallas kernels for 29%

profile of v2, /device:TPU:8, one launch (start us, length us, event | category | flops | bytes accessed | tf_op | source)
XLA Modules:
  0.0 200.4 jit_solution(2737178742741981987)
XLA Ops:
  0.0 0.7 multiply_bitcast_fusion
  0.8 0.7 copy.17.ratio_ref
  1.5 0.7 pad_add_fusion.sides_ref
  2.1 5.2 %spread.2 = (f32[5,2,64,256]{3,2,1,0:T(8,128)}, f32[5,2,64,256]{3,2,1,0:T(8,128)}, f32[6,2,64,256]{3,2,1,0:T(8,128)}, f32[6,2,64,256]{3,2,1,0:T(8,128)}) custom-call(s32[2]{0:T(128)} %pad_add_fusion.sides_ref, f32[64,1]{1,0:T(8,128)} %copy.17.ratio_ref, f32[64,2,32,256]{3,2,1,0:T(8,128)} %in_ref.3), custom_call_target="tpu_custom_call" | custom-call | flops 2097152 | bytes 10485760 | tf_op jit(solution)/shard_map/spread/pallas_call | solution.py:54
  7.4 1.5 collective-permute-start.6
  8.9 1.5 collective-permute-start.1
  10.4 0.5 collective-permute-start.2
  10.9 0.5 collective-permute-start
  11.4 0.1 fusion.17
  11.5 0.6 gather_fusion
  12.1 0.1 compare_and_fusion.1
  12.2 0.1 select_bitcast_fusion.1
  12.5 0.1 copy.11
  12.6 0.2 copy.12
  12.8 0.6 gather_fusion.1
  13.4 0.1 select_bitcast_fusion
  13.6 0.1 copy.13
  13.7 0.1 copy.14
  13.9 0.2 multiply_subtract_fusion
  14.0 0.1 multiply_add_fusion
  14.2 1.4 fusion
  15.8 4.9 %spread.3 = (f32[4,2,64,256]{3,2,1,0:T(8,128)}, f32[4,2,64,256]{3,2,1,0:T(8,128)}, f32[4,2,64,256]{3,2,1,0:T(8,128)}, f32[4,2,64,256]{3,2,1,0:T(8,128)}) custom-call(s32[2]{0:T(128)} %pad_add_fusion.sides_ref, f32[64,1]{1,0:T(8,128)} %copy.17.ratio_ref, f32[64,2,32,256]{3,2,1,0:T(8,128)} %in_ref.3), custom_call_target="tpu_custom_call" | custom-call | flops 2097152 | bytes 10485760 | tf_op jit(solution)/shard_map/spread/pallas_call | solution.py:54
  20.8 20.2 %collective-permute-done.refs_1_ = f32[5,2,64,256]{3,2,1,0:T(8,128)} collective-permute-done((f32[5,2,64,256]{3,2,1,0:T(8,128)}, f32[5,2,64,256]{3,2,1,0:T(8,128)}, u32[]{:S(2)}, u32[]{:S(2)}) %collective-permute-start) | collective-permute-done | bytes 655392 | tf_op jit(solution)/shard_map/ppermute | solution.py:300
  41.0 1.2 collective-permute-done.2.refs_2_
  42.2 1.5 collective-permute-start.3
  43.8 0.6 collective-permute-start.9
  44.4 0.5 collective-permute-start.7
  44.9 1.5 collective-permute-start.13
  46.5 0.9 pad_maximum_fusion.2.far_ref
  47.3 0.8 pad_maximum_fusion.1.far_ref
  48.1 20.8 %collective-permute-done.9.refs_6_ = f32[4,2,64,256]{3,2,1,0:T(8,128)S(1)} collective-permute-done((f32[4,2,64,256]{3,2,1,0:T(8,128)}, f32[4,2,64,256]{3,2,1,0:T(8,128)S(1)}, u32[]{:S(2)}, u32[]{:S(2)}) %collective-permute-start.9) | collective-permute-done | bytes 524320 | tf_op jit(solution)/shard_map/ppermute | solution.py:300
  69.0 1.5 collective-permute-start.10
  70.5 0.8 collective-permute-start.8
  71.3 0.1 copy-done.12
  71.4 6.7 %apply.4 = (f32[4,2,128,256]{3,2,1,0:T(8,128)}, f32[4,2,128,256]{3,2,1,0:T(8,128)}, f32[2,4,128,256]{3,2,1,0:T(8,128)}, f32[2,4,128,256]{3,2,1,0:T(8,128)}) custom-call(bf16[256,1536]{1,0:T(8,128)(2,1)} %copy-done.8, bf16[256,768]{1,0:T(8,128)(2,1)} %pad_maximum_fusion.1.far_ref, f32[5,2,64,256]{3,2,1,0:T(8,128)} %get-tuple-element.41.refs_0_, ...), custom_call_target="tpu_custom_call" | custom-call | flops 2415919104 | bytes 12582912 | tf_op jit(solution)/shard_map/apply/pallas_call | solution.py:134
  78.1 1.9 collective-permute-start.4
  80.0 3.8 %collective-permute-start.5 = (f32[2,4,128,256]{3,2,1,0:T(8,128)}, f32[2,4,128,256]{3,2,1,0:T(8,128)S(1)}, u32[]{:S(2)}, u32[]{:S(2)}) collective-permute-start(f32[2,4,128,256]{3,2,1,0:T(8,128)} %get-tuple-element.47), channel_id=1, source_target_pairs={{1,0},{2,1},{3,2},{4,3},{5,4},{6,5},{7,6},{9,8},{10,9},{11,10},{12... | collective-permute-start | bytes 3145736 | tf_op jit(solution)/shard_map/ppermute | solution.py:340
  83.8 6.8 %apply.6 = (f32[4,2,128,256]{3,2,1,0:T(8,128)}, f32[4,2,128,256]{3,2,1,0:T(8,128)}, f32[2,4,128,256]{3,2,1,0:T(8,128)}, f32[2,4,128,256]{3,2,1,0:T(8,128)}) custom-call(bf16[256,1536]{1,0:T(8,128)(2,1)} %copy-done.9, bf16[256,768]{1,0:T(8,128)(2,1)} %pad_maximum_fusion.2.far_ref, f32[6,2,64,256]{3,2,1,0:T(8,128)} %get-tuple-element.50.refs_0_, ...), custom_call_target="tpu_custom_call" | custom-call | flops 2415919104 | bytes 12582912 | tf_op jit(solution)/shard_map/apply/pallas_call | solution.py:134
  90.7 2.1 %collective-permute-start.14 = (f32[2,4,128,256]{3,2,1,0:T(8,128)}, f32[2,4,128,256]{3,2,1,0:T(8,128)S(1)}, u32[]{:S(2)}, u32[]{:S(2)}) collective-permute-start(f32[2,4,128,256]{3,2,1,0:T(8,128)} %get-tuple-element.61), channel_id=1, source_target_pairs={{0,1},{1,2},{2,3},{3,4},{4,5},{5,6},{6,7},{8,9},{9,10},{10,11},{11... | collective-permute-start | bytes 3145736 | tf_op jit(solution)/shard_map/ppermute | solution.py:339
  92.8 0.7 collective-permute-start.17
  93.5 1.4 collective-permute-start.16
  94.9 7.3 %apply.5 = (f32[4,2,128,256]{3,2,1,0:T(8,128)}, f32[4,2,128,256]{3,2,1,0:T(8,128)}, f32[2,4,128,256]{3,2,1,0:T(8,128)}, f32[2,4,128,256]{3,2,1,0:T(8,128)}) custom-call(bf16[256,1536]{1,0:T(8,128)(2,1)} %copy-done.8, bf16[256,768]{1,0:T(8,128)(2,1)} %pad_maximum_fusion.1.far_ref, f32[5,2,64,256]{3,2,1,0:T(8,128)} %get-tuple-element.41.refs_0_, ...), custom_call_target="tpu_custom_call" | custom-call | flops 2415919104 | bytes 12582912 | tf_op jit(solution)/shard_map/apply/pallas_call | solution.py:134
  102.1 4.9 %collective-permute-done.17.refs_7_ = f32[4,2,64,256]{3,2,1,0:T(8,128)} collective-permute-done((f32[4,2,64,256]{3,2,1,0:T(8,128)S(1)}, f32[4,2,64,256]{3,2,1,0:T(8,128)}, u32[]{:S(2)}, u32[]{:S(2)}) %collective-permute-start.17) | collective-permute-done | bytes 524320 | tf_op jit(solution)/shard_map/ppermute | solution.py:300
  107.1 3.4 %collective-permute-start.15 = (f32[2,4,128,256]{3,2,1,0:T(8,128)}, f32[2,4,128,256]{3,2,1,0:T(8,128)}, u32[]{:S(2)}, u32[]{:S(2)}) collective-permute-start(f32[2,4,128,256]{3,2,1,0:T(8,128)} %get-tuple-element.62), channel_id=1, source_target_pairs={{1,0},{2,1},{3,2},{4,3},{5,4},{6,5},{7,6},{9,8},{10,9},{11,10},{12... | collective-permute-start | bytes 3145736 | tf_op jit(solution)/shard_map/ppermute | solution.py:340
  110.5 7.8 %collective-permute-done.16.refs_5_ = f32[4,2,64,256]{3,2,1,0:T(8,128)} collective-permute-done((f32[4,2,64,256]{3,2,1,0:T(8,128)}, f32[4,2,64,256]{3,2,1,0:T(8,128)}, u32[]{:S(2)}, u32[]{:S(2)}) %collective-permute-start.16) | collective-permute-done | bytes 524320 | tf_op jit(solution)/shard_map/ppermute | solution.py:300
  118.3 2.4 %collective-permute-start.11 = (f32[2,4,128,256]{3,2,1,0:T(8,128)}, f32[2,4,128,256]{3,2,1,0:T(8,128)}, u32[]{:S(2)}, u32[]{:S(2)}) collective-permute-start(f32[2,4,128,256]{3,2,1,0:T(8,128)} %get-tuple-element.57), channel_id=1, source_target_pairs={{0,1},{1,2},{2,3},{3,4},{4,5},{5,6},{6,7},{8,9},{9,10},{10,11},{11... | collective-permute-start | bytes 3145736 | tf_op jit(solution)/shard_map/ppermute | solution.py:339
  120.7 3.2 %collective-permute-start.12 = (f32[2,4,128,256]{3,2,1,0:T(8,128)}, f32[2,4,128,256]{3,2,1,0:T(8,128)}, u32[]{:S(2)}, u32[]{:S(2)}) collective-permute-start(f32[2,4,128,256]{3,2,1,0:T(8,128)} %get-tuple-element.58), channel_id=1, source_target_pairs={{1,0},{2,1},{3,2},{4,3},{5,4},{6,5},{7,6},{9,8},{10,9},{11,10},{12... | collective-permute-start | bytes 3145736 | tf_op jit(solution)/shard_map/ppermute | solution.py:340
  123.9 7.5 %apply.7 = (f32[4,2,128,256]{3,2,1,0:T(8,128)}, f32[4,2,128,256]{3,2,1,0:T(8,128)}, f32[2,4,128,256]{3,2,1,0:T(8,128)}, f32[2,4,128,256]{3,2,1,0:T(8,128)}) custom-call(bf16[256,1536]{1,0:T(8,128)(2,1)} %copy-done.9, bf16[256,768]{1,0:T(8,128)(2,1)} %pad_maximum_fusion.2.far_ref, f32[6,2,64,256]{3,2,1,0:T(8,128)} %get-tuple-element.50.refs_0_, ...), custom_call_target="tpu_custom_call" | custom-call | flops 2415919104 | bytes 12582912 | tf_op jit(solution)/shard_map/apply/pallas_call | solution.py:134
  131.4 1.9 collective-permute-start.18
  133.3 3.6 %collective-permute-start.19 = (f32[2,4,128,256]{3,2,1,0:T(8,128)}, f32[2,4,128,256]{3,2,1,0:T(8,128)}, u32[]{:S(2)}, u32[]{:S(2)}) collective-permute-start(f32[2,4,128,256]{3,2,1,0:T(8,128)} %get-tuple-element.68), channel_id=1, source_target_pairs={{1,0},{2,1},{3,2},{4,3},{5,4},{6,5},{7,6},{9,8},{10,9},{11,10},{12... | collective-permute-start | bytes 3145736 | tf_op jit(solution)/shard_map/ppermute | solution.py:340
  137.0 3.6 %add_far.4 = f32[4,2,128,256]{3,2,1,0:T(8,128)} custom-call(f32[4,2,128,256]{3,2,1,0:T(8,128)} %get-tuple-element.69.send_ref, f32[2,4,128,256]{3,2,1,0:T(8,128)} %copy-done.2, f32[2,4,128,256]{3,2,1,0:T(8,128)} %copy-done.3), custom_call_target="tpu_custom_call" | custom-call | flops 262144 | bytes 3145728 | tf_op jit(solution)/shard_map/add_far/pallas_call | solution.py:158
  140.5 0.6 collective-permute-start.20
  141.2 3.6 %add_far.6 = f32[4,2,128,256]{3,2,1,0:T(8,128)} custom-call(f32[4,2,128,256]{3,2,1,0:T(8,128)} %get-tuple-element.73.send_ref, f32[2,4,128,256]{3,2,1,0:T(8,128)} %copy-done.4, f32[2,4,128,256]{3,2,1,0:T(8,128)} %collective-permute-done.15.refs_8_.high_ref), custom_call_target="tpu_custom_call" | custom-call | flops 262144 | bytes 3145728 | tf_op jit(solution)/shard_map/add_far/pallas_call | solution.py:158
  144.7 1.2 collective-permute-start.22
  145.9 3.6 %add_far.5 = f32[4,2,128,256]{3,2,1,0:T(8,128)} custom-call(f32[4,2,128,256]{3,2,1,0:T(8,128)} %get-tuple-element.71.send_ref, f32[2,4,128,256]{3,2,1,0:T(8,128)} %collective-permute-done.11.refs_4_.low_ref, f32[2,4,128,256]{3,2,1,0:T(8,128)} %collective-permute-done.12.refs_5_.high_ref), custom_call_target="tpu_custom_call" | custom-call | flops 262144 | bytes 3145728 | tf_op jit(solution)/shard_map/add_far/pallas_call | solution.py:158
  149.5 1.4 collective-permute-start.21
  150.9 3.6 %add_far.7 = f32[4,2,128,256]{3,2,1,0:T(8,128)} custom-call(f32[4,2,128,256]{3,2,1,0:T(8,128)} %get-tuple-element.75.send_ref, f32[2,4,128,256]{3,2,1,0:T(8,128)} %collective-permute-done.18.refs_10_.low_ref, f32[2,4,128,256]{3,2,1,0:T(8,128)} %collective-permute-done.19.refs_11_.high_ref), custom_call_target="tpu_custom_call" | custom-call | flops 262144 | bytes 3145728 | tf_op jit(solution)/shard_map/add_far/pallas_call | solution.py:158
  154.6 0.8 collective-permute-start.23
  155.4 9.7 %place_own.1.refs_0_ = f32[128,2,32,256]{3,2,1,0:T(8,128)} custom-call(s32[2]{0:T(128)} %pad_add_fusion.sides_ref, f32[4,2,128,256]{3,2,1,0:T(8,128)} %get-tuple-element.45.refs_0_, f32[2,4,128,256]{3,2,1,0:T(8,128)} %copy-done.2, f32[2,4,128,256]{3,2,1,0:T(8,128)} %copy-done.3, f32[4,2,128,256]{3,2,1,0:T(8,128)} %get-tuple-element.56.refs_3_, ...), custom_call_target="tpu_custom_call" | custom-call | bytes 16777216 | tf_op jit(solution)/shard_map/place_own/pallas_call | solution.py:233
  165.1 1.7 collective-permute-done.20.refs_1_
  166.8 4.2 %collective-permute-done.22.refs_3_ = f32[4,2,128,256]{3,2,1,0:T(8,128)S(1)} collective-permute-done((f32[4,2,128,256]{3,2,1,0:T(8,128)}, f32[4,2,128,256]{3,2,1,0:T(8,128)S(1)}, u32[]{:S(2)}, u32[]{:S(2)}) %collective-permute-start.22) | collective-permute-done | bytes 1048608 | tf_op jit(solution)/shard_map/ppermute | solution.py:300
  171.0 17.4 %collective-permute-done.21.refs_2_ = f32[4,2,128,256]{3,2,1,0:T(8,128)} collective-permute-done((f32[4,2,128,256]{3,2,1,0:T(8,128)}, f32[4,2,128,256]{3,2,1,0:T(8,128)}, u32[]{:S(2)}, u32[]{:S(2)}) %collective-permute-start.21) | collective-permute-done | bytes 1048608 | tf_op jit(solution)/shard_map/ppermute | solution.py:300
  188.4 3.9 %collective-permute-done.23.refs_4_ = f32[4,2,128,256]{3,2,1,0:T(8,128)} collective-permute-done((f32[4,2,128,256]{3,2,1,0:T(8,128)}, f32[4,2,128,256]{3,2,1,0:T(8,128)}, u32[]{:S(2)}, u32[]{:S(2)}) %collective-permute-start.23) | collective-permute-done | bytes 1048608 | tf_op jit(solution)/shard_map/ppermute | solution.py:300
  192.2 8.1 %place_got.1 = f32[128,2,32,256]{3,2,1,0:T(8,128)} custom-call(s32[2]{0:T(128)} %pad_add_fusion.sides_ref, f32[128,2,32,256]{3,2,1,0:T(8,128)} %place_own.1.refs_0_, f32[4,2,128,256]{3,2,1,0:T(8,128)} %copy-done.5, f32[4,2,128,256]{3,2,1,0:T(8,128)} %collective-permute-done.21.refs_2_, f32[4,2,128,256]{3,2,1,0:T(8,128)} %copy-done.6, ...), custom_call_target="tpu_custom_call", output_to_operand_aliasing={{}: (1, {})} | custom-call | bytes 16777216 | tf_op jit(solution)/shard_map/place_got/pallas_call | solution.py:233
  (65 shorter events, 0.7 us)
Async XLA Ops:
  0.0 11.5 %copy-start = (f32[2,256,256]{2,1,0:T(8,128)S(1)}, f32[2,256,256]{2,1,0:T(8,128)}, u32[]{:S(2)}) copy-start(f32[2,256,256]{2,1,0:T(8,128)} %param.8) | copy-start | bytes 1572868
  0.0 12.6 %copy-start.7 = (f32[2,256,256]{2,1,0:T(8,128)S(1)}, f32[2,256,256]{2,1,0:T(8,128)}, u32[]{:S(2)}) copy-start(f32[2,256,256]{2,1,0:T(8,128)} %param.7) | copy-start | bytes 1572868
  2.1 11.7 %copy-start.10 = (f32[2,256]{1,0:T(2,128)S(1)}, f32[2,256]{1,0:T(2,128)}, u32[]{:S(2)}) copy-start(f32[2,256]{1,0:T(2,128)} %param.9) | copy-start | bytes 6148
  7.4 37.0 %collective-permute-start.6 = (f32[6,2,64,256]{3,2,1,0:T(8,128)}, f32[6,2,64,256]{3,2,1,0:T(8,128)}, u32[]{:S(2)}, u32[]{:S(2)}) collective-permute-start(f32[6,2,64,256]{3,2,1,0:T(8,128)} %get-tuple-element.50.refs_0_), channel_id=1, source_target_pairs={{0,8},{8,0},{16,24},{24,16},{1,9},{9,1},{17,25},{25,17},{2,10},{10... | collective-permute-start | bytes 2359304 | tf_op jit(solution)/shard_map/ppermute | solution.py:300
  8.9 34.9 %collective-permute-start.1 = (f32[5,2,64,256]{3,2,1,0:T(8,128)}, f32[5,2,64,256]{3,2,1,0:T(8,128)S(1)}, u32[]{:S(2)}, u32[]{:S(2)}) collective-permute-start(f32[5,2,64,256]{3,2,1,0:T(8,128)} %get-tuple-element.41.refs_0_), channel_id=1, source_target_pairs={{0,16},{8,24},{16,0},{24,8},{1,17},{9,25},{17,1},{25,9},{2,18},{10... | collective-permute-start | bytes 1966088 | tf_op jit(solution)/shard_map/ppermute | solution.py:300
  10.4 31.8 %collective-permute-start.2 = (f32[6,2,64,256]{3,2,1,0:T(8,128)}, f32[6,2,64,256]{3,2,1,0:T(8,128)}, u32[]{:S(2)}, u32[]{:S(2)}) collective-permute-start(f32[6,2,64,256]{3,2,1,0:T(8,128)} %get-tuple-element.43), channel_id=1, source_target_pairs={{0,16},{8,24},{16,0},{24,8},{1,17},{9,25},{17,1},{25,9},{2,18},{10... | collective-permute-start | bytes 2359304 | tf_op jit(solution)/shard_map/ppermute | solution.py:300
  10.9 30.1 %collective-permute-start = (f32[5,2,64,256]{3,2,1,0:T(8,128)}, f32[5,2,64,256]{3,2,1,0:T(8,128)}, u32[]{:S(2)}, u32[]{:S(2)}) collective-permute-start(f32[5,2,64,256]{3,2,1,0:T(8,128)} %get-tuple-element.42), channel_id=1, source_target_pairs={{0,8},{8,0},{16,24},{24,16},{1,9},{9,1},{17,25},{25,17},{2,10},{10... | collective-permute-start | bytes 1966088 | tf_op jit(solution)/shard_map/ppermute | solution.py:300
  42.2 28.3 %collective-permute-start.3 = (f32[5,2,64,256]{3,2,1,0:T(8,128)}, f32[5,2,64,256]{3,2,1,0:T(8,128)S(1)}, u32[]{:S(2)}, u32[]{:S(2)}) collective-permute-start(f32[5,2,64,256]{3,2,1,0:T(8,128)} %collective-permute-done.refs_1_), channel_id=1, source_target_pairs={{0,16},{8,24},{16,0},{24,8},{1,17},{9,25},{17,1},{25,9},{2,18},{10... | collective-permute-start | bytes 1966088 | tf_op jit(solution)/shard_map/ppermute | solution.py:300
  43.8 27.5 %copy-start.11 = (f32[5,2,64,256]{3,2,1,0:T(8,128)}, f32[5,2,64,256]{3,2,1,0:T(8,128)S(1)}, u32[]{:S(2)}) copy-start(f32[5,2,64,256]{3,2,1,0:T(8,128)S(1)} %collective-permute-done.1.refs_2_) | copy-start | bytes 1966084
  43.8 25.2 %collective-permute-start.9 = (f32[4,2,64,256]{3,2,1,0:T(8,128)}, f32[4,2,64,256]{3,2,1,0:T(8,128)S(1)}, u32[]{:S(2)}, u32[]{:S(2)}) collective-permute-start(f32[4,2,64,256]{3,2,1,0:T(8,128)} %get-tuple-element.54), channel_id=1, source_target_pairs={{0,16},{8,24},{16,0},{24,8},{1,17},{9,25},{17,1},{25,9},{2,18},{10... | collective-permute-start | bytes 1572872 | tf_op jit(solution)/shard_map/ppermute | solution.py:300
  44.4 24.6 %collective-permute-start.7 = (f32[4,2,64,256]{3,2,1,0:T(8,128)}, f32[4,2,64,256]{3,2,1,0:T(8,128)}, u32[]{:S(2)}, u32[]{:S(2)}) collective-permute-start(f32[4,2,64,256]{3,2,1,0:T(8,128)} %get-tuple-element.51), channel_id=1, source_target_pairs={{0,8},{8,0},{16,24},{24,16},{1,9},{9,1},{17,25},{25,17},{2,10},{10... | collective-permute-start | bytes 1572872 | tf_op jit(solution)/shard_map/ppermute | solution.py:300
  44.9 38.9 %collective-permute-start.13 = (f32[6,2,64,256]{3,2,1,0:T(8,128)}, f32[6,2,64,256]{3,2,1,0:T(8,128)}, u32[]{:S(2)}, u32[]{:S(2)}) collective-permute-start(f32[6,2,64,256]{3,2,1,0:T(8,128)} %collective-permute-done.2.refs_2_), channel_id=1, source_target_pairs={{0,8},{8,0},{16,24},{24,16},{1,9},{9,1},{17,25},{25,17},{2,10},{10... | collective-permute-start | bytes 2359304 | tf_op jit(solution)/shard_map/ppermute | solution.py:300
  46.5 24.8 %copy-start.8 = (bf16[256,1536]{1,0:T(8,128)(2,1)}, bf16[256,1536]{1,0:T(8,128)(2,1)S(1)}, u32[]{:S(2)}) copy-start(bf16[256,1536]{1,0:T(8,128)(2,1)S(1)} %constant_dynamic-update-slice_fusion.near_ref) | copy-start | bytes 2359300
  69.0 1.5 copy-start.13
  69.0 23.8 %collective-permute-start.10 = (f32[4,2,64,256]{3,2,1,0:T(8,128)}, f32[4,2,64,256]{3,2,1,0:T(8,128)}, u32[]{:S(2)}, u32[]{:S(2)}) collective-permute-start(f32[4,2,64,256]{3,2,1,0:T(8,128)} %collective-permute-done.7.refs_5_), channel_id=1, source_target_pairs={{0,16},{8,24},{16,0},{24,8},{1,17},{9,25},{17,1},{25,9},{2,18},{10... | collective-permute-start | bytes 1572872 | tf_op jit(solution)/shard_map/ppermute | solution.py:300
  70.5 0.9 copy-start.12
  70.5 23.0 %collective-permute-start.8 = (f32[4,2,64,256]{3,2,1,0:T(8,128)}, f32[4,2,64,256]{3,2,1,0:T(8,128)}, u32[]{:S(2)}, u32[]{:S(2)}) collective-permute-start(f32[4,2,64,256]{3,2,1,0:T(8,128)} %get-tuple-element.52.refs_4_), channel_id=1, source_target_pairs={{0,16},{8,24},{16,0},{24,8},{1,17},{9,25},{17,1},{25,9},{2,18},{10... | collective-permute-start | bytes 1572872 | tf_op jit(solution)/shard_map/ppermute | solution.py:300
  78.1 42.7 %collective-permute-start.4 = (f32[2,4,128,256]{3,2,1,0:T(8,128)}, f32[2,4,128,256]{3,2,1,0:T(8,128)S(1)}, u32[]{:S(2)}, u32[]{:S(2)}) collective-permute-start(f32[2,4,128,256]{3,2,1,0:T(8,128)} %get-tuple-element.46), channel_id=1, source_target_pairs={{0,1},{1,2},{2,3},{3,4},{4,5},{5,6},{6,7},{8,9},{9,10},{10,11},{11... | collective-permute-start | bytes 3145736 | tf_op jit(solution)/shard_map/ppermute | solution.py:339
  80.0 3.8 %copy-start.9 = (bf16[256,1536]{1,0:T(8,128)(2,1)}, bf16[256,1536]{1,0:T(8,128)(2,1)S(1)}, u32[]{:S(2)}) copy-start(bf16[256,1536]{1,0:T(8,128)(2,1)S(1)} %constant_dynamic-update-slice_fusion.5.near_ref) | copy-start | bytes 2359300
  80.0 12.8 %copy-start.14 = (f32[4,2,64,256]{3,2,1,0:T(8,128)S(1)}, f32[4,2,64,256]{3,2,1,0:T(8,128)}, u32[]{:S(2)}) copy-start(f32[4,2,64,256]{3,2,1,0:T(8,128)} %copy-done.13) | copy-start | bytes 1572868
  80.0 51.3 %collective-permute-start.5 = (f32[2,4,128,256]{3,2,1,0:T(8,128)}, f32[2,4,128,256]{3,2,1,0:T(8,128)S(1)}, u32[]{:S(2)}, u32[]{:S(2)}) collective-permute-start(f32[2,4,128,256]{3,2,1,0:T(8,128)} %get-tuple-element.47), channel_id=1, source_target_pairs={{1,0},{2,1},{3,2},{4,3},{5,4},{6,5},{7,6},{9,8},{10,9},{11,10},{12... | collective-permute-start | bytes 3145736 | tf_op jit(solution)/shard_map/ppermute | solution.py:340
  90.7 42.6 %collective-permute-start.14 = (f32[2,4,128,256]{3,2,1,0:T(8,128)}, f32[2,4,128,256]{3,2,1,0:T(8,128)S(1)}, u32[]{:S(2)}, u32[]{:S(2)}) collective-permute-start(f32[2,4,128,256]{3,2,1,0:T(8,128)} %get-tuple-element.61), channel_id=1, source_target_pairs={{0,1},{1,2},{2,3},{3,4},{4,5},{5,6},{6,7},{8,9},{9,10},{10,11},{11... | collective-permute-start | bytes 3145736 | tf_op jit(solution)/shard_map/ppermute | solution.py:339
  92.8 14.3 %collective-permute-start.17 = (f32[4,2,64,256]{3,2,1,0:T(8,128)S(1)}, f32[4,2,64,256]{3,2,1,0:T(8,128)}, u32[]{:S(2)}, u32[]{:S(2)}) collective-permute-start(f32[4,2,64,256]{3,2,1,0:T(8,128)S(1)} %copy-done.14), channel_id=1, source_target_pairs={{0,8},{8,0},{16,24},{24,16},{1,9},{9,1},{17,25},{25,17},{2,10},{10... | collective-permute-start | bytes 1572872 | tf_op jit(solution)/shard_map/ppermute | solution.py:300
  93.5 24.9 %collective-permute-start.16 = (f32[4,2,64,256]{3,2,1,0:T(8,128)}, f32[4,2,64,256]{3,2,1,0:T(8,128)}, u32[]{:S(2)}, u32[]{:S(2)}) collective-permute-start(f32[4,2,64,256]{3,2,1,0:T(8,128)} %get-tuple-element.64.refs_4_), channel_id=1, source_target_pairs={{0,8},{8,0},{16,24},{24,16},{1,9},{9,1},{17,25},{25,17},{2,10},{10... | collective-permute-start | bytes 1572872 | tf_op jit(solution)/shard_map/ppermute | solution.py:300
  107.1 33.5 %collective-permute-start.15 = (f32[2,4,128,256]{3,2,1,0:T(8,128)}, f32[2,4,128,256]{3,2,1,0:T(8,128)}, u32[]{:S(2)}, u32[]{:S(2)}) collective-permute-start(f32[2,4,128,256]{3,2,1,0:T(8,128)} %get-tuple-element.62), channel_id=1, source_target_pairs={{1,0},{2,1},{3,2},{4,3},{5,4},{6,5},{7,6},{9,8},{10,9},{11,10},{12... | collective-permute-start | bytes 3145736 | tf_op jit(solution)/shard_map/ppermute | solution.py:340
  118.3 26.4 %collective-permute-start.11 = (f32[2,4,128,256]{3,2,1,0:T(8,128)}, f32[2,4,128,256]{3,2,1,0:T(8,128)}, u32[]{:S(2)}, u32[]{:S(2)}) collective-permute-start(f32[2,4,128,256]{3,2,1,0:T(8,128)} %get-tuple-element.57), channel_id=1, source_target_pairs={{0,1},{1,2},{2,3},{3,4},{4,5},{5,6},{6,7},{8,9},{9,10},{10,11},{11... | collective-permute-start | bytes 3145736 | tf_op jit(solution)/shard_map/ppermute | solution.py:339
  120.7 16.2 %copy-start.2 = (f32[2,4,128,256]{3,2,1,0:T(8,128)}, f32[2,4,128,256]{3,2,1,0:T(8,128)S(1)}, u32[]{:S(2)}) copy-start(f32[2,4,128,256]{3,2,1,0:T(8,128)S(1)} %collective-permute-done.4.refs_1_.low_ref) | copy-start | bytes 3145732
  120.7 25.2 %collective-permute-start.12 = (f32[2,4,128,256]{3,2,1,0:T(8,128)}, f32[2,4,128,256]{3,2,1,0:T(8,128)}, u32[]{:S(2)}, u32[]{:S(2)}) collective-permute-start(f32[2,4,128,256]{3,2,1,0:T(8,128)} %get-tuple-element.58), channel_id=1, source_target_pairs={{1,0},{2,1},{3,2},{4,3},{5,4},{6,5},{7,6},{9,8},{10,9},{11,10},{12... | collective-permute-start | bytes 3145736 | tf_op jit(solution)/shard_map/ppermute | solution.py:340
  131.4 5.6 %copy-start.3 = (f32[2,4,128,256]{3,2,1,0:T(8,128)}, f32[2,4,128,256]{3,2,1,0:T(8,128)S(1)}, u32[]{:S(2)}) copy-start(f32[2,4,128,256]{3,2,1,0:T(8,128)S(1)} %collective-permute-done.5.refs_2_.high_ref) | copy-start | bytes 3145732
  131.4 19.6 %collective-permute-start.18 = (f32[2,4,128,256]{3,2,1,0:T(8,128)}, f32[2,4,128,256]{3,2,1,0:T(8,128)}, u32[]{:S(2)}, u32[]{:S(2)}) collective-permute-start(f32[2,4,128,256]{3,2,1,0:T(8,128)} %get-tuple-element.67), channel_id=1, source_target_pairs={{0,1},{1,2},{2,3},{3,4},{4,5},{5,6},{6,7},{8,9},{9,10},{10,11},{11... | collective-permute-start | bytes 3145736 | tf_op jit(solution)/shard_map/ppermute | solution.py:339
  133.3 7.9 %copy-start.4 = (f32[2,4,128,256]{3,2,1,0:T(8,128)}, f32[2,4,128,256]{3,2,1,0:T(8,128)S(1)}, u32[]{:S(2)}) copy-start(f32[2,4,128,256]{3,2,1,0:T(8,128)S(1)} %collective-permute-done.14.refs_7_.low_ref) | copy-start | bytes 3145732
  133.3 17.6 %collective-permute-start.19 = (f32[2,4,128,256]{3,2,1,0:T(8,128)}, f32[2,4,128,256]{3,2,1,0:T(8,128)}, u32[]{:S(2)}, u32[]{:S(2)}) collective-permute-start(f32[2,4,128,256]{3,2,1,0:T(8,128)} %get-tuple-element.68), channel_id=1, source_target_pairs={{1,0},{2,1},{3,2},{4,3},{5,4},{6,5},{7,6},{9,8},{10,9},{11,10},{12... | collective-permute-start | bytes 3145736 | tf_op jit(solution)/shard_map/ppermute | solution.py:340
  140.5 26.2 %collective-permute-start.20 = (f32[4,2,128,256]{3,2,1,0:T(8,128)}, f32[4,2,128,256]{3,2,1,0:T(8,128)S(1)}, u32[]{:S(2)}, u32[]{:S(2)}) collective-permute-start(f32[4,2,128,256]{3,2,1,0:T(8,128)} %add_far.4), channel_id=1, source_target_pairs={{0,8},{8,0},{16,24},{24,16},{1,9},{9,1},{17,25},{25,17},{2,10},{10... | collective-permute-start | bytes 3145736 | tf_op jit(solution)/shard_map/ppermute | solution.py:300
  144.7 26.3 %collective-permute-start.22 = (f32[4,2,128,256]{3,2,1,0:T(8,128)}, f32[4,2,128,256]{3,2,1,0:T(8,128)S(1)}, u32[]{:S(2)}, u32[]{:S(2)}) collective-permute-start(f32[4,2,128,256]{3,2,1,0:T(8,128)} %add_far.6), channel_id=1, source_target_pairs={{0,16},{8,24},{16,0},{24,8},{1,17},{9,25},{17,1},{25,9},{2,18},{10... | collective-permute-start | bytes 3145736 | tf_op jit(solution)/shard_map/ppermute | solution.py:300
  149.5 38.9 %collective-permute-start.21 = (f32[4,2,128,256]{3,2,1,0:T(8,128)}, f32[4,2,128,256]{3,2,1,0:T(8,128)}, u32[]{:S(2)}, u32[]{:S(2)}) collective-permute-start(f32[4,2,128,256]{3,2,1,0:T(8,128)} %add_far.5), channel_id=1, source_target_pairs={{0,8},{8,0},{16,24},{24,16},{1,9},{9,1},{17,25},{25,17},{2,10},{10... | collective-permute-start | bytes 3145736 | tf_op jit(solution)/shard_map/ppermute | solution.py:300
  154.6 37.7 %collective-permute-start.23 = (f32[4,2,128,256]{3,2,1,0:T(8,128)}, f32[4,2,128,256]{3,2,1,0:T(8,128)}, u32[]{:S(2)}, u32[]{:S(2)}) collective-permute-start(f32[4,2,128,256]{3,2,1,0:T(8,128)} %add_far.7), channel_id=1, source_target_pairs={{0,16},{8,24},{16,0},{24,8},{1,17},{9,25},{17,1},{25,9},{2,18},{10... | collective-permute-start | bytes 3145736 | tf_op jit(solution)/shard_map/ppermute | solution.py:300
  155.4 45.0 %copy-start.1 = (f32[2,256,256]{2,1,0:T(8,128)S(1)}, f32[2,256,256]{2,1,0:T(8,128)}, u32[]{:S(2)}) copy-start(f32[2,256,256]{2,1,0:T(8,128)} %param.8) | copy-start | bytes 1572868
  166.8 25.5 %copy-start.5 = (f32[4,2,128,256]{3,2,1,0:T(8,128)}, f32[4,2,128,256]{3,2,1,0:T(8,128)S(1)}, u32[]{:S(2)}) copy-start(f32[4,2,128,256]{3,2,1,0:T(8,128)S(1)} %collective-permute-done.20.refs_1_) | copy-start | bytes 3145732
  171.0 21.2 %copy-start.6 = (f32[4,2,128,256]{3,2,1,0:T(8,128)}, f32[4,2,128,256]{3,2,1,0:T(8,128)S(1)}, u32[]{:S(2)}) copy-start(f32[4,2,128,256]{3,2,1,0:T(8,128)S(1)} %collective-permute-done.22.refs_3_) | copy-start | bytes 3145732

commit v3 on v0

v3 whole, which is shorter than its diff:
```python
import functools

import jax
import jax.numpy as jnp
from jax import lax
from jax.experimental import pallas as pl
from jax.experimental.pallas import tpu as pltpu
from jax.sharding import PartitionSpec as P


CUTS = 2
VMEM_LIMIT = 28 * 2**20
HBM = pl.BlockSpec(memory_space=pl.ANY)
SCALARS = pl.BlockSpec(memory_space=pltpu.SMEM)
LIGHT = pl.CostEstimate(flops=1024, bytes_accessed=4096, transcendentals=0)
HEAVY = pl.CostEstimate(flops=2**33, bytes_accessed=2**25, transcendentals=0)
PARAMS = pltpu.CompilerParams(vmem_limit_bytes=4 * 2**20)


def block_row(stream, side, row, depth, rows_x):
    if stream == 0:
        return row + side * (rows_x - 1 - 2 * row)
    return depth * (1 + side) + row


def own_rows(chunk, depth):
    high = depth // CUTS
    return list(range(chunk * high, (chunk + 1) * high))


def chunk_rows(stream, chunk, depth):
    rows = own_rows(chunk, depth)
    first = rows[0] + 1 if chunk else (0 if stream == 0 else -1)
    return list(range(first, rows[-1] + 2))


def where_rows(stream, chunk, depth):
    places = {}
    for back in (1, 0):
        if chunk >= back:
            for at, row in enumerate(chunk_rows(stream, chunk - back, depth)):
                places[row] = (1 - back, at)
    return places


def run(copies):
    for copy in copies:
        copy.start()
    for copy in copies:
        copy.wait()


def pick_kernel(chunk, depth, sides_ref, in_ref, *refs):
    outs, sems = refs[:-1], refs[-1]
    _, planes, rows_x, _ = in_ref.shape
    copies = []
    for stream in range(2):
        for other in range(2):
            side = 1 - sides_ref[stream] if other else sides_ref[stream]
            for at, row in enumerate(chunk_rows(stream, chunk, depth)):
                x = block_row(stream, side, row, depth, rows_x)
                for z in range(planes):
                    out = outs[2 * stream + other].at[at, z]
                    copies.append(pltpu.make_async_copy(in_ref.at[:, z, x], out, sems.at[len(copies)]))
    run(copies)


def pick(chunk, residual, sides, depth):
    steps, planes, _, rows_y = residual.shape
    counts = [len(chunk_rows(stream, chunk, depth)) for stream in (0, 0, 1, 1)]
    outs = pl.pallas_call(
        functools.partial(pick_kernel, chunk, depth),
        out_shape=[jax.ShapeDtypeStruct((c, planes, steps, rows_y), jnp.float32) for c in counts],
        in_specs=[SCALARS, HBM],
        out_specs=[HBM] * 4,
        scratch_shapes=[pltpu.SemaphoreType.DMA((sum(counts) * planes,))],
        compiler_params=PARAMS,
        cost_estimate=LIGHT,
        name="pick",
    )(sides, residual)
    return [outs[0:2], outs[2:4]]


def edge_kernel(chunk, depth, groups, *refs):
    raws, (up_ref, down_ref, sems) = refs[:-3], refs[-3:]
    planes = raws[0].shape[1]
    backs = 2 if chunk else 1
    copies = []
    for stream in range(2):
        places = where_rows(stream, chunk, depth)
        for at, row in enumerate(own_rows(chunk, depth)):
            back, index = places[row]
            for group in range(groups):
                raw = raws[(stream * backs + back - 2 + backs) * groups + group]
                for z, out in ((planes - 1, up_ref), (0, down_ref)):
                    copy = pltpu.make_async_copy(
                        raw.at[index, z], out.at[stream, at, group], sems.at[len(copies)]
                    )
                    copies.append(copy)
    run(copies)


def edges(chunk, depth, raws):
    groups = len(raws[0][0])
    _, _, steps, rows_y = raws[0][0][0].shape
    flat = [raw for stream in raws for arrays in stream for raw in arrays]
    high = depth // CUTS
    shape = jax.ShapeDtypeStruct((2, high, groups, steps, rows_y), jnp.float32)
    return pl.pallas_call(
        functools.partial(edge_kernel, chunk, depth, groups),
        out_shape=[shape] * 2,
        in_specs=[HBM] * len(flat),
        out_specs=[HBM] * 2,
        scratch_shapes=[pltpu.SemaphoreType.DMA((4 * high * groups,))],
        compiler_params=PARAMS,
        cost_estimate=LIGHT,
        name="edges",
    )(*flat)


def halves(value):
    high = value.astype(jnp.bfloat16)
    return high, (value - high.astype(jnp.float32)).astype(jnp.bfloat16)


def map_halves(value):
    high = lax.reduce_precision(value, exponent_bits=8, mantissa_bits=7)
    return high.astype(jnp.bfloat16), (value - high).astype(jnp.bfloat16)


def apply_kernel(chunk, depth, order, sides_ref, map_a_ref, map_b_ref, *refs):
    refs = list(refs)
    early_low, early_high, late_low, late_high = refs[:4]
    out_ref, gives = refs[-11], refs[-10:-8]
    cells, low_cells, high_cells, own, give, raw_sems, edge_sems, out_sems = refs[-8:]
    raws = refs[4:-11]
    if chunk:
        raws = raws[:-1]
    groups = len(order[0][0]) + len(order[0][1])
    backs = 2 if chunk else 1
    _, planes, rows_x, rows_y = out_ref.shape
    steps = cells.shape[2] // groups
    high = depth // CUTS
    loads, edge_loads, slots = [{}, {}], [{}, {}], [{}, {}]
    slot = 0
    number = 0
    for stream in range(2):
        places = where_rows(stream, chunk, depth)
        rows = own_rows(chunk, depth)
        for row in range(rows[0] - 1, rows[-1] + 2):
            if row in places:
                back, index = places[row]
                copies = []
                for group in range(groups):
                    raw = raws[(stream * backs + back - 2 + backs) * groups + group]
                    span = pl.ds(group * steps, steps)
                    copies.append(
                        pltpu.make_async_copy(raw.at[index], cells.at[slot, :, span], raw_sems.at[slot, group])
                    )
                loads[stream][row] = copies
                slots[stream][row] = slot
                slot += 1
            if row in rows:
                at = row - rows[0]
                copies = []
                for kind, (low, up) in enumerate(((early_low, early_high), (late_low, late_high))):
                    for place, group in enumerate(order[stream][kind]):
                        span = pl.ds(group * steps, steps)
                        for way, (source, target) in enumerate(((low, low_cells), (up, high_cells))):
                            copies.append(
                                pltpu.make_async_copy(
                                    source.at[stream, at, place],
                                    target.at[number, span],
                                    edge_sems.at[number, group, way],
                                )
                            )
                edge_loads[stream][row] = (number, copies)
                number += 1
    for stream in range(2):
        for row in sorted(loads[stream]):
            for copy in loads[stream][row]:
                copy.start()
            if row in edge_loads[stream]:
                for copy in edge_loads[stream][row][1]:
                    copy.start()

    stores = []
    for stream in range(2):
        maps = (map_a_ref, map_b_ref)[stream][...]
        half = maps.shape[0] // 2
        waited = set()
        for at, row in enumerate(own_rows(chunk, depth)):
            for beside in (row - 1, row, row + 1):
                if beside in loads[stream] and beside not in waited:
                    waited.add(beside)
                    for copy in loads[stream][beside]:
                        copy.wait()
            number, copies = edge_loads[stream][row]
            for copy in copies:
                copy.wait()
            x = block_row(stream, sides_ref[stream], row, depth, rows_x)
            for z in range(planes):
                mid = cells[slots[stream][row], z]
                lane = lax.broadcasted_iota(jnp.int32, mid.shape, 1)
                total = jnp.where(lane == 0, 0.0, pltpu.roll(mid, 1, 1))
                total = total + jnp.where(lane == rows_y - 1, 0.0, pltpu.roll(mid, rows_y - 1, 1))
                for beside in (row - 1, row + 1):
                    if beside in slots[stream]:
                        total = total + cells[slots[stream][beside], z]
                total = total + (cells[slots[stream][row], z - 1] if z else low_cells[number])
                total = total + (
                    cells[slots[stream][row], z + 1] if z < planes - 1 else high_cells[number]
                )
                mid_h, mid_l = halves(mid)
                sum_h, sum_l = halves(total)
                stack = jnp.concatenate([mid_h, mid_h, mid_l, sum_h, sum_h, sum_l], axis=0)
                value = jnp.dot(maps, stack, preferred_element_type=jnp.float32)
                own[number, z] = value[:half]
                give[number, z] = value[half:]
                stores.append(
                    pltpu.make_async_copy(own.at[number, z], out_ref.at[:, z, x], out_sems.at[number, z])
                )
                stores[-1].start()
            stores.append(
                pltpu.make_async_copy(give.at[number], gives[stream].at[at], out_sems.at[number, planes])
            )
            stores[-1].start()
    for copy in stores:
        copy.wait()


def apply(chunk, depth, order, sides, maps, early, late, raws, shape, result):
    groups = len(raws[0][0])
    _, planes, steps, rows_y = raws[0][0][0].shape
    high = depth // CUTS
    half = shape[0]
    flat = [raw for stream in raws for arrays in stream for raw in arrays]
    first = [] if result is None else [result]
    give = jax.ShapeDtypeStruct((high, planes, half, rows_y), jnp.float32)
    total = groups * steps
    slots = sum(len([r for r in range(-1 + chunk * high, (chunk + 1) * high + 1) if s or r >= 0]) for s in range(2))
    vmem = pl.BlockSpec(memory_space=pltpu.VMEM)
    count = 3 + 4 + len(flat)
    return pl.pallas_call(
        functools.partial(apply_kernel, chunk, depth, order),
        out_shape=[jax.ShapeDtypeStruct(shape, jnp.float32), give, give],
        in_specs=[SCALARS, vmem, vmem] + [HBM] * (4 + len(flat) + len(first)),
        out_specs=[HBM] * 3,
        scratch_shapes=[
            pltpu.VMEM((slots, planes, total, rows_y), jnp.float32),
            pltpu.VMEM((2 * high, total, rows_y), jnp.float32),
            pltpu.VMEM((2 * high, total, rows_y), jnp.float32),
            pltpu.VMEM((2 * high, planes, half, rows_y), jnp.float32),
            pltpu.VMEM((2 * high, planes, half, rows_y), jnp.float32),
            pltpu.SemaphoreType.DMA((slots, groups)),
            pltpu.SemaphoreType.DMA((2 * high, groups, 2)),
            pltpu.SemaphoreType.DMA((2 * high, planes + 1)),
        ],
        input_output_aliases={count: 0} if first else {},
        compiler_params=pltpu.CompilerParams(vmem_limit_bytes=VMEM_LIMIT),
        cost_estimate=HEAVY,
        name="apply",
    )(sides, *maps, *early, *late, *flat, *first)


def place_kernel(chunk, depth, sides_ref, got_a, got_b, _, out_ref, sems):
    _, planes, rows_x, _ = out_ref.shape
    copies = []
    for stream, got in enumerate((got_a, got_b)):
        for at, row in enumerate(own_rows(chunk, depth)):
            x = block_row(stream, 1 - sides_ref[stream], row, depth, rows_x)
            for z in range(planes):
                copies.append(pltpu.make_async_copy(got.at[at, z], out_ref.at[:, z, x], sems.at[len(copies)]))
    run(copies)


def place(chunk, depth, sides, got, result):
    planes = result.shape[1]
    return pl.pallas_call(
        functools.partial(place_kernel, chunk, depth),
        out_shape=jax.ShapeDtypeStruct(result.shape, jnp.float32),
        in_specs=[SCALARS] + [HBM] * 3,
        out_specs=HBM,
        scratch_shapes=[pltpu.SemaphoreType.DMA((2 * depth // CUTS * planes,))],
        input_output_aliases={3: 0},
        compiler_params=PARAMS,
        cost_estimate=LIGHT,
        name="place",
    )(sides, *got, result)


def after(value, *others):
    return lax.optimization_barrier((value, *others))[0]


def make_maps(forward_map, back_map, eigen_values, ratio, me, count, bits):
    steps = forward_map.shape[1]
    local_steps = steps // count
    highest = lax.Precision.HIGHEST
    real_part = 6.0 + eigen_values[0]
    imag_part = eigen_values[1]
    denom = real_part * real_part + imag_part * imag_part
    coef_re = (real_part / denom)[:, None]
    coef_im = (-imag_part / denom)[:, None]
    order = jnp.bitwise_xor(me, jnp.arange(count))
    ahead = (forward_map * ratio).reshape(2, steps, count, local_steps)
    ahead = jnp.take(ahead, order, axis=2).reshape(2, steps, steps)
    once_re = coef_re * ahead[0] - coef_im * ahead[1]
    once_im = coef_re * ahead[1] + coef_im * ahead[0]
    twice_re = coef_re * once_re - coef_im * once_im
    twice_im = coef_re * once_im + coef_im * once_re
    right = jnp.concatenate(
        [jnp.concatenate([once_re, twice_re], axis=1), jnp.concatenate([once_im, twice_im], axis=1)], axis=0
    )
    blocks = jnp.stack([me, jnp.bitwise_xor(me, bits[0]), jnp.bitwise_xor(me, bits[1])])
    back = jnp.take(back_map.reshape(2, count, local_steps, steps), blocks, axis=1)
    left_re = jnp.concatenate([back[0], -back[1]], axis=2)
    left_im = jnp.concatenate([back[1], back[0]], axis=2)
    left = jnp.stack([left_re, left_im], axis=1).reshape(3, 2 * local_steps, 2 * steps)
    maps = jnp.einsum("bmk,kn->bmn", left, right, precision=highest)
    result = []
    for other in (1, 2):
        both = jnp.concatenate([maps[0], maps[other]], axis=0)
        one_h, one_l = map_halves(both[:, :steps])
        two_h, two_l = map_halves(both[:, steps:])
        result.append(jnp.concatenate([one_h, one_l, one_h, two_h, two_l, two_h], axis=1))
    return result


def local(residual, step_ratio, forward_map, back_map, eigen_values):
    local_steps, planes, rows_x, rows_y = residual.shape
    depth = rows_x // 4
    count = lax.axis_size("tm")
    bits = (1, count // 2)
    all_bits = [1 << k for k in range(count.bit_length() - 1)]
    me = lax.axis_index("tm")
    sides = jnp.stack([jnp.where(jnp.bitwise_and(me, b) > 0, 1, 0) for b in bits]).astype(jnp.int32)
    ratio = lax.all_gather(step_ratio, "tm", tiled=True).astype(jnp.float32) / 8.0

    def swap(data, bit):
        return lax.ppermute(data, "tm", [(i, i ^ bit) for i in range(count)])

    spaces = lax.axis_size("space")
    upward = [(i, i + 1) for i in range(spaces - 1)]
    downward = [(i + 1, i) for i in range(spaces - 1)]

    queues = [[], []]

    def swap_in_turn(data, bit, *others, flight=2):
        queue = queues[0 if bit == bits[0] else 1]
        if len(queue) >= flight:
            others = (queue[-flight], *others)
        if others:
            data = after(data, *others)
        got = swap(data, bit)
        queue.append(got)
        return got

    masks = range(count)
    order = [[[m for m in masks if m in (0, b)], [m for m in masks if m not in (0, b)]] for b in bits]
    held = [[None] * CUTS for _ in range(2)]

    maps = make_maps(forward_map, back_map, eigen_values, ratio, me, count, bits)
    firsts = []

    def raw(chunk):
        data = after(residual, *firsts[-1]) if firsts else residual
        mine = pick(chunk, data, sides, depth)
        have = [{0: mine[s][0], bits[s]: swap_in_turn(mine[s][1], bits[s])} for s in range(2)]
        firsts.append([have[s][bits[s]] for s in range(2)])
        for bit in all_bits:
            for mask in masks:
                for stream in (1, 0):
                    now = have[stream]
                    free = bit != bits[stream] and not mask & bit
                    if free and mask in now and (mask | bit) not in now:
                        others = maps if mask and chunk == 0 else []
                        now[mask | bit] = swap_in_turn(now[mask], bit, *others)
        for stream in range(2):
            held[stream][chunk] = [have[stream][mask] for mask in masks]

    def beside(chunk, kind, *others):
        arrays = [
            [[a[m] for m in order[s][kind]] for a in held[s][max(chunk - 1, 0) : chunk + 1]] for s in range(2)
        ]
        if others:
            arrays[0][-1][0] = after(arrays[0][-1][0], *others)
        up, down = edges(chunk, depth, arrays)
        return lax.ppermute(up, "space", upward), lax.ppermute(down, "space", downward)

    gives = []
    result = None
    for chunk in range(CUTS):
        raw(chunk)
    shape = (2 * local_steps, planes, rows_x, rows_y)
    for chunk in range(CUTS):
        early = beside(chunk, 0, *(gives[-1] if gives else []))
        late = beside(chunk, 1, *early)
        if chunk + 1 < CUTS:
            late = [after(a, *firsts[chunk + 1]) for a in late]
        used = [held[s][max(chunk - 1, 0) : chunk + 1] for s in range(2)]
        result, *give = apply(chunk, depth, order, sides, maps, early, late, used, shape, result)
        gives.append(give)
    for chunk in range(CUTS):
        flight = 1 if chunk else 2
        got = [swap_in_turn(gives[chunk][s], bits[s], flight=flight) for s in range(2)]
        result = place(chunk, depth, sides, got, result)
    return result.reshape(2, local_steps, planes, rows_x, rows_y)


def solution(mesh):
    in_specs = (P("tm", "space", None, None), P("tm"), P(), P(), P())
    out_specs = P(None, "tm", "space", None, None)
    return jax.shard_map(local, mesh=mesh, in_specs=in_specs, out_specs=out_specs, check_vma=False)
```

time: 884 us -> 242 us (0.27)
  local copies, waits for them, and re-layouts: 269 us -> 16.3 us
  blocking collectives: 249 us -> 25.2 us
  other arithmetic: 195 us -> 10.7 us
  Pallas kernels: 0 us -> 62 us
  matrix products: 43.8 us -> 2.73 us
  starting transfers between devices: 10.5 us -> 42.1 us
  waiting for transfers between devices: 107 us -> 81.1 us
    all_to_all x3 -> x0, blocking collectives: 249 us -> none  [the longest x2 154 us: transform(): moved = lax.all_to_all(data, 'tm', split_axis=2, concat_axis=1, tiled=True)]
    unnamed x2 -> x8, other arithmetic: 95.7 us -> 0.27 us
    all_to_all x1 -> x0, waiting for transfers between devices: 91.1 us -> none  [transform(): back = lax.all_to_all(mixed, 'tm', split_axis=1, concat_axis=2, tiled=True)]
    all_to_all x8 -> x0, local copies, waits for them, and re-layouts: 84.7 us -> none  [the longest x4 44.1 us: transform(): moved = lax.all_to_all(data, 'tm', split_axis=2, concat_axis=1, tiled=True)]
    unnamed x19 -> x10, local copies, waits for them, and re-layouts: 87.8 us -> 6.4 us
    ppermute x2 -> x24, waiting for transfers between devices: 16 us -> 81.1 us  [the longest x16 62 us: swap(): return lax.ppermute(data, 'tm', [(i, i ^ bit) for i in range(count)])]
    pallas_call x0 -> x10, Pallas kernels: none -> 62 us  [the longest x2 42.2 us: apply(): pl.pallas_call(functools.partial(apply_kernel, chunk, depth, order), out_...]
    all_to_all x2 -> x0, other arithmetic: 43.8 us -> none  [transform(): moved = lax.all_to_all(data, 'tm', split_axis=2, concat_axis=1, tiled=True)]
  transfers between devices with their start and end apart: 3 -> 24, of which waited for: 3 -> 13; matrix products, arithmetic and copies ran while one was open for 4% -> 11% of each run, Pallas kernels for 0% -> 12%
where the time goes in v3:
time: 242 us; the launch traced here: 241 us
  waiting for transfers between devices  81.1 us (34%)
  Pallas kernels  62 us (26%)
  starting transfers between devices  42.1 us (17%)
  blocking collectives  25.2 us (10%)
  local copies, waits for them, and re-layouts  16.3 us (7%)
  other arithmetic  10.7 us (4%)
  matrix products  2.73 us (1%)
    ppermute x16, waiting for transfers between devices, swap(): return lax.ppermute(data, 'tm', [(i, i ^ bit) for i in range(count)])  62 us
    pallas_call x2, Pallas kernels, apply(): pl.pallas_call(functools.partial(apply_kernel, chunk, depth, order), out_...  42.2 us
    unnamed x1, blocking collectives  25.2 us
    ppermute x16, starting transfers between devices, swap(): return lax.ppermute(data, 'tm', [(i, i ^ bit) for i in range(count)])  19.5 us
    ppermute x4, waiting for transfers between devices, beside(): lax.ppermute(up, 'space', upward)  15.6 us
    ppermute x4, starting transfers between devices, beside(): lax.ppermute(down, 'space', downward)  15 us
    pallas_call x4, Pallas kernels, edges(): pl.pallas_call(functools.partial(edge_kernel, chunk, depth, groups), out_...  10.5 us
    ppermute x4, starting transfers between devices, beside(): lax.ppermute(up, 'space', upward)  7.68 us
  transfers between devices with their start and end apart: 24, of which 13 were waited for; matrix products, arithmetic and copies ran while one was open for 11% of the time, Pallas kernels for 12%

profile of v3, /device:TPU:8, one launch (start us, length us, event | category | flops | bytes accessed | tf_op | source)
XLA Modules:
  0.0 241.4 jit_solution(5844918982862775029)
XLA Ops:
  0.1 2.2 copy-done.1
  2.3 3.0 %pick.2 = (f32[5,2,64,256]{3,2,1,0:T(8,128)S(1)}, f32[5,2,64,256]{3,2,1,0:T(8,128)}, f32[6,2,64,256]{3,2,1,0:T(8,128)S(1)}, f32[6,2,64,256]{3,2,1,0:T(8,128)}) custom-call(s32[2]{0:T(128)S(1)} %pad_add_fusion.sides_ref, f32[64,2,32,256]{3,2,1,0:T(8,128)S(1)} %copy-done.1), custom_call_target="tpu_custom_call" | custom-call | flops 1024 | bytes 4096 | tf_op jit(solution)/shard_map/pick/pallas_call | solution.py:71
  5.3 1.6 collective-permute-start
  6.9 1.5 collective-permute-start.4
  9.4 0.6 compare_and_fusion
  10.1 1.3 gather_fusion
  11.5 1.1 select_bitcast_fusion.1
  12.6 0.7 fusion.26
  13.3 0.8 slice_bitcast_fusion.3
  14.1 1.3 dynamic-slice
  16.0 0.9 dynamic-update-slice
  16.9 25.2 %all-reduce = s32[256]{0:T(256)S(1)} all-reduce(s32[256]{0:T(256)S(1)} %dynamic-update-slice), channel_id=1, replica_groups=mesh['tm'=4,'space'=8] {'tm'}, use_global_device_ids=true, to_apply=%add | all-reduce | flops 256 | bytes 2048
  42.1 1.3 slice_add_fusion
  43.5 1.3 maximum_bitcast_fusion.2
  44.8 0.9 copy.11
  45.8 2.0 copy.12
  47.8 1.9 broadcast_multiply_fusion
  49.7 2.4 gather_fusion.1
  52.2 1.2 select_bitcast_fusion
  53.3 0.8 fusion.27
  54.1 1.8 copy.14
  55.9 1.8 copy.13
  57.7 0.7 fusion.22
  58.4 1.2 multiply_subtract_fusion
  59.7 2.7 %fusion = f32[3,128,512]{2,1,0:T(8,128)S(1)} fusion(f32[3,128,512]{2,1,0:T(8,128)} %bitcast.50, f32[256,256]{1,0:T(8,128)S(1)} %multiply_add_fusion, f32[256,256]{1,0:T(8,128)S(1)} %get-tuple-element.90, f32[256,256]{1,0:T(8,128)S(1)} %get-tuple-element.89, f32[256,256]{1,0:T(8,128)S(1)} %get-tuple-element.91), kind=kOutput, calls=%fused_computation.3 | convolution fusion | flops 1208745984 | bytes 2621440 | tf_op jit(solution)/shard_map/bmk,kn->bmn/dot_general | solution.py:320
  62.8 2.4 edges.4
  65.2 1.9 collective-permute-start.2
  67.1 3.6 %collective-permute-start.3 = (f32[2,4,2,64,256]{4,3,2,1,0:T(8,128)S(1)}, f32[2,4,2,64,256]{4,3,2,1,0:T(8,128)S(1)}, u32[]{:S(2)}, u32[]{:S(2)}) collective-permute-start(f32[2,4,2,64,256]{4,3,2,1,0:T(8,128)S(1)} %get-tuple-element.52), channel_id=1, source_target_pairs={{1,0},{2,1},{3,2},{4,3},{5,4},{6,5},{7,6},{9,8},{10,9},{11,10},{12... | collective-permute-start | bytes 3145736 | tf_op jit(solution)/shard_map/ppermute | solution.py:389
  70.9 1.6 collective-permute-start.7
  72.9 8.4 %collective-permute-done.2.refs_0_ = f32[2,4,2,64,256]{4,3,2,1,0:T(8,128)S(1)} collective-permute-done((f32[2,4,2,64,256]{4,3,2,1,0:T(8,128)S(1)}, f32[2,4,2,64,256]{4,3,2,1,0:T(8,128)S(1)}, u32[]{:S(2)}, u32[]{:S(2)}) %collective-permute-start.2) | collective-permute-done | bytes 1048608 | tf_op jit(solution)/shard_map/ppermute | solution.py:389
  81.3 1.8 collective-permute-done.3.refs_1_
  83.1 5.9 %collective-permute-done.5.refs_1_.refs_7_ = f32[5,2,64,256]{3,2,1,0:T(8,128)S(1)} collective-permute-done((f32[5,2,64,256]{3,2,1,0:T(8,128)}, f32[5,2,64,256]{3,2,1,0:T(8,128)S(1)}, u32[]{:S(2)}, u32[]{:S(2)}) %collective-permute-start.5) | collective-permute-done | bytes 655392 | tf_op jit(solution)/shard_map/ppermute | solution.py:341
  89.0 1.4 collective-permute-done.7.refs_3_.refs_11_.refs_5_.refs_15_
  90.3 2.4 edges.5
  92.7 1.9 collective-permute-start.8
  94.6 3.8 %collective-permute-start.11 = (f32[2,4,2,64,256]{4,3,2,1,0:T(8,128)S(1)}, f32[2,4,2,64,256]{4,3,2,1,0:T(8,128)S(1)}, u32[]{:S(2)}, u32[]{:S(2)}) collective-permute-start(f32[2,4,2,64,256]{4,3,2,1,0:T(8,128)S(1)} %get-tuple-element.62), channel_id=1, source_target_pairs={{1,0},{2,1},{3,2},{4,3},{5,4},{6,5},{7,6},{9,8},{10,9},{11,10},{12... | collective-permute-start | bytes 3145736 | tf_op jit(solution)/shard_map/ppermute | solution.py:389
  98.5 2.5 %pick.3 = (f32[4,2,64,256]{3,2,1,0:T(8,128)S(1)}, f32[4,2,64,256]{3,2,1,0:T(8,128)S(1)}, f32[4,2,64,256]{3,2,1,0:T(8,128)S(1)}, f32[4,2,64,256]{3,2,1,0:T(8,128)S(1)}) custom-call(s32[2]{0:T(128)S(1)} %pad_add_fusion.sides_ref, f32[64,2,32,256]{3,2,1,0:T(8,128)S(1)} %copy-done.2), custom_call_target="tpu_custom_call" | custom-call | flops 1024 | bytes 4096 | tf_op jit(solution)/shard_map/pick/pallas_call | solution.py:71
  100.9 0.6 collective-permute-start.10
  101.5 1.5 collective-permute-start.9
  103.0 11.8 %collective-permute-done.10.refs_7_.refs_18_ = f32[4,2,64,256]{3,2,1,0:T(8,128)S(1)} collective-permute-done((f32[4,2,64,256]{3,2,1,0:T(8,128)S(1)}, f32[4,2,64,256]{3,2,1,0:T(8,128)S(1)}, u32[]{:S(2)}, u32[]{:S(2)}) %collective-permute-start.10) | collective-permute-done | bytes 524320 | tf_op jit(solution)/shard_map/ppermute | solution.py:341
  115.0 20.0 %apply.2 = (f32[128,2,32,256]{3,2,1,0:T(8,128)}, f32[4,2,128,256]{3,2,1,0:T(8,128)S(1)}, f32[4,2,128,256]{3,2,1,0:T(8,128)S(1)}) custom-call(s32[2]{0:T(128)S(1)} %pad_add_fusion.sides_ref, bf16[256,1536]{1,0:T(8,128)(2,1)S(1)} %constant_dynamic-update-slice_fusion.map_a_ref, bf16[256,1536]{1,0:T(8,128)(2,1)S(1)} %constant_dynamic-update-slice_fusion.2.map_b_ref, ...), custom_call_target="tpu_custom_call" | custom-call | flops 8589934592 | bytes 33554432 | tf_op jit(solution)/shard_map/apply/pallas_call | solution.py:244
  135.0 2.9 %edges.6 = (f32[2,4,2,64,256]{4,3,2,1,0:T(8,128)S(1)}, f32[2,4,2,64,256]{4,3,2,1,0:T(8,128)S(1)}) custom-call(f32[5,2,64,256]{3,2,1,0:T(8,128)S(1)} %get-tuple-element.45.refs_0_.refs_4_, f32[5,2,64,256]{3,2,1,0:T(8,128)} %collective-permute-done.refs_1_.refs_5_, f32[4,2,64,256]{3,2,1,0:T(8,128)S(1)} %get-tuple-element.70.refs_2_.refs_8_, ...), custom_call_target="tpu_custom_call" | custom-call | flops 1024 | bytes 4096 | tf_op jit(solution)/shard_map/edges/pallas_call | solution.py:109
  137.9 1.9 collective-permute-start.12
  139.8 3.6 %collective-permute-start.13 = (f32[2,4,2,64,256]{4,3,2,1,0:T(8,128)S(1)}, f32[2,4,2,64,256]{4,3,2,1,0:T(8,128)S(1)}, u32[]{:S(2)}, u32[]{:S(2)}) collective-permute-start(f32[2,4,2,64,256]{4,3,2,1,0:T(8,128)S(1)} %get-tuple-element.69), channel_id=1, source_target_pairs={{1,0},{2,1},{3,2},{4,3},{5,4},{6,5},{7,6},{9,8},{10,9},{11,10},{12... | collective-permute-start | bytes 3145736 | tf_op jit(solution)/shard_map/ppermute | solution.py:389
  143.5 1.6 collective-permute-start.14
  145.6 1.5 collective-permute-start.17
  147.1 11.3 %collective-permute-done.14.refs_2_.refs_10_ = f32[4,2,64,256]{3,2,1,0:T(8,128)S(1)} collective-permute-done((f32[4,2,64,256]{3,2,1,0:T(8,128)S(1)}, f32[4,2,64,256]{3,2,1,0:T(8,128)S(1)}, u32[]{:S(2)}, u32[]{:S(2)}) %collective-permute-start.14) | collective-permute-done | bytes 524320 | tf_op jit(solution)/shard_map/ppermute | solution.py:341
  158.4 1.5 collective-permute-start.16
  159.9 7.5 %collective-permute-done.15.refs_3_.refs_11_ = f32[4,2,64,256]{3,2,1,0:T(8,128)S(1)} collective-permute-done((f32[4,2,64,256]{3,2,1,0:T(8,128)S(1)}, f32[4,2,64,256]{3,2,1,0:T(8,128)S(1)}, u32[]{:S(2)}, u32[]{:S(2)}) %collective-permute-start.15) | collective-permute-done | bytes 524320 | tf_op jit(solution)/shard_map/ppermute | solution.py:341
  167.5 1.5 collective-permute-done.16.refs_6_.refs_17_
  168.9 2.9 %edges.7 = (f32[2,4,2,64,256]{4,3,2,1,0:T(8,128)S(1)}, f32[2,4,2,64,256]{4,3,2,1,0:T(8,128)S(1)}) custom-call(f32[5,2,64,256]{3,2,1,0:T(8,128)} %collective-permute-done.4.refs_0_.refs_6_, f32[5,2,64,256]{3,2,1,0:T(8,128)S(1)} %collective-permute-done.5.refs_1_.refs_7_, f32[4,2,64,256]{3,2,1,0:T(8,128)S(1)} %collective-permute-done.14.refs_2_.refs_10_, ...), custom_call_target="tpu_custom_call" | custom-call | flops 1024 | bytes 4096 | tf_op jit(solution)/shard_map/edges/pallas_call | solution.py:109
  171.8 1.9 collective-permute-start.18
  173.7 3.9 %collective-permute-start.19 = (f32[2,4,2,64,256]{4,3,2,1,0:T(8,128)S(1)}, f32[2,4,2,64,256]{4,3,2,1,0:T(8,128)S(1)}, u32[]{:S(2)}, u32[]{:S(2)}) collective-permute-start(f32[2,4,2,64,256]{4,3,2,1,0:T(8,128)S(1)} %get-tuple-element.76), channel_id=1, source_target_pairs={{1,0},{2,1},{3,2},{4,3},{5,4},{6,5},{7,6},{9,8},{10,9},{11,10},{12... | collective-permute-start | bytes 3145736 | tf_op jit(solution)/shard_map/ppermute | solution.py:389
  177.6 1.6 collective-permute-start.20
  179.2 1.5 collective-permute-start.22
  180.7 7.2 %collective-permute-done.18.refs_2_ = f32[2,4,2,64,256]{4,3,2,1,0:T(8,128)S(1)} collective-permute-done((f32[2,4,2,64,256]{4,3,2,1,0:T(8,128)S(1)}, f32[2,4,2,64,256]{4,3,2,1,0:T(8,128)S(1)}, u32[]{:S(2)}, u32[]{:S(2)}) %collective-permute-start.18) | collective-permute-done | bytes 1048608 | tf_op jit(solution)/shard_map/ppermute | solution.py:389
  187.9 1.8 collective-permute-done.19.refs_3_
  189.7 22.2 %apply.3 = (f32[128,2,32,256]{3,2,1,0:T(8,128)}, f32[4,2,128,256]{3,2,1,0:T(8,128)S(1)}, f32[4,2,128,256]{3,2,1,0:T(8,128)S(1)}) custom-call(s32[2]{0:T(128)S(1)} %pad_add_fusion.sides_ref, bf16[256,1536]{1,0:T(8,128)(2,1)S(1)} %constant_dynamic-update-slice_fusion.map_a_ref, ...), custom_call_target="tpu_custom_call", output_to_operand_aliasing={{0}: (23, {})} | custom-call | flops 8589934592 | bytes 33554432 | tf_op jit(solution)/shard_map/apply/pallas_call | solution.py:244
  211.9 1.6 collective-permute-start.23
  213.4 1.5 collective-permute-start.21
  214.9 2.0 place.2._
  216.9 21.0 %collective-permute-done.23.got_b = f32[4,2,128,256]{3,2,1,0:T(8,128)S(1)} collective-permute-done((f32[4,2,128,256]{3,2,1,0:T(8,128)S(1)}, f32[4,2,128,256]{3,2,1,0:T(8,128)S(1)}, u32[]{:S(2)}, u32[]{:S(2)}) %collective-permute-start.23) | collective-permute-done | bytes 1048608 | tf_op jit(solution)/shard_map/ppermute | solution.py:341
  237.9 1.4 collective-permute-done.21.got_a
  239.3 2.0 place.3
  (41 shorter events, 3.1 us)
Async XLA Ops:
  0.0 10.1 %copy-start = (f32[2,256,256]{2,1,0:T(8,128)S(1)}, f32[2,256,256]{2,1,0:T(8,128)}, u32[]{:S(2)}) copy-start(f32[2,256,256]{2,1,0:T(8,128)} %param.8) | copy-start | bytes 1572868
  0.1 2.2 copy-start.1
  5.3 57.5 %collective-permute-start = (f32[5,2,64,256]{3,2,1,0:T(8,128)}, f32[5,2,64,256]{3,2,1,0:T(8,128)}, u32[]{:S(2)}, u32[]{:S(2)}) collective-permute-start(f32[5,2,64,256]{3,2,1,0:T(8,128)} %get-tuple-element.46), channel_id=1, source_target_pairs={{0,8},{8,0},{16,24},{24,16},{1,9},{9,1},{17,25},{25,17},{2,10},{10... | collective-permute-start | bytes 1966088 | tf_op jit(solution)/shard_map/ppermute | solution.py:341
  6.9 65.6 %collective-permute-start.4 = (f32[5,2,64,256]{3,2,1,0:T(8,128)S(1)}, f32[5,2,64,256]{3,2,1,0:T(8,128)}, u32[]{:S(2)}, u32[]{:S(2)}) collective-permute-start(f32[5,2,64,256]{3,2,1,0:T(8,128)S(1)} %get-tuple-element.45.refs_0_.refs_4_), channel_id=1, source_target_pairs={{0,16},{8,24},{16,0},{24,8},{1,17},{9,25},{17,1},{25,9},{2,18},{10... | collective-permute-start | bytes 1966088 | tf_op jit(solution)/shard_map/ppermute | solution.py:341
  8.4 54.4 %collective-permute-start.1 = (f32[6,2,64,256]{3,2,1,0:T(8,128)}, f32[6,2,64,256]{3,2,1,0:T(8,128)S(1)}, u32[]{:S(2)}, u32[]{:S(2)}) collective-permute-start(f32[6,2,64,256]{3,2,1,0:T(8,128)} %get-tuple-element.47), channel_id=1, source_target_pairs={{0,16},{8,24},{16,0},{24,8},{1,17},{9,25},{17,1},{25,9},{2,18},{10... | collective-permute-start | bytes 2359304 | tf_op jit(solution)/shard_map/ppermute | solution.py:341
  8.9 74.2 %collective-permute-start.6 = (f32[6,2,64,256]{3,2,1,0:T(8,128)S(1)}, f32[6,2,64,256]{3,2,1,0:T(8,128)S(1)}, u32[]{:S(2)}, u32[]{:S(2)}) collective-permute-start(f32[6,2,64,256]{3,2,1,0:T(8,128)S(1)} %get-tuple-element.50.refs_2_.refs_8_.refs_4_.refs_12_), channel_id=1, source_target_pairs={{0,8},{8,0},{16,24},{24,16},{1,9},{9,1},{17,25},{25,17},{2,10},{10... | collective-permute-start | bytes 2359304 | tf_op jit(solution)/shard_map/ppermute | solution.py:341
  59.7 38.7 %copy-start.2 = (f32[64,2,32,256]{3,2,1,0:T(8,128)S(1)}, f32[64,2,32,256]{3,2,1,0:T(8,128)}, u32[]{:S(2)}) copy-start(f32[64,2,32,256]{3,2,1,0:T(8,128)} %in_ref.2) | copy-start | bytes 12582916
  65.2 16.1 %collective-permute-start.2 = (f32[2,4,2,64,256]{4,3,2,1,0:T(8,128)S(1)}, f32[2,4,2,64,256]{4,3,2,1,0:T(8,128)S(1)}, u32[]{:S(2)}, u32[]{:S(2)}) collective-permute-start(f32[2,4,2,64,256]{4,3,2,1,0:T(8,128)S(1)} %get-tuple-element.51), channel_id=1, source_target_pairs={{0,1},{1,2},{2,3},{3,4},{4,5},{5,6},{6,7},{8,9},{9,10},{10,11},{11... | collective-permute-start | bytes 3145736 | tf_op jit(solution)/shard_map/ppermute | solution.py:389
  67.1 15.9 %collective-permute-start.3 = (f32[2,4,2,64,256]{4,3,2,1,0:T(8,128)S(1)}, f32[2,4,2,64,256]{4,3,2,1,0:T(8,128)S(1)}, u32[]{:S(2)}, u32[]{:S(2)}) collective-permute-start(f32[2,4,2,64,256]{4,3,2,1,0:T(8,128)S(1)} %get-tuple-element.52), channel_id=1, source_target_pairs={{1,0},{2,1},{3,2},{4,3},{5,4},{6,5},{7,6},{9,8},{10,9},{11,10},{12... | collective-permute-start | bytes 3145736 | tf_op jit(solution)/shard_map/ppermute | solution.py:389
  70.9 19.5 %collective-permute-start.7 = (f32[6,2,64,256]{3,2,1,0:T(8,128)S(1)}, f32[6,2,64,256]{3,2,1,0:T(8,128)S(1)}, u32[]{:S(2)}, u32[]{:S(2)}) collective-permute-start(f32[6,2,64,256]{3,2,1,0:T(8,128)S(1)} %collective-permute-done.1.refs_3_.refs_10_.refs_5_.refs_14_), channel_id=1, source_target_pairs={{0,8},{8,0},{16,24},{24,16},{1,9},{9,1},{17,25},{25,17},{2,10},{10... | collective-permute-start | bytes 2359304 | tf_op jit(solution)/shard_map/ppermute | solution.py:341
  72.4 16.5 %collective-permute-start.5 = (f32[5,2,64,256]{3,2,1,0:T(8,128)}, f32[5,2,64,256]{3,2,1,0:T(8,128)S(1)}, u32[]{:S(2)}, u32[]{:S(2)}) collective-permute-start(f32[5,2,64,256]{3,2,1,0:T(8,128)} %collective-permute-done.refs_1_.refs_5_), channel_id=1, source_target_pairs={{0,16},{8,24},{16,0},{24,8},{1,17},{9,25},{17,1},{25,9},{2,18},{10... | collective-permute-start | bytes 1966088 | tf_op jit(solution)/shard_map/ppermute | solution.py:341
  92.7 22.3 %collective-permute-start.8 = (f32[2,4,2,64,256]{4,3,2,1,0:T(8,128)S(1)}, f32[2,4,2,64,256]{4,3,2,1,0:T(8,128)S(1)}, u32[]{:S(2)}, u32[]{:S(2)}) collective-permute-start(f32[2,4,2,64,256]{4,3,2,1,0:T(8,128)S(1)} %get-tuple-element.56), channel_id=1, source_target_pairs={{0,1},{1,2},{2,3},{3,4},{4,5},{5,6},{6,7},{8,9},{9,10},{10,11},{11... | collective-permute-start | bytes 3145736 | tf_op jit(solution)/shard_map/ppermute | solution.py:389
  94.6 20.4 %collective-permute-start.11 = (f32[2,4,2,64,256]{4,3,2,1,0:T(8,128)S(1)}, f32[2,4,2,64,256]{4,3,2,1,0:T(8,128)S(1)}, u32[]{:S(2)}, u32[]{:S(2)}) collective-permute-start(f32[2,4,2,64,256]{4,3,2,1,0:T(8,128)S(1)} %get-tuple-element.62), channel_id=1, source_target_pairs={{1,0},{2,1},{3,2},{4,3},{5,4},{6,5},{7,6},{9,8},{10,9},{11,10},{12... | collective-permute-start | bytes 3145736 | tf_op jit(solution)/shard_map/ppermute | solution.py:389
  100.9 13.9 %collective-permute-start.10 = (f32[4,2,64,256]{3,2,1,0:T(8,128)S(1)}, f32[4,2,64,256]{3,2,1,0:T(8,128)S(1)}, u32[]{:S(2)}, u32[]{:S(2)}) collective-permute-start(f32[4,2,64,256]{3,2,1,0:T(8,128)S(1)} %get-tuple-element.60), channel_id=1, source_target_pairs={{0,16},{8,24},{16,0},{24,8},{1,17},{9,25},{17,1},{25,9},{2,18},{10... | collective-permute-start | bytes 1572872 | tf_op jit(solution)/shard_map/ppermute | solution.py:341
  101.5 13.5 %collective-permute-start.9 = (f32[4,2,64,256]{3,2,1,0:T(8,128)S(1)}, f32[4,2,64,256]{3,2,1,0:T(8,128)S(1)}, u32[]{:S(2)}, u32[]{:S(2)}) collective-permute-start(f32[4,2,64,256]{3,2,1,0:T(8,128)S(1)} %get-tuple-element.58), channel_id=1, source_target_pairs={{0,8},{8,0},{16,24},{24,16},{1,9},{9,1},{17,25},{25,17},{2,10},{10... | collective-permute-start | bytes 1572872 | tf_op jit(solution)/shard_map/ppermute | solution.py:341
  137.9 22.0 %collective-permute-start.12 = (f32[2,4,2,64,256]{4,3,2,1,0:T(8,128)S(1)}, f32[2,4,2,64,256]{4,3,2,1,0:T(8,128)S(1)}, u32[]{:S(2)}, u32[]{:S(2)}) collective-permute-start(f32[2,4,2,64,256]{4,3,2,1,0:T(8,128)S(1)} %get-tuple-element.68), channel_id=1, source_target_pairs={{0,1},{1,2},{2,3},{3,4},{4,5},{5,6},{6,7},{8,9},{9,10},{10,11},{11... | collective-permute-start | bytes 3145736 | tf_op jit(solution)/shard_map/ppermute | solution.py:389
  139.8 20.1 %collective-permute-start.13 = (f32[2,4,2,64,256]{4,3,2,1,0:T(8,128)S(1)}, f32[2,4,2,64,256]{4,3,2,1,0:T(8,128)S(1)}, u32[]{:S(2)}, u32[]{:S(2)}) collective-permute-start(f32[2,4,2,64,256]{4,3,2,1,0:T(8,128)S(1)} %get-tuple-element.69), channel_id=1, source_target_pairs={{1,0},{2,1},{3,2},{4,3},{5,4},{6,5},{7,6},{9,8},{10,9},{11,10},{12... | collective-permute-start | bytes 3145736 | tf_op jit(solution)/shard_map/ppermute | solution.py:389
  143.5 14.9 %collective-permute-start.14 = (f32[4,2,64,256]{3,2,1,0:T(8,128)S(1)}, f32[4,2,64,256]{3,2,1,0:T(8,128)S(1)}, u32[]{:S(2)}, u32[]{:S(2)}) collective-permute-start(f32[4,2,64,256]{3,2,1,0:T(8,128)S(1)} %get-tuple-element.70.refs_2_.refs_8_), channel_id=1, source_target_pairs={{0,16},{8,24},{16,0},{24,8},{1,17},{9,25},{17,1},{25,9},{2,18},{10... | collective-permute-start | bytes 1572872 | tf_op jit(solution)/shard_map/ppermute | solution.py:341
  145.1 22.4 %collective-permute-start.15 = (f32[4,2,64,256]{3,2,1,0:T(8,128)S(1)}, f32[4,2,64,256]{3,2,1,0:T(8,128)S(1)}, u32[]{:S(2)}, u32[]{:S(2)}) collective-permute-start(f32[4,2,64,256]{3,2,1,0:T(8,128)S(1)} %collective-permute-done.9.refs_3_.refs_9_), channel_id=1, source_target_pairs={{0,16},{8,24},{16,0},{24,8},{1,17},{9,25},{17,1},{25,9},{2,18},{10... | collective-permute-start | bytes 1572872 | tf_op jit(solution)/shard_map/ppermute | solution.py:341
  145.6 21.9 %collective-permute-start.17 = (f32[4,2,64,256]{3,2,1,0:T(8,128)S(1)}, f32[4,2,64,256]{3,2,1,0:T(8,128)S(1)}, u32[]{:S(2)}, u32[]{:S(2)}) collective-permute-start(f32[4,2,64,256]{3,2,1,0:T(8,128)S(1)} %collective-permute-done.10.refs_7_.refs_18_), channel_id=1, source_target_pairs={{0,8},{8,0},{16,24},{24,16},{1,9},{9,1},{17,25},{25,17},{2,10},{10... | collective-permute-start | bytes 1572872 | tf_op jit(solution)/shard_map/ppermute | solution.py:341
  158.4 10.5 %collective-permute-start.16 = (f32[4,2,64,256]{3,2,1,0:T(8,128)S(1)}, f32[4,2,64,256]{3,2,1,0:T(8,128)S(1)}, u32[]{:S(2)}, u32[]{:S(2)}) collective-permute-start(f32[4,2,64,256]{3,2,1,0:T(8,128)S(1)} %get-tuple-element.73.refs_6_.refs_16_), channel_id=1, source_target_pairs={{0,8},{8,0},{16,24},{24,16},{1,9},{9,1},{17,25},{25,17},{2,10},{10... | collective-permute-start | bytes 1572872 | tf_op jit(solution)/shard_map/ppermute | solution.py:341
  171.8 16.1 %collective-permute-start.18 = (f32[2,4,2,64,256]{4,3,2,1,0:T(8,128)S(1)}, f32[2,4,2,64,256]{4,3,2,1,0:T(8,128)S(1)}, u32[]{:S(2)}, u32[]{:S(2)}) collective-permute-start(f32[2,4,2,64,256]{4,3,2,1,0:T(8,128)S(1)} %get-tuple-element.75), channel_id=1, source_target_pairs={{0,1},{1,2},{2,3},{3,4},{4,5},{5,6},{6,7},{8,9},{9,10},{10,11},{11... | collective-permute-start | bytes 3145736 | tf_op jit(solution)/shard_map/ppermute | solution.py:389
  173.7 15.9 %collective-permute-start.19 = (f32[2,4,2,64,256]{4,3,2,1,0:T(8,128)S(1)}, f32[2,4,2,64,256]{4,3,2,1,0:T(8,128)S(1)}, u32[]{:S(2)}, u32[]{:S(2)}) collective-permute-start(f32[2,4,2,64,256]{4,3,2,1,0:T(8,128)S(1)} %get-tuple-element.76), channel_id=1, source_target_pairs={{1,0},{2,1},{3,2},{4,3},{5,4},{6,5},{7,6},{9,8},{10,9},{11,10},{12... | collective-permute-start | bytes 3145736 | tf_op jit(solution)/shard_map/ppermute | solution.py:389
  177.6 34.2 %collective-permute-start.20 = (f32[4,2,128,256]{3,2,1,0:T(8,128)S(1)}, f32[4,2,128,256]{3,2,1,0:T(8,128)S(1)}, u32[]{:S(2)}, u32[]{:S(2)}) collective-permute-start(f32[4,2,128,256]{3,2,1,0:T(8,128)S(1)} %get-tuple-element.79), channel_id=1, source_target_pairs={{0,8},{8,0},{16,24},{24,16},{1,9},{9,1},{17,25},{25,17},{2,10},{10... | collective-permute-start | bytes 3145736 | tf_op jit(solution)/shard_map/ppermute | solution.py:341
  179.2 32.7 %collective-permute-start.22 = (f32[4,2,128,256]{3,2,1,0:T(8,128)S(1)}, f32[4,2,128,256]{3,2,1,0:T(8,128)S(1)}, u32[]{:S(2)}, u32[]{:S(2)}) collective-permute-start(f32[4,2,128,256]{3,2,1,0:T(8,128)S(1)} %get-tuple-element.82), channel_id=1, source_target_pairs={{0,16},{8,24},{16,0},{24,8},{1,17},{9,25},{17,1},{25,9},{2,18},{10... | collective-permute-start | bytes 3145736 | tf_op jit(solution)/shard_map/ppermute | solution.py:341
  211.9 26.0 %collective-permute-start.23 = (f32[4,2,128,256]{3,2,1,0:T(8,128)S(1)}, f32[4,2,128,256]{3,2,1,0:T(8,128)S(1)}, u32[]{:S(2)}, u32[]{:S(2)}) collective-permute-start(f32[4,2,128,256]{3,2,1,0:T(8,128)S(1)} %get-tuple-element.83), channel_id=1, source_target_pairs={{0,16},{8,24},{16,0},{24,8},{1,17},{9,25},{17,1},{25,9},{2,18},{10... | collective-permute-start | bytes 3145736 | tf_op jit(solution)/shard_map/ppermute | solution.py:341
  213.4 25.8 %collective-permute-start.21 = (f32[4,2,128,256]{3,2,1,0:T(8,128)S(1)}, f32[4,2,128,256]{3,2,1,0:T(8,128)S(1)}, u32[]{:S(2)}, u32[]{:S(2)}) collective-permute-start(f32[4,2,128,256]{3,2,1,0:T(8,128)S(1)} %get-tuple-element.80), channel_id=1, source_target_pairs={{0,8},{8,0},{16,24},{24,16},{1,9},{9,1},{17,25},{25,17},{2,10},{10... | collective-permute-start | bytes 3145736 | tf_op jit(solution)/shard_map/ppermute | solution.py:341

commit v4 on v3

v4 whole, which is shorter than its diff:
```python
import functools

import jax
import jax.numpy as jnp
from jax import lax
from jax.experimental import pallas as pl
from jax.experimental.pallas import tpu as pltpu
from jax.sharding import PartitionSpec as P


CUTS = 2
VMEM_LIMIT = 28 * 2**20
HBM = pl.BlockSpec(memory_space=pl.ANY)
VMEM = pl.BlockSpec(memory_space=pltpu.VMEM)
SCALARS = pl.BlockSpec(memory_space=pltpu.SMEM)
LIGHT = pl.CostEstimate(flops=1024, bytes_accessed=4096, transcendentals=0)
PARAMS = pltpu.CompilerParams(vmem_limit_bytes=4 * 2**20)


def block_row(stream, side, row, depth, rows_x):
    if stream == 0:
        return row + side * (rows_x - 1 - 2 * row)
    return depth * (1 + side) + row


def own_rows(chunk, depth):
    high = depth // CUTS
    return list(range(chunk * high, (chunk + 1) * high))


def chunk_rows(stream, chunk, depth):
    rows = own_rows(chunk, depth)
    first = rows[0] + 1 if chunk else (0 if stream == 0 else -1)
    return list(range(first, rows[-1] + 2))


def where_rows(stream, chunk, depth):
    places = {}
    for back in (1, 0):
        if chunk >= back:
            for at, row in enumerate(chunk_rows(stream, chunk - back, depth)):
                places[row] = (1 - back, at)
    return places


def run(copies):
    for copy in copies:
        copy.start()
    for copy in copies:
        copy.wait()


def pick_kernel(chunk, depth, sides_ref, ratio_ref, in_ref, *refs):
    outs, sems = refs[:-1], refs[-1]
    _, planes, rows_x, _ = in_ref.shape
    jobs = []
    for stream in range(2):
        for other in (1, 0):
            side = 1 - sides_ref[stream] if other else sides_ref[stream]
            for at, row in enumerate(chunk_rows(stream, chunk, depth)):
                x = block_row(stream, side, row, depth, rows_x)
                for z in range(planes):
                    out = outs[2 * stream + other].at[at, z]
                    jobs.append((pltpu.make_async_copy(in_ref.at[:, z, x], out, sems.at[len(jobs)]), out))
    for copy, _ in jobs:
        copy.start()
    ratio = ratio_ref[...]
    for copy, out in jobs:
        copy.wait()
        out[...] = out[...] * ratio


def pick(chunk, residual, ratio, sides, depth):
    steps, planes, _, rows_y = residual.shape
    counts = [len(chunk_rows(stream, chunk, depth)) for stream in (0, 0, 1, 1)]
    outs = pl.pallas_call(
        functools.partial(pick_kernel, chunk, depth),
        out_shape=[jax.ShapeDtypeStruct((c, planes, steps, rows_y), jnp.float32) for c in counts],
        in_specs=[SCALARS, VMEM, HBM],
        out_specs=[VMEM] * 4,
        scratch_shapes=[pltpu.SemaphoreType.DMA((sum(counts) * planes,))],
        compiler_params=pltpu.CompilerParams(vmem_limit_bytes=56 * 2**20),
        cost_estimate=LIGHT,
        name="pick",
    )(sides, ratio, residual)
    return [outs[0:2], outs[2:4]]


def edge_kernel(chunk, depth, groups, *refs):
    raws, (up_ref, down_ref, sems) = refs[:-3], refs[-3:]
    planes = raws[0].shape[1]
    backs = 2 if chunk else 1
    copies = []
    for stream in range(2):
        places = where_rows(stream, chunk, depth)
        for at, row in enumerate(own_rows(chunk, depth)):
            back, index = places[row]
            for group in range(groups):
                raw = raws[(stream * backs + back - 2 + backs) * groups + group]
                for z, out in ((planes - 1, up_ref), (0, down_ref)):
                    copy = pltpu.make_async_copy(
                        raw.at[index, z], out.at[stream, at, group], sems.at[len(copies)]
                    )
                    copies.append(copy)
    run(copies)


def edges(chunk, depth, raws):
    groups = len(raws[0][0])
    _, _, steps, rows_y = raws[0][0][0].shape
    flat = [raw for stream in raws for arrays in stream for raw in arrays]
    high = depth // CUTS
    shape = jax.ShapeDtypeStruct((2, high, groups, steps, rows_y), jnp.float32)
    return pl.pallas_call(
        functools.partial(edge_kernel, chunk, depth, groups),
        out_shape=[shape] * 2,
        in_specs=[HBM] * len(flat),
        out_specs=[HBM] * 2,
        scratch_shapes=[pltpu.SemaphoreType.DMA((4 * high * groups,))],
        compiler_params=PARAMS,
        cost_estimate=LIGHT,
        name="edges",
    )(*flat)


def halves(value):
    high = value.astype(jnp.bfloat16)
    return high, (value - high.astype(jnp.float32)).astype(jnp.bfloat16)


def apply_kernel(chunk, depth, order, sides_ref, map_a_ref, map_b_ref, *refs):
    (early_low, early_high, late_low, late_high), raws = refs[:4], refs[4:-5]
    out_ref, gives, own, sems = refs[-5], refs[-4:-2], refs[-2], refs[-1]
    groups = sum(len(part) for part in order[0])
    backs = 2 if chunk else 1
    _, planes, rows_x, rows_y = out_ref.shape
    stores = []
    for stream in range(2):
        maps = (map_a_ref, map_b_ref)[stream][...]
        half = maps.shape[0] // 2
        places = where_rows(stream, chunk, depth)

        def load(row, z):
            back, index = places[row]
            start = (stream * backs + back - 2 + backs) * groups
            return jnp.concatenate([raw[index, z] for raw in raws[start : start + groups]], axis=0)

        def outside(early, late, at):
            parts = {}
            for kind, ref in enumerate((early, late)):
                for place, group in enumerate(order[stream][kind]):
                    parts[group] = ref[stream, at, place]
            return jnp.concatenate([parts[group] for group in range(groups)], axis=0)

        for at, row in enumerate(own_rows(chunk, depth)):
            number = stream * (depth // CUTS) + at
            x = block_row(stream, sides_ref[stream], row, depth, rows_x)
            mids = [load(row, z) for z in range(planes)]
            for z, mid in enumerate(mids):
                lane = lax.broadcasted_iota(jnp.int32, mid.shape, 1)
                total = jnp.where(lane == 0, 0.0, pltpu.roll(mid, 1, 1))
                total = total + jnp.where(lane == rows_y - 1, 0.0, pltpu.roll(mid, rows_y - 1, 1))
                for beside in (row - 1, row + 1):
                    if beside in places:
                        total = total + load(beside, z)
                total = total + (mids[z - 1] if z else outside(early_low, late_low, at))
                total = total + (mids[z + 1] if z < planes - 1 else outside(early_high, late_high, at))
                mid_h, mid_l = halves(mid)
                sum_h, sum_l = halves(total)
                stack = jnp.concatenate([mid_h, mid_h, mid_l, sum_h, sum_h, sum_l], axis=0)
                value = jnp.dot(maps, stack, preferred_element_type=jnp.float32)
                own[number, z] = value[:half]
                gives[stream][at, z] = value[half:]
                store = pltpu.make_async_copy(own.at[number, z], out_ref.at[:, z, x], sems.at[number, z])
                store.start()
                stores.append(store)
    for store in stores:
        store.wait()


def apply(chunk, depth, order, sides, maps, early, late, raws, shape, result):
    _, planes, _, rows_y = raws[0][0][0].shape
    high = depth // CUTS
    half = shape[0]
    flat = [raw for stream in raws for arrays in stream for raw in arrays]
    first = [] if result is None else [result]
    give = jax.ShapeDtypeStruct((high, planes, half, rows_y), jnp.float32)
    count = 3 + 4 + len(flat)

    def body(*refs):
        refs = refs[:count] + refs[count + len(first) :]
        apply_kernel(chunk, depth, order, *refs)

    return pl.pallas_call(
        body,
        out_shape=[jax.ShapeDtypeStruct(shape, jnp.float32), give, give],
        in_specs=[SCALARS] + [VMEM] * (count - 1) + [HBM] * len(first),
        out_specs=[HBM, VMEM, VMEM],
        scratch_shapes=[
            pltpu.VMEM((2 * high, planes, half, rows_y), jnp.float32),
            pltpu.SemaphoreType.DMA((2 * high, planes)),
        ],
        input_output_aliases={count: 0} if first else {},
        compiler_params=pltpu.CompilerParams(vmem_limit_bytes=VMEM_LIMIT),
        cost_estimate=LIGHT,
        name="apply",
    )(sides, *maps, *early, *late, *flat, *first)


def place_kernel(chunk, depth, sides_ref, got_a, got_b, _, out_ref, sems):
    _, planes, rows_x, _ = out_ref.shape
    copies = []
    for stream, got in enumerate((got_a, got_b)):
        for at, row in enumerate(own_rows(chunk, depth)):
            x = block_row(stream, 1 - sides_ref[stream], row, depth, rows_x)
            for z in range(planes):
                copies.append(pltpu.make_async_copy(got.at[at, z], out_ref.at[:, z, x], sems.at[len(copies)]))
    run(copies)


def place(chunk, depth, sides, got, result):
    planes = result.shape[1]
    return pl.pallas_call(
        functools.partial(place_kernel, chunk, depth),
        out_shape=jax.ShapeDtypeStruct(result.shape, jnp.float32),
        in_specs=[SCALARS] + [HBM] * 3,
        out_specs=HBM,
        scratch_shapes=[pltpu.SemaphoreType.DMA((2 * depth // CUTS * planes,))],
        input_output_aliases={3: 0},
        compiler_params=PARAMS,
        cost_estimate=LIGHT,
        name="place",
    )(sides, *got, result)


def after(value, *others):
    return lax.optimization_barrier((value, *others))[0]


def maps_kernel(bits, me_ref, ahead_ref, back_ref, eigen_ref, *outs):
    steps = ahead_ref.shape[1]
    local_steps = outs[0].shape[0] // 4
    me = me_ref[0]
    real_part = 6.0 + eigen_ref[0:1, :]
    imag_part = eigen_ref[1:2, :]
    denom = real_part * real_part + imag_part * imag_part
    coef_re = real_part / denom
    coef_im = -imag_part / denom
    left = []
    for block in (me, jnp.bitwise_xor(me, bits[0]), jnp.bitwise_xor(me, bits[1])):
        span = pl.ds(pl.multiple_of(block * local_steps, local_steps), local_steps)
        back_re, back_im = back_ref[0, span, :], back_ref[1, span, :]
        for _ in range(2):
            back_re, back_im = back_re * coef_re - back_im * coef_im, back_re * coef_im + back_im * coef_re
            left += [back_re, back_im]
    left = jnp.concatenate(left, axis=0)
    by_re = jnp.dot(left, ahead_ref[0], precision=lax.Precision.HIGHEST, preferred_element_type=jnp.float32)
    by_im = jnp.dot(left, ahead_ref[1], precision=lax.Precision.HIGHEST, preferred_element_type=jnp.float32)

    def piece(data, which):
        return data[which * local_steps : (which + 1) * local_steps]

    row = lax.broadcasted_iota(jnp.int32, (steps, steps), 0)
    column = lax.broadcasted_iota(jnp.int32, (steps, steps), 1)
    turn = (row == jnp.bitwise_xor(column, me * local_steps)).astype(jnp.float32).astype(jnp.bfloat16)
    parts = []
    for block in range(3):
        for power in range(2):
            at = 2 * (2 * block + power)
            both = jnp.concatenate(
                [piece(by_re, at) - piece(by_im, at + 1), piece(by_im, at) + piece(by_re, at + 1)], axis=0
            )
            pair = jnp.concatenate(halves(both), axis=0)
            parts.append(jnp.dot(pair, turn, preferred_element_type=jnp.float32).astype(jnp.bfloat16))
    half = 2 * local_steps
    for out, blocks in zip(outs, ((0, 1), (0, 2))):
        for place, block in enumerate(blocks):
            once, twice = parts[2 * block], parts[2 * block + 1]
            columns = (once[:half], once[half:], once[:half], twice[:half], twice[half:], twice[:half])
            for c, value in enumerate(columns):
                out[place * half : (place + 1) * half, c * steps : (c + 1) * steps] = value


def make_maps(forward_map, back_map, eigen_values, me, count, bits):
    steps = forward_map.shape[1]
    shape = jax.ShapeDtypeStruct((4 * steps // count, 6 * steps), jnp.bfloat16)
    return pl.pallas_call(
        functools.partial(maps_kernel, bits),
        out_shape=[shape, shape],
        in_specs=[SCALARS] + [VMEM] * 3,
        out_specs=[VMEM] * 2,
        compiler_params=pltpu.CompilerParams(vmem_limit_bytes=VMEM_LIMIT),
        cost_estimate=LIGHT,
        name="maps",
    )(me.astype(jnp.int32).reshape(1), forward_map, back_map, eigen_values)


def local(residual, step_ratio, forward_map, back_map, eigen_values):
    local_steps, planes, rows_x, rows_y = residual.shape
    depth = rows_x // 4
    count = lax.axis_size("tm")
    bits = (1, count // 2)
    all_bits = [1 << k for k in range(count.bit_length() - 1)]
    me = lax.axis_index("tm")
    sides = jnp.stack([jnp.where(jnp.bitwise_and(me, b) > 0, 1, 0) for b in bits]).astype(jnp.int32)
    ratio = jnp.broadcast_to((step_ratio.astype(jnp.float32) / 8.0)[:, None], (local_steps, rows_y))

    def swap(data, bit):
        return lax.ppermute(data, "tm", [(i, i ^ bit) for i in range(count)])

    spaces = lax.axis_size("space")
    upward = [(i, i + 1) for i in range(spaces - 1)]
    downward = [(i + 1, i) for i in range(spaces - 1)]

    queues = [[], []]

    def swap_in_turn(data, bit, *others, flight=2):
        queue = queues[0 if bit == bits[0] else 1]
        if len(queue) >= flight:
            others = (queue[-flight], *others)
        if others:
            data = after(data, *others)
        got = swap(data, bit)
        queue.append(got)
        return got

    masks = range(count)
    order = [[[m for m in masks if m in (0, b)], [m for m in masks if m not in (0, b)]] for b in bits]
    held = [[None] * CUTS for _ in range(2)]

    maps = make_maps(forward_map, back_map, eigen_values, me, count, bits)
    firsts = []

    def raw(chunk):
        data = after(residual, *firsts[-1]) if firsts else residual
        mine = pick(chunk, data, ratio, sides, depth)
        have = [{0: mine[s][0], bits[s]: swap_in_turn(mine[s][1], bits[s])} for s in range(2)]
        firsts.append([have[s][bits[s]] for s in range(2)])
        for bit in all_bits:
            for mask in masks:
                for stream in (1, 0):
                    now = have[stream]
                    free = bit != bits[stream] and not mask & bit
                    if free and mask in now and (mask | bit) not in now:
                        others = maps if mask and chunk == 0 else []
                        now[mask | bit] = swap_in_turn(now[mask], bit, *others)
        for stream in range(2):
            held[stream][chunk] = [have[stream][mask] for mask in masks]

    def beside(chunk, kind, *others):
        arrays = [
            [[a[m] for m in order[s][kind]] for a in held[s][max(chunk - 1, 0) : chunk + 1]] for s in range(2)
        ]
        if others:
            arrays[0][-1][0] = after(arrays[0][-1][0], *others)
        up, down = edges(chunk, depth, arrays)
        return lax.ppermute(up, "space", upward), lax.ppermute(down, "space", downward)

    gives = []
    result = None
    for chunk in range(CUTS):
        raw(chunk)
    shape = (2 * local_steps, planes, rows_x, rows_y)
    for chunk in range(CUTS):
        early = beside(chunk, 0)
        late = beside(chunk, 1, *early, *(gives[-1] if gives else []))
        used = [held[s][max(chunk - 1, 0) : chunk + 1] for s in range(2)]
        result, *give = apply(chunk, depth, order, sides, maps, early, late, used, shape, result)
        gives.append(give)
    for chunk in range(CUTS):
        flight = 1 if chunk else 2
        got = [swap_in_turn(gives[chunk][s], bits[s], flight=flight) for s in range(2)]
        result = place(chunk, depth, sides, got, result)
    return result.reshape(2, local_steps, planes, rows_x, rows_y)


def solution(mesh):
    in_specs = (P("tm", "space", None, None), P("tm"), P(), P(), P())
    out_specs = P(None, "tm", "space", None, None)
    return jax.shard_map(local, mesh=mesh, in_specs=in_specs, out_specs=out_specs, check_vma=False)
```

time: 242 us -> 193 us (0.80)
  blocking collectives: 25.2 us -> 0 us
  waiting for transfers between devices: 81.1 us -> 98.1 us
  Pallas kernels: 62 us -> 45.4 us
  local copies, waits for them, and re-layouts: 16.3 us -> 6.73 us
  other arithmetic: 10.7 us -> 1.3 us
  matrix products: 2.73 us -> 0 us
    unnamed x1 -> x0, blocking collectives: 25.2 us -> none
    ppermute x16, waiting for transfers between devices: 62 us -> 87.1 us  [swap(): return lax.ppermute(data, 'tm', [(i, i ^ bit) for i in range(count)])]
    pallas_call x2 -> x3, Pallas kernels: 42.2 us -> 21.3 us  [the longest x2 19.3 us: apply(): pl.pallas_call(body, out_shape=[jax.ShapeDtypeStruct(shape, jnp.float32),...]
    ppermute x4, waiting for transfers between devices: 15.6 us -> 9.22 us  [beside(): lax.ppermute(up, 'space', upward)]
    squeeze x4 -> x0, local copies, waits for them, and re-layouts: 4.42 us -> none  [the longest x2 3.56 us: make_maps(): once_re = coef_re * ahead[0] - coef_im * ahead[1]]
    pallas_call x2, Pallas kernels: 5.44 us -> 9.37 us  [pick(): pl.pallas_call(functools.partial(pick_kernel, chunk, depth), out_shape=[j...]
    gather x2 -> x0, local copies, waits for them, and re-layouts: 3.73 us -> none  [the longest x1 2.41 us: make_maps(): ahead = jnp.take(ahead, order, axis=2).reshape(2, steps, steps)]
    dot_general x1 -> x0, matrix products: 2.73 us -> none  [make_maps(): maps = jnp.einsum('bmk,kn->bmn', left, right, precision=highest)]
  transfers between devices with their start and end apart: 24 -> 24, of which waited for: 13 -> 15; matrix products, arithmetic and copies ran while one was open for 11% -> 0% of each run, Pallas kernels for 12% -> 18%
where the time goes in v4:
time: 193 us; the launch traced here: 192 us
  waiting for transfers between devices  98.1 us (51%)
  Pallas kernels  45.4 us (24%)
  starting transfers between devices  40 us (21%)
  local copies, waits for them, and re-layouts  6.73 us (3%)
    ppermute x16, waiting for transfers between devices, swap(): return lax.ppermute(data, 'tm', [(i, i ^ bit) for i in range(count)])  87.1 us
    pallas_call x2, Pallas kernels, apply(): pl.pallas_call(body, out_shape=[jax.ShapeDtypeStruct(shape, jnp.float32),...  19.3 us
    ppermute x16, starting transfers between devices, swap(): return lax.ppermute(data, 'tm', [(i, i ^ bit) for i in range(count)])  17.5 us
    ppermute x4, starting transfers between devices, beside(): lax.ppermute(down, 'space', downward)  14.7 us
    pallas_call x4, Pallas kernels, edges(): pl.pallas_call(functools.partial(edge_kernel, chunk, depth, groups), out_...  10.8 us
    pallas_call x2, Pallas kernels, pick(): pl.pallas_call(functools.partial(pick_kernel, chunk, depth), out_shape=[j...  9.37 us
    ppermute x4, waiting for transfers between devices, beside(): lax.ppermute(up, 'space', upward)  9.22 us
    ppermute x4, starting transfers between devices, beside(): lax.ppermute(up, 'space', upward)  7.82 us
  transfers between devices with their start and end apart: 24, of which 15 were waited for; matrix products, arithmetic and copies ran while one was open for 0% of the time, Pallas kernels for 18%

profile of v4, /device:TPU:8, one launch (start us, length us, event | category | flops | bytes accessed | tf_op | source)
XLA Modules:
  0.0 191.9 jit_solution(9546598524424296185)
XLA Ops:
  0.0 0.7 convert_multiply_fusion
  0.7 0.6 pad_add_fusion.sides_ref.refs_0_
  1.3 0.7 broadcast_in_dim.2.ratio_ref
  2.0 5.0 %pick.2 = (f32[5,2,64,256]{3,2,1,0:T(8,128)}, f32[5,2,64,256]{3,2,1,0:T(8,128)}, f32[6,2,64,256]{3,2,1,0:T(8,128)}, f32[6,2,64,256]{3,2,1,0:T(8,128)}) custom-call(s32[2]{0:T(128)} %pad_add_fusion.sides_ref.refs_0_, f32[64,256]{1,0:T(8,128)} %broadcast_in_dim.2.ratio_ref, f32[64,2,32,256]{3,2,1,0:T(8,128)} %in_ref.2), custom_call_target="tpu_custom_call" | custom-call | flops 1024 | bytes 4096 | tf_op jit(solution)/shard_map/pick/pallas_call | solution.py:76
  7.0 1.6 collective-permute-start.1
  8.6 1.5 collective-permute-start
  10.1 0.5 collective-permute-start.2
  10.6 15.8 %collective-permute-done.refs_1_.refs_8_ = f32[5,2,64,256]{3,2,1,0:T(8,128)S(1)} collective-permute-done((f32[5,2,64,256]{3,2,1,0:T(8,128)}, f32[5,2,64,256]{3,2,1,0:T(8,128)S(1)}, u32[]{:S(2)}, u32[]{:S(2)}) %collective-permute-start) | collective-permute-done | bytes 655392 | tf_op jit(solution)/shard_map/ppermute | solution.py:309
  26.5 0.1 collective-permute-done.1.refs_5_.refs_3_.refs_13_.refs_17_
  26.6 1.1 copy-done
  27.7 1.1 copy-done.2
  28.8 1.6 edges.5
  30.4 1.9 %collective-permute-start.10 = (f32[2,4,2,64,256]{4,3,2,1,0:T(8,128)}, f32[2,4,2,64,256]{4,3,2,1,0:T(8,128)}, u32[]{:S(2)}, u32[]{:S(2)}) collective-permute-start(f32[2,4,2,64,256]{4,3,2,1,0:T(8,128)} %get-tuple-element.61), channel_id=1, source_target_pairs={{0,1},{1,2},{2,3},{3,4},{4,5},{5,6},{6,7},{8,9},{9,10},{10,11},{11... | collective-permute-start | bytes 3145736 | tf_op jit(solution)/shard_map/ppermute | solution.py:357
  32.3 3.6 %collective-permute-start.11 = (f32[2,4,2,64,256]{4,3,2,1,0:T(8,128)}, f32[2,4,2,64,256]{4,3,2,1,0:T(8,128)}, u32[]{:S(2)}, u32[]{:S(2)}) collective-permute-start(f32[2,4,2,64,256]{4,3,2,1,0:T(8,128)} %get-tuple-element.62), channel_id=1, source_target_pairs={{1,0},{2,1},{3,2},{4,3},{5,4},{6,5},{7,6},{9,8},{10,9},{11,10},{12... | collective-permute-start | bytes 3145736 | tf_op jit(solution)/shard_map/ppermute | solution.py:357
  36.0 0.0 copy-start.6
  36.0 1.0 copy-done.6
  37.0 1.0 copy-done.7
  38.1 0.7 copy-done.9
  38.7 2.0 %maps.1 = (bf16[256,1536]{1,0:T(8,128)(2,1)S(1)}, bf16[256,1536]{1,0:T(8,128)(2,1)S(1)}) custom-call(s32[1]{0:T(128)} %bitcast.2.me_ref, f32[2,256,256]{2,1,0:T(8,128)S(1)} %copy-done.6, f32[2,256,256]{2,1,0:T(8,128)S(1)} %copy-done.7, f32[2,256]{1,0:T(2,128)S(1)} %copy-done.9), custom_call_target="tpu_custom_call" | custom-call | flops 1024 | bytes 4096 | tf_op jit(solution)/shard_map/maps/pallas_call | solution.py:287
  40.8 1.6 collective-permute-start.12
  42.3 1.5 collective-permute-start.4
  43.8 0.5 collective-permute-start.8
  44.3 4.4 %pick.3 = (f32[4,2,64,256]{3,2,1,0:T(8,128)}, f32[4,2,64,256]{3,2,1,0:T(8,128)}, f32[4,2,64,256]{3,2,1,0:T(8,128)}, f32[4,2,64,256]{3,2,1,0:T(8,128)}) custom-call(s32[2]{0:T(128)} %pad_add_fusion.sides_ref.refs_0_, f32[64,256]{1,0:T(8,128)} %broadcast_in_dim.2.ratio_ref, f32[64,2,32,256]{3,2,1,0:T(8,128)} %in_ref.2), custom_call_target="tpu_custom_call" | custom-call | flops 1024 | bytes 4096 | tf_op jit(solution)/shard_map/pick/pallas_call | solution.py:76
  48.7 11.5 %collective-permute-done.4.refs_0_.refs_9_ = f32[5,2,64,256]{3,2,1,0:T(8,128)S(1)} collective-permute-done((f32[5,2,64,256]{3,2,1,0:T(8,128)}, f32[5,2,64,256]{3,2,1,0:T(8,128)S(1)}, u32[]{:S(2)}, u32[]{:S(2)}) %collective-permute-start.4) | collective-permute-done | bytes 655392 | tf_op jit(solution)/shard_map/ppermute | solution.py:309
  60.2 1.5 collective-permute-start.5
  61.7 0.0 collective-permute-done.10.refs_3_
  61.7 0.5 collective-permute-start.3
  62.2 0.0 collective-permute-done.11.refs_4_
  62.2 12.0 %collective-permute-done.8.refs_1_.refs_10_ = f32[5,2,64,256]{3,2,1,0:T(8,128)S(1)} collective-permute-done((f32[5,2,64,256]{3,2,1,0:T(8,128)S(1)}, f32[5,2,64,256]{3,2,1,0:T(8,128)S(1)}, u32[]{:S(2)}, u32[]{:S(2)}) %collective-permute-start.8) | collective-permute-done | bytes 655392 | tf_op jit(solution)/shard_map/ppermute | solution.py:309
  74.2 3.0 %edges.6 = (f32[2,4,2,64,256]{4,3,2,1,0:T(8,128)S(1)}, f32[2,4,2,64,256]{4,3,2,1,0:T(8,128)S(1)}) custom-call(f32[5,2,64,256]{3,2,1,0:T(8,128)S(1)} %collective-permute-done.4.refs_0_.refs_9_, f32[5,2,64,256]{3,2,1,0:T(8,128)S(1)} %collective-permute-done.8.refs_1_.refs_10_, f32[6,2,64,256]{3,2,1,0:T(8,128)S(1)} %collective-permute-done.2.refs_2_.refs_12_.refs_4_.refs_16_, ...), custom_call_target="tpu_custom_call" | custom-call | flops 1024 | bytes 4096 | tf_op jit(solution)/shard_map/edges/pallas_call | solution.py:114
  77.2 1.9 %collective-permute-start.13 = (f32[2,4,2,64,256]{4,3,2,1,0:T(8,128)S(1)}, f32[2,4,2,64,256]{4,3,2,1,0:T(8,128)S(1)}, u32[]{:S(2)}, u32[]{:S(2)}) collective-permute-start(f32[2,4,2,64,256]{4,3,2,1,0:T(8,128)S(1)} %get-tuple-element.65), channel_id=1, source_target_pairs={{0,1},{1,2},{2,3},{3,4},{4,5},{5,6},{6,7},{8,9},{9,10},{10,11},{11... | collective-permute-start | bytes 3145736 | tf_op jit(solution)/shard_map/ppermute | solution.py:357
  79.2 3.6 %collective-permute-start.14 = (f32[2,4,2,64,256]{4,3,2,1,0:T(8,128)S(1)}, f32[2,4,2,64,256]{4,3,2,1,0:T(8,128)S(1)}, u32[]{:S(2)}, u32[]{:S(2)}) collective-permute-start(f32[2,4,2,64,256]{4,3,2,1,0:T(8,128)S(1)} %get-tuple-element.66), channel_id=1, source_target_pairs={{1,0},{2,1},{3,2},{4,3},{5,4},{6,5},{7,6},{9,8},{10,9},{11,10},{12... | collective-permute-start | bytes 3145736 | tf_op jit(solution)/shard_map/ppermute | solution.py:357
  82.8 1.3 collective-permute-done.5.refs_7_.refs_21_
  84.1 0.0 collective-permute-done.3.refs_3_.refs_12_
  84.1 1.0 copy-done.4
  85.2 3.2 %edges.4 = (f32[2,4,2,64,256]{4,3,2,1,0:T(8,128)S(1)}, f32[2,4,2,64,256]{4,3,2,1,0:T(8,128)S(1)}) custom-call(f32[5,2,64,256]{3,2,1,0:T(8,128)S(1)} %copy-done.3, f32[5,2,64,256]{3,2,1,0:T(8,128)S(1)} %collective-permute-done.refs_1_.refs_8_, f32[4,2,64,256]{3,2,1,0:T(8,128)S(1)} %copy-done.4, f32[4,2,64,256]{3,2,1,0:T(8,128)S(1)} %collective-permute-done.3.refs_3_.refs_12_, ...), custom_call_target="tpu_custom_call" | custom-call | flops 1024 | bytes 4096 | tf_op jit(solution)/shard_map/edges/pallas_call | solution.py:114
  88.4 2.1 %collective-permute-start.6 = (f32[2,4,2,64,256]{4,3,2,1,0:T(8,128)S(1)}, f32[2,4,2,64,256]{4,3,2,1,0:T(8,128)S(1)}, u32[]{:S(2)}, u32[]{:S(2)}) collective-permute-start(f32[2,4,2,64,256]{4,3,2,1,0:T(8,128)S(1)} %get-tuple-element.57), channel_id=1, source_target_pairs={{0,1},{1,2},{2,3},{3,4},{4,5},{5,6},{6,7},{8,9},{9,10},{10,11},{11... | collective-permute-start | bytes 3145736 | tf_op jit(solution)/shard_map/ppermute | solution.py:357
  90.4 1.6 collective-permute-start.9
  92.0 3.5 %collective-permute-start.7 = (f32[2,4,2,64,256]{4,3,2,1,0:T(8,128)S(1)}, f32[2,4,2,64,256]{4,3,2,1,0:T(8,128)S(1)}, u32[]{:S(2)}, u32[]{:S(2)}) collective-permute-start(f32[2,4,2,64,256]{4,3,2,1,0:T(8,128)S(1)} %get-tuple-element.58), channel_id=1, source_target_pairs={{1,0},{2,1},{3,2},{4,3},{5,4},{6,5},{7,6},{9,8},{10,9},{11,10},{12... | collective-permute-start | bytes 3145736 | tf_op jit(solution)/shard_map/ppermute | solution.py:357
  95.6 9.1 %collective-permute-done.9.refs_2_.refs_13_ = f32[4,2,64,256]{3,2,1,0:T(8,128)S(1)} collective-permute-done((f32[4,2,64,256]{3,2,1,0:T(8,128)S(1)}, f32[4,2,64,256]{3,2,1,0:T(8,128)S(1)}, u32[]{:S(2)}, u32[]{:S(2)}) %collective-permute-start.9) | collective-permute-done | bytes 524320 | tf_op jit(solution)/shard_map/ppermute | solution.py:309
  104.6 1.5 collective-permute-start.15
  106.2 0.0 collective-permute-done.13.refs_5_
  106.2 0.5 collective-permute-start.17
  106.7 1.5 collective-permute-start.16
  108.2 9.9 %apply.2 = (f32[128,2,32,256]{3,2,1,0:T(8,128)}, f32[4,2,128,256]{3,2,1,0:T(8,128)S(1)}, f32[4,2,128,256]{3,2,1,0:T(8,128)S(1)}) custom-call(s32[2]{0:T(128)S(1)} %copy-done.8, bf16[256,1536]{1,0:T(8,128)(2,1)S(1)} %get-tuple-element.44.refs_1_, bf16[256,1536]{1,0:T(8,128)(2,1)S(1)} %get-tuple-element.45.refs_2_, ...), custom_call_target="tpu_custom_call" | custom-call | flops 1024 | bytes 4096 | tf_op jit(solution)/shard_map/apply/pallas_call | solution.py:194
  118.1 0.9 collective-permute-done.15.refs_3_.refs_14_
  119.0 2.0 %collective-permute-done.17.refs_7_.refs_22_ = f32[4,2,64,256]{3,2,1,0:T(8,128)S(1)} collective-permute-done((f32[4,2,64,256]{3,2,1,0:T(8,128)S(1)}, f32[4,2,64,256]{3,2,1,0:T(8,128)S(1)}, u32[]{:S(2)}, u32[]{:S(2)}) %collective-permute-start.17) | collective-permute-done | bytes 524320 | tf_op jit(solution)/shard_map/ppermute | solution.py:309
  120.9 10.5 %collective-permute-done.16.refs_6_.refs_20_ = f32[4,2,64,256]{3,2,1,0:T(8,128)S(1)} collective-permute-done((f32[4,2,64,256]{3,2,1,0:T(8,128)}, f32[4,2,64,256]{3,2,1,0:T(8,128)S(1)}, u32[]{:S(2)}, u32[]{:S(2)}) %collective-permute-start.16) | collective-permute-done | bytes 524320 | tf_op jit(solution)/shard_map/ppermute | solution.py:309
  131.4 3.0 %edges.7 = (f32[2,4,2,64,256]{4,3,2,1,0:T(8,128)S(1)}, f32[2,4,2,64,256]{4,3,2,1,0:T(8,128)S(1)}) custom-call(f32[5,2,64,256]{3,2,1,0:T(8,128)S(1)} %collective-permute-done.4.refs_0_.refs_9_, f32[5,2,64,256]{3,2,1,0:T(8,128)S(1)} %collective-permute-done.8.refs_1_.refs_10_, f32[4,2,64,256]{3,2,1,0:T(8,128)S(1)} %collective-permute-done.9.refs_2_.refs_13_, ...), custom_call_target="tpu_custom_call" | custom-call | flops 1024 | bytes 4096 | tf_op jit(solution)/shard_map/edges/pallas_call | solution.py:114
  134.5 1.9 %collective-permute-start.18 = (f32[2,4,2,64,256]{4,3,2,1,0:T(8,128)S(1)}, f32[2,4,2,64,256]{4,3,2,1,0:T(8,128)S(1)}, u32[]{:S(2)}, u32[]{:S(2)}) collective-permute-start(f32[2,4,2,64,256]{4,3,2,1,0:T(8,128)S(1)} %get-tuple-element.73), channel_id=1, source_target_pairs={{0,1},{1,2},{2,3},{3,4},{4,5},{5,6},{6,7},{8,9},{9,10},{10,11},{11... | collective-permute-start | bytes 3145736 | tf_op jit(solution)/shard_map/ppermute | solution.py:357
  136.4 3.9 %collective-permute-start.19 = (f32[2,4,2,64,256]{4,3,2,1,0:T(8,128)S(1)}, f32[2,4,2,64,256]{4,3,2,1,0:T(8,128)S(1)}, u32[]{:S(2)}, u32[]{:S(2)}) collective-permute-start(f32[2,4,2,64,256]{4,3,2,1,0:T(8,128)S(1)} %get-tuple-element.74), channel_id=1, source_target_pairs={{1,0},{2,1},{3,2},{4,3},{5,4},{6,5},{7,6},{9,8},{10,9},{11,10},{12... | collective-permute-start | bytes 3145736 | tf_op jit(solution)/shard_map/ppermute | solution.py:357
  140.3 0.6 collective-permute-start.20
  140.9 0.5 collective-permute-start.22
  141.4 9.2 %collective-permute-done.18.refs_5_ = f32[2,4,2,64,256]{4,3,2,1,0:T(8,128)S(1)} collective-permute-done((f32[2,4,2,64,256]{4,3,2,1,0:T(8,128)S(1)}, f32[2,4,2,64,256]{4,3,2,1,0:T(8,128)S(1)}, u32[]{:S(2)}, u32[]{:S(2)}) %collective-permute-start.18) | collective-permute-done | bytes 1048608 | tf_op jit(solution)/shard_map/ppermute | solution.py:357
  150.6 1.8 collective-permute-done.19.refs_6_
  152.3 9.4 %apply.3 = (f32[128,2,32,256]{3,2,1,0:T(8,128)}, f32[4,2,128,256]{3,2,1,0:T(8,128)S(1)}, f32[4,2,128,256]{3,2,1,0:T(8,128)S(1)}) custom-call(s32[2]{0:T(128)S(1)} %copy-done.8, bf16[256,1536]{1,0:T(8,128)(2,1)S(1)} %get-tuple-element.44.refs_1_, bf16[256,1536]{1,0:T(8,128)(2,1)S(1)} %get-tuple-element.45.refs_2_, ...), custom_call_target="tpu_custom_call", output_to_operand_aliasing={{0}: (23, {})} | custom-call | flops 1024 | bytes 4096 | tf_op jit(solution)/shard_map/apply/pallas_call | solution.py:194
  161.7 3.6 %collective-permute-done.20.got_a = f32[4,2,128,256]{3,2,1,0:T(8,128)S(1)} collective-permute-done((f32[4,2,128,256]{3,2,1,0:T(8,128)S(1)}, f32[4,2,128,256]{3,2,1,0:T(8,128)S(1)}, u32[]{:S(2)}, u32[]{:S(2)}) %collective-permute-start.20) | collective-permute-done | bytes 1048608 | tf_op jit(solution)/shard_map/ppermute | solution.py:309
  165.3 0.3 collective-permute-done.22.got_b
  165.6 0.5 collective-permute-start.23
  166.1 1.5 collective-permute-start.21
  167.6 2.0 %place.2._ = f32[128,2,32,256]{3,2,1,0:T(8,128)} custom-call(s32[2]{0:T(128)S(1)} %copy-done.8, f32[4,2,128,256]{3,2,1,0:T(8,128)S(1)} %collective-permute-done.20.got_a, f32[4,2,128,256]{3,2,1,0:T(8,128)S(1)} %collective-permute-done.22.got_b, f32[128,2,32,256]{3,2,1,0:T(8,128)} %get-tuple-element.82._), custom_call_target="tpu_custom_call", output_to_operand_aliasing={{}: (3, {})} | custom-call | flops 1024 | bytes 4096 | tf_op jit(solution)/shard_map/place/pallas_call | solution.py:223
  169.6 19.9 %collective-permute-done.23.got_b = f32[4,2,128,256]{3,2,1,0:T(8,128)S(1)} collective-permute-done((f32[4,2,128,256]{3,2,1,0:T(8,128)S(1)}, f32[4,2,128,256]{3,2,1,0:T(8,128)S(1)}, u32[]{:S(2)}, u32[]{:S(2)}) %collective-permute-start.23) | collective-permute-done | bytes 1048608 | tf_op jit(solution)/shard_map/ppermute | solution.py:309
  189.5 0.2 collective-permute-done.21.got_a
  189.7 2.0 %place.3 = f32[128,2,32,256]{3,2,1,0:T(8,128)} custom-call(s32[2]{0:T(128)S(1)} %copy-done.8, f32[4,2,128,256]{3,2,1,0:T(8,128)S(1)} %collective-permute-done.21.got_a, f32[4,2,128,256]{3,2,1,0:T(8,128)S(1)} %collective-permute-done.23.got_b, f32[128,2,32,256]{3,2,1,0:T(8,128)} %place.2._), custom_call_target="tpu_custom_call", output_to_operand_aliasing={{}: (3, {})} | custom-call | flops 1024 | bytes 4096 | tf_op jit(solution)/shard_map/place/pallas_call | solution.py:223
  (18 shorter events, 0.0 us)
Async XLA Ops:
  7.0 101.2 %copy-start.8 = (s32[2]{0:T(128)S(1)}, s32[2]{0:T(128)}, u32[]{:S(2)}) copy-start(s32[2]{0:T(128)} %pad_add_fusion.sides_ref.refs_0_) | copy-start | bytes 28
  7.0 19.6 %collective-permute-start.1 = (f32[6,2,64,256]{3,2,1,0:T(8,128)}, f32[6,2,64,256]{3,2,1,0:T(8,128)S(1)}, u32[]{:S(2)}, u32[]{:S(2)}) collective-permute-start(f32[6,2,64,256]{3,2,1,0:T(8,128)} %get-tuple-element.48), channel_id=1, source_target_pairs={{0,16},{8,24},{16,0},{24,8},{1,17},{9,25},{17,1},{25,9},{2,18},{10... | collective-permute-start | bytes 2359304 | tf_op jit(solution)/shard_map/ppermute | solution.py:309
  8.6 17.9 %collective-permute-start = (f32[5,2,64,256]{3,2,1,0:T(8,128)}, f32[5,2,64,256]{3,2,1,0:T(8,128)S(1)}, u32[]{:S(2)}, u32[]{:S(2)}) collective-permute-start(f32[5,2,64,256]{3,2,1,0:T(8,128)} %get-tuple-element.47), channel_id=1, source_target_pairs={{0,8},{8,0},{16,24},{24,16},{1,9},{9,1},{17,25},{25,17},{2,10},{10... | collective-permute-start | bytes 1966088 | tf_op jit(solution)/shard_map/ppermute | solution.py:309
  10.1 33.7 %collective-permute-start.2 = (f32[6,2,64,256]{3,2,1,0:T(8,128)}, f32[6,2,64,256]{3,2,1,0:T(8,128)S(1)}, u32[]{:S(2)}, u32[]{:S(2)}) collective-permute-start(f32[6,2,64,256]{3,2,1,0:T(8,128)} %get-tuple-element.52.refs_4_.refs_2_.refs_11_.refs_15_), channel_id=1, source_target_pairs={{0,8},{8,0},{16,24},{24,16},{1,9},{9,1},{17,25},{25,17},{2,10},{10... | collective-permute-start | bytes 2359304 | tf_op jit(solution)/shard_map/ppermute | solution.py:309
  26.6 1.1 copy-start
  27.7 1.1 copy-start.2
  28.8 55.3 %copy-start.1 = (f32[6,2,64,256]{3,2,1,0:T(8,128)S(1)}, f32[6,2,64,256]{3,2,1,0:T(8,128)}, u32[]{:S(2)}) copy-start(f32[6,2,64,256]{3,2,1,0:T(8,128)} %get-tuple-element.52.refs_4_.refs_2_.refs_11_.refs_15_) | copy-start | bytes 2359300
  28.8 55.3 %copy-start.3 = (f32[5,2,64,256]{3,2,1,0:T(8,128)S(1)}, f32[5,2,64,256]{3,2,1,0:T(8,128)}, u32[]{:S(2)}) copy-start(f32[5,2,64,256]{3,2,1,0:T(8,128)} %get-tuple-element.46.refs_0_.refs_7_) | copy-start | bytes 1966084
  30.4 31.3 %collective-permute-start.10 = (f32[2,4,2,64,256]{4,3,2,1,0:T(8,128)}, f32[2,4,2,64,256]{4,3,2,1,0:T(8,128)}, u32[]{:S(2)}, u32[]{:S(2)}) collective-permute-start(f32[2,4,2,64,256]{4,3,2,1,0:T(8,128)} %get-tuple-element.61), channel_id=1, source_target_pairs={{0,1},{1,2},{2,3},{3,4},{4,5},{5,6},{6,7},{8,9},{9,10},{10,11},{11... | collective-permute-start | bytes 3145736 | tf_op jit(solution)/shard_map/ppermute | solution.py:357
  32.3 29.9 %collective-permute-start.11 = (f32[2,4,2,64,256]{4,3,2,1,0:T(8,128)}, f32[2,4,2,64,256]{4,3,2,1,0:T(8,128)}, u32[]{:S(2)}, u32[]{:S(2)}) collective-permute-start(f32[2,4,2,64,256]{4,3,2,1,0:T(8,128)} %get-tuple-element.62), channel_id=1, source_target_pairs={{1,0},{2,1},{3,2},{4,3},{5,4},{6,5},{7,6},{9,8},{10,9},{11,10},{12... | collective-permute-start | bytes 3145736 | tf_op jit(solution)/shard_map/ppermute | solution.py:357
  36.0 1.0 copy-start.6
  37.0 1.0 copy-start.7
  38.1 0.7 copy-start.9
  40.8 33.5 %collective-permute-start.12 = (f32[6,2,64,256]{3,2,1,0:T(8,128)S(1)}, f32[6,2,64,256]{3,2,1,0:T(8,128)S(1)}, u32[]{:S(2)}, u32[]{:S(2)}) collective-permute-start(f32[6,2,64,256]{3,2,1,0:T(8,128)S(1)} %collective-permute-done.1.refs_5_.refs_3_.refs_13_.refs_17_), channel_id=1, source_target_pairs={{0,8},{8,0},{16,24},{24,16},{1,9},{9,1},{17,25},{25,17},{2,10},{10... | collective-permute-start | bytes 2359304 | tf_op jit(solution)/shard_map/ppermute | solution.py:309
  42.3 17.9 %collective-permute-start.4 = (f32[5,2,64,256]{3,2,1,0:T(8,128)}, f32[5,2,64,256]{3,2,1,0:T(8,128)S(1)}, u32[]{:S(2)}, u32[]{:S(2)}) collective-permute-start(f32[5,2,64,256]{3,2,1,0:T(8,128)} %get-tuple-element.46.refs_0_.refs_7_), channel_id=1, source_target_pairs={{0,16},{8,24},{16,0},{24,8},{1,17},{9,25},{17,1},{25,9},{2,18},{10... | collective-permute-start | bytes 1966088 | tf_op jit(solution)/shard_map/ppermute | solution.py:309
  43.8 30.4 %collective-permute-start.8 = (f32[5,2,64,256]{3,2,1,0:T(8,128)S(1)}, f32[5,2,64,256]{3,2,1,0:T(8,128)S(1)}, u32[]{:S(2)}, u32[]{:S(2)}) collective-permute-start(f32[5,2,64,256]{3,2,1,0:T(8,128)S(1)} %collective-permute-done.refs_1_.refs_8_), channel_id=1, source_target_pairs={{0,16},{8,24},{16,0},{24,8},{1,17},{9,25},{17,1},{25,9},{2,18},{10... | collective-permute-start | bytes 1966088 | tf_op jit(solution)/shard_map/ppermute | solution.py:309
  60.2 24.0 %collective-permute-start.5 = (f32[4,2,64,256]{3,2,1,0:T(8,128)}, f32[4,2,64,256]{3,2,1,0:T(8,128)S(1)}, u32[]{:S(2)}, u32[]{:S(2)}) collective-permute-start(f32[4,2,64,256]{3,2,1,0:T(8,128)} %get-tuple-element.56), channel_id=1, source_target_pairs={{0,16},{8,24},{16,0},{24,8},{1,17},{9,25},{17,1},{25,9},{2,18},{10... | collective-permute-start | bytes 1572872 | tf_op jit(solution)/shard_map/ppermute | solution.py:309
  61.7 22.4 %collective-permute-start.3 = (f32[4,2,64,256]{3,2,1,0:T(8,128)}, f32[4,2,64,256]{3,2,1,0:T(8,128)S(1)}, u32[]{:S(2)}, u32[]{:S(2)}) collective-permute-start(f32[4,2,64,256]{3,2,1,0:T(8,128)} %get-tuple-element.53), channel_id=1, source_target_pairs={{0,8},{8,0},{16,24},{24,16},{1,9},{9,1},{17,25},{25,17},{2,10},{10... | collective-permute-start | bytes 1572872 | tf_op jit(solution)/shard_map/ppermute | solution.py:309
  77.2 28.9 %collective-permute-start.13 = (f32[2,4,2,64,256]{4,3,2,1,0:T(8,128)S(1)}, f32[2,4,2,64,256]{4,3,2,1,0:T(8,128)S(1)}, u32[]{:S(2)}, u32[]{:S(2)}) collective-permute-start(f32[2,4,2,64,256]{4,3,2,1,0:T(8,128)S(1)} %get-tuple-element.65), channel_id=1, source_target_pairs={{0,1},{1,2},{2,3},{3,4},{4,5},{5,6},{6,7},{8,9},{9,10},{10,11},{11... | collective-permute-start | bytes 3145736 | tf_op jit(solution)/shard_map/ppermute | solution.py:357
  79.2 27.5 %collective-permute-start.14 = (f32[2,4,2,64,256]{4,3,2,1,0:T(8,128)S(1)}, f32[2,4,2,64,256]{4,3,2,1,0:T(8,128)S(1)}, u32[]{:S(2)}, u32[]{:S(2)}) collective-permute-start(f32[2,4,2,64,256]{4,3,2,1,0:T(8,128)S(1)} %get-tuple-element.66), channel_id=1, source_target_pairs={{1,0},{2,1},{3,2},{4,3},{5,4},{6,5},{7,6},{9,8},{10,9},{11,10},{12... | collective-permute-start | bytes 3145736 | tf_op jit(solution)/shard_map/ppermute | solution.py:357
  84.1 1.0 copy-start.4
  88.4 64.0 %copy-start.5 = (f32[4,2,64,256]{3,2,1,0:T(8,128)S(1)}, f32[4,2,64,256]{3,2,1,0:T(8,128)}, u32[]{:S(2)}) copy-start(f32[4,2,64,256]{3,2,1,0:T(8,128)} %get-tuple-element.60.refs_2_.refs_11_) | copy-start | bytes 1572868
  88.4 29.7 %collective-permute-start.6 = (f32[2,4,2,64,256]{4,3,2,1,0:T(8,128)S(1)}, f32[2,4,2,64,256]{4,3,2,1,0:T(8,128)S(1)}, u32[]{:S(2)}, u32[]{:S(2)}) collective-permute-start(f32[2,4,2,64,256]{4,3,2,1,0:T(8,128)S(1)} %get-tuple-element.57), channel_id=1, source_target_pairs={{0,1},{1,2},{2,3},{3,4},{4,5},{5,6},{6,7},{8,9},{9,10},{10,11},{11... | collective-permute-start | bytes 3145736 | tf_op jit(solution)/shard_map/ppermute | solution.py:357
  90.4 14.2 %collective-permute-start.9 = (f32[4,2,64,256]{3,2,1,0:T(8,128)S(1)}, f32[4,2,64,256]{3,2,1,0:T(8,128)S(1)}, u32[]{:S(2)}, u32[]{:S(2)}) collective-permute-start(f32[4,2,64,256]{3,2,1,0:T(8,128)S(1)} %copy-done.4), channel_id=1, source_target_pairs={{0,16},{8,24},{16,0},{24,8},{1,17},{9,25},{17,1},{25,9},{2,18},{10... | collective-permute-start | bytes 1572872 | tf_op jit(solution)/shard_map/ppermute | solution.py:309
  92.0 26.1 %collective-permute-start.7 = (f32[2,4,2,64,256]{4,3,2,1,0:T(8,128)S(1)}, f32[2,4,2,64,256]{4,3,2,1,0:T(8,128)S(1)}, u32[]{:S(2)}, u32[]{:S(2)}) collective-permute-start(f32[2,4,2,64,256]{4,3,2,1,0:T(8,128)S(1)} %get-tuple-element.58), channel_id=1, source_target_pairs={{1,0},{2,1},{3,2},{4,3},{5,4},{6,5},{7,6},{9,8},{10,9},{11,10},{12... | collective-permute-start | bytes 3145736 | tf_op jit(solution)/shard_map/ppermute | solution.py:357
  104.6 14.3 %collective-permute-start.15 = (f32[4,2,64,256]{3,2,1,0:T(8,128)S(1)}, f32[4,2,64,256]{3,2,1,0:T(8,128)S(1)}, u32[]{:S(2)}, u32[]{:S(2)}) collective-permute-start(f32[4,2,64,256]{3,2,1,0:T(8,128)S(1)} %collective-permute-done.3.refs_3_.refs_12_), channel_id=1, source_target_pairs={{0,16},{8,24},{16,0},{24,8},{1,17},{9,25},{17,1},{25,9},{2,18},{10... | collective-permute-start | bytes 1572872 | tf_op jit(solution)/shard_map/ppermute | solution.py:309
  106.2 14.8 %collective-permute-start.17 = (f32[4,2,64,256]{3,2,1,0:T(8,128)S(1)}, f32[4,2,64,256]{3,2,1,0:T(8,128)S(1)}, u32[]{:S(2)}, u32[]{:S(2)}) collective-permute-start(f32[4,2,64,256]{3,2,1,0:T(8,128)S(1)} %collective-permute-done.5.refs_7_.refs_21_), channel_id=1, source_target_pairs={{0,8},{8,0},{16,24},{24,16},{1,9},{9,1},{17,25},{25,17},{2,10},{10... | collective-permute-start | bytes 1572872 | tf_op jit(solution)/shard_map/ppermute | solution.py:309
  106.7 24.7 %collective-permute-start.16 = (f32[4,2,64,256]{3,2,1,0:T(8,128)}, f32[4,2,64,256]{3,2,1,0:T(8,128)S(1)}, u32[]{:S(2)}, u32[]{:S(2)}) collective-permute-start(f32[4,2,64,256]{3,2,1,0:T(8,128)} %get-tuple-element.71.refs_6_.refs_19_), channel_id=1, source_target_pairs={{0,8},{8,0},{16,24},{24,16},{1,9},{9,1},{17,25},{25,17},{2,10},{10... | collective-permute-start | bytes 1572872 | tf_op jit(solution)/shard_map/ppermute | solution.py:309
  134.5 16.1 %collective-permute-start.18 = (f32[2,4,2,64,256]{4,3,2,1,0:T(8,128)S(1)}, f32[2,4,2,64,256]{4,3,2,1,0:T(8,128)S(1)}, u32[]{:S(2)}, u32[]{:S(2)}) collective-permute-start(f32[2,4,2,64,256]{4,3,2,1,0:T(8,128)S(1)} %get-tuple-element.73), channel_id=1, source_target_pairs={{0,1},{1,2},{2,3},{3,4},{4,5},{5,6},{6,7},{8,9},{9,10},{10,11},{11... | collective-permute-start | bytes 3145736 | tf_op jit(solution)/shard_map/ppermute | solution.py:357
  136.4 15.9 %collective-permute-start.19 = (f32[2,4,2,64,256]{4,3,2,1,0:T(8,128)S(1)}, f32[2,4,2,64,256]{4,3,2,1,0:T(8,128)S(1)}, u32[]{:S(2)}, u32[]{:S(2)}) collective-permute-start(f32[2,4,2,64,256]{4,3,2,1,0:T(8,128)S(1)} %get-tuple-element.74), channel_id=1, source_target_pairs={{1,0},{2,1},{3,2},{4,3},{5,4},{6,5},{7,6},{9,8},{10,9},{11,10},{12... | collective-permute-start | bytes 3145736 | tf_op jit(solution)/shard_map/ppermute | solution.py:357
  140.3 25.1 %collective-permute-start.20 = (f32[4,2,128,256]{3,2,1,0:T(8,128)S(1)}, f32[4,2,128,256]{3,2,1,0:T(8,128)S(1)}, u32[]{:S(2)}, u32[]{:S(2)}) collective-permute-start(f32[4,2,128,256]{3,2,1,0:T(8,128)S(1)} %get-tuple-element.77), channel_id=1, source_target_pairs={{0,8},{8,0},{16,24},{24,16},{1,9},{9,1},{17,25},{25,17},{2,10},{10... | collective-permute-start | bytes 3145736 | tf_op jit(solution)/shard_map/ppermute | solution.py:309
  140.9 24.7 %collective-permute-start.22 = (f32[4,2,128,256]{3,2,1,0:T(8,128)S(1)}, f32[4,2,128,256]{3,2,1,0:T(8,128)S(1)}, u32[]{:S(2)}, u32[]{:S(2)}) collective-permute-start(f32[4,2,128,256]{3,2,1,0:T(8,128)S(1)} %get-tuple-element.80), channel_id=1, source_target_pairs={{0,16},{8,24},{16,0},{24,8},{1,17},{9,25},{17,1},{25,9},{2,18},{10... | collective-permute-start | bytes 3145736 | tf_op jit(solution)/shard_map/ppermute | solution.py:309
  165.6 23.9 %collective-permute-start.23 = (f32[4,2,128,256]{3,2,1,0:T(8,128)S(1)}, f32[4,2,128,256]{3,2,1,0:T(8,128)S(1)}, u32[]{:S(2)}, u32[]{:S(2)}) collective-permute-start(f32[4,2,128,256]{3,2,1,0:T(8,128)S(1)} %get-tuple-element.81), channel_id=1, source_target_pairs={{0,16},{8,24},{16,0},{24,8},{1,17},{9,25},{17,1},{25,9},{2,18},{10... | collective-permute-start | bytes 3145736 | tf_op jit(solution)/shard_map/ppermute | solution.py:309
  166.1 23.6 %collective-permute-start.21 = (f32[4,2,128,256]{3,2,1,0:T(8,128)S(1)}, f32[4,2,128,256]{3,2,1,0:T(8,128)S(1)}, u32[]{:S(2)}, u32[]{:S(2)}) collective-permute-start(f32[4,2,128,256]{3,2,1,0:T(8,128)S(1)} %get-tuple-element.78), channel_id=1, source_target_pairs={{0,8},{8,0},{16,24},{24,16},{1,9},{9,1},{17,25},{25,17},{2,10},{10... | collective-permute-start | bytes 3145736 | tf_op jit(solution)/shard_map/ppermute | solution.py:309

commit v5 on v4

--- a/solution.py
+++ b/solution.py
@@ -8,12 +8,19 @@
 from jax.sharding import PartitionSpec as P
 
 
-CUTS = 2
+CUTS = (0, 4, 8)
+CHUNKS = len(CUTS) - 1
 VMEM_LIMIT = 28 * 2**20
 HBM = pl.BlockSpec(memory_space=pl.ANY)
 VMEM = pl.BlockSpec(memory_space=pltpu.VMEM)
 SCALARS = pl.BlockSpec(memory_space=pltpu.SMEM)
-LIGHT = pl.CostEstimate(flops=1024, bytes_accessed=4096, transcendentals=0)
+COST = 370000
+
+
+def cost(weight):
+    return pl.CostEstimate(flops=0, bytes_accessed=weight * COST, transcendentals=0)
+
+
 PARAMS = pltpu.CompilerParams(vmem_limit_bytes=4 * 2**20)
 
 
@@ -24,8 +31,8 @@
 
 
 def own_rows(chunk, depth):
-    high = depth // CUTS
-    return list(range(chunk * high, (chunk + 1) * high))
+    bounds = [depth * cut // 8 for cut in CUTS]
+    return list(range(bounds[chunk], bounds[chunk + 1]))
 
 
 def chunk_rows(stream, chunk, depth):
@@ -80,7 +87,7 @@
         out_specs=[VMEM] * 4,
         scratch_shapes=[pltpu.SemaphoreType.DMA((sum(counts) * planes,))],
         compiler_params=pltpu.CompilerParams(vmem_limit_bytes=56 * 2**20),
-        cost_estimate=LIGHT,
+        cost_estimate=cost(5),
         name="pick",
     )(sides, ratio, residual)
     return [outs[0:2], outs[2:4]]
@@ -109,7 +116,7 @@
     groups = len(raws[0][0])
     _, _, steps, rows_y = raws[0][0][0].shape
     flat = [raw for stream in raws for arrays in stream for raw in arrays]
-    high = depth // CUTS
+    high = len(own_rows(chunk, depth))
     shape = jax.ShapeDtypeStruct((2, high, groups, steps, rows_y), jnp.float32)
     return pl.pallas_call(
         functools.partial(edge_kernel, chunk, depth, groups),
@@ -118,7 +125,7 @@
         out_specs=[HBM] * 2,
         scratch_shapes=[pltpu.SemaphoreType.DMA((4 * high * groups,))],
         compiler_params=PARAMS,
-        cost_estimate=LIGHT,
+        cost_estimate=cost(3),
         name="edges",
     )(*flat)
 
@@ -153,7 +160,7 @@
             return jnp.concatenate([parts[group] for group in range(groups)], axis=0)
 
         for at, row in enumerate(own_rows(chunk, depth)):
-            number = stream * (depth // CUTS) + at
+            number = stream * len(own_rows(chunk, depth)) + at
             x = block_row(stream, sides_ref[stream], row, depth, rows_x)
             mids = [load(row, z) for z in range(planes)]
             for z, mid in enumerate(mids):
@@ -180,7 +187,7 @@
 
 def apply(chunk, depth, order, sides, maps, early, late, raws, shape, result):
     _, planes, _, rows_y = raws[0][0][0].shape
-    high = depth // CUTS
+    high = len(own_rows(chunk, depth))
     half = shape[0]
     flat = [raw for stream in raws for arrays in stream for raw in arrays]
     first = [] if result is None else [result]
@@ -202,7 +209,7 @@
         ],
         input_output_aliases={count: 0} if first else {},
         compiler_params=pltpu.CompilerParams(vmem_limit_bytes=VMEM_LIMIT),
-        cost_estimate=LIGHT,
+        cost_estimate=cost(10),
         name="apply",
     )(sides, *maps, *early, *late, *flat, *first)
 
@@ -225,10 +232,10 @@
         out_shape=jax.ShapeDtypeStruct(result.shape, jnp.float32),
         in_specs=[SCALARS] + [HBM] * 3,
         out_specs=HBM,
-        scratch_shapes=[pltpu.SemaphoreType.DMA((2 * depth // CUTS * planes,))],
+        scratch_shapes=[pltpu.SemaphoreType.DMA((2 * len(own_rows(chunk, depth)) * planes,))],
         input_output_aliases={3: 0},
         compiler_params=PARAMS,
-        cost_estimate=LIGHT,
+        cost_estimate=cost(2),
         name="place",
     )(sides, *got, result)
 
@@ -290,7 +297,7 @@
         in_specs=[SCALARS] + [VMEM] * 3,
         out_specs=[VMEM] * 2,
         compiler_params=pltpu.CompilerParams(vmem_limit_bytes=VMEM_LIMIT),
-        cost_estimate=LIGHT,
+        cost_estimate=cost(2),
         name="maps",
     )(me.astype(jnp.int32).reshape(1), forward_map, back_map, eigen_values)
 
@@ -314,7 +321,7 @@
 
     queues = [[], []]
 
-    def swap_in_turn(data, bit, *others, flight=2):
+    def swap_in_turn(data, bit, *others, flight=1):
         queue = queues[0 if bit == bits[0] else 1]
         if len(queue) >= flight:
             others = (queue[-flight], *others)
@@ -326,7 +333,7 @@
 
     masks = range(count)
     order = [[[m for m in masks if m in (0, b)], [m for m in masks if m not in (0, b)]] for b in bits]
-    held = [[None] * CUTS for _ in range(2)]
+    held = [[None] * CHUNKS for _ in range(2)]
 
     maps = make_maps(forward_map, back_map, eigen_values, me, count, bits)
     firsts = []
@@ -358,18 +365,17 @@
 
     gives = []
     result = None
-    for chunk in range(CUTS):
+    for chunk in range(CHUNKS):
         raw(chunk)
     shape = (2 * local_steps, planes, rows_x, rows_y)
-    for chunk in range(CUTS):
+    for chunk in range(CHUNKS):
         early = beside(chunk, 0)
-        late = beside(chunk, 1, *early, *(gives[-1] if gives else []))
+        late = beside(chunk, 1, *early)
         used = [held[s][max(chunk - 1, 0) : chunk + 1] for s in range(2)]
         result, *give = apply(chunk, depth, order, sides, maps, early, late, used, shape, result)
         gives.append(give)
-    for chunk in range(CUTS):
-        flight = 1 if chunk else 2
-        got = [swap_in_turn(gives[chunk][s], bits[s], flight=flight) for s in range(2)]
+    for chunk in range(CHUNKS):
+        got = [swap_in_turn(gives[chunk][s], bits[s]) for s in range(2)]
         result = place(chunk, depth, sides, got, result)
     return result.reshape(2, local_steps, planes, rows_x, rows_y)
 

time: 193 us -> 177 us (0.917)
  waiting for transfers between devices: 98.1 us -> 80.4 us
    ppermute x16, waiting for transfers between devices: 87.1 us -> 70.3 us  [swap(): return lax.ppermute(data, 'tm', [(i, i ^ bit) for i in range(count)])]
    ppermute x4, starting transfers between devices: 14.7 us -> 12.5 us  [beside(): lax.ppermute(down, 'space', downward)]
    unnamed x20 -> x24, local copies, waits for them, and re-layouts: 6.03 us -> 7.08 us
  transfers between devices with their start and end apart: 24 -> 24, of which waited for: 15 -> 12; matrix products, arithmetic and copies ran while one was open for 0% -> 0% of each run, Pallas kernels for 18% -> 20%
where the time goes in v5:
time: 177 us; the launch traced here: 175 us
  waiting for transfers between devices  80.4 us (45%)
  Pallas kernels  45.2 us (26%)
  starting transfers between devices  39.6 us (22%)
  local copies, waits for them, and re-layouts  7.79 us (4%)
    ppermute x16, waiting for transfers between devices, swap(): return lax.ppermute(data, 'tm', [(i, i ^ bit) for i in range(count)])  70.3 us
    pallas_call x2, Pallas kernels, apply(): pl.pallas_call(body, out_shape=[jax.ShapeDtypeStruct(shape, jnp.float32),...  19.2 us
    ppermute x16, starting transfers between devices, swap(): return lax.ppermute(data, 'tm', [(i, i ^ bit) for i in range(count)])  18.6 us
    ppermute x4, starting transfers between devices, beside(): lax.ppermute(down, 'space', downward)  12.5 us
    pallas_call x4, Pallas kernels, edges(): pl.pallas_call(functools.partial(edge_kernel, chunk, depth, groups), out_...  10.6 us
    pallas_call x2, Pallas kernels, pick(): pl.pallas_call(functools.partial(pick_kernel, chunk, depth), out_shape=[j...  9.38 us
    ppermute x4, starting transfers between devices, beside(): lax.ppermute(up, 'space', upward)  8.55 us
    ppermute x4, waiting for transfers between devices, beside(): lax.ppermute(up, 'space', upward)  8.21 us
  transfers between devices with their start and end apart: 24, of which 12 were waited for; matrix products, arithmetic and copies ran while one was open for 0% of the time, Pallas kernels for 20%

profile of v5, /device:TPU:8, one launch (start us, length us, event | category | flops | bytes accessed | tf_op | source)
XLA Modules:
  0.0 174.7 jit_solution(4916644007872703484)
XLA Ops:
  0.0 0.7 convert_multiply_fusion
  0.7 0.6 pad_add_fusion.sides_ref.refs_0_
  1.2 0.7 broadcast_in_dim.2.ratio_ref
  1.9 5.0 %pick.2 = (f32[5,2,64,256]{3,2,1,0:T(8,128)}, f32[5,2,64,256]{3,2,1,0:T(8,128)}, f32[6,2,64,256]{3,2,1,0:T(8,128)}, f32[6,2,64,256]{3,2,1,0:T(8,128)}) custom-call(s32[2]{0:T(128)} %pad_add_fusion.sides_ref.refs_0_, f32[64,256]{1,0:T(8,128)} %broadcast_in_dim.2.ratio_ref, f32[64,2,32,256]{3,2,1,0:T(8,128)} %in_ref.2), custom_call_target="tpu_custom_call" | custom-call | bytes 1850000 | tf_op jit(solution)/shard_map/pick/pallas_call | solution.py:83
  7.0 1.6 collective-permute-start.1
  8.6 1.5 collective-permute-start
  10.0 16.5 %collective-permute-done.1.refs_5_.refs_3_.refs_13_.refs_17_ = f32[6,2,64,256]{3,2,1,0:T(8,128)S(1)} collective-permute-done((f32[6,2,64,256]{3,2,1,0:T(8,128)}, f32[6,2,64,256]{3,2,1,0:T(8,128)S(1)}, u32[]{:S(2)}, u32[]{:S(2)}) %collective-permute-start.1) | collective-permute-done | bytes 786464 | tf_op jit(solution)/shard_map/ppermute | solution.py:316
  26.5 1.5 collective-permute-start.5
  28.1 1.5 collective-permute-start.2
  29.5 1.0 copy-done.8
  30.6 1.0 copy-done.9
  31.6 0.7 copy-done.11
  32.3 2.0 %maps.1 = (bf16[256,1536]{1,0:T(8,128)(2,1)S(1)}, bf16[256,1536]{1,0:T(8,128)(2,1)S(1)}) custom-call(s32[1]{0:T(128)} %bitcast.2.me_ref, f32[2,256,256]{2,1,0:T(8,128)S(1)} %copy-done.8, f32[2,256,256]{2,1,0:T(8,128)S(1)} %copy-done.9, f32[2,256]{1,0:T(2,128)S(1)} %copy-done.11), custom_call_target="tpu_custom_call" | custom-call | bytes 740000 | tf_op jit(solution)/shard_map/maps/pallas_call | solution.py:294
  34.3 8.0 %collective-permute-done.5.refs_0_.refs_9_ = f32[5,2,64,256]{3,2,1,0:T(8,128)S(1)} collective-permute-done((f32[5,2,64,256]{3,2,1,0:T(8,128)}, f32[5,2,64,256]{3,2,1,0:T(8,128)S(1)}, u32[]{:S(2)}, u32[]{:S(2)}) %collective-permute-start.5) | collective-permute-done | bytes 655392 | tf_op jit(solution)/shard_map/ppermute | solution.py:316
  42.3 1.5 collective-permute-start.6
  43.9 1.1 copy-done
  45.0 1.1 copy-done.2
  46.1 1.6 edges.6
  47.6 1.9 %collective-permute-start.16 = (f32[2,4,2,64,256]{4,3,2,1,0:T(8,128)}, f32[2,4,2,64,256]{4,3,2,1,0:T(8,128)}, u32[]{:S(2)}, u32[]{:S(2)}) collective-permute-start(f32[2,4,2,64,256]{4,3,2,1,0:T(8,128)} %get-tuple-element.72), channel_id=1, source_target_pairs={{0,1},{1,2},{2,3},{3,4},{4,5},{5,6},{6,7},{8,9},{9,10},{10,11},{11... | collective-permute-start | bytes 3145736 | tf_op jit(solution)/shard_map/ppermute | solution.py:364
  49.6 3.6 %collective-permute-start.17 = (f32[2,4,2,64,256]{4,3,2,1,0:T(8,128)}, f32[2,4,2,64,256]{4,3,2,1,0:T(8,128)}, u32[]{:S(2)}, u32[]{:S(2)}) collective-permute-start(f32[2,4,2,64,256]{4,3,2,1,0:T(8,128)} %get-tuple-element.73), channel_id=1, source_target_pairs={{1,0},{2,1},{3,2},{4,3},{5,4},{6,5},{7,6},{9,8},{10,9},{11,10},{12... | collective-permute-start | bytes 3145736 | tf_op jit(solution)/shard_map/ppermute | solution.py:364
  53.2 0.0 collective-permute-done.2.refs_4_.refs_2_.refs_12_.refs_16_
  53.2 1.6 collective-permute-start.3
  54.8 4.4 %pick.3 = (f32[4,2,64,256]{3,2,1,0:T(8,128)}, f32[4,2,64,256]{3,2,1,0:T(8,128)}, f32[4,2,64,256]{3,2,1,0:T(8,128)}, f32[4,2,64,256]{3,2,1,0:T(8,128)}) custom-call(s32[2]{0:T(128)} %pad_add_fusion.sides_ref.refs_0_, f32[64,256]{1,0:T(8,128)} %broadcast_in_dim.2.ratio_ref, f32[64,2,32,256]{3,2,1,0:T(8,128)} %in_ref.2), custom_call_target="tpu_custom_call" | custom-call | bytes 1850000 | tf_op jit(solution)/shard_map/pick/pallas_call | solution.py:83
  59.2 0.0 collective-permute-done.6.refs_1_.refs_10_
  59.2 0.6 collective-permute-start.7
  59.8 13.0 %collective-permute-done.3.refs_5_.refs_3_.refs_14_.refs_18_ = f32[6,2,64,256]{3,2,1,0:T(8,128)S(1)} collective-permute-done((f32[6,2,64,256]{3,2,1,0:T(8,128)S(1)}, f32[6,2,64,256]{3,2,1,0:T(8,128)S(1)}, u32[]{:S(2)}, u32[]{:S(2)}) %collective-permute-start.3) | collective-permute-done | bytes 786464 | tf_op jit(solution)/shard_map/ppermute | solution.py:316
  72.7 1.5 collective-permute-start.4
  74.2 0.0 collective-permute-done.16.refs_3_
  74.2 0.0 collective-permute-done.17.refs_4_
  74.2 0.0 collective-permute-done.7.refs_7_.refs_21_
  74.2 0.6 collective-permute-start.10
  74.8 3.0 %edges.7 = (f32[2,4,2,64,256]{4,3,2,1,0:T(8,128)S(1)}, f32[2,4,2,64,256]{4,3,2,1,0:T(8,128)S(1)}) custom-call(f32[5,2,64,256]{3,2,1,0:T(8,128)S(1)} %collective-permute-done.5.refs_0_.refs_9_, f32[5,2,64,256]{3,2,1,0:T(8,128)S(1)} %collective-permute-done.6.refs_1_.refs_10_, f32[6,2,64,256]{3,2,1,0:T(8,128)S(1)} %collective-permute-done.2.refs_4_.refs_2_.refs_12_.refs_16_, ...), custom_call_target="tpu_custom_call" | custom-call | bytes 1110000 | tf_op jit(solution)/shard_map/edges/pallas_call | solution.py:121
  77.8 1.9 %collective-permute-start.18 = (f32[2,4,2,64,256]{4,3,2,1,0:T(8,128)S(1)}, f32[2,4,2,64,256]{4,3,2,1,0:T(8,128)S(1)}, u32[]{:S(2)}, u32[]{:S(2)}) collective-permute-start(f32[2,4,2,64,256]{4,3,2,1,0:T(8,128)S(1)} %get-tuple-element.75), channel_id=1, source_target_pairs={{0,1},{1,2},{2,3},{3,4},{4,5},{5,6},{6,7},{8,9},{9,10},{10,11},{11... | collective-permute-start | bytes 3145736 | tf_op jit(solution)/shard_map/ppermute | solution.py:364
  79.7 6.1 %collective-permute-done.4.refs_3_.refs_12_ = f32[4,2,64,256]{3,2,1,0:T(8,128)S(1)} collective-permute-done((f32[4,2,64,256]{3,2,1,0:T(8,128)}, f32[4,2,64,256]{3,2,1,0:T(8,128)S(1)}, u32[]{:S(2)}, u32[]{:S(2)}) %collective-permute-start.4) | collective-permute-done | bytes 524320 | tf_op jit(solution)/shard_map/ppermute | solution.py:316
  85.8 1.5 collective-permute-start.12
  87.3 1.9 %collective-permute-start.19 = (f32[2,4,2,64,256]{4,3,2,1,0:T(8,128)S(1)}, f32[2,4,2,64,256]{4,3,2,1,0:T(8,128)S(1)}, u32[]{:S(2)}, u32[]{:S(2)}) collective-permute-start(f32[2,4,2,64,256]{4,3,2,1,0:T(8,128)S(1)} %get-tuple-element.76), channel_id=1, source_target_pairs={{1,0},{2,1},{3,2},{4,3},{5,4},{6,5},{7,6},{9,8},{10,9},{11,10},{12... | collective-permute-start | bytes 3145736 | tf_op jit(solution)/shard_map/ppermute | solution.py:364
  89.3 1.0 copy-done.4
  90.3 1.0 copy-done.6
  91.4 3.0 %edges.4 = (f32[2,4,2,64,256]{4,3,2,1,0:T(8,128)S(1)}, f32[2,4,2,64,256]{4,3,2,1,0:T(8,128)S(1)}) custom-call(f32[5,2,64,256]{3,2,1,0:T(8,128)S(1)} %copy-done.3, f32[5,2,64,256]{3,2,1,0:T(8,128)S(1)} %collective-permute-done.refs_1_.refs_8_, f32[4,2,64,256]{3,2,1,0:T(8,128)S(1)} %copy-done.4, f32[4,2,64,256]{3,2,1,0:T(8,128)S(1)} %collective-permute-done.4.refs_3_.refs_12_, ...), custom_call_target="tpu_custom_call" | custom-call | bytes 1110000 | tf_op jit(solution)/shard_map/edges/pallas_call | solution.py:121
  94.4 2.5 %collective-permute-start.8 = (f32[2,4,2,64,256]{4,3,2,1,0:T(8,128)S(1)}, f32[2,4,2,64,256]{4,3,2,1,0:T(8,128)S(1)}, u32[]{:S(2)}, u32[]{:S(2)}) collective-permute-start(f32[2,4,2,64,256]{4,3,2,1,0:T(8,128)S(1)} %get-tuple-element.63), channel_id=1, source_target_pairs={{0,1},{1,2},{2,3},{3,4},{4,5},{5,6},{6,7},{8,9},{9,10},{10,11},{11... | collective-permute-start | bytes 3145736 | tf_op jit(solution)/shard_map/ppermute | solution.py:364
  96.9 0.0 collective-permute-done.10.refs_2_.refs_13_
  97.0 3.3 %collective-permute-start.9 = (f32[2,4,2,64,256]{4,3,2,1,0:T(8,128)S(1)}, f32[2,4,2,64,256]{4,3,2,1,0:T(8,128)S(1)}, u32[]{:S(2)}, u32[]{:S(2)}) collective-permute-start(f32[2,4,2,64,256]{4,3,2,1,0:T(8,128)S(1)} %get-tuple-element.64), channel_id=1, source_target_pairs={{1,0},{2,1},{3,2},{4,3},{5,4},{6,5},{7,6},{9,8},{10,9},{11,10},{12... | collective-permute-start | bytes 3145736 | tf_op jit(solution)/shard_map/ppermute | solution.py:364
  100.3 0.0 collective-permute-done.12.refs_6_.refs_20_
  100.3 0.6 collective-permute-start.11
  100.9 0.5 collective-permute-start.13
  101.4 0.1 collective-permute-done.19.refs_6_
  101.6 10.0 %apply.2 = (f32[128,2,32,256]{3,2,1,0:T(8,128)}, f32[4,2,128,256]{3,2,1,0:T(8,128)S(1)}, f32[4,2,128,256]{3,2,1,0:T(8,128)S(1)}) custom-call(s32[2]{0:T(128)S(1)} %copy-done.10, bf16[256,1536]{1,0:T(8,128)(2,1)S(1)} %get-tuple-element.46.refs_1_, bf16[256,1536]{1,0:T(8,128)(2,1)S(1)} %get-tuple-element.47.refs_2_, ...), custom_call_target="tpu_custom_call" | custom-call | bytes 3700000 | tf_op jit(solution)/shard_map/apply/pallas_call | solution.py:201
  111.6 2.6 %collective-permute-done.11.refs_3_.refs_14_ = f32[4,2,64,256]{3,2,1,0:T(8,128)S(1)} collective-permute-done((f32[4,2,64,256]{3,2,1,0:T(8,128)S(1)}, f32[4,2,64,256]{3,2,1,0:T(8,128)S(1)}, u32[]{:S(2)}, u32[]{:S(2)}) %collective-permute-start.11) | collective-permute-done | bytes 524320 | tf_op jit(solution)/shard_map/ppermute | solution.py:316
  114.2 0.2 collective-permute-done.13.refs_7_.refs_22_
  114.4 3.0 %edges.5 = (f32[2,4,2,64,256]{4,3,2,1,0:T(8,128)S(1)}, f32[2,4,2,64,256]{4,3,2,1,0:T(8,128)S(1)}) custom-call(f32[5,2,64,256]{3,2,1,0:T(8,128)S(1)} %collective-permute-done.5.refs_0_.refs_9_, f32[5,2,64,256]{3,2,1,0:T(8,128)S(1)} %collective-permute-done.6.refs_1_.refs_10_, f32[4,2,64,256]{3,2,1,0:T(8,128)S(1)} %collective-permute-done.10.refs_2_.refs_13_, ...), custom_call_target="tpu_custom_call" | custom-call | bytes 1110000 | tf_op jit(solution)/shard_map/edges/pallas_call | solution.py:121
  117.4 2.2 %collective-permute-start.14 = (f32[2,4,2,64,256]{4,3,2,1,0:T(8,128)S(1)}, f32[2,4,2,64,256]{4,3,2,1,0:T(8,128)S(1)}, u32[]{:S(2)}, u32[]{:S(2)}) collective-permute-start(f32[2,4,2,64,256]{4,3,2,1,0:T(8,128)S(1)} %get-tuple-element.70), channel_id=1, source_target_pairs={{0,1},{1,2},{2,3},{3,4},{4,5},{5,6},{6,7},{8,9},{9,10},{10,11},{11... | collective-permute-start | bytes 3145736 | tf_op jit(solution)/shard_map/ppermute | solution.py:364
  119.6 3.6 %collective-permute-start.15 = (f32[2,4,2,64,256]{4,3,2,1,0:T(8,128)S(1)}, f32[2,4,2,64,256]{4,3,2,1,0:T(8,128)S(1)}, u32[]{:S(2)}, u32[]{:S(2)}) collective-permute-start(f32[2,4,2,64,256]{4,3,2,1,0:T(8,128)S(1)} %get-tuple-element.71), channel_id=1, source_target_pairs={{1,0},{2,1},{3,2},{4,3},{5,4},{6,5},{7,6},{9,8},{10,9},{11,10},{12... | collective-permute-start | bytes 3145736 | tf_op jit(solution)/shard_map/ppermute | solution.py:364
  123.2 1.6 collective-permute-start.22
  124.8 0.5 collective-permute-start.20
  125.3 8.2 %collective-permute-done.14.refs_5_ = f32[2,4,2,64,256]{4,3,2,1,0:T(8,128)S(1)} collective-permute-done((f32[2,4,2,64,256]{4,3,2,1,0:T(8,128)S(1)}, f32[2,4,2,64,256]{4,3,2,1,0:T(8,128)S(1)}, u32[]{:S(2)}, u32[]{:S(2)}) %collective-permute-start.14) | collective-permute-done | bytes 1048608 | tf_op jit(solution)/shard_map/ppermute | solution.py:364
  133.5 1.8 %collective-permute-done.15.refs_6_ = f32[2,4,2,64,256]{4,3,2,1,0:T(8,128)S(1)} collective-permute-done((f32[2,4,2,64,256]{4,3,2,1,0:T(8,128)S(1)}, f32[2,4,2,64,256]{4,3,2,1,0:T(8,128)S(1)}, u32[]{:S(2)}, u32[]{:S(2)}) %collective-permute-start.15) | collective-permute-done | bytes 1048608 | tf_op jit(solution)/shard_map/ppermute | solution.py:364
  135.3 9.2 %apply.3 = (f32[128,2,32,256]{3,2,1,0:T(8,128)}, f32[4,2,128,256]{3,2,1,0:T(8,128)S(1)}, f32[4,2,128,256]{3,2,1,0:T(8,128)S(1)}) custom-call(s32[2]{0:T(128)S(1)} %copy-done.10, bf16[256,1536]{1,0:T(8,128)(2,1)S(1)} %get-tuple-element.46.refs_1_, bf16[256,1536]{1,0:T(8,128)(2,1)S(1)} %get-tuple-element.47.refs_2_, ...), custom_call_target="tpu_custom_call", output_to_operand_aliasing={{0}: (23, {})} | custom-call | bytes 3700000 | tf_op jit(solution)/shard_map/apply/pallas_call | solution.py:201
  144.5 3.2 %collective-permute-done.22.got_b = f32[4,2,128,256]{3,2,1,0:T(8,128)S(1)} collective-permute-done((f32[4,2,128,256]{3,2,1,0:T(8,128)S(1)}, f32[4,2,128,256]{3,2,1,0:T(8,128)S(1)}, u32[]{:S(2)}, u32[]{:S(2)}) %collective-permute-start.22) | collective-permute-done | bytes 1048608 | tf_op jit(solution)/shard_map/ppermute | solution.py:316
  147.7 1.5 collective-permute-start.23
  149.3 0.5 collective-permute-start.21
  149.8 2.0 %place.2._ = f32[128,2,32,256]{3,2,1,0:T(8,128)} custom-call(s32[2]{0:T(128)S(1)} %copy-done.10, f32[4,2,128,256]{3,2,1,0:T(8,128)S(1)} %collective-permute-done.20.got_a, f32[4,2,128,256]{3,2,1,0:T(8,128)S(1)} %collective-permute-done.22.got_b, f32[128,2,32,256]{3,2,1,0:T(8,128)} %get-tuple-element.86._), custom_call_target="tpu_custom_call", output_to_operand_aliasing={{}: (3, {})} | custom-call | bytes 740000 | tf_op jit(solution)/shard_map/place/pallas_call | solution.py:230
  151.8 19.5 %collective-permute-done.23.got_b = f32[4,2,128,256]{3,2,1,0:T(8,128)S(1)} collective-permute-done((f32[4,2,128,256]{3,2,1,0:T(8,128)S(1)}, f32[4,2,128,256]{3,2,1,0:T(8,128)S(1)}, u32[]{:S(2)}, u32[]{:S(2)}) %collective-permute-start.23) | collective-permute-done | bytes 1048608 | tf_op jit(solution)/shard_map/ppermute | solution.py:316
  171.2 1.2 collective-permute-done.21.got_a
  172.5 2.0 %place.3 = f32[128,2,32,256]{3,2,1,0:T(8,128)} custom-call(s32[2]{0:T(128)S(1)} %copy-done.10, f32[4,2,128,256]{3,2,1,0:T(8,128)S(1)} %collective-permute-done.21.got_a, f32[4,2,128,256]{3,2,1,0:T(8,128)S(1)} %collective-permute-done.23.got_b, f32[128,2,32,256]{3,2,1,0:T(8,128)} %place.2._), custom_call_target="tpu_custom_call", output_to_operand_aliasing={{}: (3, {})} | custom-call | bytes 740000 | tf_op jit(solution)/shard_map/place/pallas_call | solution.py:230
  (22 shorter events, 0.0 us)
Async XLA Ops:
  1.9 99.6 %copy-start.10 = (s32[2]{0:T(128)S(1)}, s32[2]{0:T(128)}, u32[]{:S(2)}) copy-start(s32[2]{0:T(128)} %pad_add_fusion.sides_ref.refs_0_) | copy-start | bytes 28
  7.0 82.3 %copy-start.1 = (f32[6,2,64,256]{3,2,1,0:T(8,128)S(1)}, f32[6,2,64,256]{3,2,1,0:T(8,128)}, u32[]{:S(2)}) copy-start(f32[6,2,64,256]{3,2,1,0:T(8,128)} %get-tuple-element.55.refs_4_.refs_2_.refs_11_.refs_15_) | copy-start | bytes 2359300
  7.0 19.6 %collective-permute-start.1 = (f32[6,2,64,256]{3,2,1,0:T(8,128)}, f32[6,2,64,256]{3,2,1,0:T(8,128)S(1)}, u32[]{:S(2)}, u32[]{:S(2)}) collective-permute-start(f32[6,2,64,256]{3,2,1,0:T(8,128)} %get-tuple-element.50), channel_id=1, source_target_pairs={{0,16},{8,24},{16,0},{24,8},{1,17},{9,25},{17,1},{25,9},{2,18},{10... | collective-permute-start | bytes 2359304 | tf_op jit(solution)/shard_map/ppermute | solution.py:316
  8.6 19.5 %collective-permute-start = (f32[5,2,64,256]{3,2,1,0:T(8,128)}, f32[5,2,64,256]{3,2,1,0:T(8,128)S(1)}, u32[]{:S(2)}, u32[]{:S(2)}) collective-permute-start(f32[5,2,64,256]{3,2,1,0:T(8,128)} %get-tuple-element.49), channel_id=1, source_target_pairs={{0,8},{8,0},{16,24},{24,16},{1,9},{9,1},{17,25},{25,17},{2,10},{10... | collective-permute-start | bytes 1966088 | tf_op jit(solution)/shard_map/ppermute | solution.py:316
  26.5 15.8 %collective-permute-start.5 = (f32[5,2,64,256]{3,2,1,0:T(8,128)}, f32[5,2,64,256]{3,2,1,0:T(8,128)S(1)}, u32[]{:S(2)}, u32[]{:S(2)}) collective-permute-start(f32[5,2,64,256]{3,2,1,0:T(8,128)} %get-tuple-element.60.refs_0_.refs_7_), channel_id=1, source_target_pairs={{0,16},{8,24},{16,0},{24,8},{1,17},{9,25},{17,1},{25,9},{2,18},{10... | collective-permute-start | bytes 1966088 | tf_op jit(solution)/shard_map/ppermute | solution.py:316
  28.1 25.2 %collective-permute-start.2 = (f32[6,2,64,256]{3,2,1,0:T(8,128)}, f32[6,2,64,256]{3,2,1,0:T(8,128)S(1)}, u32[]{:S(2)}, u32[]{:S(2)}) collective-permute-start(f32[6,2,64,256]{3,2,1,0:T(8,128)} %get-tuple-element.55.refs_4_.refs_2_.refs_11_.refs_15_), channel_id=1, source_target_pairs={{0,8},{8,0},{16,24},{24,16},{1,9},{9,1},{17,25},{25,17},{2,10},{10... | collective-permute-start | bytes 2359304 | tf_op jit(solution)/shard_map/ppermute | solution.py:316
  29.5 1.0 copy-start.8
  30.6 1.0 copy-start.9
  31.6 0.7 copy-start.11
  42.3 16.8 %collective-permute-start.6 = (f32[5,2,64,256]{3,2,1,0:T(8,128)S(1)}, f32[5,2,64,256]{3,2,1,0:T(8,128)S(1)}, u32[]{:S(2)}, u32[]{:S(2)}) collective-permute-start(f32[5,2,64,256]{3,2,1,0:T(8,128)S(1)} %collective-permute-done.refs_1_.refs_8_), channel_id=1, source_target_pairs={{0,16},{8,24},{16,0},{24,8},{1,17},{9,25},{17,1},{25,9},{2,18},{10... | collective-permute-start | bytes 1966088 | tf_op jit(solution)/shard_map/ppermute | solution.py:316
  43.9 1.1 copy-start
  45.0 1.1 copy-start.2
  46.1 43.2 %copy-start.3 = (f32[5,2,64,256]{3,2,1,0:T(8,128)S(1)}, f32[5,2,64,256]{3,2,1,0:T(8,128)}, u32[]{:S(2)}) copy-start(f32[5,2,64,256]{3,2,1,0:T(8,128)} %get-tuple-element.60.refs_0_.refs_7_) | copy-start | bytes 1966084
  47.6 26.6 %collective-permute-start.16 = (f32[2,4,2,64,256]{4,3,2,1,0:T(8,128)}, f32[2,4,2,64,256]{4,3,2,1,0:T(8,128)}, u32[]{:S(2)}, u32[]{:S(2)}) collective-permute-start(f32[2,4,2,64,256]{4,3,2,1,0:T(8,128)} %get-tuple-element.72), channel_id=1, source_target_pairs={{0,1},{1,2},{2,3},{3,4},{4,5},{5,6},{6,7},{8,9},{9,10},{10,11},{11... | collective-permute-start | bytes 3145736 | tf_op jit(solution)/shard_map/ppermute | solution.py:364
  49.6 24.6 %collective-permute-start.17 = (f32[2,4,2,64,256]{4,3,2,1,0:T(8,128)}, f32[2,4,2,64,256]{4,3,2,1,0:T(8,128)}, u32[]{:S(2)}, u32[]{:S(2)}) collective-permute-start(f32[2,4,2,64,256]{4,3,2,1,0:T(8,128)} %get-tuple-element.73), channel_id=1, source_target_pairs={{1,0},{2,1},{3,2},{4,3},{5,4},{6,5},{7,6},{9,8},{10,9},{11,10},{12... | collective-permute-start | bytes 3145736 | tf_op jit(solution)/shard_map/ppermute | solution.py:364
  53.2 19.5 %collective-permute-start.3 = (f32[6,2,64,256]{3,2,1,0:T(8,128)S(1)}, f32[6,2,64,256]{3,2,1,0:T(8,128)S(1)}, u32[]{:S(2)}, u32[]{:S(2)}) collective-permute-start(f32[6,2,64,256]{3,2,1,0:T(8,128)S(1)} %collective-permute-done.1.refs_5_.refs_3_.refs_13_.refs_17_), channel_id=1, source_target_pairs={{0,8},{8,0},{16,24},{24,16},{1,9},{9,1},{17,25},{25,17},{2,10},{10... | collective-permute-start | bytes 2359304 | tf_op jit(solution)/shard_map/ppermute | solution.py:316
  59.2 15.0 %collective-permute-start.7 = (f32[4,2,64,256]{3,2,1,0:T(8,128)}, f32[4,2,64,256]{3,2,1,0:T(8,128)S(1)}, u32[]{:S(2)}, u32[]{:S(2)}) collective-permute-start(f32[4,2,64,256]{3,2,1,0:T(8,128)} %get-tuple-element.62), channel_id=1, source_target_pairs={{0,16},{8,24},{16,0},{24,8},{1,17},{9,25},{17,1},{25,9},{2,18},{10... | collective-permute-start | bytes 1572872 | tf_op jit(solution)/shard_map/ppermute | solution.py:316
  72.7 13.1 %collective-permute-start.4 = (f32[4,2,64,256]{3,2,1,0:T(8,128)}, f32[4,2,64,256]{3,2,1,0:T(8,128)S(1)}, u32[]{:S(2)}, u32[]{:S(2)}) collective-permute-start(f32[4,2,64,256]{3,2,1,0:T(8,128)} %get-tuple-element.57), channel_id=1, source_target_pairs={{0,8},{8,0},{16,24},{24,16},{1,9},{9,1},{17,25},{25,17},{2,10},{10... | collective-permute-start | bytes 1572872 | tf_op jit(solution)/shard_map/ppermute | solution.py:316
  74.2 22.7 %collective-permute-start.10 = (f32[4,2,64,256]{3,2,1,0:T(8,128)}, f32[4,2,64,256]{3,2,1,0:T(8,128)S(1)}, u32[]{:S(2)}, u32[]{:S(2)}) collective-permute-start(f32[4,2,64,256]{3,2,1,0:T(8,128)} %get-tuple-element.65.refs_2_.refs_11_), channel_id=1, source_target_pairs={{0,16},{8,24},{16,0},{24,8},{1,17},{9,25},{17,1},{25,9},{2,18},{10... | collective-permute-start | bytes 1572872 | tf_op jit(solution)/shard_map/ppermute | solution.py:316
  77.8 23.1 %collective-permute-start.18 = (f32[2,4,2,64,256]{4,3,2,1,0:T(8,128)S(1)}, f32[2,4,2,64,256]{4,3,2,1,0:T(8,128)S(1)}, u32[]{:S(2)}, u32[]{:S(2)}) collective-permute-start(f32[2,4,2,64,256]{4,3,2,1,0:T(8,128)S(1)} %get-tuple-element.75), channel_id=1, source_target_pairs={{0,1},{1,2},{2,3},{3,4},{4,5},{5,6},{6,7},{8,9},{9,10},{10,11},{11... | collective-permute-start | bytes 3145736 | tf_op jit(solution)/shard_map/ppermute | solution.py:364
  85.8 14.5 %collective-permute-start.12 = (f32[4,2,64,256]{3,2,1,0:T(8,128)}, f32[4,2,64,256]{3,2,1,0:T(8,128)S(1)}, u32[]{:S(2)}, u32[]{:S(2)}) collective-permute-start(f32[4,2,64,256]{3,2,1,0:T(8,128)} %get-tuple-element.68.refs_6_.refs_19_), channel_id=1, source_target_pairs={{0,8},{8,0},{16,24},{24,16},{1,9},{9,1},{17,25},{25,17},{2,10},{10... | collective-permute-start | bytes 1572872 | tf_op jit(solution)/shard_map/ppermute | solution.py:316
  87.3 14.2 %collective-permute-start.19 = (f32[2,4,2,64,256]{4,3,2,1,0:T(8,128)S(1)}, f32[2,4,2,64,256]{4,3,2,1,0:T(8,128)S(1)}, u32[]{:S(2)}, u32[]{:S(2)}) collective-permute-start(f32[2,4,2,64,256]{4,3,2,1,0:T(8,128)S(1)} %get-tuple-element.76), channel_id=1, source_target_pairs={{1,0},{2,1},{3,2},{4,3},{5,4},{6,5},{7,6},{9,8},{10,9},{11,10},{12... | collective-permute-start | bytes 3145736 | tf_op jit(solution)/shard_map/ppermute | solution.py:364
  89.3 1.0 copy-start.4
  90.3 1.0 copy-start.6
  94.4 40.9 %copy-start.5 = (f32[4,2,64,256]{3,2,1,0:T(8,128)S(1)}, f32[4,2,64,256]{3,2,1,0:T(8,128)}, u32[]{:S(2)}) copy-start(f32[4,2,64,256]{3,2,1,0:T(8,128)} %get-tuple-element.65.refs_2_.refs_11_) | copy-start | bytes 1572868
  94.4 40.9 %copy-start.7 = (f32[4,2,64,256]{3,2,1,0:T(8,128)S(1)}, f32[4,2,64,256]{3,2,1,0:T(8,128)}, u32[]{:S(2)}) copy-start(f32[4,2,64,256]{3,2,1,0:T(8,128)} %get-tuple-element.68.refs_6_.refs_19_) | copy-start | bytes 1572868
  94.4 19.8 %collective-permute-start.8 = (f32[2,4,2,64,256]{4,3,2,1,0:T(8,128)S(1)}, f32[2,4,2,64,256]{4,3,2,1,0:T(8,128)S(1)}, u32[]{:S(2)}, u32[]{:S(2)}) collective-permute-start(f32[2,4,2,64,256]{4,3,2,1,0:T(8,128)S(1)} %get-tuple-element.63), channel_id=1, source_target_pairs={{0,1},{1,2},{2,3},{3,4},{4,5},{5,6},{6,7},{8,9},{9,10},{10,11},{11... | collective-permute-start | bytes 3145736 | tf_op jit(solution)/shard_map/ppermute | solution.py:364
  97.0 17.2 %collective-permute-start.9 = (f32[2,4,2,64,256]{4,3,2,1,0:T(8,128)S(1)}, f32[2,4,2,64,256]{4,3,2,1,0:T(8,128)S(1)}, u32[]{:S(2)}, u32[]{:S(2)}) collective-permute-start(f32[2,4,2,64,256]{4,3,2,1,0:T(8,128)S(1)} %get-tuple-element.64), channel_id=1, source_target_pairs={{1,0},{2,1},{3,2},{4,3},{5,4},{6,5},{7,6},{9,8},{10,9},{11,10},{12... | collective-permute-start | bytes 3145736 | tf_op jit(solution)/shard_map/ppermute | solution.py:364
  100.3 13.9 %collective-permute-start.11 = (f32[4,2,64,256]{3,2,1,0:T(8,128)S(1)}, f32[4,2,64,256]{3,2,1,0:T(8,128)S(1)}, u32[]{:S(2)}, u32[]{:S(2)}) collective-permute-start(f32[4,2,64,256]{3,2,1,0:T(8,128)S(1)} %collective-permute-done.4.refs_3_.refs_12_), channel_id=1, source_target_pairs={{0,16},{8,24},{16,0},{24,8},{1,17},{9,25},{17,1},{25,9},{2,18},{10... | collective-permute-start | bytes 1572872 | tf_op jit(solution)/shard_map/ppermute | solution.py:316
  100.9 13.5 %collective-permute-start.13 = (f32[4,2,64,256]{3,2,1,0:T(8,128)S(1)}, f32[4,2,64,256]{3,2,1,0:T(8,128)S(1)}, u32[]{:S(2)}, u32[]{:S(2)}) collective-permute-start(f32[4,2,64,256]{3,2,1,0:T(8,128)S(1)} %collective-permute-done.7.refs_7_.refs_21_), channel_id=1, source_target_pairs={{0,8},{8,0},{16,24},{24,16},{1,9},{9,1},{17,25},{25,17},{2,10},{10... | collective-permute-start | bytes 1572872 | tf_op jit(solution)/shard_map/ppermute | solution.py:316
  117.4 16.1 %collective-permute-start.14 = (f32[2,4,2,64,256]{4,3,2,1,0:T(8,128)S(1)}, f32[2,4,2,64,256]{4,3,2,1,0:T(8,128)S(1)}, u32[]{:S(2)}, u32[]{:S(2)}) collective-permute-start(f32[2,4,2,64,256]{4,3,2,1,0:T(8,128)S(1)} %get-tuple-element.70), channel_id=1, source_target_pairs={{0,1},{1,2},{2,3},{3,4},{4,5},{5,6},{6,7},{8,9},{9,10},{10,11},{11... | collective-permute-start | bytes 3145736 | tf_op jit(solution)/shard_map/ppermute | solution.py:364
  119.6 15.7 %collective-permute-start.15 = (f32[2,4,2,64,256]{4,3,2,1,0:T(8,128)S(1)}, f32[2,4,2,64,256]{4,3,2,1,0:T(8,128)S(1)}, u32[]{:S(2)}, u32[]{:S(2)}) collective-permute-start(f32[2,4,2,64,256]{4,3,2,1,0:T(8,128)S(1)} %get-tuple-element.71), channel_id=1, source_target_pairs={{1,0},{2,1},{3,2},{4,3},{5,4},{6,5},{7,6},{9,8},{10,9},{11,10},{12... | collective-permute-start | bytes 3145736 | tf_op jit(solution)/shard_map/ppermute | solution.py:364
  123.2 24.5 %collective-permute-start.22 = (f32[4,2,128,256]{3,2,1,0:T(8,128)S(1)}, f32[4,2,128,256]{3,2,1,0:T(8,128)S(1)}, u32[]{:S(2)}, u32[]{:S(2)}) collective-permute-start(f32[4,2,128,256]{3,2,1,0:T(8,128)S(1)} %get-tuple-element.84), channel_id=1, source_target_pairs={{0,16},{8,24},{16,0},{24,8},{1,17},{9,25},{17,1},{25,9},{2,18},{10... | collective-permute-start | bytes 3145736 | tf_op jit(solution)/shard_map/ppermute | solution.py:316
  124.8 24.4 %collective-permute-start.20 = (f32[4,2,128,256]{3,2,1,0:T(8,128)S(1)}, f32[4,2,128,256]{3,2,1,0:T(8,128)S(1)}, u32[]{:S(2)}, u32[]{:S(2)}) collective-permute-start(f32[4,2,128,256]{3,2,1,0:T(8,128)S(1)} %get-tuple-element.80), channel_id=1, source_target_pairs={{0,8},{8,0},{16,24},{24,16},{1,9},{9,1},{17,25},{25,17},{2,10},{10... | collective-permute-start | bytes 3145736 | tf_op jit(solution)/shard_map/ppermute | solution.py:316
  147.7 23.5 %collective-permute-start.23 = (f32[4,2,128,256]{3,2,1,0:T(8,128)S(1)}, f32[4,2,128,256]{3,2,1,0:T(8,128)S(1)}, u32[]{:S(2)}, u32[]{:S(2)}) collective-permute-start(f32[4,2,128,256]{3,2,1,0:T(8,128)S(1)} %get-tuple-element.85), channel_id=1, source_target_pairs={{0,16},{8,24},{16,0},{24,8},{1,17},{9,25},{17,1},{25,9},{2,18},{10... | collective-permute-start | bytes 3145736 | tf_op jit(solution)/shard_map/ppermute | solution.py:316
  149.3 23.2 %collective-permute-start.21 = (f32[4,2,128,256]{3,2,1,0:T(8,128)S(1)}, f32[4,2,128,256]{3,2,1,0:T(8,128)S(1)}, u32[]{:S(2)}, u32[]{:S(2)}) collective-permute-start(f32[4,2,128,256]{3,2,1,0:T(8,128)S(1)} %get-tuple-element.81), channel_id=1, source_target_pairs={{0,8},{8,0},{16,24},{24,16},{1,9},{9,1},{17,25},{25,17},{2,10},{10... | collective-permute-start | bytes 3145736 | tf_op jit(solution)/shard_map/ppermute | solution.py:316

commit v6 on v5

--- a/solution.py
+++ b/solution.py
@@ -350,7 +350,7 @@
                     free = bit != bits[stream] and not mask & bit
                     if free and mask in now and (mask | bit) not in now:
                         others = maps if mask and chunk == 0 else []
-                        now[mask | bit] = swap_in_turn(now[mask], bit, *others)
+                        now[mask | bit] = swap_in_turn(now[mask], bit, *others, flight=2 if chunk == 0 else 1)
         for stream in range(2):
             held[stream][chunk] = [have[stream][mask] for mask in masks]
 
@@ -363,6 +363,7 @@
         up, down = edges(chunk, depth, arrays)
         return lax.ppermute(up, "space", upward), lax.ppermute(down, "space", downward)
 
+    gots = []
     gives = []
     result = None
     for chunk in range(CHUNKS):
@@ -370,13 +371,13 @@
     shape = (2 * local_steps, planes, rows_x, rows_y)
     for chunk in range(CHUNKS):
         early = beside(chunk, 0)
-        late = beside(chunk, 1, *early)
+        late = beside(chunk, 1, *early, *(gives[-1] if gives else []))
         used = [held[s][max(chunk - 1, 0) : chunk + 1] for s in range(2)]
         result, *give = apply(chunk, depth, order, sides, maps, early, late, used, shape, result)
         gives.append(give)
+        gots.append([swap_in_turn(give[s], bits[s], flight=1 + min(chunk, 1)) for s in range(2)])
     for chunk in range(CHUNKS):
-        got = [swap_in_turn(gives[chunk][s], bits[s]) for s in range(2)]
-        result = place(chunk, depth, sides, got, result)
+        result = place(chunk, depth, sides, gots[chunk], result)
     return result.reshape(2, local_steps, planes, rows_x, rows_y)
 
 

time: 177 us -> 194 us (1.096)
  Pallas kernels: 45.2 us -> 77.1 us
  waiting for transfers between devices: 80.4 us -> 66.1 us
  starting transfers between devices: 39.6 us -> 42.2 us
  local copies, waits for them, and re-layouts: 7.79 us -> 5.56 us
    pallas_call x4, Pallas kernels: 10.6 us -> 41.9 us  [edges(): pl.pallas_call(functools.partial(edge_kernel, chunk, depth, groups), out_...]
    ppermute x16, waiting for transfers between devices: 70.3 us -> 56.1 us  [swap(): return lax.ppermute(data, 'tm', [(i, i ^ bit) for i in range(count)])]
    ppermute x4, starting transfers between devices: 12.5 us -> 15 us  [beside(): lax.ppermute(down, 'space', downward)]
    unnamed x24 -> x16, local copies, waits for them, and re-layouts: 7.08 us -> 4.86 us
  transfers between devices with their start and end apart: 24 -> 24, of which waited for: 12 -> 11; matrix products, arithmetic and copies ran while one was open for 0% -> 0% of each run, Pallas kernels for 20% -> 35%
where the time goes in v6:
time: 194 us; the launch traced here: 193 us
  Pallas kernels  77.1 us (40%)
  waiting for transfers between devices  66.1 us (34%)
  starting transfers between devices  42.2 us (22%)
  local copies, waits for them, and re-layouts  5.56 us (3%)
    ppermute x16, waiting for transfers between devices, swap(): return lax.ppermute(data, 'tm', [(i, i ^ bit) for i in range(count)])  56.1 us
    pallas_call x4, Pallas kernels, edges(): pl.pallas_call(functools.partial(edge_kernel, chunk, depth, groups), out_...  41.9 us
    pallas_call x2, Pallas kernels, apply(): pl.pallas_call(body, out_shape=[jax.ShapeDtypeStruct(shape, jnp.float32),...  19.8 us
    ppermute x16, starting transfers between devices, swap(): return lax.ppermute(data, 'tm', [(i, i ^ bit) for i in range(count)])  19.5 us
    ppermute x4, starting transfers between devices, beside(): lax.ppermute(down, 'space', downward)  15 us
    pallas_call x2, Pallas kernels, pick(): pl.pallas_call(functools.partial(pick_kernel, chunk, depth), out_shape=[j...  9.38 us
    ppermute x4, waiting for transfers between devices, beside(): lax.ppermute(up, 'space', upward)  8.26 us
    ppermute x4, starting transfers between devices, beside(): lax.ppermute(up, 'space', upward)  7.81 us
  transfers between devices with their start and end apart: 24, of which 11 were waited for; matrix products, arithmetic and copies ran while one was open for 0% of the time, Pallas kernels for 35%

profile of v6, /device:TPU:8, one launch (start us, length us, event | category | flops | bytes accessed | tf_op | source)
XLA Modules:
  0.0 192.7 jit_solution(4754726239756906338)
XLA Ops:
  0.0 0.7 convert_multiply_fusion
  0.7 0.6 pad_add_fusion.sides_ref.refs_0_
  1.3 0.7 broadcast_in_dim.2.ratio_ref
  2.0 5.0 %pick.2 = (f32[5,2,64,256]{3,2,1,0:T(8,128)}, f32[5,2,64,256]{3,2,1,0:T(8,128)}, f32[6,2,64,256]{3,2,1,0:T(8,128)}, f32[6,2,64,256]{3,2,1,0:T(8,128)}) custom-call(s32[2]{0:T(128)} %pad_add_fusion.sides_ref.refs_0_, f32[64,256]{1,0:T(8,128)} %broadcast_in_dim.2.ratio_ref, f32[64,2,32,256]{3,2,1,0:T(8,128)} %in_ref.2), custom_call_target="tpu_custom_call" | custom-call | bytes 1850000 | tf_op jit(solution)/shard_map/pick/pallas_call | solution.py:83
  7.0 1.6 collective-permute-start.1
  8.6 1.5 collective-permute-start
  10.1 1.0 copy-done.4
  11.1 1.0 copy-done.5
  12.2 0.7 copy-done.7
  12.8 2.0 %maps.1 = (bf16[256,1536]{1,0:T(8,128)(2,1)S(1)}, bf16[256,1536]{1,0:T(8,128)(2,1)S(1)}) custom-call(s32[1]{0:T(128)} %bitcast.2.me_ref, f32[2,256,256]{2,1,0:T(8,128)S(1)} %copy-done.4, f32[2,256,256]{2,1,0:T(8,128)S(1)} %copy-done.5, f32[2,256]{1,0:T(2,128)S(1)} %copy-done.7), custom_call_target="tpu_custom_call" | custom-call | bytes 740000 | tf_op jit(solution)/shard_map/maps/pallas_call | solution.py:294
  14.9 10.1 %collective-permute-done.refs_1_.refs_8_ = f32[5,2,64,256]{3,2,1,0:T(8,128)S(1)} collective-permute-done((f32[5,2,64,256]{3,2,1,0:T(8,128)}, f32[5,2,64,256]{3,2,1,0:T(8,128)S(1)}, u32[]{:S(2)}, u32[]{:S(2)}) %collective-permute-start) | collective-permute-done | bytes 655392 | tf_op jit(solution)/shard_map/ppermute | solution.py:316
  25.0 1.6 collective-permute-done.1.refs_5_.refs_3_.refs_13_.refs_17_
  26.6 1.5 collective-permute-start.4
  28.1 1.5 collective-permute-start.2
  29.6 33.2 %edges.5 = (f32[2,4,2,64,256]{4,3,2,1,0:T(8,128)}, f32[2,4,2,64,256]{4,3,2,1,0:T(8,128)}) custom-call(f32[5,2,64,256]{3,2,1,0:T(8,128)} %get-tuple-element.46.refs_0_.refs_7_, f32[5,2,64,256]{3,2,1,0:T(8,128)S(1)} %collective-permute-done.refs_1_.refs_8_, f32[6,2,64,256]{3,2,1,0:T(8,128)} %get-tuple-element.54.refs_4_.refs_2_.refs_11_.refs_15_, ...), custom_call_target="tpu_custom_call" | custom-call | bytes 1110000 | tf_op jit(solution)/shard_map/edges/pallas_call | solution.py:121
  62.7 1.9 collective-permute-start.10
  64.7 3.6 %collective-permute-start.11 = (f32[2,4,2,64,256]{4,3,2,1,0:T(8,128)}, f32[2,4,2,64,256]{4,3,2,1,0:T(8,128)S(1)}, u32[]{:S(2)}, u32[]{:S(2)}) collective-permute-start(f32[2,4,2,64,256]{4,3,2,1,0:T(8,128)} %get-tuple-element.63), channel_id=1, source_target_pairs={{1,0},{2,1},{3,2},{4,3},{5,4},{6,5},{7,6},{9,8},{10,9},{11,10},{12... | collective-permute-start | bytes 3145736 | tf_op jit(solution)/shard_map/ppermute | solution.py:364
  68.3 0.6 collective-permute-start.12
  68.9 0.0 collective-permute-done.4.refs_1_.refs_10_
  68.9 0.5 collective-permute-start.8
  69.4 4.4 %pick.3 = (f32[4,2,64,256]{3,2,1,0:T(8,128)}, f32[4,2,64,256]{3,2,1,0:T(8,128)}, f32[4,2,64,256]{3,2,1,0:T(8,128)}, f32[4,2,64,256]{3,2,1,0:T(8,128)}) custom-call(s32[2]{0:T(128)} %pad_add_fusion.sides_ref.refs_0_, f32[64,256]{1,0:T(8,128)} %broadcast_in_dim.2.ratio_ref, f32[64,2,32,256]{3,2,1,0:T(8,128)} %in_ref.2), custom_call_target="tpu_custom_call" | custom-call | bytes 1850000 | tf_op jit(solution)/shard_map/pick/pallas_call | solution.py:83
  73.8 0.0 collective-permute-done.2.refs_3_.refs_14_.refs_5_.refs_18_
  73.8 1.6 collective-permute-start.5
  75.4 11.4 %collective-permute-done.8.refs_0_.refs_9_ = f32[5,2,64,256]{3,2,1,0:T(8,128)S(1)} collective-permute-done((f32[5,2,64,256]{3,2,1,0:T(8,128)}, f32[5,2,64,256]{3,2,1,0:T(8,128)S(1)}, u32[]{:S(2)}, u32[]{:S(2)}) %collective-permute-start.8) | collective-permute-done | bytes 655392 | tf_op jit(solution)/shard_map/ppermute | solution.py:316
  86.8 1.5 collective-permute-start.3
  88.3 0.0 collective-permute-done.10.refs_3_
  88.3 0.0 collective-permute-done.11.refs_4_
  88.3 8.4 %collective-permute-done.5.refs_7_.refs_21_ = f32[4,2,64,256]{3,2,1,0:T(8,128)S(1)} collective-permute-done((f32[4,2,64,256]{3,2,1,0:T(8,128)}, f32[4,2,64,256]{3,2,1,0:T(8,128)S(1)}, u32[]{:S(2)}, u32[]{:S(2)}) %collective-permute-start.5) | collective-permute-done | bytes 524320 | tf_op jit(solution)/shard_map/ppermute | solution.py:316
  96.7 0.5 collective-permute-start.9
  97.2 0.0 collective-permute-done.12.refs_2_.refs_12_.refs_4_.refs_16_
  97.2 3.0 %edges.6 = (f32[2,4,2,64,256]{4,3,2,1,0:T(8,128)S(1)}, f32[2,4,2,64,256]{4,3,2,1,0:T(8,128)S(1)}) custom-call(f32[5,2,64,256]{3,2,1,0:T(8,128)S(1)} %collective-permute-done.8.refs_0_.refs_9_, f32[5,2,64,256]{3,2,1,0:T(8,128)S(1)} %collective-permute-done.4.refs_1_.refs_10_, f32[6,2,64,256]{3,2,1,0:T(8,128)S(1)} %collective-permute-done.12.refs_2_.refs_12_.refs_4_.refs_16_, ...), custom_call_target="tpu_custom_call" | custom-call | bytes 1110000 | tf_op jit(solution)/shard_map/edges/pallas_call | solution.py:121
  100.2 1.9 collective-permute-start.13
  102.1 3.6 %collective-permute-start.14 = (f32[2,4,2,64,256]{4,3,2,1,0:T(8,128)S(1)}, f32[2,4,2,64,256]{4,3,2,1,0:T(8,128)S(1)}, u32[]{:S(2)}, u32[]{:S(2)}) collective-permute-start(f32[2,4,2,64,256]{4,3,2,1,0:T(8,128)S(1)} %get-tuple-element.66), channel_id=1, source_target_pairs={{1,0},{2,1},{3,2},{4,3},{5,4},{6,5},{7,6},{9,8},{10,9},{11,10},{12... | collective-permute-start | bytes 3145736 | tf_op jit(solution)/shard_map/ppermute | solution.py:364
  105.8 0.0 collective-permute-done.3.refs_3_.refs_12_
  105.8 1.6 collective-permute-start.16
  107.4 1.0 copy-done
  108.4 1.0 copy-done.2
  109.4 2.7 %edges.4 = (f32[2,4,2,64,256]{4,3,2,1,0:T(8,128)S(1)}, f32[2,4,2,64,256]{4,3,2,1,0:T(8,128)S(1)}) custom-call(f32[5,2,64,256]{3,2,1,0:T(8,128)} %get-tuple-element.46.refs_0_.refs_7_, f32[5,2,64,256]{3,2,1,0:T(8,128)S(1)} %collective-permute-done.refs_1_.refs_8_, f32[4,2,64,256]{3,2,1,0:T(8,128)S(1)} %copy-done, ...), custom_call_target="tpu_custom_call" | custom-call | bytes 1110000 | tf_op jit(solution)/shard_map/edges/pallas_call | solution.py:121
  112.2 2.1 %collective-permute-start.6 = (f32[2,4,2,64,256]{4,3,2,1,0:T(8,128)S(1)}, f32[2,4,2,64,256]{4,3,2,1,0:T(8,128)S(1)}, u32[]{:S(2)}, u32[]{:S(2)}) collective-permute-start(f32[2,4,2,64,256]{4,3,2,1,0:T(8,128)S(1)} %get-tuple-element.59), channel_id=1, source_target_pairs={{0,1},{1,2},{2,3},{3,4},{4,5},{5,6},{6,7},{8,9},{9,10},{10,11},{11... | collective-permute-start | bytes 3145736 | tf_op jit(solution)/shard_map/ppermute | solution.py:364
  114.2 0.0 collective-permute-done.9.refs_2_.refs_13_
  114.2 3.8 %collective-permute-start.7 = (f32[2,4,2,64,256]{4,3,2,1,0:T(8,128)S(1)}, f32[2,4,2,64,256]{4,3,2,1,0:T(8,128)S(1)}, u32[]{:S(2)}, u32[]{:S(2)}) collective-permute-start(f32[2,4,2,64,256]{4,3,2,1,0:T(8,128)S(1)} %get-tuple-element.60), channel_id=1, source_target_pairs={{1,0},{2,1},{3,2},{4,3},{5,4},{6,5},{7,6},{9,8},{10,9},{11,10},{12... | collective-permute-start | bytes 3145736 | tf_op jit(solution)/shard_map/ppermute | solution.py:364
  118.1 1.8 collective-permute-done.16.refs_6_.refs_20_
  119.9 1.5 collective-permute-start.15
  121.4 0.0 collective-permute-done.13.refs_5_
  121.4 1.5 collective-permute-start.17
  122.9 0.0 collective-permute-done.14.refs_6_
  122.9 9.8 %apply.2 = (f32[128,2,32,256]{3,2,1,0:T(8,128)}, f32[4,2,128,256]{3,2,1,0:T(8,128)S(1)}, f32[4,2,128,256]{3,2,1,0:T(8,128)S(1)}) custom-call(s32[2]{0:T(128)S(1)} %copy-done.6, bf16[256,1536]{1,0:T(8,128)(2,1)S(1)} %get-tuple-element.44.refs_1_, bf16[256,1536]{1,0:T(8,128)(2,1)S(1)} %get-tuple-element.45.refs_2_, ...), custom_call_target="tpu_custom_call" | custom-call | bytes 3700000 | tf_op jit(solution)/shard_map/apply/pallas_call | solution.py:201
  132.7 0.0 collective-permute-done.6.refs_3_
  132.7 0.1 collective-permute-done.15.refs_3_.refs_14_
  132.8 1.2 collective-permute-done.17.refs_7_.refs_22_
  134.0 3.0 %edges.7 = (f32[2,4,2,64,256]{4,3,2,1,0:T(8,128)S(1)}, f32[2,4,2,64,256]{4,3,2,1,0:T(8,128)S(1)}) custom-call(f32[5,2,64,256]{3,2,1,0:T(8,128)S(1)} %collective-permute-done.8.refs_0_.refs_9_, f32[5,2,64,256]{3,2,1,0:T(8,128)S(1)} %collective-permute-done.4.refs_1_.refs_10_, f32[4,2,64,256]{3,2,1,0:T(8,128)S(1)} %collective-permute-done.9.refs_2_.refs_13_, ...), custom_call_target="tpu_custom_call" | custom-call | bytes 1110000 | tf_op jit(solution)/shard_map/edges/pallas_call | solution.py:121
  137.1 1.9 collective-permute-start.18
  139.0 3.9 %collective-permute-start.19 = (f32[2,4,2,64,256]{4,3,2,1,0:T(8,128)S(1)}, f32[2,4,2,64,256]{4,3,2,1,0:T(8,128)S(1)}, u32[]{:S(2)}, u32[]{:S(2)}) collective-permute-start(f32[2,4,2,64,256]{4,3,2,1,0:T(8,128)S(1)} %get-tuple-element.74), channel_id=1, source_target_pairs={{1,0},{2,1},{3,2},{4,3},{5,4},{6,5},{7,6},{9,8},{10,9},{11,10},{12... | collective-permute-start | bytes 3145736 | tf_op jit(solution)/shard_map/ppermute | solution.py:364
  142.9 0.6 collective-permute-start.23
  143.4 1.5 collective-permute-start.22
  144.9 8.3 %collective-permute-done.18.refs_5_ = f32[2,4,2,64,256]{4,3,2,1,0:T(8,128)S(1)} collective-permute-done((f32[2,4,2,64,256]{4,3,2,1,0:T(8,128)S(1)}, f32[2,4,2,64,256]{4,3,2,1,0:T(8,128)S(1)}, u32[]{:S(2)}, u32[]{:S(2)}) %collective-permute-start.18) | collective-permute-done | bytes 1048608 | tf_op jit(solution)/shard_map/ppermute | solution.py:364
  153.2 1.8 collective-permute-done.19.refs_6_
  154.9 10.0 %apply.3 = (f32[128,2,32,256]{3,2,1,0:T(8,128)}, f32[4,2,128,256]{3,2,1,0:T(8,128)S(1)}, f32[4,2,128,256]{3,2,1,0:T(8,128)S(1)}) custom-call(s32[2]{0:T(128)S(1)} %copy-done.6, bf16[256,1536]{1,0:T(8,128)(2,1)S(1)} %get-tuple-element.44.refs_1_, bf16[256,1536]{1,0:T(8,128)(2,1)S(1)} %get-tuple-element.45.refs_2_, ...), custom_call_target="tpu_custom_call", output_to_operand_aliasing={{0}: (23, {})} | custom-call | bytes 3700000 | tf_op jit(solution)/shard_map/apply/pallas_call | solution.py:201
  165.0 0.6 collective-permute-start.21
  165.6 1.5 collective-permute-start.20
  167.1 2.0 %place.2._ = f32[128,2,32,256]{3,2,1,0:T(8,128)} custom-call(s32[2]{0:T(128)S(1)} %copy-done.6, f32[4,2,128,256]{3,2,1,0:T(8,128)S(1)} %collective-permute-done.22.got_a, f32[4,2,128,256]{3,2,1,0:T(8,128)S(1)} %collective-permute-done.23.got_b, f32[128,2,32,256]{3,2,1,0:T(8,128)} %get-tuple-element.82._), custom_call_target="tpu_custom_call", output_to_operand_aliasing={{}: (3, {})} | custom-call | bytes 740000 | tf_op jit(solution)/shard_map/place/pallas_call | solution.py:230
  169.1 21.2 %collective-permute-done.21.got_b = f32[4,2,128,256]{3,2,1,0:T(8,128)S(1)} collective-permute-done((f32[4,2,128,256]{3,2,1,0:T(8,128)S(1)}, f32[4,2,128,256]{3,2,1,0:T(8,128)S(1)}, u32[]{:S(2)}, u32[]{:S(2)}) %collective-permute-start.21) | collective-permute-done | bytes 1048608 | tf_op jit(solution)/shard_map/ppermute | solution.py:316
  190.3 0.2 collective-permute-done.20.got_a
  190.5 2.0 %place.3 = f32[128,2,32,256]{3,2,1,0:T(8,128)} custom-call(s32[2]{0:T(128)S(1)} %copy-done.6, f32[4,2,128,256]{3,2,1,0:T(8,128)S(1)} %collective-permute-done.20.got_a, f32[4,2,128,256]{3,2,1,0:T(8,128)S(1)} %collective-permute-done.21.got_b, f32[128,2,32,256]{3,2,1,0:T(8,128)} %place.2._), custom_call_target="tpu_custom_call", output_to_operand_aliasing={{}: (3, {})} | custom-call | bytes 740000 | tf_op jit(solution)/shard_map/place/pallas_call | solution.py:230
  (14 shorter events, 0.0 us)
Async XLA Ops:
  7.0 115.9 %copy-start.6 = (s32[2]{0:T(128)S(1)}, s32[2]{0:T(128)}, u32[]{:S(2)}) copy-start(s32[2]{0:T(128)} %pad_add_fusion.sides_ref.refs_0_) | copy-start | bytes 28
  7.0 19.6 %collective-permute-start.1 = (f32[6,2,64,256]{3,2,1,0:T(8,128)}, f32[6,2,64,256]{3,2,1,0:T(8,128)S(1)}, u32[]{:S(2)}, u32[]{:S(2)}) collective-permute-start(f32[6,2,64,256]{3,2,1,0:T(8,128)} %get-tuple-element.48), channel_id=1, source_target_pairs={{0,16},{8,24},{16,0},{24,8},{1,17},{9,25},{17,1},{25,9},{2,18},{10... | collective-permute-start | bytes 2359304 | tf_op jit(solution)/shard_map/ppermute | solution.py:316
  8.6 16.4 %collective-permute-start = (f32[5,2,64,256]{3,2,1,0:T(8,128)}, f32[5,2,64,256]{3,2,1,0:T(8,128)S(1)}, u32[]{:S(2)}, u32[]{:S(2)}) collective-permute-start(f32[5,2,64,256]{3,2,1,0:T(8,128)} %get-tuple-element.47), channel_id=1, source_target_pairs={{0,8},{8,0},{16,24},{24,16},{1,9},{9,1},{17,25},{25,17},{2,10},{10... | collective-permute-start | bytes 1966088 | tf_op jit(solution)/shard_map/ppermute | solution.py:316
  10.1 1.0 copy-start.4
  11.1 1.0 copy-start.5
  12.2 0.7 copy-start.7
  26.6 42.4 %collective-permute-start.4 = (f32[5,2,64,256]{3,2,1,0:T(8,128)S(1)}, f32[5,2,64,256]{3,2,1,0:T(8,128)S(1)}, u32[]{:S(2)}, u32[]{:S(2)}) collective-permute-start(f32[5,2,64,256]{3,2,1,0:T(8,128)S(1)} %collective-permute-done.refs_1_.refs_8_), channel_id=1, source_target_pairs={{0,16},{8,24},{16,0},{24,8},{1,17},{9,25},{17,1},{25,9},{2,18},{10... | collective-permute-start | bytes 1966088 | tf_op jit(solution)/shard_map/ppermute | solution.py:316
  28.1 45.7 %collective-permute-start.2 = (f32[6,2,64,256]{3,2,1,0:T(8,128)S(1)}, f32[6,2,64,256]{3,2,1,0:T(8,128)S(1)}, u32[]{:S(2)}, u32[]{:S(2)}) collective-permute-start(f32[6,2,64,256]{3,2,1,0:T(8,128)S(1)} %collective-permute-done.1.refs_5_.refs_3_.refs_13_.refs_17_), channel_id=1, source_target_pairs={{0,8},{8,0},{16,24},{24,16},{1,9},{9,1},{17,25},{25,17},{2,10},{10... | collective-permute-start | bytes 2359304 | tf_op jit(solution)/shard_map/ppermute | solution.py:316
  62.7 25.5 %collective-permute-start.10 = (f32[2,4,2,64,256]{4,3,2,1,0:T(8,128)}, f32[2,4,2,64,256]{4,3,2,1,0:T(8,128)S(1)}, u32[]{:S(2)}, u32[]{:S(2)}) collective-permute-start(f32[2,4,2,64,256]{4,3,2,1,0:T(8,128)} %get-tuple-element.62), channel_id=1, source_target_pairs={{0,1},{1,2},{2,3},{3,4},{4,5},{5,6},{6,7},{8,9},{9,10},{10,11},{11... | collective-permute-start | bytes 3145736 | tf_op jit(solution)/shard_map/ppermute | solution.py:364
  64.7 23.6 %collective-permute-start.11 = (f32[2,4,2,64,256]{4,3,2,1,0:T(8,128)}, f32[2,4,2,64,256]{4,3,2,1,0:T(8,128)S(1)}, u32[]{:S(2)}, u32[]{:S(2)}) collective-permute-start(f32[2,4,2,64,256]{4,3,2,1,0:T(8,128)} %get-tuple-element.63), channel_id=1, source_target_pairs={{1,0},{2,1},{3,2},{4,3},{5,4},{6,5},{7,6},{9,8},{10,9},{11,10},{12... | collective-permute-start | bytes 3145736 | tf_op jit(solution)/shard_map/ppermute | solution.py:364
  68.3 28.9 %collective-permute-start.12 = (f32[6,2,64,256]{3,2,1,0:T(8,128)}, f32[6,2,64,256]{3,2,1,0:T(8,128)S(1)}, u32[]{:S(2)}, u32[]{:S(2)}) collective-permute-start(f32[6,2,64,256]{3,2,1,0:T(8,128)} %get-tuple-element.54.refs_4_.refs_2_.refs_11_.refs_15_), channel_id=1, source_target_pairs={{0,8},{8,0},{16,24},{24,16},{1,9},{9,1},{17,25},{25,17},{2,10},{10... | collective-permute-start | bytes 2359304 | tf_op jit(solution)/shard_map/ppermute | solution.py:316
  68.9 17.9 %collective-permute-start.8 = (f32[5,2,64,256]{3,2,1,0:T(8,128)}, f32[5,2,64,256]{3,2,1,0:T(8,128)S(1)}, u32[]{:S(2)}, u32[]{:S(2)}) collective-permute-start(f32[5,2,64,256]{3,2,1,0:T(8,128)} %get-tuple-element.46.refs_0_.refs_7_), channel_id=1, source_target_pairs={{0,16},{8,24},{16,0},{24,8},{1,17},{9,25},{17,1},{25,9},{2,18},{10... | collective-permute-start | bytes 1966088 | tf_op jit(solution)/shard_map/ppermute | solution.py:316
  73.8 22.9 %collective-permute-start.5 = (f32[4,2,64,256]{3,2,1,0:T(8,128)}, f32[4,2,64,256]{3,2,1,0:T(8,128)S(1)}, u32[]{:S(2)}, u32[]{:S(2)}) collective-permute-start(f32[4,2,64,256]{3,2,1,0:T(8,128)} %get-tuple-element.58), channel_id=1, source_target_pairs={{0,16},{8,24},{16,0},{24,8},{1,17},{9,25},{17,1},{25,9},{2,18},{10... | collective-permute-start | bytes 1572872 | tf_op jit(solution)/shard_map/ppermute | solution.py:316
  86.8 19.0 %collective-permute-start.3 = (f32[4,2,64,256]{3,2,1,0:T(8,128)}, f32[4,2,64,256]{3,2,1,0:T(8,128)S(1)}, u32[]{:S(2)}, u32[]{:S(2)}) collective-permute-start(f32[4,2,64,256]{3,2,1,0:T(8,128)} %get-tuple-element.53), channel_id=1, source_target_pairs={{0,8},{8,0},{16,24},{24,16},{1,9},{9,1},{17,25},{25,17},{2,10},{10... | collective-permute-start | bytes 1572872 | tf_op jit(solution)/shard_map/ppermute | solution.py:316
  96.7 17.5 %collective-permute-start.9 = (f32[4,2,64,256]{3,2,1,0:T(8,128)}, f32[4,2,64,256]{3,2,1,0:T(8,128)S(1)}, u32[]{:S(2)}, u32[]{:S(2)}) collective-permute-start(f32[4,2,64,256]{3,2,1,0:T(8,128)} %get-tuple-element.61.refs_2_.refs_11_), channel_id=1, source_target_pairs={{0,16},{8,24},{16,0},{24,8},{1,17},{9,25},{17,1},{25,9},{2,18},{10... | collective-permute-start | bytes 1572872 | tf_op jit(solution)/shard_map/ppermute | solution.py:316
  100.2 21.2 %collective-permute-start.13 = (f32[2,4,2,64,256]{4,3,2,1,0:T(8,128)S(1)}, f32[2,4,2,64,256]{4,3,2,1,0:T(8,128)S(1)}, u32[]{:S(2)}, u32[]{:S(2)}) collective-permute-start(f32[2,4,2,64,256]{4,3,2,1,0:T(8,128)S(1)} %get-tuple-element.65), channel_id=1, source_target_pairs={{0,1},{1,2},{2,3},{3,4},{4,5},{5,6},{6,7},{8,9},{9,10},{10,11},{11... | collective-permute-start | bytes 3145736 | tf_op jit(solution)/shard_map/ppermute | solution.py:364
  102.1 20.7 %collective-permute-start.14 = (f32[2,4,2,64,256]{4,3,2,1,0:T(8,128)S(1)}, f32[2,4,2,64,256]{4,3,2,1,0:T(8,128)S(1)}, u32[]{:S(2)}, u32[]{:S(2)}) collective-permute-start(f32[2,4,2,64,256]{4,3,2,1,0:T(8,128)S(1)} %get-tuple-element.66), channel_id=1, source_target_pairs={{1,0},{2,1},{3,2},{4,3},{5,4},{6,5},{7,6},{9,8},{10,9},{11,10},{12... | collective-permute-start | bytes 3145736 | tf_op jit(solution)/shard_map/ppermute | solution.py:364
  105.8 14.1 %collective-permute-start.16 = (f32[4,2,64,256]{3,2,1,0:T(8,128)}, f32[4,2,64,256]{3,2,1,0:T(8,128)S(1)}, u32[]{:S(2)}, u32[]{:S(2)}) collective-permute-start(f32[4,2,64,256]{3,2,1,0:T(8,128)} %get-tuple-element.71.refs_6_.refs_19_), channel_id=1, source_target_pairs={{0,8},{8,0},{16,24},{24,16},{1,9},{9,1},{17,25},{25,17},{2,10},{10... | collective-permute-start | bytes 1572872 | tf_op jit(solution)/shard_map/ppermute | solution.py:316
  107.4 1.0 copy-start
  108.4 1.0 copy-start.2
  112.1 42.8 %copy-start.1 = (f32[4,2,64,256]{3,2,1,0:T(8,128)S(1)}, f32[4,2,64,256]{3,2,1,0:T(8,128)}, u32[]{:S(2)}) copy-start(f32[4,2,64,256]{3,2,1,0:T(8,128)} %get-tuple-element.61.refs_2_.refs_11_) | copy-start | bytes 1572868
  112.1 42.8 %copy-start.3 = (f32[4,2,64,256]{3,2,1,0:T(8,128)S(1)}, f32[4,2,64,256]{3,2,1,0:T(8,128)}, u32[]{:S(2)}) copy-start(f32[4,2,64,256]{3,2,1,0:T(8,128)} %get-tuple-element.71.refs_6_.refs_19_) | copy-start | bytes 1572868
  112.2 20.5 %collective-permute-start.6 = (f32[2,4,2,64,256]{4,3,2,1,0:T(8,128)S(1)}, f32[2,4,2,64,256]{4,3,2,1,0:T(8,128)S(1)}, u32[]{:S(2)}, u32[]{:S(2)}) collective-permute-start(f32[2,4,2,64,256]{4,3,2,1,0:T(8,128)S(1)} %get-tuple-element.59), channel_id=1, source_target_pairs={{0,1},{1,2},{2,3},{3,4},{4,5},{5,6},{6,7},{8,9},{9,10},{10,11},{11... | collective-permute-start | bytes 3145736 | tf_op jit(solution)/shard_map/ppermute | solution.py:364
  114.2 18.5 %collective-permute-start.7 = (f32[2,4,2,64,256]{4,3,2,1,0:T(8,128)S(1)}, f32[2,4,2,64,256]{4,3,2,1,0:T(8,128)S(1)}, u32[]{:S(2)}, u32[]{:S(2)}) collective-permute-start(f32[2,4,2,64,256]{4,3,2,1,0:T(8,128)S(1)} %get-tuple-element.60), channel_id=1, source_target_pairs={{1,0},{2,1},{3,2},{4,3},{5,4},{6,5},{7,6},{9,8},{10,9},{11,10},{12... | collective-permute-start | bytes 3145736 | tf_op jit(solution)/shard_map/ppermute | solution.py:364
  119.9 12.9 %collective-permute-start.15 = (f32[4,2,64,256]{3,2,1,0:T(8,128)S(1)}, f32[4,2,64,256]{3,2,1,0:T(8,128)S(1)}, u32[]{:S(2)}, u32[]{:S(2)}) collective-permute-start(f32[4,2,64,256]{3,2,1,0:T(8,128)S(1)} %collective-permute-done.3.refs_3_.refs_12_), channel_id=1, source_target_pairs={{0,16},{8,24},{16,0},{24,8},{1,17},{9,25},{17,1},{25,9},{2,18},{10... | collective-permute-start | bytes 1572872 | tf_op jit(solution)/shard_map/ppermute | solution.py:316
  121.4 12.6 %collective-permute-start.17 = (f32[4,2,64,256]{3,2,1,0:T(8,128)S(1)}, f32[4,2,64,256]{3,2,1,0:T(8,128)S(1)}, u32[]{:S(2)}, u32[]{:S(2)}) collective-permute-start(f32[4,2,64,256]{3,2,1,0:T(8,128)S(1)} %collective-permute-done.5.refs_7_.refs_21_), channel_id=1, source_target_pairs={{0,8},{8,0},{16,24},{24,16},{1,9},{9,1},{17,25},{25,17},{2,10},{10... | collective-permute-start | bytes 1572872 | tf_op jit(solution)/shard_map/ppermute | solution.py:316
  137.1 16.1 %collective-permute-start.18 = (f32[2,4,2,64,256]{4,3,2,1,0:T(8,128)S(1)}, f32[2,4,2,64,256]{4,3,2,1,0:T(8,128)S(1)}, u32[]{:S(2)}, u32[]{:S(2)}) collective-permute-start(f32[2,4,2,64,256]{4,3,2,1,0:T(8,128)S(1)} %get-tuple-element.73), channel_id=1, source_target_pairs={{0,1},{1,2},{2,3},{3,4},{4,5},{5,6},{6,7},{8,9},{9,10},{10,11},{11... | collective-permute-start | bytes 3145736 | tf_op jit(solution)/shard_map/ppermute | solution.py:364
  139.0 15.9 %collective-permute-start.19 = (f32[2,4,2,64,256]{4,3,2,1,0:T(8,128)S(1)}, f32[2,4,2,64,256]{4,3,2,1,0:T(8,128)S(1)}, u32[]{:S(2)}, u32[]{:S(2)}) collective-permute-start(f32[2,4,2,64,256]{4,3,2,1,0:T(8,128)S(1)} %get-tuple-element.74), channel_id=1, source_target_pairs={{1,0},{2,1},{3,2},{4,3},{5,4},{6,5},{7,6},{9,8},{10,9},{11,10},{12... | collective-permute-start | bytes 3145736 | tf_op jit(solution)/shard_map/ppermute | solution.py:364
  142.9 24.2 %collective-permute-start.23 = (f32[4,2,128,256]{3,2,1,0:T(8,128)S(1)}, f32[4,2,128,256]{3,2,1,0:T(8,128)S(1)}, u32[]{:S(2)}, u32[]{:S(2)}) collective-permute-start(f32[4,2,128,256]{3,2,1,0:T(8,128)S(1)} %get-tuple-element.81), channel_id=1, source_target_pairs={{0,16},{8,24},{16,0},{24,8},{1,17},{9,25},{17,1},{25,9},{2,18},{10... | collective-permute-start | bytes 3145736 | tf_op jit(solution)/shard_map/ppermute | solution.py:316
  143.4 23.6 %collective-permute-start.22 = (f32[4,2,128,256]{3,2,1,0:T(8,128)S(1)}, f32[4,2,128,256]{3,2,1,0:T(8,128)S(1)}, u32[]{:S(2)}, u32[]{:S(2)}) collective-permute-start(f32[4,2,128,256]{3,2,1,0:T(8,128)S(1)} %get-tuple-element.80), channel_id=1, source_target_pairs={{0,8},{8,0},{16,24},{24,16},{1,9},{9,1},{17,25},{25,17},{2,10},{10... | collective-permute-start | bytes 3145736 | tf_op jit(solution)/shard_map/ppermute | solution.py:316
  165.0 25.3 %collective-permute-start.21 = (f32[4,2,128,256]{3,2,1,0:T(8,128)S(1)}, f32[4,2,128,256]{3,2,1,0:T(8,128)S(1)}, u32[]{:S(2)}, u32[]{:S(2)}) collective-permute-start(f32[4,2,128,256]{3,2,1,0:T(8,128)S(1)} %get-tuple-element.79), channel_id=1, source_target_pairs={{0,16},{8,24},{16,0},{24,8},{1,17},{9,25},{17,1},{25,9},{2,18},{10... | collective-permute-start | bytes 3145736 | tf_op jit(solution)/shard_map/ppermute | solution.py:316
  165.6 24.9 %collective-permute-start.20 = (f32[4,2,128,256]{3,2,1,0:T(8,128)S(1)}, f32[4,2,128,256]{3,2,1,0:T(8,128)S(1)}, u32[]{:S(2)}, u32[]{:S(2)}) collective-permute-start(f32[4,2,128,256]{3,2,1,0:T(8,128)S(1)} %get-tuple-element.77), channel_id=1, source_target_pairs={{0,8},{8,0},{16,24},{24,16},{1,9},{9,1},{17,25},{25,17},{2,10},{10... | collective-permute-start | bytes 3145736 | tf_op jit(solution)/shard_map/ppermute | solution.py:316

commit v7 on v6

--- a/solution.py
+++ b/solution.py
@@ -19,9 +19,6 @@
 
 def cost(weight):
     return pl.CostEstimate(flops=0, bytes_accessed=weight * COST, transcendentals=0)
-
-
-PARAMS = pltpu.CompilerParams(vmem_limit_bytes=4 * 2**20)
 
 
 def block_row(stream, side, row, depth, rows_x):
@@ -122,9 +119,9 @@
         functools.partial(edge_kernel, chunk, depth, groups),
         out_shape=[shape] * 2,
         in_specs=[HBM] * len(flat),
-        out_specs=[HBM] * 2,
+        out_specs=[VMEM] * 2,
         scratch_shapes=[pltpu.SemaphoreType.DMA((4 * high * groups,))],
-        compiler_params=PARAMS,
+        compiler_params=pltpu.CompilerParams(vmem_limit_bytes=12 * 2**20),
         cost_estimate=cost(3),
         name="edges",
     )(*flat)
@@ -230,11 +227,11 @@
     return pl.pallas_call(
         functools.partial(place_kernel, chunk, depth),
         out_shape=jax.ShapeDtypeStruct(result.shape, jnp.float32),
-        in_specs=[SCALARS] + [HBM] * 3,
+        in_specs=[SCALARS, VMEM, VMEM, HBM],
         out_specs=HBM,
         scratch_shapes=[pltpu.SemaphoreType.DMA((2 * len(own_rows(chunk, depth)) * planes,))],
         input_output_aliases={3: 0},
-        compiler_params=PARAMS,
+        compiler_params=pltpu.CompilerParams(vmem_limit_bytes=12 * 2**20),
         cost_estimate=cost(2),
         name="place",
     )(sides, *got, result)

time: 194 us -> 167 us (0.86)
  Pallas kernels: 77.1 us -> 47.6 us
  starting transfers between devices: 42.2 us -> 44.2 us
    pallas_call x4, Pallas kernels: 41.9 us -> 12.4 us  [edges(): pl.pallas_call(functools.partial(edge_kernel, chunk, depth, groups), out_...]
    ppermute x16, starting transfers between devices: 19.5 us -> 21.4 us  [swap(): return lax.ppermute(data, 'tm', [(i, i ^ bit) for i in range(count)])]
  transfers between devices with their start and end apart: 24 -> 24, of which waited for: 11 -> 14; matrix products, arithmetic and copies ran while one was open for 0% -> 0% of each run, Pallas kernels for 35% -> 23%
where the time goes in v7:
time: 167 us; the launch traced here: 166 us
  waiting for transfers between devices  66.5 us (40%)
  Pallas kernels  47.6 us (29%)
  starting transfers between devices  44.2 us (26%)
  local copies, waits for them, and re-layouts  5.56 us (3%)
    ppermute x16, waiting for transfers between devices, swap(): return lax.ppermute(data, 'tm', [(i, i ^ bit) for i in range(count)])  57.4 us
    ppermute x16, starting transfers between devices, swap(): return lax.ppermute(data, 'tm', [(i, i ^ bit) for i in range(count)])  21.4 us
    pallas_call x2, Pallas kernels, apply(): pl.pallas_call(body, out_shape=[jax.ShapeDtypeStruct(shape, jnp.float32),...  19.8 us
    ppermute x4, starting transfers between devices, beside(): lax.ppermute(down, 'space', downward)  15 us
    pallas_call x4, Pallas kernels, edges(): pl.pallas_call(functools.partial(edge_kernel, chunk, depth, groups), out_...  12.4 us
    pallas_call x2, Pallas kernels, pick(): pl.pallas_call(functools.partial(pick_kernel, chunk, depth), out_shape=[j...  9.38 us
    ppermute x4, starting transfers between devices, beside(): lax.ppermute(up, 'space', upward)  7.81 us
    ppermute x4, waiting for transfers between devices, beside(): lax.ppermute(up, 'space', upward)  7.25 us
  transfers between devices with their start and end apart: 24, of which 14 were waited for; matrix products, arithmetic and copies ran while one was open for 0% of the time, Pallas kernels for 23%

profile of v7, /device:TPU:8, one launch (start us, length us, event | category | flops | bytes accessed | tf_op | source)
XLA Modules:
  0.0 165.5 jit_solution(13685474287222047370)
XLA Ops:
  0.0 0.7 convert_multiply_fusion
  0.7 0.6 pad_add_fusion.sides_ref.refs_0_
  1.3 0.7 broadcast_in_dim.2.ratio_ref
  2.0 5.0 %pick.2 = (f32[5,2,64,256]{3,2,1,0:T(8,128)}, f32[5,2,64,256]{3,2,1,0:T(8,128)}, f32[6,2,64,256]{3,2,1,0:T(8,128)}, f32[6,2,64,256]{3,2,1,0:T(8,128)}) custom-call(s32[2]{0:T(128)} %pad_add_fusion.sides_ref.refs_0_, f32[64,256]{1,0:T(8,128)} %broadcast_in_dim.2.ratio_ref, f32[64,2,32,256]{3,2,1,0:T(8,128)} %in_ref.2), custom_call_target="tpu_custom_call" | custom-call | bytes 1850000 | tf_op jit(solution)/shard_map/pick/pallas_call | solution.py:80
  7.0 1.6 collective-permute-start.1
  8.6 1.5 collective-permute-start
  10.1 1.0 copy-done.4
  11.1 1.0 copy-done.5
  12.2 0.7 copy-done.7
  12.8 2.0 %maps.1 = (bf16[256,1536]{1,0:T(8,128)(2,1)S(1)}, bf16[256,1536]{1,0:T(8,128)(2,1)S(1)}) custom-call(s32[1]{0:T(128)} %bitcast.2.me_ref, f32[2,256,256]{2,1,0:T(8,128)S(1)} %copy-done.4, f32[2,256,256]{2,1,0:T(8,128)S(1)} %copy-done.5, f32[2,256]{1,0:T(2,128)S(1)} %copy-done.7), custom_call_target="tpu_custom_call" | custom-call | bytes 740000 | tf_op jit(solution)/shard_map/maps/pallas_call | solution.py:291
  14.9 10.1 %collective-permute-done.refs_1_.refs_8_ = f32[5,2,64,256]{3,2,1,0:T(8,128)S(1)} collective-permute-done((f32[5,2,64,256]{3,2,1,0:T(8,128)}, f32[5,2,64,256]{3,2,1,0:T(8,128)S(1)}, u32[]{:S(2)}, u32[]{:S(2)}) %collective-permute-start) | collective-permute-done | bytes 655392 | tf_op jit(solution)/shard_map/ppermute | solution.py:313
  25.0 1.6 collective-permute-done.1.refs_5_.refs_3_.refs_13_.refs_17_
  26.6 1.5 collective-permute-start.4
  28.1 1.5 collective-permute-start.2
  29.6 3.7 %edges.5 = (f32[2,4,2,64,256]{4,3,2,1,0:T(8,128)}, f32[2,4,2,64,256]{4,3,2,1,0:T(8,128)}) custom-call(f32[5,2,64,256]{3,2,1,0:T(8,128)} %get-tuple-element.46.refs_0_.refs_7_, f32[5,2,64,256]{3,2,1,0:T(8,128)S(1)} %collective-permute-done.refs_1_.refs_8_, f32[6,2,64,256]{3,2,1,0:T(8,128)} %get-tuple-element.54.refs_4_.refs_2_.refs_11_.refs_15_, ...), custom_call_target="tpu_custom_call" | custom-call | bytes 1110000 | tf_op jit(solution)/shard_map/edges/pallas_call | solution.py:118
  33.3 1.9 %collective-permute-start.10 = (f32[2,4,2,64,256]{4,3,2,1,0:T(8,128)}, f32[2,4,2,64,256]{4,3,2,1,0:T(8,128)S(1)}, u32[]{:S(2)}, u32[]{:S(2)}) collective-permute-start(f32[2,4,2,64,256]{4,3,2,1,0:T(8,128)} %get-tuple-element.62), channel_id=1, source_target_pairs={{0,1},{1,2},{2,3},{3,4},{4,5},{5,6},{6,7},{8,9},{9,10},{10,11},{11... | collective-permute-start | bytes 3145736 | tf_op jit(solution)/shard_map/ppermute | solution.py:361
  35.2 3.6 %collective-permute-start.11 = (f32[2,4,2,64,256]{4,3,2,1,0:T(8,128)}, f32[2,4,2,64,256]{4,3,2,1,0:T(8,128)S(1)}, u32[]{:S(2)}, u32[]{:S(2)}) collective-permute-start(f32[2,4,2,64,256]{4,3,2,1,0:T(8,128)} %get-tuple-element.63), channel_id=1, source_target_pairs={{1,0},{2,1},{3,2},{4,3},{5,4},{6,5},{7,6},{9,8},{10,9},{11,10},{12... | collective-permute-start | bytes 3145736 | tf_op jit(solution)/shard_map/ppermute | solution.py:361
  38.9 0.6 collective-permute-start.12
  39.5 2.7 %collective-permute-done.4.refs_1_.refs_10_ = f32[5,2,64,256]{3,2,1,0:T(8,128)S(1)} collective-permute-done((f32[5,2,64,256]{3,2,1,0:T(8,128)S(1)}, f32[5,2,64,256]{3,2,1,0:T(8,128)S(1)}, u32[]{:S(2)}, u32[]{:S(2)}) %collective-permute-start.4) | collective-permute-done | bytes 655392 | tf_op jit(solution)/shard_map/ppermute | solution.py:313
  42.2 1.5 collective-permute-start.8
  43.7 4.4 %pick.3 = (f32[4,2,64,256]{3,2,1,0:T(8,128)}, f32[4,2,64,256]{3,2,1,0:T(8,128)}, f32[4,2,64,256]{3,2,1,0:T(8,128)}, f32[4,2,64,256]{3,2,1,0:T(8,128)}) custom-call(s32[2]{0:T(128)} %pad_add_fusion.sides_ref.refs_0_, f32[64,256]{1,0:T(8,128)} %broadcast_in_dim.2.ratio_ref, f32[64,2,32,256]{3,2,1,0:T(8,128)} %in_ref.2), custom_call_target="tpu_custom_call" | custom-call | bytes 1850000 | tf_op jit(solution)/shard_map/pick/pallas_call | solution.py:80
  48.0 0.5 collective-permute-done.2.refs_3_.refs_14_.refs_5_.refs_18_
  48.6 0.5 collective-permute-start.5
  49.1 11.0 %collective-permute-done.8.refs_0_.refs_9_ = f32[5,2,64,256]{3,2,1,0:T(8,128)S(1)} collective-permute-done((f32[5,2,64,256]{3,2,1,0:T(8,128)}, f32[5,2,64,256]{3,2,1,0:T(8,128)S(1)}, u32[]{:S(2)}, u32[]{:S(2)}) %collective-permute-start.8) | collective-permute-done | bytes 655392 | tf_op jit(solution)/shard_map/ppermute | solution.py:313
  60.0 1.5 collective-permute-start.3
  61.5 0.0 collective-permute-done.10.refs_3_
  61.5 0.0 collective-permute-done.11.refs_4_
  61.5 6.8 %collective-permute-done.5.refs_7_.refs_21_ = f32[4,2,64,256]{3,2,1,0:T(8,128)S(1)} collective-permute-done((f32[4,2,64,256]{3,2,1,0:T(8,128)}, f32[4,2,64,256]{3,2,1,0:T(8,128)S(1)}, u32[]{:S(2)}, u32[]{:S(2)}) %collective-permute-start.5) | collective-permute-done | bytes 524320 | tf_op jit(solution)/shard_map/ppermute | solution.py:313
  68.3 1.5 collective-permute-start.9
  69.8 0.0 collective-permute-done.12.refs_2_.refs_12_.refs_4_.refs_16_
  69.8 3.0 %edges.6 = (f32[2,4,2,64,256]{4,3,2,1,0:T(8,128)S(1)}, f32[2,4,2,64,256]{4,3,2,1,0:T(8,128)S(1)}) custom-call(f32[5,2,64,256]{3,2,1,0:T(8,128)S(1)} %collective-permute-done.8.refs_0_.refs_9_, f32[5,2,64,256]{3,2,1,0:T(8,128)S(1)} %collective-permute-done.4.refs_1_.refs_10_, f32[6,2,64,256]{3,2,1,0:T(8,128)S(1)} %collective-permute-done.12.refs_2_.refs_12_.refs_4_.refs_16_, ...), custom_call_target="tpu_custom_call" | custom-call | bytes 1110000 | tf_op jit(solution)/shard_map/edges/pallas_call | solution.py:118
  72.8 1.9 %collective-permute-start.13 = (f32[2,4,2,64,256]{4,3,2,1,0:T(8,128)S(1)}, f32[2,4,2,64,256]{4,3,2,1,0:T(8,128)S(1)}, u32[]{:S(2)}, u32[]{:S(2)}) collective-permute-start(f32[2,4,2,64,256]{4,3,2,1,0:T(8,128)S(1)} %get-tuple-element.65), channel_id=1, source_target_pairs={{0,1},{1,2},{2,3},{3,4},{4,5},{5,6},{6,7},{8,9},{9,10},{10,11},{11... | collective-permute-start | bytes 3145736 | tf_op jit(solution)/shard_map/ppermute | solution.py:361
  74.8 3.6 %collective-permute-start.14 = (f32[2,4,2,64,256]{4,3,2,1,0:T(8,128)S(1)}, f32[2,4,2,64,256]{4,3,2,1,0:T(8,128)S(1)}, u32[]{:S(2)}, u32[]{:S(2)}) collective-permute-start(f32[2,4,2,64,256]{4,3,2,1,0:T(8,128)S(1)} %get-tuple-element.66), channel_id=1, source_target_pairs={{1,0},{2,1},{3,2},{4,3},{5,4},{6,5},{7,6},{9,8},{10,9},{11,10},{12... | collective-permute-start | bytes 3145736 | tf_op jit(solution)/shard_map/ppermute | solution.py:361
  78.4 0.0 collective-permute-done.3.refs_3_.refs_12_
  78.4 1.6 collective-permute-start.16
  80.0 1.0 copy-done
  81.0 1.0 copy-done.2
  82.1 2.7 %edges.4 = (f32[2,4,2,64,256]{4,3,2,1,0:T(8,128)S(1)}, f32[2,4,2,64,256]{4,3,2,1,0:T(8,128)S(1)}) custom-call(f32[5,2,64,256]{3,2,1,0:T(8,128)} %get-tuple-element.46.refs_0_.refs_7_, f32[5,2,64,256]{3,2,1,0:T(8,128)S(1)} %collective-permute-done.refs_1_.refs_8_, f32[4,2,64,256]{3,2,1,0:T(8,128)S(1)} %copy-done, ...), custom_call_target="tpu_custom_call" | custom-call | bytes 1110000 | tf_op jit(solution)/shard_map/edges/pallas_call | solution.py:118
  84.8 2.1 %collective-permute-start.6 = (f32[2,4,2,64,256]{4,3,2,1,0:T(8,128)S(1)}, f32[2,4,2,64,256]{4,3,2,1,0:T(8,128)S(1)}, u32[]{:S(2)}, u32[]{:S(2)}) collective-permute-start(f32[2,4,2,64,256]{4,3,2,1,0:T(8,128)S(1)} %get-tuple-element.59), channel_id=1, source_target_pairs={{0,1},{1,2},{2,3},{3,4},{4,5},{5,6},{6,7},{8,9},{9,10},{10,11},{11... | collective-permute-start | bytes 3145736 | tf_op jit(solution)/shard_map/ppermute | solution.py:361
  86.8 0.0 collective-permute-done.9.refs_2_.refs_13_
  86.9 3.8 %collective-permute-start.7 = (f32[2,4,2,64,256]{4,3,2,1,0:T(8,128)S(1)}, f32[2,4,2,64,256]{4,3,2,1,0:T(8,128)S(1)}, u32[]{:S(2)}, u32[]{:S(2)}) collective-permute-start(f32[2,4,2,64,256]{4,3,2,1,0:T(8,128)S(1)} %get-tuple-element.60), channel_id=1, source_target_pairs={{1,0},{2,1},{3,2},{4,3},{5,4},{6,5},{7,6},{9,8},{10,9},{11,10},{12... | collective-permute-start | bytes 3145736 | tf_op jit(solution)/shard_map/ppermute | solution.py:361
  90.7 1.8 %collective-permute-done.16.refs_6_.refs_20_ = f32[4,2,64,256]{3,2,1,0:T(8,128)S(1)} collective-permute-done((f32[4,2,64,256]{3,2,1,0:T(8,128)}, f32[4,2,64,256]{3,2,1,0:T(8,128)S(1)}, u32[]{:S(2)}, u32[]{:S(2)}) %collective-permute-start.16) | collective-permute-done | bytes 524320 | tf_op jit(solution)/shard_map/ppermute | solution.py:313
  92.5 0.5 collective-permute-start.15
  93.0 1.5 collective-permute-start.17
  94.5 9.8 %apply.2 = (f32[128,2,32,256]{3,2,1,0:T(8,128)}, f32[4,2,128,256]{3,2,1,0:T(8,128)S(1)}, f32[4,2,128,256]{3,2,1,0:T(8,128)S(1)}) custom-call(s32[2]{0:T(128)S(1)} %copy-done.6, bf16[256,1536]{1,0:T(8,128)(2,1)S(1)} %get-tuple-element.44.refs_1_, bf16[256,1536]{1,0:T(8,128)(2,1)S(1)} %get-tuple-element.45.refs_2_, ...), custom_call_target="tpu_custom_call" | custom-call | bytes 3700000 | tf_op jit(solution)/shard_map/apply/pallas_call | solution.py:198
  104.3 0.0 collective-permute-done.7.refs_4_
  104.3 1.1 collective-permute-done.15.refs_3_.refs_14_
  105.4 0.2 collective-permute-done.17.refs_7_.refs_22_
  105.7 3.0 %edges.7 = (f32[2,4,2,64,256]{4,3,2,1,0:T(8,128)S(1)}, f32[2,4,2,64,256]{4,3,2,1,0:T(8,128)S(1)}) custom-call(f32[5,2,64,256]{3,2,1,0:T(8,128)S(1)} %collective-permute-done.8.refs_0_.refs_9_, f32[5,2,64,256]{3,2,1,0:T(8,128)S(1)} %collective-permute-done.4.refs_1_.refs_10_, f32[4,2,64,256]{3,2,1,0:T(8,128)S(1)} %collective-permute-done.9.refs_2_.refs_13_, ...), custom_call_target="tpu_custom_call" | custom-call | bytes 1110000 | tf_op jit(solution)/shard_map/edges/pallas_call | solution.py:118
  108.7 1.9 %collective-permute-start.18 = (f32[2,4,2,64,256]{4,3,2,1,0:T(8,128)S(1)}, f32[2,4,2,64,256]{4,3,2,1,0:T(8,128)S(1)}, u32[]{:S(2)}, u32[]{:S(2)}) collective-permute-start(f32[2,4,2,64,256]{4,3,2,1,0:T(8,128)S(1)} %get-tuple-element.73), channel_id=1, source_target_pairs={{0,1},{1,2},{2,3},{3,4},{4,5},{5,6},{6,7},{8,9},{9,10},{10,11},{11... | collective-permute-start | bytes 3145736 | tf_op jit(solution)/shard_map/ppermute | solution.py:361
  110.6 3.9 %collective-permute-start.19 = (f32[2,4,2,64,256]{4,3,2,1,0:T(8,128)S(1)}, f32[2,4,2,64,256]{4,3,2,1,0:T(8,128)S(1)}, u32[]{:S(2)}, u32[]{:S(2)}) collective-permute-start(f32[2,4,2,64,256]{4,3,2,1,0:T(8,128)S(1)} %get-tuple-element.74), channel_id=1, source_target_pairs={{1,0},{2,1},{3,2},{4,3},{5,4},{6,5},{7,6},{9,8},{10,9},{11,10},{12... | collective-permute-start | bytes 3145736 | tf_op jit(solution)/shard_map/ppermute | solution.py:361
  114.5 1.6 collective-permute-start.23
  116.1 1.5 collective-permute-start.22
  117.6 7.2 %collective-permute-done.18.refs_5_ = f32[2,4,2,64,256]{4,3,2,1,0:T(8,128)S(1)} collective-permute-done((f32[2,4,2,64,256]{4,3,2,1,0:T(8,128)S(1)}, f32[2,4,2,64,256]{4,3,2,1,0:T(8,128)S(1)}, u32[]{:S(2)}, u32[]{:S(2)}) %collective-permute-start.18) | collective-permute-done | bytes 1048608 | tf_op jit(solution)/shard_map/ppermute | solution.py:361
  124.8 1.8 %collective-permute-done.19.refs_6_ = f32[2,4,2,64,256]{4,3,2,1,0:T(8,128)S(1)} collective-permute-done((f32[2,4,2,64,256]{4,3,2,1,0:T(8,128)S(1)}, f32[2,4,2,64,256]{4,3,2,1,0:T(8,128)S(1)}, u32[]{:S(2)}, u32[]{:S(2)}) %collective-permute-start.19) | collective-permute-done | bytes 1048608 | tf_op jit(solution)/shard_map/ppermute | solution.py:361
  126.6 10.0 %apply.3 = (f32[128,2,32,256]{3,2,1,0:T(8,128)}, f32[4,2,128,256]{3,2,1,0:T(8,128)S(1)}, f32[4,2,128,256]{3,2,1,0:T(8,128)S(1)}) custom-call(s32[2]{0:T(128)S(1)} %copy-done.6, bf16[256,1536]{1,0:T(8,128)(2,1)S(1)} %get-tuple-element.44.refs_1_, bf16[256,1536]{1,0:T(8,128)(2,1)S(1)} %get-tuple-element.45.refs_2_, ...), custom_call_target="tpu_custom_call", output_to_operand_aliasing={{0}: (23, {})} | custom-call | bytes 3700000 | tf_op jit(solution)/shard_map/apply/pallas_call | solution.py:198
  136.6 1.6 collective-permute-start.21
  138.2 1.5 collective-permute-start.20
  139.7 0.0 collective-permute-done.23.got_b
  139.7 1.1 collective-permute-done.22.got_a
  140.8 2.0 %place.2._ = f32[128,2,32,256]{3,2,1,0:T(8,128)} custom-call(s32[2]{0:T(128)S(1)} %copy-done.6, f32[4,2,128,256]{3,2,1,0:T(8,128)S(1)} %collective-permute-done.22.got_a, f32[4,2,128,256]{3,2,1,0:T(8,128)S(1)} %collective-permute-done.23.got_b, f32[128,2,32,256]{3,2,1,0:T(8,128)} %get-tuple-element.82._), custom_call_target="tpu_custom_call", output_to_operand_aliasing={{}: (3, {})} | custom-call | bytes 740000 | tf_op jit(solution)/shard_map/place/pallas_call | solution.py:227
  142.8 18.7 %collective-permute-done.21.got_b = f32[4,2,128,256]{3,2,1,0:T(8,128)S(1)} collective-permute-done((f32[4,2,128,256]{3,2,1,0:T(8,128)S(1)}, f32[4,2,128,256]{3,2,1,0:T(8,128)S(1)}, u32[]{:S(2)}, u32[]{:S(2)}) %collective-permute-start.21) | collective-permute-done | bytes 1048608 | tf_op jit(solution)/shard_map/ppermute | solution.py:313
  161.5 1.8 %collective-permute-done.20.got_a = f32[4,2,128,256]{3,2,1,0:T(8,128)S(1)} collective-permute-done((f32[4,2,128,256]{3,2,1,0:T(8,128)S(1)}, f32[4,2,128,256]{3,2,1,0:T(8,128)S(1)}, u32[]{:S(2)}, u32[]{:S(2)}) %collective-permute-start.20) | collective-permute-done | bytes 1048608 | tf_op jit(solution)/shard_map/ppermute | solution.py:313
  163.4 2.0 %place.3 = f32[128,2,32,256]{3,2,1,0:T(8,128)} custom-call(s32[2]{0:T(128)S(1)} %copy-done.6, f32[4,2,128,256]{3,2,1,0:T(8,128)S(1)} %collective-permute-done.20.got_a, f32[4,2,128,256]{3,2,1,0:T(8,128)S(1)} %collective-permute-done.21.got_b, f32[128,2,32,256]{3,2,1,0:T(8,128)} %place.2._), custom_call_target="tpu_custom_call", output_to_operand_aliasing={{}: (3, {})} | custom-call | bytes 740000 | tf_op jit(solution)/shard_map/place/pallas_call | solution.py:227
  (14 shorter events, 0.0 us)
Async XLA Ops:
  7.0 87.5 %copy-start.6 = (s32[2]{0:T(128)S(1)}, s32[2]{0:T(128)}, u32[]{:S(2)}) copy-start(s32[2]{0:T(128)} %pad_add_fusion.sides_ref.refs_0_) | copy-start | bytes 28
  7.0 19.6 %collective-permute-start.1 = (f32[6,2,64,256]{3,2,1,0:T(8,128)}, f32[6,2,64,256]{3,2,1,0:T(8,128)S(1)}, u32[]{:S(2)}, u32[]{:S(2)}) collective-permute-start(f32[6,2,64,256]{3,2,1,0:T(8,128)} %get-tuple-element.48), channel_id=1, source_target_pairs={{0,16},{8,24},{16,0},{24,8},{1,17},{9,25},{17,1},{25,9},{2,18},{10... | collective-permute-start | bytes 2359304 | tf_op jit(solution)/shard_map/ppermute | solution.py:313
  8.6 16.4 %collective-permute-start = (f32[5,2,64,256]{3,2,1,0:T(8,128)}, f32[5,2,64,256]{3,2,1,0:T(8,128)S(1)}, u32[]{:S(2)}, u32[]{:S(2)}) collective-permute-start(f32[5,2,64,256]{3,2,1,0:T(8,128)} %get-tuple-element.47), channel_id=1, source_target_pairs={{0,8},{8,0},{16,24},{24,16},{1,9},{9,1},{17,25},{25,17},{2,10},{10... | collective-permute-start | bytes 1966088 | tf_op jit(solution)/shard_map/ppermute | solution.py:313
  10.1 1.0 copy-start.4
  11.1 1.0 copy-start.5
  12.2 0.7 copy-start.7
  26.6 15.6 %collective-permute-start.4 = (f32[5,2,64,256]{3,2,1,0:T(8,128)S(1)}, f32[5,2,64,256]{3,2,1,0:T(8,128)S(1)}, u32[]{:S(2)}, u32[]{:S(2)}) collective-permute-start(f32[5,2,64,256]{3,2,1,0:T(8,128)S(1)} %collective-permute-done.refs_1_.refs_8_), channel_id=1, source_target_pairs={{0,16},{8,24},{16,0},{24,8},{1,17},{9,25},{17,1},{25,9},{2,18},{10... | collective-permute-start | bytes 1966088 | tf_op jit(solution)/shard_map/ppermute | solution.py:313
  28.1 20.5 %collective-permute-start.2 = (f32[6,2,64,256]{3,2,1,0:T(8,128)S(1)}, f32[6,2,64,256]{3,2,1,0:T(8,128)S(1)}, u32[]{:S(2)}, u32[]{:S(2)}) collective-permute-start(f32[6,2,64,256]{3,2,1,0:T(8,128)S(1)} %collective-permute-done.1.refs_5_.refs_3_.refs_13_.refs_17_), channel_id=1, source_target_pairs={{0,8},{8,0},{16,24},{24,16},{1,9},{9,1},{17,25},{25,17},{2,10},{10... | collective-permute-start | bytes 2359304 | tf_op jit(solution)/shard_map/ppermute | solution.py:313
  33.3 28.3 %collective-permute-start.10 = (f32[2,4,2,64,256]{4,3,2,1,0:T(8,128)}, f32[2,4,2,64,256]{4,3,2,1,0:T(8,128)S(1)}, u32[]{:S(2)}, u32[]{:S(2)}) collective-permute-start(f32[2,4,2,64,256]{4,3,2,1,0:T(8,128)} %get-tuple-element.62), channel_id=1, source_target_pairs={{0,1},{1,2},{2,3},{3,4},{4,5},{5,6},{6,7},{8,9},{9,10},{10,11},{11... | collective-permute-start | bytes 3145736 | tf_op jit(solution)/shard_map/ppermute | solution.py:361
  35.2 26.3 %collective-permute-start.11 = (f32[2,4,2,64,256]{4,3,2,1,0:T(8,128)}, f32[2,4,2,64,256]{4,3,2,1,0:T(8,128)S(1)}, u32[]{:S(2)}, u32[]{:S(2)}) collective-permute-start(f32[2,4,2,64,256]{4,3,2,1,0:T(8,128)} %get-tuple-element.63), channel_id=1, source_target_pairs={{1,0},{2,1},{3,2},{4,3},{5,4},{6,5},{7,6},{9,8},{10,9},{11,10},{12... | collective-permute-start | bytes 3145736 | tf_op jit(solution)/shard_map/ppermute | solution.py:361
  38.9 31.0 %collective-permute-start.12 = (f32[6,2,64,256]{3,2,1,0:T(8,128)}, f32[6,2,64,256]{3,2,1,0:T(8,128)S(1)}, u32[]{:S(2)}, u32[]{:S(2)}) collective-permute-start(f32[6,2,64,256]{3,2,1,0:T(8,128)} %get-tuple-element.54.refs_4_.refs_2_.refs_11_.refs_15_), channel_id=1, source_target_pairs={{0,8},{8,0},{16,24},{24,16},{1,9},{9,1},{17,25},{25,17},{2,10},{10... | collective-permute-start | bytes 2359304 | tf_op jit(solution)/shard_map/ppermute | solution.py:313
  42.2 17.9 %collective-permute-start.8 = (f32[5,2,64,256]{3,2,1,0:T(8,128)}, f32[5,2,64,256]{3,2,1,0:T(8,128)S(1)}, u32[]{:S(2)}, u32[]{:S(2)}) collective-permute-start(f32[5,2,64,256]{3,2,1,0:T(8,128)} %get-tuple-element.46.refs_0_.refs_7_), channel_id=1, source_target_pairs={{0,16},{8,24},{16,0},{24,8},{1,17},{9,25},{17,1},{25,9},{2,18},{10... | collective-permute-start | bytes 1966088 | tf_op jit(solution)/shard_map/ppermute | solution.py:313
  48.6 19.7 %collective-permute-start.5 = (f32[4,2,64,256]{3,2,1,0:T(8,128)}, f32[4,2,64,256]{3,2,1,0:T(8,128)S(1)}, u32[]{:S(2)}, u32[]{:S(2)}) collective-permute-start(f32[4,2,64,256]{3,2,1,0:T(8,128)} %get-tuple-element.58), channel_id=1, source_target_pairs={{0,16},{8,24},{16,0},{24,8},{1,17},{9,25},{17,1},{25,9},{2,18},{10... | collective-permute-start | bytes 1572872 | tf_op jit(solution)/shard_map/ppermute | solution.py:313
  60.0 18.4 %collective-permute-start.3 = (f32[4,2,64,256]{3,2,1,0:T(8,128)}, f32[4,2,64,256]{3,2,1,0:T(8,128)S(1)}, u32[]{:S(2)}, u32[]{:S(2)}) collective-permute-start(f32[4,2,64,256]{3,2,1,0:T(8,128)} %get-tuple-element.53), channel_id=1, source_target_pairs={{0,8},{8,0},{16,24},{24,16},{1,9},{9,1},{17,25},{25,17},{2,10},{10... | collective-permute-start | bytes 1572872 | tf_op jit(solution)/shard_map/ppermute | solution.py:313
  68.3 18.6 %collective-permute-start.9 = (f32[4,2,64,256]{3,2,1,0:T(8,128)}, f32[4,2,64,256]{3,2,1,0:T(8,128)S(1)}, u32[]{:S(2)}, u32[]{:S(2)}) collective-permute-start(f32[4,2,64,256]{3,2,1,0:T(8,128)} %get-tuple-element.61.refs_2_.refs_11_), channel_id=1, source_target_pairs={{0,16},{8,24},{16,0},{24,8},{1,17},{9,25},{17,1},{25,9},{2,18},{10... | collective-permute-start | bytes 1572872 | tf_op jit(solution)/shard_map/ppermute | solution.py:313
  72.8 20.2 %collective-permute-start.13 = (f32[2,4,2,64,256]{4,3,2,1,0:T(8,128)S(1)}, f32[2,4,2,64,256]{4,3,2,1,0:T(8,128)S(1)}, u32[]{:S(2)}, u32[]{:S(2)}) collective-permute-start(f32[2,4,2,64,256]{4,3,2,1,0:T(8,128)S(1)} %get-tuple-element.65), channel_id=1, source_target_pairs={{0,1},{1,2},{2,3},{3,4},{4,5},{5,6},{6,7},{8,9},{9,10},{10,11},{11... | collective-permute-start | bytes 3145736 | tf_op jit(solution)/shard_map/ppermute | solution.py:361
  74.8 19.7 %collective-permute-start.14 = (f32[2,4,2,64,256]{4,3,2,1,0:T(8,128)S(1)}, f32[2,4,2,64,256]{4,3,2,1,0:T(8,128)S(1)}, u32[]{:S(2)}, u32[]{:S(2)}) collective-permute-start(f32[2,4,2,64,256]{4,3,2,1,0:T(8,128)S(1)} %get-tuple-element.66), channel_id=1, source_target_pairs={{1,0},{2,1},{3,2},{4,3},{5,4},{6,5},{7,6},{9,8},{10,9},{11,10},{12... | collective-permute-start | bytes 3145736 | tf_op jit(solution)/shard_map/ppermute | solution.py:361
  78.4 14.1 %collective-permute-start.16 = (f32[4,2,64,256]{3,2,1,0:T(8,128)}, f32[4,2,64,256]{3,2,1,0:T(8,128)S(1)}, u32[]{:S(2)}, u32[]{:S(2)}) collective-permute-start(f32[4,2,64,256]{3,2,1,0:T(8,128)} %get-tuple-element.71.refs_6_.refs_19_), channel_id=1, source_target_pairs={{0,8},{8,0},{16,24},{24,16},{1,9},{9,1},{17,25},{25,17},{2,10},{10... | collective-permute-start | bytes 1572872 | tf_op jit(solution)/shard_map/ppermute | solution.py:313
  80.0 1.0 copy-start
  81.0 1.0 copy-start.2
  84.8 41.8 %copy-start.1 = (f32[4,2,64,256]{3,2,1,0:T(8,128)S(1)}, f32[4,2,64,256]{3,2,1,0:T(8,128)}, u32[]{:S(2)}) copy-start(f32[4,2,64,256]{3,2,1,0:T(8,128)} %get-tuple-element.61.refs_2_.refs_11_) | copy-start | bytes 1572868
  84.8 41.8 %copy-start.3 = (f32[4,2,64,256]{3,2,1,0:T(8,128)S(1)}, f32[4,2,64,256]{3,2,1,0:T(8,128)}, u32[]{:S(2)}) copy-start(f32[4,2,64,256]{3,2,1,0:T(8,128)} %get-tuple-element.71.refs_6_.refs_19_) | copy-start | bytes 1572868
  84.8 19.5 %collective-permute-start.6 = (f32[2,4,2,64,256]{4,3,2,1,0:T(8,128)S(1)}, f32[2,4,2,64,256]{4,3,2,1,0:T(8,128)S(1)}, u32[]{:S(2)}, u32[]{:S(2)}) collective-permute-start(f32[2,4,2,64,256]{4,3,2,1,0:T(8,128)S(1)} %get-tuple-element.59), channel_id=1, source_target_pairs={{0,1},{1,2},{2,3},{3,4},{4,5},{5,6},{6,7},{8,9},{9,10},{10,11},{11... | collective-permute-start | bytes 3145736 | tf_op jit(solution)/shard_map/ppermute | solution.py:361
  86.9 17.5 %collective-permute-start.7 = (f32[2,4,2,64,256]{4,3,2,1,0:T(8,128)S(1)}, f32[2,4,2,64,256]{4,3,2,1,0:T(8,128)S(1)}, u32[]{:S(2)}, u32[]{:S(2)}) collective-permute-start(f32[2,4,2,64,256]{4,3,2,1,0:T(8,128)S(1)} %get-tuple-element.60), channel_id=1, source_target_pairs={{1,0},{2,1},{3,2},{4,3},{5,4},{6,5},{7,6},{9,8},{10,9},{11,10},{12... | collective-permute-start | bytes 3145736 | tf_op jit(solution)/shard_map/ppermute | solution.py:361
  92.5 12.9 %collective-permute-start.15 = (f32[4,2,64,256]{3,2,1,0:T(8,128)S(1)}, f32[4,2,64,256]{3,2,1,0:T(8,128)S(1)}, u32[]{:S(2)}, u32[]{:S(2)}) collective-permute-start(f32[4,2,64,256]{3,2,1,0:T(8,128)S(1)} %collective-permute-done.3.refs_3_.refs_12_), channel_id=1, source_target_pairs={{0,16},{8,24},{16,0},{24,8},{1,17},{9,25},{17,1},{25,9},{2,18},{10... | collective-permute-start | bytes 1572872 | tf_op jit(solution)/shard_map/ppermute | solution.py:313
  93.0 12.6 %collective-permute-start.17 = (f32[4,2,64,256]{3,2,1,0:T(8,128)S(1)}, f32[4,2,64,256]{3,2,1,0:T(8,128)S(1)}, u32[]{:S(2)}, u32[]{:S(2)}) collective-permute-start(f32[4,2,64,256]{3,2,1,0:T(8,128)S(1)} %collective-permute-done.5.refs_7_.refs_21_), channel_id=1, source_target_pairs={{0,8},{8,0},{16,24},{24,16},{1,9},{9,1},{17,25},{25,17},{2,10},{10... | collective-permute-start | bytes 1572872 | tf_op jit(solution)/shard_map/ppermute | solution.py:313
  108.7 16.1 %collective-permute-start.18 = (f32[2,4,2,64,256]{4,3,2,1,0:T(8,128)S(1)}, f32[2,4,2,64,256]{4,3,2,1,0:T(8,128)S(1)}, u32[]{:S(2)}, u32[]{:S(2)}) collective-permute-start(f32[2,4,2,64,256]{4,3,2,1,0:T(8,128)S(1)} %get-tuple-element.73), channel_id=1, source_target_pairs={{0,1},{1,2},{2,3},{3,4},{4,5},{5,6},{6,7},{8,9},{9,10},{10,11},{11... | collective-permute-start | bytes 3145736 | tf_op jit(solution)/shard_map/ppermute | solution.py:361
  110.6 15.9 %collective-permute-start.19 = (f32[2,4,2,64,256]{4,3,2,1,0:T(8,128)S(1)}, f32[2,4,2,64,256]{4,3,2,1,0:T(8,128)S(1)}, u32[]{:S(2)}, u32[]{:S(2)}) collective-permute-start(f32[2,4,2,64,256]{4,3,2,1,0:T(8,128)S(1)} %get-tuple-element.74), channel_id=1, source_target_pairs={{1,0},{2,1},{3,2},{4,3},{5,4},{6,5},{7,6},{9,8},{10,9},{11,10},{12... | collective-permute-start | bytes 3145736 | tf_op jit(solution)/shard_map/ppermute | solution.py:361
  114.5 25.2 %collective-permute-start.23 = (f32[4,2,128,256]{3,2,1,0:T(8,128)S(1)}, f32[4,2,128,256]{3,2,1,0:T(8,128)S(1)}, u32[]{:S(2)}, u32[]{:S(2)}) collective-permute-start(f32[4,2,128,256]{3,2,1,0:T(8,128)S(1)} %get-tuple-element.81), channel_id=1, source_target_pairs={{0,16},{8,24},{16,0},{24,8},{1,17},{9,25},{17,1},{25,9},{2,18},{10... | collective-permute-start | bytes 3145736 | tf_op jit(solution)/shard_map/ppermute | solution.py:313
  116.1 24.7 %collective-permute-start.22 = (f32[4,2,128,256]{3,2,1,0:T(8,128)S(1)}, f32[4,2,128,256]{3,2,1,0:T(8,128)S(1)}, u32[]{:S(2)}, u32[]{:S(2)}) collective-permute-start(f32[4,2,128,256]{3,2,1,0:T(8,128)S(1)} %get-tuple-element.80), channel_id=1, source_target_pairs={{0,8},{8,0},{16,24},{24,16},{1,9},{9,1},{17,25},{25,17},{2,10},{10... | collective-permute-start | bytes 3145736 | tf_op jit(solution)/shard_map/ppermute | solution.py:313
  136.6 24.9 %collective-permute-start.21 = (f32[4,2,128,256]{3,2,1,0:T(8,128)S(1)}, f32[4,2,128,256]{3,2,1,0:T(8,128)S(1)}, u32[]{:S(2)}, u32[]{:S(2)}) collective-permute-start(f32[4,2,128,256]{3,2,1,0:T(8,128)S(1)} %get-tuple-element.79), channel_id=1, source_target_pairs={{0,16},{8,24},{16,0},{24,8},{1,17},{9,25},{17,1},{25,9},{2,18},{10... | collective-permute-start | bytes 3145736 | tf_op jit(solution)/shard_map/ppermute | solution.py:313
  138.2 25.2 %collective-permute-start.20 = (f32[4,2,128,256]{3,2,1,0:T(8,128)S(1)}, f32[4,2,128,256]{3,2,1,0:T(8,128)S(1)}, u32[]{:S(2)}, u32[]{:S(2)}) collective-permute-start(f32[4,2,128,256]{3,2,1,0:T(8,128)S(1)} %get-tuple-element.77), channel_id=1, source_target_pairs={{0,8},{8,0},{16,24},{24,16},{1,9},{9,1},{17,25},{25,17},{2,10},{10... | collective-permute-start | bytes 3145736 | tf_op jit(solution)/shard_map/ppermute | solution.py:313

commit v8 on v7

--- a/solution.py
+++ b/solution.py
@@ -54,40 +54,44 @@
         copy.wait()
 
 
-def pick_kernel(chunk, depth, sides_ref, ratio_ref, in_ref, *refs):
+def pick_kernel(chunk, depth, kinds, bits, step_ref, in_ref, *refs):
     outs, sems = refs[:-1], refs[-1]
-    _, planes, rows_x, _ = in_ref.shape
+    steps, planes, rows_x, _ = in_ref.shape
+    me = lax.axis_index("tm")
     jobs = []
-    for stream in range(2):
-        for other in (1, 0):
-            side = 1 - sides_ref[stream] if other else sides_ref[stream]
-            for at, row in enumerate(chunk_rows(stream, chunk, depth)):
-                x = block_row(stream, side, row, depth, rows_x)
-                for z in range(planes):
-                    out = outs[2 * stream + other].at[at, z]
-                    jobs.append((pltpu.make_async_copy(in_ref.at[:, z, x], out, sems.at[len(jobs)]), out))
+    for place, (stream, other) in enumerate(kinds):
+        side = jnp.where(jnp.bitwise_and(me, bits[stream]) > 0, 1, 0)
+        side = 1 - side if other else side
+        for at, row in enumerate(chunk_rows(stream, chunk, depth)):
+            x = block_row(stream, side, row, depth, rows_x)
+            for z in range(planes):
+                out = outs[place].at[at, z]
+                jobs.append((pltpu.make_async_copy(in_ref.at[:, z, x], out, sems.at[len(jobs)]), out))
     for copy, _ in jobs:
         copy.start()
-    ratio = ratio_ref[...]
+    line = step_ref[...].astype(jnp.float32) / 8.0
+    down = lax.broadcasted_iota(jnp.int32, (steps, steps), 0)
+    along = lax.broadcasted_iota(jnp.int32, (steps, steps), 1)
+    ratio = jnp.sum(jnp.where(down == along, line, 0.0), axis=1, keepdims=True)
     for copy, out in jobs:
         copy.wait()
         out[...] = out[...] * ratio
 
 
-def pick(chunk, residual, ratio, sides, depth):
+def pick(chunk, kinds, residual, step_ratio, bits, depth):
     steps, planes, _, rows_y = residual.shape
-    counts = [len(chunk_rows(stream, chunk, depth)) for stream in (0, 0, 1, 1)]
+    counts = [len(chunk_rows(stream, chunk, depth)) for stream, _ in kinds]
     outs = pl.pallas_call(
-        functools.partial(pick_kernel, chunk, depth),
+        functools.partial(pick_kernel, chunk, depth, kinds, bits),
         out_shape=[jax.ShapeDtypeStruct((c, planes, steps, rows_y), jnp.float32) for c in counts],
-        in_specs=[SCALARS, VMEM, HBM],
-        out_specs=[VMEM] * 4,
+        in_specs=[VMEM, HBM],
+        out_specs=[VMEM] * len(kinds),
         scratch_shapes=[pltpu.SemaphoreType.DMA((sum(counts) * planes,))],
         compiler_params=pltpu.CompilerParams(vmem_limit_bytes=56 * 2**20),
         cost_estimate=cost(5),
         name="pick",
-    )(sides, ratio, residual)
-    return [outs[0:2], outs[2:4]]
+    )(step_ratio.reshape(1, steps), residual)
+    return dict(zip(kinds, outs))
 
 
 def edge_kernel(chunk, depth, groups, *refs):
@@ -337,8 +341,11 @@
 
     def raw(chunk):
         data = after(residual, *firsts[-1]) if firsts else residual
-        mine = pick(chunk, data, ratio, sides, depth)
-        have = [{0: mine[s][0], bits[s]: swap_in_turn(mine[s][1], bits[s])} for s in range(2)]
+        sent, kept = ((0, 1), (1, 1)), ((0, 0), (1, 0))
+        mine = {}
+        for kinds in (sent + kept,) if chunk else (sent, kept):
+            mine.update(pick(chunk, kinds, data, step_ratio, bits, depth))
+        have = [{0: mine[s, 0], bits[s]: swap_in_turn(mine[s, 1], bits[s])} for s in range(2)]
         firsts.append([have[s][bits[s]] for s in range(2)])
         for bit in all_bits:
             for mask in masks:

time: 167 us -> 177 us (1.060)
  local copies, waits for them, and re-layouts: 5.56 us -> 17.4 us
  Pallas kernels: 47.6 us -> 52.8 us
  starting transfers between devices: 44.2 us -> 40.3 us
  waiting for transfers between devices: 66.5 us -> 64.3 us
    unnamed x16 -> x54, local copies, waits for them, and re-layouts: 4.86 us -> 17.4 us
    ppermute x16, waiting for transfers between devices: 57.4 us -> 53.4 us  [swap(): return lax.ppermute(data, 'tm', [(i, i ^ bit) for i in range(count)])]
    ppermute x16, starting transfers between devices: 21.4 us -> 17.6 us  [swap(): return lax.ppermute(data, 'tm', [(i, i ^ bit) for i in range(count)])]
    ppermute x4, waiting for transfers between devices: 7.25 us -> 9.15 us  [beside(): lax.ppermute(up, 'space', upward)]
    pallas_call x2 -> x3, Pallas kernels: 9.38 us -> 11.2 us  [pick(): pl.pallas_call(functools.partial(pick_kernel, chunk, depth, kinds, bits),...]
    pallas_call x4, Pallas kernels: 12.4 us -> 14.2 us  [edges(): pl.pallas_call(functools.partial(edge_kernel, chunk, depth, groups), out_...]
  transfers between devices with their start and end apart: 24 -> 24, of which waited for: 14 -> 9; matrix products, arithmetic and copies ran while one was open for 0% -> 0% of each run, Pallas kernels for 23% -> 25%
where the time goes in v8:
time: 177 us; the launch traced here: 175 us
  waiting for transfers between devices  64.3 us (36%)
  Pallas kernels  52.8 us (30%)
  starting transfers between devices  40.3 us (23%)
  local copies, waits for them, and re-layouts  17.4 us (10%)
    ppermute x16, waiting for transfers between devices, swap(): return lax.ppermute(data, 'tm', [(i, i ^ bit) for i in range(count)])  53.4 us
    pallas_call x2, Pallas kernels, apply(): pl.pallas_call(body, out_shape=[jax.ShapeDtypeStruct(shape, jnp.float32),...  21.4 us
    ppermute x16, starting transfers between devices, swap(): return lax.ppermute(data, 'tm', [(i, i ^ bit) for i in range(count)])  17.6 us
    unnamed x54, local copies, waits for them, and re-layouts  17.4 us
    ppermute x4, starting transfers between devices, beside(): lax.ppermute(down, 'space', downward)  15 us
    pallas_call x4, Pallas kernels, edges(): pl.pallas_call(functools.partial(edge_kernel, chunk, depth, groups), out_...  14.2 us
    pallas_call x3, Pallas kernels, pick(): pl.pallas_call(functools.partial(pick_kernel, chunk, depth, kinds, bits),...  11.2 us
    ppermute x4, waiting for transfers between devices, beside(): lax.ppermute(up, 'space', upward)  9.15 us
  transfers between devices with their start and end apart: 24, of which 9 were waited for; matrix products, arithmetic and copies ran while one was open for 0% of the time, Pallas kernels for 25%

profile of v8, /device:TPU:8, one launch (start us, length us, event | category | flops | bytes accessed | tf_op | source)
XLA Modules:
  0.0 175.4 jit_solution(1391657373261135651)
XLA Ops:
  0.0 3.5 %pick.4 = (f32[5,2,64,256]{3,2,1,0:T(8,128)}, f32[6,2,64,256]{3,2,1,0:T(8,128)}) custom-call(s32[1,64]{1,0:T(1,128)} %bitcast.5, f32[64,2,32,256]{3,2,1,0:T(8,128)} %in_ref.4), custom_call_target="tpu_custom_call" | custom-call | bytes 1850000 | tf_op jit(solution)/shard_map/pick/pallas_call | solution.py:84
  3.5 1.6 collective-permute-start.1
  5.1 1.5 collective-permute-start
  6.6 1.0 copy-done.24
  7.6 1.0 copy-done.25
  8.7 0.7 copy-done.26
  9.3 2.0 %maps.1 = (bf16[256,1536]{1,0:T(8,128)(2,1)S(1)}, bf16[256,1536]{1,0:T(8,128)(2,1)S(1)}) custom-call(s32[1]{0:T(128)} %bitcast.2.me_ref, f32[2,256,256]{2,1,0:T(8,128)S(1)} %copy-done.24, f32[2,256,256]{2,1,0:T(8,128)S(1)} %copy-done.25, f32[2,256]{1,0:T(2,128)S(1)} %copy-done.26), custom_call_target="tpu_custom_call" | custom-call | bytes 740000 | tf_op jit(solution)/shard_map/maps/pallas_call | solution.py:295
  11.4 0.9 copy-done.6
  12.3 0.9 copy-done.8
  13.2 8.3 %collective-permute-done.refs_1_.refs_8_ = f32[5,2,64,256]{3,2,1,0:T(8,128)S(1)} collective-permute-done((f32[5,2,64,256]{3,2,1,0:T(8,128)}, f32[5,2,64,256]{3,2,1,0:T(8,128)S(1)}, u32[]{:S(2)}, u32[]{:S(2)}) %collective-permute-start) | collective-permute-done | bytes 655392 | tf_op jit(solution)/shard_map/ppermute | solution.py:317
  21.5 1.6 collective-permute-done.1.refs_5_.refs_3_.refs_13_.refs_17_
  23.1 1.5 collective-permute-start.4
  24.6 1.5 collective-permute-start.2
  26.1 3.5 %pick.3 = (f32[5,2,64,256]{3,2,1,0:T(8,128)}, f32[6,2,64,256]{3,2,1,0:T(8,128)}) custom-call(s32[1,64]{1,0:T(1,128)} %bitcast.6, f32[64,2,32,256]{3,2,1,0:T(8,128)} %in_ref.4), custom_call_target="tpu_custom_call" | custom-call | bytes 1850000 | tf_op jit(solution)/shard_map/pick/pallas_call | solution.py:84
  29.6 3.4 %edges.5 = (f32[2,4,2,64,256]{4,3,2,1,0:T(8,128)}, f32[2,4,2,64,256]{4,3,2,1,0:T(8,128)S(1)}) custom-call(f32[5,2,64,256]{3,2,1,0:T(8,128)} %get-tuple-element.46.refs_0_.refs_7_, f32[5,2,64,256]{3,2,1,0:T(8,128)S(1)} %collective-permute-done.refs_1_.refs_8_, f32[6,2,64,256]{3,2,1,0:T(8,128)} %get-tuple-element.54.refs_4_.refs_2_.refs_11_.refs_15_, ...), custom_call_target="tpu_custom_call" | custom-call | bytes 1110000 | tf_op jit(solution)/shard_map/edges/pallas_call | solution.py:122
  33.0 1.9 %collective-permute-start.10 = (f32[2,4,2,64,256]{4,3,2,1,0:T(8,128)}, f32[2,4,2,64,256]{4,3,2,1,0:T(8,128)S(1)}, u32[]{:S(2)}, u32[]{:S(2)}) collective-permute-start(f32[2,4,2,64,256]{4,3,2,1,0:T(8,128)} %get-tuple-element.62), channel_id=1, source_target_pairs={{0,1},{1,2},{2,3},{3,4},{4,5},{5,6},{6,7},{8,9},{9,10},{10,11},{11... | collective-permute-start | bytes 3145736 | tf_op jit(solution)/shard_map/ppermute | solution.py:368
  34.9 3.6 %collective-permute-start.11 = (f32[2,4,2,64,256]{4,3,2,1,0:T(8,128)S(1)}, f32[2,4,2,64,256]{4,3,2,1,0:T(8,128)S(1)}, u32[]{:S(2)}, u32[]{:S(2)}) collective-permute-start(f32[2,4,2,64,256]{4,3,2,1,0:T(8,128)S(1)} %get-tuple-element.63), channel_id=1, source_target_pairs={{1,0},{2,1},{3,2},{4,3},{5,4},{6,5},{7,6},{9,8},{10,9},{11,10},{12... | collective-permute-start | bytes 3145736 | tf_op jit(solution)/shard_map/ppermute | solution.py:368
  38.6 0.6 collective-permute-start.12
  39.2 0.0 collective-permute-done.4.refs_1_.refs_10_
  39.2 1.0 collective-permute-start.8
  40.2 4.2 %pick.5 = (f32[4,2,64,256]{3,2,1,0:T(8,128)}, f32[4,2,64,256]{3,2,1,0:T(8,128)}, f32[4,2,64,256]{3,2,1,0:T(8,128)}, f32[4,2,64,256]{3,2,1,0:T(8,128)}) custom-call(s32[1,64]{1,0:T(1,128)} %bitcast.7, f32[64,2,32,256]{3,2,1,0:T(8,128)} %in_ref.4), custom_call_target="tpu_custom_call" | custom-call | bytes 1850000 | tf_op jit(solution)/shard_map/pick/pallas_call | solution.py:84
  44.4 1.1 collective-permute-start.5
  45.5 11.6 %collective-permute-done.8.refs_0_.refs_9_ = f32[5,2,64,256]{3,2,1,0:T(8,128)S(1)} collective-permute-done((f32[5,2,64,256]{3,2,1,0:T(8,128)}, f32[5,2,64,256]{3,2,1,0:T(8,128)S(1)}, u32[]{:S(2)}, u32[]{:S(2)}) %collective-permute-start.8) | collective-permute-done | bytes 655392 | tf_op jit(solution)/shard_map/ppermute | solution.py:317
  57.0 1.5 collective-permute-start.3
  58.6 8.5 %collective-permute-done.5.refs_7_.refs_21_ = f32[4,2,64,256]{3,2,1,0:T(8,128)} collective-permute-done((f32[4,2,64,256]{3,2,1,0:T(8,128)}, f32[4,2,64,256]{3,2,1,0:T(8,128)}, u32[]{:S(2)}, u32[]{:S(2)}) %collective-permute-start.5) | collective-permute-done | bytes 524320 | tf_op jit(solution)/shard_map/ppermute | solution.py:317
  67.0 0.5 collective-permute-start.9
  67.6 4.0 %edges.6 = (f32[2,4,2,64,256]{4,3,2,1,0:T(8,128)S(1)}, f32[2,4,2,64,256]{4,3,2,1,0:T(8,128)}) custom-call(f32[5,2,64,256]{3,2,1,0:T(8,128)S(1)} %collective-permute-done.8.refs_0_.refs_9_, f32[5,2,64,256]{3,2,1,0:T(8,128)S(1)} %collective-permute-done.4.refs_1_.refs_10_, f32[6,2,64,256]{3,2,1,0:T(8,128)S(1)} %collective-permute-done.12.refs_2_.refs_12_.refs_4_.refs_16_, ...), custom_call_target="tpu_custom_call" | custom-call | bytes 1110000 | tf_op jit(solution)/shard_map/edges/pallas_call | solution.py:122
  71.6 1.9 %collective-permute-start.13 = (f32[2,4,2,64,256]{4,3,2,1,0:T(8,128)S(1)}, f32[2,4,2,64,256]{4,3,2,1,0:T(8,128)S(1)}, u32[]{:S(2)}, u32[]{:S(2)}) collective-permute-start(f32[2,4,2,64,256]{4,3,2,1,0:T(8,128)S(1)} %get-tuple-element.65), channel_id=1, source_target_pairs={{0,1},{1,2},{2,3},{3,4},{4,5},{5,6},{6,7},{8,9},{9,10},{10,11},{11... | collective-permute-start | bytes 3145736 | tf_op jit(solution)/shard_map/ppermute | solution.py:368
  73.5 3.6 %collective-permute-start.14 = (f32[2,4,2,64,256]{4,3,2,1,0:T(8,128)}, f32[2,4,2,64,256]{4,3,2,1,0:T(8,128)}, u32[]{:S(2)}, u32[]{:S(2)}) collective-permute-start(f32[2,4,2,64,256]{4,3,2,1,0:T(8,128)} %get-tuple-element.66), channel_id=1, source_target_pairs={{1,0},{2,1},{3,2},{4,3},{5,4},{6,5},{7,6},{9,8},{10,9},{11,10},{12... | collective-permute-start | bytes 3145736 | tf_op jit(solution)/shard_map/ppermute | solution.py:368
  77.2 1.6 collective-permute-start.16
  78.7 1.0 copy-done.10
  79.8 1.0 copy-done.12
  80.8 3.9 %edges.4 = (f32[2,4,2,64,256]{4,3,2,1,0:T(8,128)}, f32[2,4,2,64,256]{4,3,2,1,0:T(8,128)}) custom-call(f32[5,2,64,256]{3,2,1,0:T(8,128)} %get-tuple-element.46.refs_0_.refs_7_, f32[5,2,64,256]{3,2,1,0:T(8,128)S(1)} %collective-permute-done.refs_1_.refs_8_, f32[4,2,64,256]{3,2,1,0:T(8,128)S(1)} %copy-done.10, ...), custom_call_target="tpu_custom_call" | custom-call | bytes 1110000 | tf_op jit(solution)/shard_map/edges/pallas_call | solution.py:122
  84.7 1.9 %collective-permute-start.6 = (f32[2,4,2,64,256]{4,3,2,1,0:T(8,128)}, f32[2,4,2,64,256]{4,3,2,1,0:T(8,128)}, u32[]{:S(2)}, u32[]{:S(2)}) collective-permute-start(f32[2,4,2,64,256]{4,3,2,1,0:T(8,128)} %get-tuple-element.59), channel_id=1, source_target_pairs={{0,1},{1,2},{2,3},{3,4},{4,5},{5,6},{6,7},{8,9},{9,10},{10,11},{11... | collective-permute-start | bytes 3145736 | tf_op jit(solution)/shard_map/ppermute | solution.py:368
  86.7 0.8 copy-done.14
  87.5 3.8 %collective-permute-start.7 = (f32[2,4,2,64,256]{4,3,2,1,0:T(8,128)}, f32[2,4,2,64,256]{4,3,2,1,0:T(8,128)}, u32[]{:S(2)}, u32[]{:S(2)}) collective-permute-start(f32[2,4,2,64,256]{4,3,2,1,0:T(8,128)} %get-tuple-element.60), channel_id=1, source_target_pairs={{1,0},{2,1},{3,2},{4,3},{5,4},{6,5},{7,6},{9,8},{10,9},{11,10},{12... | collective-permute-start | bytes 3145736 | tf_op jit(solution)/shard_map/ppermute | solution.py:368
  91.3 0.8 copy-done.16
  92.1 1.5 collective-permute-start.15
  93.7 1.1 copy-done.22
  94.7 1.4 collective-permute-start.17
  96.1 0.1 pad_add_fusion.refs_0_.sides_ref
  96.2 1.1 copy-done.1
  97.3 1.1 copy-done.4
  98.4 1.1 copy-done.7
  99.5 1.1 copy-done.9
  100.6 1.2 copy-done.19
  101.9 1.2 copy-done.21
  103.1 1.2 copy-done.23
  104.3 10.3 %apply.2 = (f32[128,2,32,256]{3,2,1,0:T(8,128)}, f32[4,2,128,256]{3,2,1,0:T(8,128)S(1)}, f32[4,2,128,256]{3,2,1,0:T(8,128)S(1)}) custom-call(s32[2]{0:T(128)S(1)} %pad_add_fusion.refs_0_.sides_ref, bf16[256,1536]{1,0:T(8,128)(2,1)S(1)} %copy-done.7, bf16[256,1536]{1,0:T(8,128)(2,1)S(1)} %copy-done.9, f32[2,4,2,64,256]{4,3,2,1,0:T(8,128)S(1)} %copy-done.19, ...), custom_call_target="tpu_custom_call" | custom-call | bytes 3700000 | tf_op jit(solution)/shard_map/apply/pallas_call | solution.py:202
  114.8 2.9 %edges.7 = (f32[2,4,2,64,256]{4,3,2,1,0:T(8,128)S(1)}, f32[2,4,2,64,256]{4,3,2,1,0:T(8,128)S(1)}) custom-call(f32[5,2,64,256]{3,2,1,0:T(8,128)S(1)} %copy-done.4, f32[5,2,64,256]{3,2,1,0:T(8,128)S(1)} %copy-done.1, f32[4,2,64,256]{3,2,1,0:T(8,128)S(1)} %copy-done.15, f32[4,2,64,256]{3,2,1,0:T(8,128)} %collective-permute-done.15.refs_3_.refs_14_, ...), custom_call_target="tpu_custom_call" | custom-call | bytes 1110000 | tf_op jit(solution)/shard_map/edges/pallas_call | solution.py:122
  117.7 1.9 %collective-permute-start.18 = (f32[2,4,2,64,256]{4,3,2,1,0:T(8,128)S(1)}, f32[2,4,2,64,256]{4,3,2,1,0:T(8,128)S(1)}, u32[]{:S(2)}, u32[]{:S(2)}) collective-permute-start(f32[2,4,2,64,256]{4,3,2,1,0:T(8,128)S(1)} %get-tuple-element.73), channel_id=1, source_target_pairs={{0,1},{1,2},{2,3},{3,4},{4,5},{5,6},{6,7},{8,9},{9,10},{10,11},{11... | collective-permute-start | bytes 3145736 | tf_op jit(solution)/shard_map/ppermute | solution.py:368
  119.6 3.9 %collective-permute-start.19 = (f32[2,4,2,64,256]{4,3,2,1,0:T(8,128)S(1)}, f32[2,4,2,64,256]{4,3,2,1,0:T(8,128)S(1)}, u32[]{:S(2)}, u32[]{:S(2)}) collective-permute-start(f32[2,4,2,64,256]{4,3,2,1,0:T(8,128)S(1)} %get-tuple-element.74), channel_id=1, source_target_pairs={{1,0},{2,1},{3,2},{4,3},{5,4},{6,5},{7,6},{9,8},{10,9},{11,10},{12... | collective-permute-start | bytes 3145736 | tf_op jit(solution)/shard_map/ppermute | solution.py:368
  123.5 0.6 collective-permute-start.23
  124.0 0.6 collective-permute-start.22
  124.7 9.1 %collective-permute-done.18.refs_5_ = f32[2,4,2,64,256]{4,3,2,1,0:T(8,128)S(1)} collective-permute-done((f32[2,4,2,64,256]{4,3,2,1,0:T(8,128)S(1)}, f32[2,4,2,64,256]{4,3,2,1,0:T(8,128)S(1)}, u32[]{:S(2)}, u32[]{:S(2)}) %collective-permute-start.18) | collective-permute-done | bytes 1048608 | tf_op jit(solution)/shard_map/ppermute | solution.py:368
  133.8 1.8 %collective-permute-done.19.refs_6_ = f32[2,4,2,64,256]{4,3,2,1,0:T(8,128)S(1)} collective-permute-done((f32[2,4,2,64,256]{4,3,2,1,0:T(8,128)S(1)}, f32[2,4,2,64,256]{4,3,2,1,0:T(8,128)S(1)}, u32[]{:S(2)}, u32[]{:S(2)}) %collective-permute-start.19) | collective-permute-done | bytes 1048608 | tf_op jit(solution)/shard_map/ppermute | solution.py:368
  135.6 11.0 %apply.3 = (f32[128,2,32,256]{3,2,1,0:T(8,128)}, f32[4,2,128,256]{3,2,1,0:T(8,128)S(1)}, f32[4,2,128,256]{3,2,1,0:T(8,128)S(1)}) custom-call(s32[2]{0:T(128)S(1)} %pad_add_fusion.refs_0_.sides_ref, bf16[256,1536]{1,0:T(8,128)(2,1)S(1)} %copy-done.7, bf16[256,1536]{1,0:T(8,128)(2,1)S(1)} %copy-done.9, ...), custom_call_target="tpu_custom_call", output_to_operand_aliasing={{0}: (23, {})} | custom-call | bytes 3700000 | tf_op jit(solution)/shard_map/apply/pallas_call | solution.py:202
  146.6 0.6 collective-permute-start.21
  147.2 0.6 collective-permute-start.20
  147.8 0.1 collective-permute-done.22.got_a
  147.9 2.0 %place.2._ = f32[128,2,32,256]{3,2,1,0:T(8,128)} custom-call(s32[2]{0:T(128)S(1)} %pad_add_fusion.refs_0_.sides_ref, f32[4,2,128,256]{3,2,1,0:T(8,128)S(1)} %collective-permute-done.22.got_a, f32[4,2,128,256]{3,2,1,0:T(8,128)S(1)} %collective-permute-done.23.got_b, f32[128,2,32,256]{3,2,1,0:T(8,128)} %get-tuple-element.82._), custom_call_target="tpu_custom_call", output_to_operand_aliasing={{}: (3, {})} | custom-call | bytes 740000 | tf_op jit(solution)/shard_map/place/pallas_call | solution.py:231
  149.9 22.5 %collective-permute-done.21.got_b = f32[4,2,128,256]{3,2,1,0:T(8,128)S(1)} collective-permute-done((f32[4,2,128,256]{3,2,1,0:T(8,128)S(1)}, f32[4,2,128,256]{3,2,1,0:T(8,128)S(1)}, u32[]{:S(2)}, u32[]{:S(2)}) %collective-permute-start.21) | collective-permute-done | bytes 1048608 | tf_op jit(solution)/shard_map/ppermute | solution.py:317
  172.4 0.8 collective-permute-done.20.got_a
  173.2 2.0 %place.3 = f32[128,2,32,256]{3,2,1,0:T(8,128)} custom-call(s32[2]{0:T(128)S(1)} %pad_add_fusion.refs_0_.sides_ref, f32[4,2,128,256]{3,2,1,0:T(8,128)S(1)} %collective-permute-done.20.got_a, f32[4,2,128,256]{3,2,1,0:T(8,128)S(1)} %collective-permute-done.21.got_b, f32[128,2,32,256]{3,2,1,0:T(8,128)} %place.2._), custom_call_target="tpu_custom_call", output_to_operand_aliasing={{}: (3, {})} | custom-call | bytes 740000 | tf_op jit(solution)/shard_map/place/pallas_call | solution.py:231
  (51 shorter events, 0.1 us)
Async XLA Ops:
  3.5 19.6 %collective-permute-start.1 = (f32[6,2,64,256]{3,2,1,0:T(8,128)}, f32[6,2,64,256]{3,2,1,0:T(8,128)S(1)}, u32[]{:S(2)}, u32[]{:S(2)}) collective-permute-start(f32[6,2,64,256]{3,2,1,0:T(8,128)} %get-tuple-element.48), channel_id=1, source_target_pairs={{0,16},{8,24},{16,0},{24,8},{1,17},{9,25},{17,1},{25,9},{2,18},{10... | collective-permute-start | bytes 2359304 | tf_op jit(solution)/shard_map/ppermute | solution.py:317
  5.1 16.4 %collective-permute-start = (f32[5,2,64,256]{3,2,1,0:T(8,128)}, f32[5,2,64,256]{3,2,1,0:T(8,128)S(1)}, u32[]{:S(2)}, u32[]{:S(2)}) collective-permute-start(f32[5,2,64,256]{3,2,1,0:T(8,128)} %get-tuple-element.47), channel_id=1, source_target_pairs={{0,8},{8,0},{16,24},{24,16},{1,9},{9,1},{17,25},{25,17},{2,10},{10... | collective-permute-start | bytes 1966088 | tf_op jit(solution)/shard_map/ppermute | solution.py:317
  6.6 1.0 copy-start.24
  7.6 1.0 copy-start.25
  8.7 0.7 copy-start.26
  11.4 0.9 copy-start.6
  12.3 0.9 copy-start.8
  23.1 16.1 %collective-permute-start.4 = (f32[5,2,64,256]{3,2,1,0:T(8,128)S(1)}, f32[5,2,64,256]{3,2,1,0:T(8,128)S(1)}, u32[]{:S(2)}, u32[]{:S(2)}) collective-permute-start(f32[5,2,64,256]{3,2,1,0:T(8,128)S(1)} %collective-permute-done.refs_1_.refs_8_), channel_id=1, source_target_pairs={{0,16},{8,24},{16,0},{24,8},{1,17},{9,25},{17,1},{25,9},{2,18},{10... | collective-permute-start | bytes 1966088 | tf_op jit(solution)/shard_map/ppermute | solution.py:317
  24.6 19.8 %collective-permute-start.2 = (f32[6,2,64,256]{3,2,1,0:T(8,128)S(1)}, f32[6,2,64,256]{3,2,1,0:T(8,128)S(1)}, u32[]{:S(2)}, u32[]{:S(2)}) collective-permute-start(f32[6,2,64,256]{3,2,1,0:T(8,128)S(1)} %collective-permute-done.1.refs_5_.refs_3_.refs_13_.refs_17_), channel_id=1, source_target_pairs={{0,8},{8,0},{16,24},{24,16},{1,9},{9,1},{17,25},{25,17},{2,10},{10... | collective-permute-start | bytes 2359304 | tf_op jit(solution)/shard_map/ppermute | solution.py:317
  33.0 25.5 %collective-permute-start.10 = (f32[2,4,2,64,256]{4,3,2,1,0:T(8,128)}, f32[2,4,2,64,256]{4,3,2,1,0:T(8,128)S(1)}, u32[]{:S(2)}, u32[]{:S(2)}) collective-permute-start(f32[2,4,2,64,256]{4,3,2,1,0:T(8,128)} %get-tuple-element.62), channel_id=1, source_target_pairs={{0,1},{1,2},{2,3},{3,4},{4,5},{5,6},{6,7},{8,9},{9,10},{10,11},{11... | collective-permute-start | bytes 3145736 | tf_op jit(solution)/shard_map/ppermute | solution.py:368
  34.9 23.6 %collective-permute-start.11 = (f32[2,4,2,64,256]{4,3,2,1,0:T(8,128)S(1)}, f32[2,4,2,64,256]{4,3,2,1,0:T(8,128)S(1)}, u32[]{:S(2)}, u32[]{:S(2)}) collective-permute-start(f32[2,4,2,64,256]{4,3,2,1,0:T(8,128)S(1)} %get-tuple-element.63), channel_id=1, source_target_pairs={{1,0},{2,1},{3,2},{4,3},{5,4},{6,5},{7,6},{9,8},{10,9},{11,10},{12... | collective-permute-start | bytes 3145736 | tf_op jit(solution)/shard_map/ppermute | solution.py:368
  38.6 29.0 %collective-permute-start.12 = (f32[6,2,64,256]{3,2,1,0:T(8,128)}, f32[6,2,64,256]{3,2,1,0:T(8,128)S(1)}, u32[]{:S(2)}, u32[]{:S(2)}) collective-permute-start(f32[6,2,64,256]{3,2,1,0:T(8,128)} %get-tuple-element.54.refs_4_.refs_2_.refs_11_.refs_15_), channel_id=1, source_target_pairs={{0,8},{8,0},{16,24},{24,16},{1,9},{9,1},{17,25},{25,17},{2,10},{10... | collective-permute-start | bytes 2359304 | tf_op jit(solution)/shard_map/ppermute | solution.py:317
  39.2 28.4 %copy-start = (f32[5,2,64,256]{3,2,1,0:T(8,128)}, f32[5,2,64,256]{3,2,1,0:T(8,128)S(1)}, u32[]{:S(2)}) copy-start(f32[5,2,64,256]{3,2,1,0:T(8,128)S(1)} %collective-permute-done.4.refs_1_.refs_10_) | copy-start | bytes 1966084
  39.2 17.9 %collective-permute-start.8 = (f32[5,2,64,256]{3,2,1,0:T(8,128)}, f32[5,2,64,256]{3,2,1,0:T(8,128)S(1)}, u32[]{:S(2)}, u32[]{:S(2)}) collective-permute-start(f32[5,2,64,256]{3,2,1,0:T(8,128)} %get-tuple-element.46.refs_0_.refs_7_), channel_id=1, source_target_pairs={{0,16},{8,24},{16,0},{24,8},{1,17},{9,25},{17,1},{25,9},{2,18},{10... | collective-permute-start | bytes 1966088 | tf_op jit(solution)/shard_map/ppermute | solution.py:317
  44.4 22.7 %collective-permute-start.5 = (f32[4,2,64,256]{3,2,1,0:T(8,128)}, f32[4,2,64,256]{3,2,1,0:T(8,128)}, u32[]{:S(2)}, u32[]{:S(2)}) collective-permute-start(f32[4,2,64,256]{3,2,1,0:T(8,128)} %get-tuple-element.58), channel_id=1, source_target_pairs={{0,16},{8,24},{16,0},{24,8},{1,17},{9,25},{17,1},{25,9},{2,18},{10... | collective-permute-start | bytes 1572872 | tf_op jit(solution)/shard_map/ppermute | solution.py:317
  57.0 14.6 %copy-start.3 = (f32[5,2,64,256]{3,2,1,0:T(8,128)}, f32[5,2,64,256]{3,2,1,0:T(8,128)S(1)}, u32[]{:S(2)}) copy-start(f32[5,2,64,256]{3,2,1,0:T(8,128)S(1)} %collective-permute-done.8.refs_0_.refs_9_) | copy-start | bytes 1966084
  57.0 20.1 %collective-permute-start.3 = (f32[4,2,64,256]{3,2,1,0:T(8,128)}, f32[4,2,64,256]{3,2,1,0:T(8,128)}, u32[]{:S(2)}, u32[]{:S(2)}) collective-permute-start(f32[4,2,64,256]{3,2,1,0:T(8,128)} %get-tuple-element.53), channel_id=1, source_target_pairs={{0,8},{8,0},{16,24},{24,16},{1,9},{9,1},{17,25},{25,17},{2,10},{10... | collective-permute-start | bytes 1572872 | tf_op jit(solution)/shard_map/ppermute | solution.py:317
  58.5 32.8 %copy-start.18 = (f32[2,4,2,64,256]{4,3,2,1,0:T(8,128)}, f32[2,4,2,64,256]{4,3,2,1,0:T(8,128)S(1)}, u32[]{:S(2)}) copy-start(f32[2,4,2,64,256]{4,3,2,1,0:T(8,128)S(1)} %collective-permute-done.10.refs_3_) | copy-start | bytes 3145732
  58.5 35.1 %copy-start.20 = (f32[2,4,2,64,256]{4,3,2,1,0:T(8,128)}, f32[2,4,2,64,256]{4,3,2,1,0:T(8,128)S(1)}, u32[]{:S(2)}) copy-start(f32[2,4,2,64,256]{4,3,2,1,0:T(8,128)S(1)} %collective-permute-done.11.refs_4_) | copy-start | bytes 3145732
  67.0 19.6 %collective-permute-start.9 = (f32[4,2,64,256]{3,2,1,0:T(8,128)}, f32[4,2,64,256]{3,2,1,0:T(8,128)S(1)}, u32[]{:S(2)}, u32[]{:S(2)}) collective-permute-start(f32[4,2,64,256]{3,2,1,0:T(8,128)} %get-tuple-element.61.refs_2_.refs_11_), channel_id=1, source_target_pairs={{0,16},{8,24},{16,0},{24,8},{1,17},{9,25},{17,1},{25,9},{2,18},{10... | collective-permute-start | bytes 1572872 | tf_op jit(solution)/shard_map/ppermute | solution.py:317
  71.6 22.1 %collective-permute-start.13 = (f32[2,4,2,64,256]{4,3,2,1,0:T(8,128)S(1)}, f32[2,4,2,64,256]{4,3,2,1,0:T(8,128)S(1)}, u32[]{:S(2)}, u32[]{:S(2)}) collective-permute-start(f32[2,4,2,64,256]{4,3,2,1,0:T(8,128)S(1)} %get-tuple-element.65), channel_id=1, source_target_pairs={{0,1},{1,2},{2,3},{3,4},{4,5},{5,6},{6,7},{8,9},{9,10},{10,11},{11... | collective-permute-start | bytes 3145736 | tf_op jit(solution)/shard_map/ppermute | solution.py:368
  73.5 22.7 %collective-permute-start.14 = (f32[2,4,2,64,256]{4,3,2,1,0:T(8,128)}, f32[2,4,2,64,256]{4,3,2,1,0:T(8,128)}, u32[]{:S(2)}, u32[]{:S(2)}) collective-permute-start(f32[2,4,2,64,256]{4,3,2,1,0:T(8,128)} %get-tuple-element.66), channel_id=1, source_target_pairs={{1,0},{2,1},{3,2},{4,3},{5,4},{6,5},{7,6},{9,8},{10,9},{11,10},{12... | collective-permute-start | bytes 3145736 | tf_op jit(solution)/shard_map/ppermute | solution.py:368
  77.2 14.1 %collective-permute-start.16 = (f32[4,2,64,256]{3,2,1,0:T(8,128)}, f32[4,2,64,256]{3,2,1,0:T(8,128)S(1)}, u32[]{:S(2)}, u32[]{:S(2)}) collective-permute-start(f32[4,2,64,256]{3,2,1,0:T(8,128)} %get-tuple-element.71.refs_6_.refs_19_), channel_id=1, source_target_pairs={{0,8},{8,0},{16,24},{24,16},{1,9},{9,1},{17,25},{25,17},{2,10},{10... | collective-permute-start | bytes 1572872 | tf_op jit(solution)/shard_map/ppermute | solution.py:317
  78.7 1.0 copy-start.10
  79.8 1.0 copy-start.12
  80.8 54.7 %copy-start.11 = (f32[4,2,64,256]{3,2,1,0:T(8,128)S(1)}, f32[4,2,64,256]{3,2,1,0:T(8,128)}, u32[]{:S(2)}) copy-start(f32[4,2,64,256]{3,2,1,0:T(8,128)} %get-tuple-element.61.refs_2_.refs_11_) | copy-start | bytes 1572868
  84.7 29.9 %collective-permute-start.6 = (f32[2,4,2,64,256]{4,3,2,1,0:T(8,128)}, f32[2,4,2,64,256]{4,3,2,1,0:T(8,128)}, u32[]{:S(2)}, u32[]{:S(2)}) collective-permute-start(f32[2,4,2,64,256]{4,3,2,1,0:T(8,128)} %get-tuple-element.59), channel_id=1, source_target_pairs={{0,1},{1,2},{2,3},{3,4},{4,5},{5,6},{6,7},{8,9},{9,10},{10,11},{11... | collective-permute-start | bytes 3145736 | tf_op jit(solution)/shard_map/ppermute | solution.py:368
  86.7 0.8 copy-start.14
  87.5 27.2 %collective-permute-start.7 = (f32[2,4,2,64,256]{4,3,2,1,0:T(8,128)}, f32[2,4,2,64,256]{4,3,2,1,0:T(8,128)}, u32[]{:S(2)}, u32[]{:S(2)}) collective-permute-start(f32[2,4,2,64,256]{4,3,2,1,0:T(8,128)} %get-tuple-element.60), channel_id=1, source_target_pairs={{1,0},{2,1},{3,2},{4,3},{5,4},{6,5},{7,6},{9,8},{10,9},{11,10},{12... | collective-permute-start | bytes 3145736 | tf_op jit(solution)/shard_map/ppermute | solution.py:368
  91.3 0.8 copy-start.16
  92.1 22.6 %collective-permute-start.15 = (f32[4,2,64,256]{3,2,1,0:T(8,128)}, f32[4,2,64,256]{3,2,1,0:T(8,128)}, u32[]{:S(2)}, u32[]{:S(2)}) collective-permute-start(f32[4,2,64,256]{3,2,1,0:T(8,128)} %collective-permute-done.3.refs_3_.refs_12_), channel_id=1, source_target_pairs={{0,16},{8,24},{16,0},{24,8},{1,17},{9,25},{17,1},{25,9},{2,18},{10... | collective-permute-start | bytes 1572872 | tf_op jit(solution)/shard_map/ppermute | solution.py:317
  93.7 1.1 copy-start.22
  94.7 20.0 %collective-permute-start.17 = (f32[4,2,64,256]{3,2,1,0:T(8,128)}, f32[4,2,64,256]{3,2,1,0:T(8,128)}, u32[]{:S(2)}, u32[]{:S(2)}) collective-permute-start(f32[4,2,64,256]{3,2,1,0:T(8,128)} %collective-permute-done.5.refs_7_.refs_21_), channel_id=1, source_target_pairs={{0,8},{8,0},{16,24},{24,16},{1,9},{9,1},{17,25},{25,17},{2,10},{10... | collective-permute-start | bytes 1572872 | tf_op jit(solution)/shard_map/ppermute | solution.py:317
  96.2 1.1 copy-start.1
  97.3 1.1 copy-start.4
  98.4 1.1 copy-start.7
  99.5 1.1 copy-start.9
  100.6 1.2 copy-start.19
  101.9 1.2 copy-start.21
  103.1 1.2 copy-start.23
  104.3 10.4 %copy-start.15 = (f32[4,2,64,256]{3,2,1,0:T(8,128)S(1)}, f32[4,2,64,256]{3,2,1,0:T(8,128)}, u32[]{:S(2)}) copy-start(f32[4,2,64,256]{3,2,1,0:T(8,128)} %copy-done.14) | copy-start | bytes 1572868
  104.3 10.4 %copy-start.17 = (f32[4,2,64,256]{3,2,1,0:T(8,128)S(1)}, f32[4,2,64,256]{3,2,1,0:T(8,128)}, u32[]{:S(2)}) copy-start(f32[4,2,64,256]{3,2,1,0:T(8,128)} %copy-done.16) | copy-start | bytes 1572868
  104.3 31.2 %copy-start.2 = (f32[5,2,64,256]{3,2,1,0:T(8,128)S(1)}, f32[5,2,64,256]{3,2,1,0:T(8,128)}, u32[]{:S(2)}) copy-start(f32[5,2,64,256]{3,2,1,0:T(8,128)} %copy-done) | copy-start | bytes 1966084
  104.3 31.2 %copy-start.5 = (f32[5,2,64,256]{3,2,1,0:T(8,128)S(1)}, f32[5,2,64,256]{3,2,1,0:T(8,128)}, u32[]{:S(2)}) copy-start(f32[5,2,64,256]{3,2,1,0:T(8,128)} %copy-done.3) | copy-start | bytes 1966084
  104.3 31.2 %copy-start.13 = (f32[4,2,64,256]{3,2,1,0:T(8,128)S(1)}, f32[4,2,64,256]{3,2,1,0:T(8,128)}, u32[]{:S(2)}) copy-start(f32[4,2,64,256]{3,2,1,0:T(8,128)} %get-tuple-element.71.refs_6_.refs_19_) | copy-start | bytes 1572868
  117.7 16.1 %collective-permute-start.18 = (f32[2,4,2,64,256]{4,3,2,1,0:T(8,128)S(1)}, f32[2,4,2,64,256]{4,3,2,1,0:T(8,128)S(1)}, u32[]{:S(2)}, u32[]{:S(2)}) collective-permute-start(f32[2,4,2,64,256]{4,3,2,1,0:T(8,128)S(1)} %get-tuple-element.73), channel_id=1, source_target_pairs={{0,1},{1,2},{2,3},{3,4},{4,5},{5,6},{6,7},{8,9},{9,10},{10,11},{11... | collective-permute-start | bytes 3145736 | tf_op jit(solution)/shard_map/ppermute | solution.py:368
  119.6 15.9 %collective-permute-start.19 = (f32[2,4,2,64,256]{4,3,2,1,0:T(8,128)S(1)}, f32[2,4,2,64,256]{4,3,2,1,0:T(8,128)S(1)}, u32[]{:S(2)}, u32[]{:S(2)}) collective-permute-start(f32[2,4,2,64,256]{4,3,2,1,0:T(8,128)S(1)} %get-tuple-element.74), channel_id=1, source_target_pairs={{1,0},{2,1},{3,2},{4,3},{5,4},{6,5},{7,6},{9,8},{10,9},{11,10},{12... | collective-permute-start | bytes 3145736 | tf_op jit(solution)/shard_map/ppermute | solution.py:368
  123.5 24.3 %collective-permute-start.23 = (f32[4,2,128,256]{3,2,1,0:T(8,128)S(1)}, f32[4,2,128,256]{3,2,1,0:T(8,128)S(1)}, u32[]{:S(2)}, u32[]{:S(2)}) collective-permute-start(f32[4,2,128,256]{3,2,1,0:T(8,128)S(1)} %get-tuple-element.81), channel_id=1, source_target_pairs={{0,16},{8,24},{16,0},{24,8},{1,17},{9,25},{17,1},{25,9},{2,18},{10... | collective-permute-start | bytes 3145736 | tf_op jit(solution)/shard_map/ppermute | solution.py:317
  124.0 23.9 %collective-permute-start.22 = (f32[4,2,128,256]{3,2,1,0:T(8,128)S(1)}, f32[4,2,128,256]{3,2,1,0:T(8,128)S(1)}, u32[]{:S(2)}, u32[]{:S(2)}) collective-permute-start(f32[4,2,128,256]{3,2,1,0:T(8,128)S(1)} %get-tuple-element.80), channel_id=1, source_target_pairs={{0,8},{8,0},{16,24},{24,16},{1,9},{9,1},{17,25},{25,17},{2,10},{10... | collective-permute-start | bytes 3145736 | tf_op jit(solution)/shard_map/ppermute | solution.py:317
  146.6 25.8 %collective-permute-start.21 = (f32[4,2,128,256]{3,2,1,0:T(8,128)S(1)}, f32[4,2,128,256]{3,2,1,0:T(8,128)S(1)}, u32[]{:S(2)}, u32[]{:S(2)}) collective-permute-start(f32[4,2,128,256]{3,2,1,0:T(8,128)S(1)} %get-tuple-element.79), channel_id=1, source_target_pairs={{0,16},{8,24},{16,0},{24,8},{1,17},{9,25},{17,1},{25,9},{2,18},{10... | collective-permute-start | bytes 3145736 | tf_op jit(solution)/shard_map/ppermute | solution.py:317
  147.2 26.0 %collective-permute-start.20 = (f32[4,2,128,256]{3,2,1,0:T(8,128)S(1)}, f32[4,2,128,256]{3,2,1,0:T(8,128)S(1)}, u32[]{:S(2)}, u32[]{:S(2)}) collective-permute-start(f32[4,2,128,256]{3,2,1,0:T(8,128)S(1)} %get-tuple-element.77), channel_id=1, source_target_pairs={{0,8},{8,0},{16,24},{24,16},{1,9},{9,1},{17,25},{25,17},{2,10},{10... | collective-permute-start | bytes 3145736 | tf_op jit(solution)/shard_map/ppermute | solution.py:317

commit v9 on v8

--- a/solution.py
+++ b/solution.py
@@ -81,13 +81,15 @@
 def pick(chunk, kinds, residual, step_ratio, bits, depth):
     steps, planes, _, rows_y = residual.shape
     counts = [len(chunk_rows(stream, chunk, depth)) for stream, _ in kinds]
+    first = chunk == 0 and kinds[0][1]
+    limit = (56 if first else 8) * 2**20
     outs = pl.pallas_call(
         functools.partial(pick_kernel, chunk, depth, kinds, bits),
         out_shape=[jax.ShapeDtypeStruct((c, planes, steps, rows_y), jnp.float32) for c in counts],
         in_specs=[VMEM, HBM],
         out_specs=[VMEM] * len(kinds),
         scratch_shapes=[pltpu.SemaphoreType.DMA((sum(counts) * planes,))],
-        compiler_params=pltpu.CompilerParams(vmem_limit_bytes=56 * 2**20),
+        compiler_params=pltpu.CompilerParams(vmem_limit_bytes=limit),
         cost_estimate=cost(5),
         name="pick",
     )(step_ratio.reshape(1, steps), residual)

time: 177 us -> 177 us (level)
  Pallas kernels: 52.8 us -> 47.5 us
  waiting for transfers between devices: 64.3 us -> 67.6 us
  local copies, waits for them, and re-layouts: 17.4 us -> 19.4 us
    pallas_call x3, Pallas kernels: 11.2 us -> 7.21 us  [pick(): pl.pallas_call(functools.partial(pick_kernel, chunk, depth, kinds, bits),...]
    ppermute x16, waiting for transfers between devices: 53.4 us -> 56.6 us  [swap(): return lax.ppermute(data, 'tm', [(i, i ^ bit) for i in range(count)])]
    unnamed x54 -> x64, local copies, waits for them, and re-layouts: 17.4 us -> 19.4 us
  transfers between devices with their start and end apart: 24 -> 24, of which waited for: 9 -> 11; matrix products, arithmetic and copies ran while one was open for 0% -> 0% of each run, Pallas kernels for 25% -> 22%
where the time goes in v9:
time: 177 us; the launch traced here: 175 us
  waiting for transfers between devices  67.6 us (38%)
  Pallas kernels  47.5 us (27%)
  starting transfers between devices  40 us (23%)
  local copies, waits for them, and re-layouts  19.4 us (11%)
    ppermute x16, waiting for transfers between devices, swap(): return lax.ppermute(data, 'tm', [(i, i ^ bit) for i in range(count)])  56.6 us
    pallas_call x2, Pallas kernels, apply(): pl.pallas_call(body, out_shape=[jax.ShapeDtypeStruct(shape, jnp.float32),...  21 us
    unnamed x64, local copies, waits for them, and re-layouts  19.4 us
    ppermute x16, starting transfers between devices, swap(): return lax.ppermute(data, 'tm', [(i, i ^ bit) for i in range(count)])  17.4 us
    ppermute x4, starting transfers between devices, beside(): lax.ppermute(down, 'space', downward)  15 us
    pallas_call x4, Pallas kernels, edges(): pl.pallas_call(functools.partial(edge_kernel, chunk, depth, groups), out_...  13.4 us
    ppermute x4, waiting for transfers between devices, beside(): lax.ppermute(up, 'space', upward)  9.22 us
    ppermute x4, starting transfers between devices, beside(): lax.ppermute(up, 'space', upward)  7.68 us
  transfers between devices with their start and end apart: 24, of which 11 were waited for; matrix products, arithmetic and copies ran while one was open for 0% of the time, Pallas kernels for 22%

profile of v9, /device:TPU:8, one launch (start us, length us, event | category | flops | bytes accessed | tf_op | source)
XLA Modules:
  0.0 175.2 jit_solution(7171507114668691426)
XLA Ops:
  0.0 3.6 %pick.4 = (f32[5,2,64,256]{3,2,1,0:T(8,128)}, f32[6,2,64,256]{3,2,1,0:T(8,128)}) custom-call(s32[1,64]{1,0:T(1,128)} %bitcast.5, f32[64,2,32,256]{3,2,1,0:T(8,128)} %in_ref.4), custom_call_target="tpu_custom_call" | custom-call | bytes 1850000 | tf_op jit(solution)/shard_map/pick/pallas_call | solution.py:86
  3.6 1.6 collective-permute-start.1
  5.2 1.5 collective-permute-start
  6.7 1.0 copy-done.27
  7.7 1.0 copy-done.28
  8.7 0.7 copy-done.31
  9.4 2.0 %maps.1 = (bf16[256,1536]{1,0:T(8,128)(2,1)S(1)}, bf16[256,1536]{1,0:T(8,128)(2,1)S(1)}) custom-call(s32[1]{0:T(128)} %bitcast.2.me_ref, f32[2,256,256]{2,1,0:T(8,128)S(1)} %copy-done.27, f32[2,256,256]{2,1,0:T(8,128)S(1)} %copy-done.28, f32[2,256]{1,0:T(2,128)S(1)} %copy-done.31), custom_call_target="tpu_custom_call" | custom-call | bytes 740000 | tf_op jit(solution)/shard_map/maps/pallas_call | solution.py:297
  11.5 10.2 %collective-permute-done.refs_1_.refs_8_ = f32[5,2,64,256]{3,2,1,0:T(8,128)} collective-permute-done((f32[5,2,64,256]{3,2,1,0:T(8,128)}, f32[5,2,64,256]{3,2,1,0:T(8,128)}, u32[]{:S(2)}, u32[]{:S(2)}) %collective-permute-start) | collective-permute-done | bytes 655392 | tf_op jit(solution)/shard_map/ppermute | solution.py:319
  21.7 1.5 collective-permute-done.1.refs_5_.refs_3_.refs_13_.refs_17_
  23.1 1.5 collective-permute-start.4
  24.7 1.5 collective-permute-start.2
  26.1 2.2 %copy-done = f32[64,2,32,256]{3,2,1,0:T(8,128)S(1)} copy-done((f32[64,2,32,256]{3,2,1,0:T(8,128)S(1)}, f32[64,2,32,256]{3,2,1,0:T(8,128)}, u32[]{:S(2)}) %copy-start) | copy-done | bytes 4194328
  28.3 0.7 copy-done.29
  29.0 1.5 pick.3
  30.5 2.4 %edges.5 = (f32[2,4,2,64,256]{4,3,2,1,0:T(8,128)S(1)}, f32[2,4,2,64,256]{4,3,2,1,0:T(8,128)S(1)}) custom-call(f32[5,2,64,256]{3,2,1,0:T(8,128)S(1)} %get-tuple-element.46.refs_0_.refs_7_, f32[5,2,64,256]{3,2,1,0:T(8,128)} %collective-permute-done.refs_1_.refs_8_, f32[6,2,64,256]{3,2,1,0:T(8,128)S(1)} %get-tuple-element.54.refs_4_.refs_2_.refs_11_.refs_15_, ...), custom_call_target="tpu_custom_call" | custom-call | bytes 1110000 | tf_op jit(solution)/shard_map/edges/pallas_call | solution.py:124
  32.9 1.9 %collective-permute-start.10 = (f32[2,4,2,64,256]{4,3,2,1,0:T(8,128)S(1)}, f32[2,4,2,64,256]{4,3,2,1,0:T(8,128)S(1)}, u32[]{:S(2)}, u32[]{:S(2)}) collective-permute-start(f32[2,4,2,64,256]{4,3,2,1,0:T(8,128)S(1)} %get-tuple-element.62), channel_id=1, source_target_pairs={{0,1},{1,2},{2,3},{3,4},{4,5},{5,6},{6,7},{8,9},{9,10},{10,11},{11... | collective-permute-start | bytes 3145736 | tf_op jit(solution)/shard_map/ppermute | solution.py:370
  34.8 3.6 %collective-permute-start.11 = (f32[2,4,2,64,256]{4,3,2,1,0:T(8,128)S(1)}, f32[2,4,2,64,256]{4,3,2,1,0:T(8,128)S(1)}, u32[]{:S(2)}, u32[]{:S(2)}) collective-permute-start(f32[2,4,2,64,256]{4,3,2,1,0:T(8,128)S(1)} %get-tuple-element.63), channel_id=1, source_target_pairs={{1,0},{2,1},{3,2},{4,3},{5,4},{6,5},{7,6},{9,8},{10,9},{11,10},{12... | collective-permute-start | bytes 3145736 | tf_op jit(solution)/shard_map/ppermute | solution.py:370
  38.5 0.6 collective-permute-start.12
  39.1 1.4 collective-permute-start.8
  40.5 2.1 %pick.5 = (f32[4,2,64,256]{3,2,1,0:T(8,128)S(1)}, f32[4,2,64,256]{3,2,1,0:T(8,128)S(1)}, f32[4,2,64,256]{3,2,1,0:T(8,128)S(1)}, f32[4,2,64,256]{3,2,1,0:T(8,128)S(1)}) custom-call(s32[1,64]{1,0:T(1,128)S(1)} %bitcast.7, f32[64,2,32,256]{3,2,1,0:T(8,128)S(1)} %copy-done.1), custom_call_target="tpu_custom_call" | custom-call | bytes 1850000 | tf_op jit(solution)/shard_map/pick/pallas_call | solution.py:86
  42.7 1.8 %collective-permute-done.2.refs_3_.refs_14_.refs_5_.refs_18_ = f32[6,2,64,256]{3,2,1,0:T(8,128)S(1)} collective-permute-done((f32[6,2,64,256]{3,2,1,0:T(8,128)S(1)}, f32[6,2,64,256]{3,2,1,0:T(8,128)S(1)}, u32[]{:S(2)}, u32[]{:S(2)}) %collective-permute-start.2) | collective-permute-done | bytes 786464 | tf_op jit(solution)/shard_map/ppermute | solution.py:319
  44.4 0.5 collective-permute-start.5
  44.9 11.8 %collective-permute-done.8.refs_0_.refs_9_ = f32[5,2,64,256]{3,2,1,0:T(8,128)S(1)} collective-permute-done((f32[5,2,64,256]{3,2,1,0:T(8,128)S(1)}, f32[5,2,64,256]{3,2,1,0:T(8,128)S(1)}, u32[]{:S(2)}, u32[]{:S(2)}) %collective-permute-start.8) | collective-permute-done | bytes 655392 | tf_op jit(solution)/shard_map/ppermute | solution.py:319
  56.7 1.5 collective-permute-start.3
  58.2 1.0 copy-done.21
  59.2 1.0 copy-done.23
  60.2 6.5 %collective-permute-done.5.refs_7_.refs_21_ = f32[4,2,64,256]{3,2,1,0:T(8,128)} collective-permute-done((f32[4,2,64,256]{3,2,1,0:T(8,128)S(1)}, f32[4,2,64,256]{3,2,1,0:T(8,128)}, u32[]{:S(2)}, u32[]{:S(2)}) %collective-permute-start.5) | collective-permute-done | bytes 524320 | tf_op jit(solution)/shard_map/ppermute | solution.py:319
  66.7 0.5 collective-permute-start.9
  67.3 4.0 %edges.6 = (f32[2,4,2,64,256]{4,3,2,1,0:T(8,128)S(1)}, f32[2,4,2,64,256]{4,3,2,1,0:T(8,128)}) custom-call(f32[5,2,64,256]{3,2,1,0:T(8,128)S(1)} %collective-permute-done.8.refs_0_.refs_9_, f32[5,2,64,256]{3,2,1,0:T(8,128)S(1)} %collective-permute-done.4.refs_1_.refs_10_, f32[6,2,64,256]{3,2,1,0:T(8,128)S(1)} %collective-permute-done.12.refs_2_.refs_12_.refs_4_.refs_16_, ...), custom_call_target="tpu_custom_call" | custom-call | bytes 1110000 | tf_op jit(solution)/shard_map/edges/pallas_call | solution.py:124
  71.3 1.9 %collective-permute-start.13 = (f32[2,4,2,64,256]{4,3,2,1,0:T(8,128)S(1)}, f32[2,4,2,64,256]{4,3,2,1,0:T(8,128)S(1)}, u32[]{:S(2)}, u32[]{:S(2)}) collective-permute-start(f32[2,4,2,64,256]{4,3,2,1,0:T(8,128)S(1)} %get-tuple-element.65), channel_id=1, source_target_pairs={{0,1},{1,2},{2,3},{3,4},{4,5},{5,6},{6,7},{8,9},{9,10},{10,11},{11... | collective-permute-start | bytes 3145736 | tf_op jit(solution)/shard_map/ppermute | solution.py:370
  73.2 3.6 %collective-permute-start.14 = (f32[2,4,2,64,256]{4,3,2,1,0:T(8,128)}, f32[2,4,2,64,256]{4,3,2,1,0:T(8,128)}, u32[]{:S(2)}, u32[]{:S(2)}) collective-permute-start(f32[2,4,2,64,256]{4,3,2,1,0:T(8,128)} %get-tuple-element.66), channel_id=1, source_target_pairs={{1,0},{2,1},{3,2},{4,3},{5,4},{6,5},{7,6},{9,8},{10,9},{11,10},{12... | collective-permute-start | bytes 3145736 | tf_op jit(solution)/shard_map/ppermute | solution.py:370
  76.9 1.6 collective-permute-start.16
  78.4 4.1 %edges.4 = (f32[2,4,2,64,256]{4,3,2,1,0:T(8,128)}, f32[2,4,2,64,256]{4,3,2,1,0:T(8,128)}) custom-call(f32[5,2,64,256]{3,2,1,0:T(8,128)S(1)} %get-tuple-element.46.refs_0_.refs_7_, f32[5,2,64,256]{3,2,1,0:T(8,128)} %collective-permute-done.refs_1_.refs_8_, f32[4,2,64,256]{3,2,1,0:T(8,128)S(1)} %get-tuple-element.61.refs_2_.refs_11_, ...), custom_call_target="tpu_custom_call" | custom-call | bytes 1110000 | tf_op jit(solution)/shard_map/edges/pallas_call | solution.py:124
  82.6 1.9 %collective-permute-start.6 = (f32[2,4,2,64,256]{4,3,2,1,0:T(8,128)}, f32[2,4,2,64,256]{4,3,2,1,0:T(8,128)}, u32[]{:S(2)}, u32[]{:S(2)}) collective-permute-start(f32[2,4,2,64,256]{4,3,2,1,0:T(8,128)} %get-tuple-element.59), channel_id=1, source_target_pairs={{0,1},{1,2},{2,3},{3,4},{4,5},{5,6},{6,7},{8,9},{9,10},{10,11},{11... | collective-permute-start | bytes 3145736 | tf_op jit(solution)/shard_map/ppermute | solution.py:370
  84.5 0.8 copy-done.17
  85.3 3.8 %collective-permute-start.7 = (f32[2,4,2,64,256]{4,3,2,1,0:T(8,128)}, f32[2,4,2,64,256]{4,3,2,1,0:T(8,128)}, u32[]{:S(2)}, u32[]{:S(2)}) collective-permute-start(f32[2,4,2,64,256]{4,3,2,1,0:T(8,128)} %get-tuple-element.60), channel_id=1, source_target_pairs={{1,0},{2,1},{3,2},{4,3},{5,4},{6,5},{7,6},{9,8},{10,9},{11,10},{12... | collective-permute-start | bytes 3145736 | tf_op jit(solution)/shard_map/ppermute | solution.py:370
  89.1 1.6 collective-permute-done.16.refs_6_.refs_20_
  90.7 0.8 copy-done.19
  91.5 1.5 collective-permute-start.15
  93.0 1.0 copy-done.25
  94.1 1.5 collective-permute-start.17
  95.7 1.1 copy-done.3
  96.7 1.1 copy-done.5
  97.8 1.1 copy-done.7
  98.9 1.1 copy-done.10
  100.1 1.1 copy-done.12
  101.2 1.2 copy-done.22
  102.4 1.2 copy-done.24
  103.6 1.2 copy-done.26
  104.9 10.1 %apply.2 = (f32[128,2,32,256]{3,2,1,0:T(8,128)}, f32[4,2,128,256]{3,2,1,0:T(8,128)S(1)}, f32[4,2,128,256]{3,2,1,0:T(8,128)S(1)}) custom-call(s32[2]{0:T(128)S(1)} %pad_add_fusion.refs_0_.sides_ref, bf16[256,1536]{1,0:T(8,128)(2,1)S(1)} %copy-done.10, bf16[256,1536]{1,0:T(8,128)(2,1)S(1)} %copy-done.12, f32[2,4,2,64,256]{4,3,2,1,0:T(8,128)S(1)} %copy-done.22, ...), custom_call_target="tpu_custom_call" | custom-call | bytes 3700000 | tf_op jit(solution)/shard_map/apply/pallas_call | solution.py:204
  115.1 2.9 %edges.7 = (f32[2,4,2,64,256]{4,3,2,1,0:T(8,128)S(1)}, f32[2,4,2,64,256]{4,3,2,1,0:T(8,128)S(1)}) custom-call(f32[5,2,64,256]{3,2,1,0:T(8,128)S(1)} %copy-done.7, f32[5,2,64,256]{3,2,1,0:T(8,128)S(1)} %copy-done.3, f32[4,2,64,256]{3,2,1,0:T(8,128)S(1)} %copy-done.18, f32[4,2,64,256]{3,2,1,0:T(8,128)} %collective-permute-done.15.refs_3_.refs_14_, ...), custom_call_target="tpu_custom_call" | custom-call | bytes 1110000 | tf_op jit(solution)/shard_map/edges/pallas_call | solution.py:124
  118.0 1.9 %collective-permute-start.18 = (f32[2,4,2,64,256]{4,3,2,1,0:T(8,128)S(1)}, f32[2,4,2,64,256]{4,3,2,1,0:T(8,128)S(1)}, u32[]{:S(2)}, u32[]{:S(2)}) collective-permute-start(f32[2,4,2,64,256]{4,3,2,1,0:T(8,128)S(1)} %get-tuple-element.73), channel_id=1, source_target_pairs={{0,1},{1,2},{2,3},{3,4},{4,5},{5,6},{6,7},{8,9},{9,10},{10,11},{11... | collective-permute-start | bytes 3145736 | tf_op jit(solution)/shard_map/ppermute | solution.py:370
  119.9 3.9 %collective-permute-start.19 = (f32[2,4,2,64,256]{4,3,2,1,0:T(8,128)S(1)}, f32[2,4,2,64,256]{4,3,2,1,0:T(8,128)S(1)}, u32[]{:S(2)}, u32[]{:S(2)}) collective-permute-start(f32[2,4,2,64,256]{4,3,2,1,0:T(8,128)S(1)} %get-tuple-element.74), channel_id=1, source_target_pairs={{1,0},{2,1},{3,2},{4,3},{5,4},{6,5},{7,6},{9,8},{10,9},{11,10},{12... | collective-permute-start | bytes 3145736 | tf_op jit(solution)/shard_map/ppermute | solution.py:370
  123.8 0.6 collective-permute-start.23
  124.3 0.5 collective-permute-start.22
  124.9 9.2 %collective-permute-done.18.refs_5_ = f32[2,4,2,64,256]{4,3,2,1,0:T(8,128)S(1)} collective-permute-done((f32[2,4,2,64,256]{4,3,2,1,0:T(8,128)S(1)}, f32[2,4,2,64,256]{4,3,2,1,0:T(8,128)S(1)}, u32[]{:S(2)}, u32[]{:S(2)}) %collective-permute-start.18) | collective-permute-done | bytes 1048608 | tf_op jit(solution)/shard_map/ppermute | solution.py:370
  134.1 1.8 %collective-permute-done.19.refs_6_ = f32[2,4,2,64,256]{4,3,2,1,0:T(8,128)S(1)} collective-permute-done((f32[2,4,2,64,256]{4,3,2,1,0:T(8,128)S(1)}, f32[2,4,2,64,256]{4,3,2,1,0:T(8,128)S(1)}, u32[]{:S(2)}, u32[]{:S(2)}) %collective-permute-start.19) | collective-permute-done | bytes 1048608 | tf_op jit(solution)/shard_map/ppermute | solution.py:370
  135.9 10.9 %apply.3 = (f32[128,2,32,256]{3,2,1,0:T(8,128)}, f32[4,2,128,256]{3,2,1,0:T(8,128)S(1)}, f32[4,2,128,256]{3,2,1,0:T(8,128)S(1)}) custom-call(s32[2]{0:T(128)S(1)} %pad_add_fusion.refs_0_.sides_ref, bf16[256,1536]{1,0:T(8,128)(2,1)S(1)} %copy-done.10, bf16[256,1536]{1,0:T(8,128)(2,1)S(1)} %copy-done.12, ...), custom_call_target="tpu_custom_call", output_to_operand_aliasing={{0}: (23, {})} | custom-call | bytes 3700000 | tf_op jit(solution)/shard_map/apply/pallas_call | solution.py:204
  146.7 0.6 collective-permute-start.21
  147.3 0.5 collective-permute-start.20
  147.8 0.6 collective-permute-done.22.got_a
  148.4 2.0 %place.2._ = f32[128,2,32,256]{3,2,1,0:T(8,128)} custom-call(s32[2]{0:T(128)S(1)} %pad_add_fusion.refs_0_.sides_ref, f32[4,2,128,256]{3,2,1,0:T(8,128)S(1)} %collective-permute-done.22.got_a, f32[4,2,128,256]{3,2,1,0:T(8,128)S(1)} %collective-permute-done.23.got_b, f32[128,2,32,256]{3,2,1,0:T(8,128)} %get-tuple-element.82._), custom_call_target="tpu_custom_call", output_to_operand_aliasing={{}: (3, {})} | custom-call | bytes 740000 | tf_op jit(solution)/shard_map/place/pallas_call | solution.py:233
  150.4 22.3 %collective-permute-done.21.got_b = f32[4,2,128,256]{3,2,1,0:T(8,128)S(1)} collective-permute-done((f32[4,2,128,256]{3,2,1,0:T(8,128)S(1)}, f32[4,2,128,256]{3,2,1,0:T(8,128)S(1)}, u32[]{:S(2)}, u32[]{:S(2)}) %collective-permute-start.21) | collective-permute-done | bytes 1048608 | tf_op jit(solution)/shard_map/ppermute | solution.py:319
  173.0 2.0 %place.3 = f32[128,2,32,256]{3,2,1,0:T(8,128)} custom-call(s32[2]{0:T(128)S(1)} %pad_add_fusion.refs_0_.sides_ref, f32[4,2,128,256]{3,2,1,0:T(8,128)S(1)} %collective-permute-done.20.got_a, f32[4,2,128,256]{3,2,1,0:T(8,128)S(1)} %collective-permute-done.21.got_b, f32[128,2,32,256]{3,2,1,0:T(8,128)} %place.2._), custom_call_target="tpu_custom_call", output_to_operand_aliasing={{}: (3, {})} | custom-call | bytes 740000 | tf_op jit(solution)/shard_map/place/pallas_call | solution.py:233
  (61 shorter events, 0.5 us)
Async XLA Ops:
  0.0 40.5 %copy-start.30 = (s32[64]{0:T(128)S(1)}, s32[64]{0:T(128)}, u32[]{:S(2)}) copy-start(s32[64]{0:T(128)} %param.6) | copy-start | bytes 772
  3.6 19.6 %collective-permute-start.1 = (f32[6,2,64,256]{3,2,1,0:T(8,128)}, f32[6,2,64,256]{3,2,1,0:T(8,128)S(1)}, u32[]{:S(2)}, u32[]{:S(2)}) collective-permute-start(f32[6,2,64,256]{3,2,1,0:T(8,128)} %get-tuple-element.48), channel_id=1, source_target_pairs={{0,16},{8,24},{16,0},{24,8},{1,17},{9,25},{17,1},{25,9},{2,18},{10... | collective-permute-start | bytes 2359304 | tf_op jit(solution)/shard_map/ppermute | solution.py:319
  5.2 16.5 %collective-permute-start = (f32[5,2,64,256]{3,2,1,0:T(8,128)}, f32[5,2,64,256]{3,2,1,0:T(8,128)}, u32[]{:S(2)}, u32[]{:S(2)}) collective-permute-start(f32[5,2,64,256]{3,2,1,0:T(8,128)} %get-tuple-element.47), channel_id=1, source_target_pairs={{0,8},{8,0},{16,24},{24,16},{1,9},{9,1},{17,25},{25,17},{2,10},{10... | collective-permute-start | bytes 1966088 | tf_op jit(solution)/shard_map/ppermute | solution.py:319
  6.7 1.0 copy-start.27
  7.7 1.0 copy-start.28
  8.7 0.7 copy-start.31
  11.4 71.1 %copy-start.9 = (bf16[256,1536]{1,0:T(8,128)(2,1)}, bf16[256,1536]{1,0:T(8,128)(2,1)S(1)}, u32[]{:S(2)}) copy-start(bf16[256,1536]{1,0:T(8,128)(2,1)S(1)} %get-tuple-element.44.refs_1_) | copy-start | bytes 2359300
  11.5 71.1 %copy-start.11 = (bf16[256,1536]{1,0:T(8,128)(2,1)}, bf16[256,1536]{1,0:T(8,128)(2,1)S(1)}, u32[]{:S(2)}) copy-start(bf16[256,1536]{1,0:T(8,128)(2,1)S(1)} %get-tuple-element.45.refs_2_) | copy-start | bytes 2359300
  23.1 15.9 %collective-permute-start.4 = (f32[5,2,64,256]{3,2,1,0:T(8,128)}, f32[5,2,64,256]{3,2,1,0:T(8,128)S(1)}, u32[]{:S(2)}, u32[]{:S(2)}) collective-permute-start(f32[5,2,64,256]{3,2,1,0:T(8,128)} %collective-permute-done.refs_1_.refs_8_), channel_id=1, source_target_pairs={{0,16},{8,24},{16,0},{24,8},{1,17},{9,25},{17,1},{25,9},{2,18},{10... | collective-permute-start | bytes 1966088 | tf_op jit(solution)/shard_map/ppermute | solution.py:319
  24.7 19.8 %collective-permute-start.2 = (f32[6,2,64,256]{3,2,1,0:T(8,128)S(1)}, f32[6,2,64,256]{3,2,1,0:T(8,128)S(1)}, u32[]{:S(2)}, u32[]{:S(2)}) collective-permute-start(f32[6,2,64,256]{3,2,1,0:T(8,128)S(1)} %collective-permute-done.1.refs_5_.refs_3_.refs_13_.refs_17_), channel_id=1, source_target_pairs={{0,8},{8,0},{16,24},{24,16},{1,9},{9,1},{17,25},{25,17},{2,10},{10... | collective-permute-start | bytes 2359304 | tf_op jit(solution)/shard_map/ppermute | solution.py:319
  26.1 2.2 %copy-start = (f32[64,2,32,256]{3,2,1,0:T(8,128)S(1)}, f32[64,2,32,256]{3,2,1,0:T(8,128)}, u32[]{:S(2)}) copy-start(f32[64,2,32,256]{3,2,1,0:T(8,128)} %in_ref.4) | copy-start | bytes 12582916
  28.3 0.7 copy-start.29
  29.0 11.5 %copy-start.1 = (f32[64,2,32,256]{3,2,1,0:T(8,128)S(1)}, f32[64,2,32,256]{3,2,1,0:T(8,128)}, u32[]{:S(2)}) copy-start(f32[64,2,32,256]{3,2,1,0:T(8,128)} %in_ref.4) | copy-start | bytes 12582916
  30.5 47.9 %copy-start.4 = (f32[5,2,64,256]{3,2,1,0:T(8,128)}, f32[5,2,64,256]{3,2,1,0:T(8,128)S(1)}, u32[]{:S(2)}) copy-start(f32[5,2,64,256]{3,2,1,0:T(8,128)S(1)} %get-tuple-element.46.refs_0_.refs_7_) | copy-start | bytes 1966084
  32.9 25.3 %collective-permute-start.10 = (f32[2,4,2,64,256]{4,3,2,1,0:T(8,128)S(1)}, f32[2,4,2,64,256]{4,3,2,1,0:T(8,128)S(1)}, u32[]{:S(2)}, u32[]{:S(2)}) collective-permute-start(f32[2,4,2,64,256]{4,3,2,1,0:T(8,128)S(1)} %get-tuple-element.62), channel_id=1, source_target_pairs={{0,1},{1,2},{2,3},{3,4},{4,5},{5,6},{6,7},{8,9},{9,10},{10,11},{11... | collective-permute-start | bytes 3145736 | tf_op jit(solution)/shard_map/ppermute | solution.py:370
  34.8 24.4 %collective-permute-start.11 = (f32[2,4,2,64,256]{4,3,2,1,0:T(8,128)S(1)}, f32[2,4,2,64,256]{4,3,2,1,0:T(8,128)S(1)}, u32[]{:S(2)}, u32[]{:S(2)}) collective-permute-start(f32[2,4,2,64,256]{4,3,2,1,0:T(8,128)S(1)} %get-tuple-element.63), channel_id=1, source_target_pairs={{1,0},{2,1},{3,2},{4,3},{5,4},{6,5},{7,6},{9,8},{10,9},{11,10},{12... | collective-permute-start | bytes 3145736 | tf_op jit(solution)/shard_map/ppermute | solution.py:370
  38.5 28.8 %collective-permute-start.12 = (f32[6,2,64,256]{3,2,1,0:T(8,128)S(1)}, f32[6,2,64,256]{3,2,1,0:T(8,128)S(1)}, u32[]{:S(2)}, u32[]{:S(2)}) collective-permute-start(f32[6,2,64,256]{3,2,1,0:T(8,128)S(1)} %get-tuple-element.54.refs_4_.refs_2_.refs_11_.refs_15_), channel_id=1, source_target_pairs={{0,8},{8,0},{16,24},{24,16},{1,9},{9,1},{17,25},{25,17},{2,10},{10... | collective-permute-start | bytes 2359304 | tf_op jit(solution)/shard_map/ppermute | solution.py:319
  39.1 28.2 %copy-start.2 = (f32[5,2,64,256]{3,2,1,0:T(8,128)}, f32[5,2,64,256]{3,2,1,0:T(8,128)S(1)}, u32[]{:S(2)}) copy-start(f32[5,2,64,256]{3,2,1,0:T(8,128)S(1)} %collective-permute-done.4.refs_1_.refs_10_) | copy-start | bytes 1966084
  39.1 17.6 %collective-permute-start.8 = (f32[5,2,64,256]{3,2,1,0:T(8,128)S(1)}, f32[5,2,64,256]{3,2,1,0:T(8,128)S(1)}, u32[]{:S(2)}, u32[]{:S(2)}) collective-permute-start(f32[5,2,64,256]{3,2,1,0:T(8,128)S(1)} %get-tuple-element.46.refs_0_.refs_7_), channel_id=1, source_target_pairs={{0,16},{8,24},{16,0},{24,8},{1,17},{9,25},{17,1},{25,9},{2,18},{10... | collective-permute-start | bytes 1966088 | tf_op jit(solution)/shard_map/ppermute | solution.py:319
  42.6 39.9 %copy-start.13 = (f32[4,2,64,256]{3,2,1,0:T(8,128)}, f32[4,2,64,256]{3,2,1,0:T(8,128)S(1)}, u32[]{:S(2)}) copy-start(f32[4,2,64,256]{3,2,1,0:T(8,128)S(1)} %get-tuple-element.61.refs_2_.refs_11_) | copy-start | bytes 1572868
  42.6 41.9 %copy-start.15 = (f32[4,2,64,256]{3,2,1,0:T(8,128)}, f32[4,2,64,256]{3,2,1,0:T(8,128)S(1)}, u32[]{:S(2)}) copy-start(f32[4,2,64,256]{3,2,1,0:T(8,128)S(1)} %get-tuple-element.71.refs_6_.refs_19_) | copy-start | bytes 1572868
  44.4 22.3 %collective-permute-start.5 = (f32[4,2,64,256]{3,2,1,0:T(8,128)S(1)}, f32[4,2,64,256]{3,2,1,0:T(8,128)}, u32[]{:S(2)}, u32[]{:S(2)}) collective-permute-start(f32[4,2,64,256]{3,2,1,0:T(8,128)S(1)} %get-tuple-element.58), channel_id=1, source_target_pairs={{0,16},{8,24},{16,0},{24,8},{1,17},{9,25},{17,1},{25,9},{2,18},{10... | collective-permute-start | bytes 1572872 | tf_op jit(solution)/shard_map/ppermute | solution.py:319
  56.7 25.8 %copy-start.6 = (f32[5,2,64,256]{3,2,1,0:T(8,128)}, f32[5,2,64,256]{3,2,1,0:T(8,128)S(1)}, u32[]{:S(2)}) copy-start(f32[5,2,64,256]{3,2,1,0:T(8,128)S(1)} %collective-permute-done.8.refs_0_.refs_9_) | copy-start | bytes 1966084
  56.7 20.1 %collective-permute-start.3 = (f32[4,2,64,256]{3,2,1,0:T(8,128)S(1)}, f32[4,2,64,256]{3,2,1,0:T(8,128)}, u32[]{:S(2)}, u32[]{:S(2)}) collective-permute-start(f32[4,2,64,256]{3,2,1,0:T(8,128)S(1)} %get-tuple-element.53), channel_id=1, source_target_pairs={{0,8},{8,0},{16,24},{24,16},{1,9},{9,1},{17,25},{25,17},{2,10},{10... | collective-permute-start | bytes 1572872 | tf_op jit(solution)/shard_map/ppermute | solution.py:319
  58.2 1.0 copy-start.21
  59.2 1.0 copy-start.23
  66.7 17.8 %collective-permute-start.9 = (f32[4,2,64,256]{3,2,1,0:T(8,128)S(1)}, f32[4,2,64,256]{3,2,1,0:T(8,128)S(1)}, u32[]{:S(2)}, u32[]{:S(2)}) collective-permute-start(f32[4,2,64,256]{3,2,1,0:T(8,128)S(1)} %get-tuple-element.61.refs_2_.refs_11_), channel_id=1, source_target_pairs={{0,16},{8,24},{16,0},{24,8},{1,17},{9,25},{17,1},{25,9},{2,18},{10... | collective-permute-start | bytes 1572872 | tf_op jit(solution)/shard_map/ppermute | solution.py:319
  71.3 21.8 %collective-permute-start.13 = (f32[2,4,2,64,256]{4,3,2,1,0:T(8,128)S(1)}, f32[2,4,2,64,256]{4,3,2,1,0:T(8,128)S(1)}, u32[]{:S(2)}, u32[]{:S(2)}) collective-permute-start(f32[2,4,2,64,256]{4,3,2,1,0:T(8,128)S(1)} %get-tuple-element.65), channel_id=1, source_target_pairs={{0,1},{1,2},{2,3},{3,4},{4,5},{5,6},{6,7},{8,9},{9,10},{10,11},{11... | collective-permute-start | bytes 3145736 | tf_op jit(solution)/shard_map/ppermute | solution.py:370
  73.2 22.4 %collective-permute-start.14 = (f32[2,4,2,64,256]{4,3,2,1,0:T(8,128)}, f32[2,4,2,64,256]{4,3,2,1,0:T(8,128)}, u32[]{:S(2)}, u32[]{:S(2)}) collective-permute-start(f32[2,4,2,64,256]{4,3,2,1,0:T(8,128)} %get-tuple-element.66), channel_id=1, source_target_pairs={{1,0},{2,1},{3,2},{4,3},{5,4},{6,5},{7,6},{9,8},{10,9},{11,10},{12... | collective-permute-start | bytes 3145736 | tf_op jit(solution)/shard_map/ppermute | solution.py:370
  76.9 13.9 %collective-permute-start.16 = (f32[4,2,64,256]{3,2,1,0:T(8,128)S(1)}, f32[4,2,64,256]{3,2,1,0:T(8,128)S(1)}, u32[]{:S(2)}, u32[]{:S(2)}) collective-permute-start(f32[4,2,64,256]{3,2,1,0:T(8,128)S(1)} %get-tuple-element.71.refs_6_.refs_19_), channel_id=1, source_target_pairs={{0,8},{8,0},{16,24},{24,16},{1,9},{9,1},{17,25},{25,17},{2,10},{10... | collective-permute-start | bytes 1572872 | tf_op jit(solution)/shard_map/ppermute | solution.py:319
  82.6 32.4 %collective-permute-start.6 = (f32[2,4,2,64,256]{4,3,2,1,0:T(8,128)}, f32[2,4,2,64,256]{4,3,2,1,0:T(8,128)}, u32[]{:S(2)}, u32[]{:S(2)}) collective-permute-start(f32[2,4,2,64,256]{4,3,2,1,0:T(8,128)} %get-tuple-element.59), channel_id=1, source_target_pairs={{0,1},{1,2},{2,3},{3,4},{4,5},{5,6},{6,7},{8,9},{9,10},{10,11},{11... | collective-permute-start | bytes 3145736 | tf_op jit(solution)/shard_map/ppermute | solution.py:370
  84.5 0.8 copy-start.17
  85.3 29.7 %collective-permute-start.7 = (f32[2,4,2,64,256]{4,3,2,1,0:T(8,128)}, f32[2,4,2,64,256]{4,3,2,1,0:T(8,128)}, u32[]{:S(2)}, u32[]{:S(2)}) collective-permute-start(f32[2,4,2,64,256]{4,3,2,1,0:T(8,128)} %get-tuple-element.60), channel_id=1, source_target_pairs={{1,0},{2,1},{3,2},{4,3},{5,4},{6,5},{7,6},{9,8},{10,9},{11,10},{12... | collective-permute-start | bytes 3145736 | tf_op jit(solution)/shard_map/ppermute | solution.py:370
  90.7 0.8 copy-start.19
  91.5 23.5 %collective-permute-start.15 = (f32[4,2,64,256]{3,2,1,0:T(8,128)}, f32[4,2,64,256]{3,2,1,0:T(8,128)}, u32[]{:S(2)}, u32[]{:S(2)}) collective-permute-start(f32[4,2,64,256]{3,2,1,0:T(8,128)} %collective-permute-done.3.refs_3_.refs_12_), channel_id=1, source_target_pairs={{0,16},{8,24},{16,0},{24,8},{1,17},{9,25},{17,1},{25,9},{2,18},{10... | collective-permute-start | bytes 1572872 | tf_op jit(solution)/shard_map/ppermute | solution.py:319
  93.0 1.0 copy-start.25
  94.1 20.9 %collective-permute-start.17 = (f32[4,2,64,256]{3,2,1,0:T(8,128)}, f32[4,2,64,256]{3,2,1,0:T(8,128)}, u32[]{:S(2)}, u32[]{:S(2)}) collective-permute-start(f32[4,2,64,256]{3,2,1,0:T(8,128)} %collective-permute-done.5.refs_7_.refs_21_), channel_id=1, source_target_pairs={{0,8},{8,0},{16,24},{24,16},{1,9},{9,1},{17,25},{25,17},{2,10},{10... | collective-permute-start | bytes 1572872 | tf_op jit(solution)/shard_map/ppermute | solution.py:319
  95.7 1.1 copy-start.3
  96.7 1.1 copy-start.5
  97.8 1.1 copy-start.7
  98.9 1.1 copy-start.10
  100.1 1.1 copy-start.12
  101.2 1.2 copy-start.22
  102.4 1.2 copy-start.24
  103.6 1.2 copy-start.26
  104.9 10.2 %copy-start.18 = (f32[4,2,64,256]{3,2,1,0:T(8,128)S(1)}, f32[4,2,64,256]{3,2,1,0:T(8,128)}, u32[]{:S(2)}) copy-start(f32[4,2,64,256]{3,2,1,0:T(8,128)} %copy-done.17) | copy-start | bytes 1572868
  104.9 10.2 %copy-start.20 = (f32[4,2,64,256]{3,2,1,0:T(8,128)S(1)}, f32[4,2,64,256]{3,2,1,0:T(8,128)}, u32[]{:S(2)}) copy-start(f32[4,2,64,256]{3,2,1,0:T(8,128)} %copy-done.19) | copy-start | bytes 1572868
  104.9 31.0 %copy-start.8 = (f32[5,2,64,256]{3,2,1,0:T(8,128)S(1)}, f32[5,2,64,256]{3,2,1,0:T(8,128)}, u32[]{:S(2)}) copy-start(f32[5,2,64,256]{3,2,1,0:T(8,128)} %copy-done.6) | copy-start | bytes 1966084
  104.9 31.0 %copy-start.14 = (f32[4,2,64,256]{3,2,1,0:T(8,128)S(1)}, f32[4,2,64,256]{3,2,1,0:T(8,128)}, u32[]{:S(2)}) copy-start(f32[4,2,64,256]{3,2,1,0:T(8,128)} %copy-done.13) | copy-start | bytes 1572868
  104.9 31.0 %copy-start.16 = (f32[4,2,64,256]{3,2,1,0:T(8,128)S(1)}, f32[4,2,64,256]{3,2,1,0:T(8,128)}, u32[]{:S(2)}) copy-start(f32[4,2,64,256]{3,2,1,0:T(8,128)} %copy-done.15) | copy-start | bytes 1572868
  118.0 16.1 %collective-permute-start.18 = (f32[2,4,2,64,256]{4,3,2,1,0:T(8,128)S(1)}, f32[2,4,2,64,256]{4,3,2,1,0:T(8,128)S(1)}, u32[]{:S(2)}, u32[]{:S(2)}) collective-permute-start(f32[2,4,2,64,256]{4,3,2,1,0:T(8,128)S(1)} %get-tuple-element.73), channel_id=1, source_target_pairs={{0,1},{1,2},{2,3},{3,4},{4,5},{5,6},{6,7},{8,9},{9,10},{10,11},{11... | collective-permute-start | bytes 3145736 | tf_op jit(solution)/shard_map/ppermute | solution.py:370
  119.9 15.9 %collective-permute-start.19 = (f32[2,4,2,64,256]{4,3,2,1,0:T(8,128)S(1)}, f32[2,4,2,64,256]{4,3,2,1,0:T(8,128)S(1)}, u32[]{:S(2)}, u32[]{:S(2)}) collective-permute-start(f32[2,4,2,64,256]{4,3,2,1,0:T(8,128)S(1)} %get-tuple-element.74), channel_id=1, source_target_pairs={{1,0},{2,1},{3,2},{4,3},{5,4},{6,5},{7,6},{9,8},{10,9},{11,10},{12... | collective-permute-start | bytes 3145736 | tf_op jit(solution)/shard_map/ppermute | solution.py:370
  123.8 24.1 %collective-permute-start.23 = (f32[4,2,128,256]{3,2,1,0:T(8,128)S(1)}, f32[4,2,128,256]{3,2,1,0:T(8,128)S(1)}, u32[]{:S(2)}, u32[]{:S(2)}) collective-permute-start(f32[4,2,128,256]{3,2,1,0:T(8,128)S(1)} %get-tuple-element.81), channel_id=1, source_target_pairs={{0,16},{8,24},{16,0},{24,8},{1,17},{9,25},{17,1},{25,9},{2,18},{10... | collective-permute-start | bytes 3145736 | tf_op jit(solution)/shard_map/ppermute | solution.py:319
  124.3 24.1 %collective-permute-start.22 = (f32[4,2,128,256]{3,2,1,0:T(8,128)S(1)}, f32[4,2,128,256]{3,2,1,0:T(8,128)S(1)}, u32[]{:S(2)}, u32[]{:S(2)}) collective-permute-start(f32[4,2,128,256]{3,2,1,0:T(8,128)S(1)} %get-tuple-element.80), channel_id=1, source_target_pairs={{0,8},{8,0},{16,24},{24,16},{1,9},{9,1},{17,25},{25,17},{2,10},{10... | collective-permute-start | bytes 3145736 | tf_op jit(solution)/shard_map/ppermute | solution.py:319
  146.7 26.0 %collective-permute-start.21 = (f32[4,2,128,256]{3,2,1,0:T(8,128)S(1)}, f32[4,2,128,256]{3,2,1,0:T(8,128)S(1)}, u32[]{:S(2)}, u32[]{:S(2)}) collective-permute-start(f32[4,2,128,256]{3,2,1,0:T(8,128)S(1)} %get-tuple-element.79), channel_id=1, source_target_pairs={{0,16},{8,24},{16,0},{24,8},{1,17},{9,25},{17,1},{25,9},{2,18},{10... | collective-permute-start | bytes 3145736 | tf_op jit(solution)/shard_map/ppermute | solution.py:319
  147.3 25.8 %collective-permute-start.20 = (f32[4,2,128,256]{3,2,1,0:T(8,128)S(1)}, f32[4,2,128,256]{3,2,1,0:T(8,128)S(1)}, u32[]{:S(2)}, u32[]{:S(2)}) collective-permute-start(f32[4,2,128,256]{3,2,1,0:T(8,128)S(1)} %get-tuple-element.77), channel_id=1, source_target_pairs={{0,8},{8,0},{16,24},{24,16},{1,9},{9,1},{17,25},{25,17},{2,10},{10... | collective-permute-start | bytes 3145736 | tf_op jit(solution)/shard_map/ppermute | solution.py:319

commit v10 on v9

--- a/solution.py
+++ b/solution.py
@@ -10,7 +10,7 @@
 
 CUTS = (0, 4, 8)
 CHUNKS = len(CUTS) - 1
-VMEM_LIMIT = 28 * 2**20
+VMEM_LIMIT = 16 * 2**20
 HBM = pl.BlockSpec(memory_space=pl.ANY)
 VMEM = pl.BlockSpec(memory_space=pltpu.VMEM)
 SCALARS = pl.BlockSpec(memory_space=pltpu.SMEM)
@@ -127,7 +127,7 @@
         in_specs=[HBM] * len(flat),
         out_specs=[VMEM] * 2,
         scratch_shapes=[pltpu.SemaphoreType.DMA((4 * high * groups,))],
-        compiler_params=pltpu.CompilerParams(vmem_limit_bytes=12 * 2**20),
+        compiler_params=pltpu.CompilerParams(vmem_limit_bytes=8 * 2**20),
         cost_estimate=cost(3),
         name="edges",
     )(*flat)
@@ -237,7 +237,7 @@
         out_specs=HBM,
         scratch_shapes=[pltpu.SemaphoreType.DMA((2 * len(own_rows(chunk, depth)) * planes,))],
         input_output_aliases={3: 0},
-        compiler_params=pltpu.CompilerParams(vmem_limit_bytes=12 * 2**20),
+        compiler_params=pltpu.CompilerParams(vmem_limit_bytes=8 * 2**20),
         cost_estimate=cost(2),
         name="place",
     )(sides, *got, result)

time: 177 us -> 177 us (level)
    unnamed x64 -> x62, local copies, waits for them, and re-layouts: 19.4 us -> 20.7 us
where the time goes in v10:
time: 177 us; the launch traced here: 175 us
  waiting for transfers between devices  66.5 us (38%)
  Pallas kernels  47.5 us (27%)
  starting transfers between devices  40 us (23%)
  local copies, waits for them, and re-layouts  20.7 us (12%)
    ppermute x16, waiting for transfers between devices, swap(): return lax.ppermute(data, 'tm', [(i, i ^ bit) for i in range(count)])  55.5 us
    pallas_call x2, Pallas kernels, apply(): pl.pallas_call(body, out_shape=[jax.ShapeDtypeStruct(shape, jnp.float32),...  21 us
    unnamed x62, local copies, waits for them, and re-layouts  20.7 us
    ppermute x16, starting transfers between devices, swap(): return lax.ppermute(data, 'tm', [(i, i ^ bit) for i in range(count)])  17.3 us
    ppermute x4, starting transfers between devices, beside(): lax.ppermute(down, 'space', downward)  15 us
    pallas_call x4, Pallas kernels, edges(): pl.pallas_call(functools.partial(edge_kernel, chunk, depth, groups), out_...  13.4 us
    ppermute x4, waiting for transfers between devices, beside(): lax.ppermute(up, 'space', upward)  9.22 us
    ppermute x4, starting transfers between devices, beside(): lax.ppermute(up, 'space', upward)  7.68 us
  transfers between devices with their start and end apart: 24, of which 11 were waited for; matrix products, arithmetic and copies ran while one was open for 0% of the time, Pallas kernels for 22%

profile of v10, /device:TPU:8, one launch (start us, length us, event | category | flops | bytes accessed | tf_op | source)
XLA Modules:
  0.0 175.2 jit_solution(14617636144126721341)
XLA Ops:
  0.0 3.5 %pick.4 = (f32[5,2,64,256]{3,2,1,0:T(8,128)}, f32[6,2,64,256]{3,2,1,0:T(8,128)}) custom-call(s32[1,64]{1,0:T(1,128)} %bitcast.5, f32[64,2,32,256]{3,2,1,0:T(8,128)} %in_ref.4), custom_call_target="tpu_custom_call" | custom-call | bytes 1850000 | tf_op jit(solution)/shard_map/pick/pallas_call | solution.py:86
  3.5 1.6 collective-permute-start.1
  5.1 1.5 collective-permute-start
  6.6 1.0 copy-done.27
  7.6 1.0 copy-done.28
  8.7 0.7 copy-done.30
  9.3 2.0 %maps.1 = (bf16[256,1536]{1,0:T(8,128)(2,1)S(1)}, bf16[256,1536]{1,0:T(8,128)(2,1)S(1)}) custom-call(s32[1]{0:T(128)} %bitcast.2.me_ref, f32[2,256,256]{2,1,0:T(8,128)S(1)} %copy-done.27, f32[2,256,256]{2,1,0:T(8,128)S(1)} %copy-done.28, f32[2,256]{1,0:T(2,128)S(1)} %copy-done.30), custom_call_target="tpu_custom_call" | custom-call | bytes 740000 | tf_op jit(solution)/shard_map/maps/pallas_call | solution.py:297
  11.4 0.9 copy-done.9
  12.3 0.9 copy-done.11
  13.2 8.4 %collective-permute-done.refs_1_.refs_8_ = f32[5,2,64,256]{3,2,1,0:T(8,128)} collective-permute-done((f32[5,2,64,256]{3,2,1,0:T(8,128)}, f32[5,2,64,256]{3,2,1,0:T(8,128)}, u32[]{:S(2)}, u32[]{:S(2)}) %collective-permute-start) | collective-permute-done | bytes 655392 | tf_op jit(solution)/shard_map/ppermute | solution.py:319
  21.6 1.5 collective-permute-done.1.refs_5_.refs_3_.refs_13_.refs_17_
  23.1 1.5 collective-permute-start.4
  24.6 1.5 collective-permute-start.2
  26.1 2.2 %copy-done = f32[64,2,32,256]{3,2,1,0:T(8,128)S(1)} copy-done((f32[64,2,32,256]{3,2,1,0:T(8,128)S(1)}, f32[64,2,32,256]{3,2,1,0:T(8,128)}, u32[]{:S(2)}) %copy-start) | copy-done | bytes 4194328
  28.3 0.7 copy-done.29
  28.9 1.5 pick.3
  30.4 2.4 %edges.5 = (f32[2,4,2,64,256]{4,3,2,1,0:T(8,128)S(1)}, f32[2,4,2,64,256]{4,3,2,1,0:T(8,128)S(1)}) custom-call(f32[5,2,64,256]{3,2,1,0:T(8,128)S(1)} %get-tuple-element.46.refs_0_.refs_7_, f32[5,2,64,256]{3,2,1,0:T(8,128)} %collective-permute-done.refs_1_.refs_8_, f32[6,2,64,256]{3,2,1,0:T(8,128)S(1)} %get-tuple-element.54.refs_4_.refs_2_.refs_11_.refs_15_, ...), custom_call_target="tpu_custom_call" | custom-call | bytes 1110000 | tf_op jit(solution)/shard_map/edges/pallas_call | solution.py:124
  32.8 1.9 %collective-permute-start.10 = (f32[2,4,2,64,256]{4,3,2,1,0:T(8,128)S(1)}, f32[2,4,2,64,256]{4,3,2,1,0:T(8,128)S(1)}, u32[]{:S(2)}, u32[]{:S(2)}) collective-permute-start(f32[2,4,2,64,256]{4,3,2,1,0:T(8,128)S(1)} %get-tuple-element.62), channel_id=1, source_target_pairs={{0,1},{1,2},{2,3},{3,4},{4,5},{5,6},{6,7},{8,9},{9,10},{10,11},{11... | collective-permute-start | bytes 3145736 | tf_op jit(solution)/shard_map/ppermute | solution.py:370
  34.8 3.6 %collective-permute-start.11 = (f32[2,4,2,64,256]{4,3,2,1,0:T(8,128)S(1)}, f32[2,4,2,64,256]{4,3,2,1,0:T(8,128)S(1)}, u32[]{:S(2)}, u32[]{:S(2)}) collective-permute-start(f32[2,4,2,64,256]{4,3,2,1,0:T(8,128)S(1)} %get-tuple-element.63), channel_id=1, source_target_pairs={{1,0},{2,1},{3,2},{4,3},{5,4},{6,5},{7,6},{9,8},{10,9},{11,10},{12... | collective-permute-start | bytes 3145736 | tf_op jit(solution)/shard_map/ppermute | solution.py:370
  38.4 0.6 collective-permute-start.12
  39.0 1.4 collective-permute-start.8
  40.4 2.1 %pick.5 = (f32[4,2,64,256]{3,2,1,0:T(8,128)S(1)}, f32[4,2,64,256]{3,2,1,0:T(8,128)S(1)}, f32[4,2,64,256]{3,2,1,0:T(8,128)S(1)}, f32[4,2,64,256]{3,2,1,0:T(8,128)S(1)}) custom-call(s32[1,64]{1,0:T(1,128)S(1)} %bitcast.7, f32[64,2,32,256]{3,2,1,0:T(8,128)S(1)} %copy-done.1), custom_call_target="tpu_custom_call" | custom-call | bytes 1850000 | tf_op jit(solution)/shard_map/pick/pallas_call | solution.py:86
  42.6 1.8 %collective-permute-done.2.refs_3_.refs_14_.refs_5_.refs_18_ = f32[6,2,64,256]{3,2,1,0:T(8,128)S(1)} collective-permute-done((f32[6,2,64,256]{3,2,1,0:T(8,128)S(1)}, f32[6,2,64,256]{3,2,1,0:T(8,128)S(1)}, u32[]{:S(2)}, u32[]{:S(2)}) %collective-permute-start.2) | collective-permute-done | bytes 786464 | tf_op jit(solution)/shard_map/ppermute | solution.py:319
  44.8 11.8 %collective-permute-done.8.refs_0_.refs_9_ = f32[5,2,64,256]{3,2,1,0:T(8,128)S(1)} collective-permute-done((f32[5,2,64,256]{3,2,1,0:T(8,128)S(1)}, f32[5,2,64,256]{3,2,1,0:T(8,128)S(1)}, u32[]{:S(2)}, u32[]{:S(2)}) %collective-permute-start.8) | collective-permute-done | bytes 655392 | tf_op jit(solution)/shard_map/ppermute | solution.py:319
  56.7 1.5 collective-permute-start.3
  58.2 1.3 copy-done.23
  59.5 7.2 %collective-permute-done.5.refs_7_.refs_21_ = f32[4,2,64,256]{3,2,1,0:T(8,128)} collective-permute-done((f32[4,2,64,256]{3,2,1,0:T(8,128)S(1)}, f32[4,2,64,256]{3,2,1,0:T(8,128)}, u32[]{:S(2)}, u32[]{:S(2)}) %collective-permute-start.5) | collective-permute-done | bytes 524320 | tf_op jit(solution)/shard_map/ppermute | solution.py:319
  66.7 0.5 collective-permute-start.9
  67.2 4.0 %edges.6 = (f32[2,4,2,64,256]{4,3,2,1,0:T(8,128)S(1)}, f32[2,4,2,64,256]{4,3,2,1,0:T(8,128)}) custom-call(f32[5,2,64,256]{3,2,1,0:T(8,128)S(1)} %collective-permute-done.8.refs_0_.refs_9_, f32[5,2,64,256]{3,2,1,0:T(8,128)S(1)} %collective-permute-done.4.refs_1_.refs_10_, f32[6,2,64,256]{3,2,1,0:T(8,128)S(1)} %collective-permute-done.12.refs_2_.refs_12_.refs_4_.refs_16_, ...), custom_call_target="tpu_custom_call" | custom-call | bytes 1110000 | tf_op jit(solution)/shard_map/edges/pallas_call | solution.py:124
  71.2 1.9 %collective-permute-start.13 = (f32[2,4,2,64,256]{4,3,2,1,0:T(8,128)S(1)}, f32[2,4,2,64,256]{4,3,2,1,0:T(8,128)S(1)}, u32[]{:S(2)}, u32[]{:S(2)}) collective-permute-start(f32[2,4,2,64,256]{4,3,2,1,0:T(8,128)S(1)} %get-tuple-element.65), channel_id=1, source_target_pairs={{0,1},{1,2},{2,3},{3,4},{4,5},{5,6},{6,7},{8,9},{9,10},{10,11},{11... | collective-permute-start | bytes 3145736 | tf_op jit(solution)/shard_map/ppermute | solution.py:370
  73.1 3.6 %collective-permute-start.14 = (f32[2,4,2,64,256]{4,3,2,1,0:T(8,128)}, f32[2,4,2,64,256]{4,3,2,1,0:T(8,128)}, u32[]{:S(2)}, u32[]{:S(2)}) collective-permute-start(f32[2,4,2,64,256]{4,3,2,1,0:T(8,128)} %get-tuple-element.66), channel_id=1, source_target_pairs={{1,0},{2,1},{3,2},{4,3},{5,4},{6,5},{7,6},{9,8},{10,9},{11,10},{12... | collective-permute-start | bytes 3145736 | tf_op jit(solution)/shard_map/ppermute | solution.py:370
  76.8 1.6 collective-permute-start.16
  78.4 4.1 %edges.4 = (f32[2,4,2,64,256]{4,3,2,1,0:T(8,128)}, f32[2,4,2,64,256]{4,3,2,1,0:T(8,128)}) custom-call(f32[5,2,64,256]{3,2,1,0:T(8,128)S(1)} %get-tuple-element.46.refs_0_.refs_7_, f32[5,2,64,256]{3,2,1,0:T(8,128)} %collective-permute-done.refs_1_.refs_8_, f32[4,2,64,256]{3,2,1,0:T(8,128)S(1)} %get-tuple-element.61.refs_2_.refs_11_, ...), custom_call_target="tpu_custom_call" | custom-call | bytes 1110000 | tf_op jit(solution)/shard_map/edges/pallas_call | solution.py:124
  82.5 1.9 %collective-permute-start.6 = (f32[2,4,2,64,256]{4,3,2,1,0:T(8,128)}, f32[2,4,2,64,256]{4,3,2,1,0:T(8,128)}, u32[]{:S(2)}, u32[]{:S(2)}) collective-permute-start(f32[2,4,2,64,256]{4,3,2,1,0:T(8,128)} %get-tuple-element.59), channel_id=1, source_target_pairs={{0,1},{1,2},{2,3},{3,4},{4,5},{5,6},{6,7},{8,9},{9,10},{10,11},{11... | collective-permute-start | bytes 3145736 | tf_op jit(solution)/shard_map/ppermute | solution.py:370
  84.4 0.8 copy-done.17
  85.2 3.8 %collective-permute-start.7 = (f32[2,4,2,64,256]{4,3,2,1,0:T(8,128)}, f32[2,4,2,64,256]{4,3,2,1,0:T(8,128)}, u32[]{:S(2)}, u32[]{:S(2)}) collective-permute-start(f32[2,4,2,64,256]{4,3,2,1,0:T(8,128)} %get-tuple-element.60), channel_id=1, source_target_pairs={{1,0},{2,1},{3,2},{4,3},{5,4},{6,5},{7,6},{9,8},{10,9},{11,10},{12... | collective-permute-start | bytes 3145736 | tf_op jit(solution)/shard_map/ppermute | solution.py:370
  89.0 1.6 collective-permute-done.16.refs_6_.refs_20_
  90.7 0.8 copy-done.19
  91.5 1.5 collective-permute-start.15
  93.0 1.1 copy-done.25
  94.1 1.5 collective-permute-start.17
  95.6 1.1 copy-done.3
  96.7 1.1 copy-done.5
  97.8 1.1 copy-done.7
  98.9 1.1 copy-done.10
  100.0 1.1 copy-done.12
  101.2 1.2 copy-done.22
  102.4 1.2 copy-done.24
  103.6 1.2 copy-done.26
  104.9 10.1 %apply.2 = (f32[128,2,32,256]{3,2,1,0:T(8,128)}, f32[4,2,128,256]{3,2,1,0:T(8,128)S(1)}, f32[4,2,128,256]{3,2,1,0:T(8,128)S(1)}) custom-call(s32[2]{0:T(128)S(1)} %pad_add_fusion.refs_0_.sides_ref, bf16[256,1536]{1,0:T(8,128)(2,1)S(1)} %copy-done.10, bf16[256,1536]{1,0:T(8,128)(2,1)S(1)} %copy-done.12, f32[2,4,2,64,256]{4,3,2,1,0:T(8,128)S(1)} %copy-done.22, ...), custom_call_target="tpu_custom_call" | custom-call | bytes 3700000 | tf_op jit(solution)/shard_map/apply/pallas_call | solution.py:204
  115.0 2.9 %edges.7 = (f32[2,4,2,64,256]{4,3,2,1,0:T(8,128)S(1)}, f32[2,4,2,64,256]{4,3,2,1,0:T(8,128)S(1)}) custom-call(f32[5,2,64,256]{3,2,1,0:T(8,128)S(1)} %copy-done.7, f32[5,2,64,256]{3,2,1,0:T(8,128)S(1)} %copy-done.3, f32[4,2,64,256]{3,2,1,0:T(8,128)S(1)} %copy-done.18, f32[4,2,64,256]{3,2,1,0:T(8,128)} %collective-permute-done.15.refs_3_.refs_14_, ...), custom_call_target="tpu_custom_call" | custom-call | bytes 1110000 | tf_op jit(solution)/shard_map/edges/pallas_call | solution.py:124
  118.0 1.9 %collective-permute-start.18 = (f32[2,4,2,64,256]{4,3,2,1,0:T(8,128)S(1)}, f32[2,4,2,64,256]{4,3,2,1,0:T(8,128)S(1)}, u32[]{:S(2)}, u32[]{:S(2)}) collective-permute-start(f32[2,4,2,64,256]{4,3,2,1,0:T(8,128)S(1)} %get-tuple-element.73), channel_id=1, source_target_pairs={{0,1},{1,2},{2,3},{3,4},{4,5},{5,6},{6,7},{8,9},{9,10},{10,11},{11... | collective-permute-start | bytes 3145736 | tf_op jit(solution)/shard_map/ppermute | solution.py:370
  119.9 3.9 %collective-permute-start.19 = (f32[2,4,2,64,256]{4,3,2,1,0:T(8,128)S(1)}, f32[2,4,2,64,256]{4,3,2,1,0:T(8,128)S(1)}, u32[]{:S(2)}, u32[]{:S(2)}) collective-permute-start(f32[2,4,2,64,256]{4,3,2,1,0:T(8,128)S(1)} %get-tuple-element.74), channel_id=1, source_target_pairs={{1,0},{2,1},{3,2},{4,3},{5,4},{6,5},{7,6},{9,8},{10,9},{11,10},{12... | collective-permute-start | bytes 3145736 | tf_op jit(solution)/shard_map/ppermute | solution.py:370
  123.8 0.6 collective-permute-start.23
  124.3 0.5 collective-permute-start.22
  124.9 9.2 %collective-permute-done.18.refs_5_ = f32[2,4,2,64,256]{4,3,2,1,0:T(8,128)S(1)} collective-permute-done((f32[2,4,2,64,256]{4,3,2,1,0:T(8,128)S(1)}, f32[2,4,2,64,256]{4,3,2,1,0:T(8,128)S(1)}, u32[]{:S(2)}, u32[]{:S(2)}) %collective-permute-start.18) | collective-permute-done | bytes 1048608 | tf_op jit(solution)/shard_map/ppermute | solution.py:370
  134.1 1.8 %collective-permute-done.19.refs_6_ = f32[2,4,2,64,256]{4,3,2,1,0:T(8,128)S(1)} collective-permute-done((f32[2,4,2,64,256]{4,3,2,1,0:T(8,128)S(1)}, f32[2,4,2,64,256]{4,3,2,1,0:T(8,128)S(1)}, u32[]{:S(2)}, u32[]{:S(2)}) %collective-permute-start.19) | collective-permute-done | bytes 1048608 | tf_op jit(solution)/shard_map/ppermute | solution.py:370
  135.8 10.9 %apply.3 = (f32[128,2,32,256]{3,2,1,0:T(8,128)}, f32[4,2,128,256]{3,2,1,0:T(8,128)S(1)}, f32[4,2,128,256]{3,2,1,0:T(8,128)S(1)}) custom-call(s32[2]{0:T(128)S(1)} %pad_add_fusion.refs_0_.sides_ref, bf16[256,1536]{1,0:T(8,128)(2,1)S(1)} %copy-done.10, bf16[256,1536]{1,0:T(8,128)(2,1)S(1)} %copy-done.12, ...), custom_call_target="tpu_custom_call", output_to_operand_aliasing={{0}: (23, {})} | custom-call | bytes 3700000 | tf_op jit(solution)/shard_map/apply/pallas_call | solution.py:204
  146.7 0.6 collective-permute-start.21
  147.3 0.5 collective-permute-start.20
  147.8 0.6 collective-permute-done.22.got_a
  148.4 2.0 %place.2._ = f32[128,2,32,256]{3,2,1,0:T(8,128)} custom-call(s32[2]{0:T(128)S(1)} %pad_add_fusion.refs_0_.sides_ref, f32[4,2,128,256]{3,2,1,0:T(8,128)S(1)} %collective-permute-done.22.got_a, f32[4,2,128,256]{3,2,1,0:T(8,128)S(1)} %collective-permute-done.23.got_b, f32[128,2,32,256]{3,2,1,0:T(8,128)} %get-tuple-element.82._), custom_call_target="tpu_custom_call", output_to_operand_aliasing={{}: (3, {})} | custom-call | bytes 740000 | tf_op jit(solution)/shard_map/place/pallas_call | solution.py:233
  150.4 22.3 %collective-permute-done.21.got_b = f32[4,2,128,256]{3,2,1,0:T(8,128)S(1)} collective-permute-done((f32[4,2,128,256]{3,2,1,0:T(8,128)S(1)}, f32[4,2,128,256]{3,2,1,0:T(8,128)S(1)}, u32[]{:S(2)}, u32[]{:S(2)}) %collective-permute-start.21) | collective-permute-done | bytes 1048608 | tf_op jit(solution)/shard_map/ppermute | solution.py:319
  173.0 2.0 %place.3 = f32[128,2,32,256]{3,2,1,0:T(8,128)} custom-call(s32[2]{0:T(128)S(1)} %pad_add_fusion.refs_0_.sides_ref, f32[4,2,128,256]{3,2,1,0:T(8,128)S(1)} %collective-permute-done.20.got_a, f32[4,2,128,256]{3,2,1,0:T(8,128)S(1)} %collective-permute-done.21.got_b, f32[128,2,32,256]{3,2,1,0:T(8,128)} %place.2._), custom_call_target="tpu_custom_call", output_to_operand_aliasing={{}: (3, {})} | custom-call | bytes 740000 | tf_op jit(solution)/shard_map/place/pallas_call | solution.py:233
  (59 shorter events, 1.0 us)
Async XLA Ops:
  3.5 19.6 %collective-permute-start.1 = (f32[6,2,64,256]{3,2,1,0:T(8,128)}, f32[6,2,64,256]{3,2,1,0:T(8,128)S(1)}, u32[]{:S(2)}, u32[]{:S(2)}) collective-permute-start(f32[6,2,64,256]{3,2,1,0:T(8,128)} %get-tuple-element.48), channel_id=1, source_target_pairs={{0,16},{8,24},{16,0},{24,8},{1,17},{9,25},{17,1},{25,9},{2,18},{10... | collective-permute-start | bytes 2359304 | tf_op jit(solution)/shard_map/ppermute | solution.py:319
  5.1 16.5 %collective-permute-start = (f32[5,2,64,256]{3,2,1,0:T(8,128)}, f32[5,2,64,256]{3,2,1,0:T(8,128)}, u32[]{:S(2)}, u32[]{:S(2)}) collective-permute-start(f32[5,2,64,256]{3,2,1,0:T(8,128)} %get-tuple-element.47), channel_id=1, source_target_pairs={{0,8},{8,0},{16,24},{24,16},{1,9},{9,1},{17,25},{25,17},{2,10},{10... | collective-permute-start | bytes 1966088 | tf_op jit(solution)/shard_map/ppermute | solution.py:319
  6.6 1.0 copy-start.27
  7.6 1.0 copy-start.28
  8.7 0.7 copy-start.30
  11.4 0.9 copy-start.9
  12.3 0.9 copy-start.11
  23.1 15.9 %collective-permute-start.4 = (f32[5,2,64,256]{3,2,1,0:T(8,128)}, f32[5,2,64,256]{3,2,1,0:T(8,128)S(1)}, u32[]{:S(2)}, u32[]{:S(2)}) collective-permute-start(f32[5,2,64,256]{3,2,1,0:T(8,128)} %collective-permute-done.refs_1_.refs_8_), channel_id=1, source_target_pairs={{0,16},{8,24},{16,0},{24,8},{1,17},{9,25},{17,1},{25,9},{2,18},{10... | collective-permute-start | bytes 1966088 | tf_op jit(solution)/shard_map/ppermute | solution.py:319
  24.6 19.8 %collective-permute-start.2 = (f32[6,2,64,256]{3,2,1,0:T(8,128)S(1)}, f32[6,2,64,256]{3,2,1,0:T(8,128)S(1)}, u32[]{:S(2)}, u32[]{:S(2)}) collective-permute-start(f32[6,2,64,256]{3,2,1,0:T(8,128)S(1)} %collective-permute-done.1.refs_5_.refs_3_.refs_13_.refs_17_), channel_id=1, source_target_pairs={{0,8},{8,0},{16,24},{24,16},{1,9},{9,1},{17,25},{25,17},{2,10},{10... | collective-permute-start | bytes 2359304 | tf_op jit(solution)/shard_map/ppermute | solution.py:319
  26.1 2.2 %copy-start = (f32[64,2,32,256]{3,2,1,0:T(8,128)S(1)}, f32[64,2,32,256]{3,2,1,0:T(8,128)}, u32[]{:S(2)}) copy-start(f32[64,2,32,256]{3,2,1,0:T(8,128)} %in_ref.4) | copy-start | bytes 12582916
  28.3 0.7 copy-start.29
  28.9 11.5 %copy-start.1 = (f32[64,2,32,256]{3,2,1,0:T(8,128)S(1)}, f32[64,2,32,256]{3,2,1,0:T(8,128)}, u32[]{:S(2)}) copy-start(f32[64,2,32,256]{3,2,1,0:T(8,128)} %in_ref.4) | copy-start | bytes 12582916
  30.4 47.9 %copy-start.4 = (f32[5,2,64,256]{3,2,1,0:T(8,128)}, f32[5,2,64,256]{3,2,1,0:T(8,128)S(1)}, u32[]{:S(2)}) copy-start(f32[5,2,64,256]{3,2,1,0:T(8,128)S(1)} %get-tuple-element.46.refs_0_.refs_7_) | copy-start | bytes 1966084
  32.8 25.3 %collective-permute-start.10 = (f32[2,4,2,64,256]{4,3,2,1,0:T(8,128)S(1)}, f32[2,4,2,64,256]{4,3,2,1,0:T(8,128)S(1)}, u32[]{:S(2)}, u32[]{:S(2)}) collective-permute-start(f32[2,4,2,64,256]{4,3,2,1,0:T(8,128)S(1)} %get-tuple-element.62), channel_id=1, source_target_pairs={{0,1},{1,2},{2,3},{3,4},{4,5},{5,6},{6,7},{8,9},{9,10},{10,11},{11... | collective-permute-start | bytes 3145736 | tf_op jit(solution)/shard_map/ppermute | solution.py:370
  34.8 23.4 %collective-permute-start.11 = (f32[2,4,2,64,256]{4,3,2,1,0:T(8,128)S(1)}, f32[2,4,2,64,256]{4,3,2,1,0:T(8,128)S(1)}, u32[]{:S(2)}, u32[]{:S(2)}) collective-permute-start(f32[2,4,2,64,256]{4,3,2,1,0:T(8,128)S(1)} %get-tuple-element.63), channel_id=1, source_target_pairs={{1,0},{2,1},{3,2},{4,3},{5,4},{6,5},{7,6},{9,8},{10,9},{11,10},{12... | collective-permute-start | bytes 3145736 | tf_op jit(solution)/shard_map/ppermute | solution.py:370
  38.4 28.8 %collective-permute-start.12 = (f32[6,2,64,256]{3,2,1,0:T(8,128)S(1)}, f32[6,2,64,256]{3,2,1,0:T(8,128)S(1)}, u32[]{:S(2)}, u32[]{:S(2)}) collective-permute-start(f32[6,2,64,256]{3,2,1,0:T(8,128)S(1)} %get-tuple-element.54.refs_4_.refs_2_.refs_11_.refs_15_), channel_id=1, source_target_pairs={{0,8},{8,0},{16,24},{24,16},{1,9},{9,1},{17,25},{25,17},{2,10},{10... | collective-permute-start | bytes 2359304 | tf_op jit(solution)/shard_map/ppermute | solution.py:319
  39.0 28.2 %copy-start.2 = (f32[5,2,64,256]{3,2,1,0:T(8,128)}, f32[5,2,64,256]{3,2,1,0:T(8,128)S(1)}, u32[]{:S(2)}) copy-start(f32[5,2,64,256]{3,2,1,0:T(8,128)S(1)} %collective-permute-done.4.refs_1_.refs_10_) | copy-start | bytes 1966084
  39.0 17.6 %collective-permute-start.8 = (f32[5,2,64,256]{3,2,1,0:T(8,128)S(1)}, f32[5,2,64,256]{3,2,1,0:T(8,128)S(1)}, u32[]{:S(2)}, u32[]{:S(2)}) collective-permute-start(f32[5,2,64,256]{3,2,1,0:T(8,128)S(1)} %get-tuple-element.46.refs_0_.refs_7_), channel_id=1, source_target_pairs={{0,16},{8,24},{16,0},{24,8},{1,17},{9,25},{17,1},{25,9},{2,18},{10... | collective-permute-start | bytes 1966088 | tf_op jit(solution)/shard_map/ppermute | solution.py:319
  42.6 39.9 %copy-start.13 = (f32[4,2,64,256]{3,2,1,0:T(8,128)}, f32[4,2,64,256]{3,2,1,0:T(8,128)S(1)}, u32[]{:S(2)}) copy-start(f32[4,2,64,256]{3,2,1,0:T(8,128)S(1)} %get-tuple-element.61.refs_2_.refs_11_) | copy-start | bytes 1572868
  42.6 41.9 %copy-start.15 = (f32[4,2,64,256]{3,2,1,0:T(8,128)}, f32[4,2,64,256]{3,2,1,0:T(8,128)S(1)}, u32[]{:S(2)}) copy-start(f32[4,2,64,256]{3,2,1,0:T(8,128)S(1)} %get-tuple-element.71.refs_6_.refs_19_) | copy-start | bytes 1572868
  44.3 22.3 %collective-permute-start.5 = (f32[4,2,64,256]{3,2,1,0:T(8,128)S(1)}, f32[4,2,64,256]{3,2,1,0:T(8,128)}, u32[]{:S(2)}, u32[]{:S(2)}) collective-permute-start(f32[4,2,64,256]{3,2,1,0:T(8,128)S(1)} %get-tuple-element.58), channel_id=1, source_target_pairs={{0,16},{8,24},{16,0},{24,8},{1,17},{9,25},{17,1},{25,9},{2,18},{10... | collective-permute-start | bytes 1572872 | tf_op jit(solution)/shard_map/ppermute | solution.py:319
  56.7 25.8 %copy-start.6 = (f32[5,2,64,256]{3,2,1,0:T(8,128)}, f32[5,2,64,256]{3,2,1,0:T(8,128)S(1)}, u32[]{:S(2)}) copy-start(f32[5,2,64,256]{3,2,1,0:T(8,128)S(1)} %collective-permute-done.8.refs_0_.refs_9_) | copy-start | bytes 1966084
  56.7 20.1 %collective-permute-start.3 = (f32[4,2,64,256]{3,2,1,0:T(8,128)S(1)}, f32[4,2,64,256]{3,2,1,0:T(8,128)}, u32[]{:S(2)}, u32[]{:S(2)}) collective-permute-start(f32[4,2,64,256]{3,2,1,0:T(8,128)S(1)} %get-tuple-element.53), channel_id=1, source_target_pairs={{0,8},{8,0},{16,24},{24,16},{1,9},{9,1},{17,25},{25,17},{2,10},{10... | collective-permute-start | bytes 1572872 | tf_op jit(solution)/shard_map/ppermute | solution.py:319
  58.1 18.7 %copy-start.21 = (f32[2,4,2,64,256]{4,3,2,1,0:T(8,128)}, f32[2,4,2,64,256]{4,3,2,1,0:T(8,128)S(1)}, u32[]{:S(2)}) copy-start(f32[2,4,2,64,256]{4,3,2,1,0:T(8,128)S(1)} %collective-permute-done.10.refs_3_) | copy-start | bytes 3145732
  58.2 1.3 copy-start.23
  66.7 17.8 %collective-permute-start.9 = (f32[4,2,64,256]{3,2,1,0:T(8,128)S(1)}, f32[4,2,64,256]{3,2,1,0:T(8,128)S(1)}, u32[]{:S(2)}, u32[]{:S(2)}) collective-permute-start(f32[4,2,64,256]{3,2,1,0:T(8,128)S(1)} %get-tuple-element.61.refs_2_.refs_11_), channel_id=1, source_target_pairs={{0,16},{8,24},{16,0},{24,8},{1,17},{9,25},{17,1},{25,9},{2,18},{10... | collective-permute-start | bytes 1572872 | tf_op jit(solution)/shard_map/ppermute | solution.py:319
  71.2 21.8 %collective-permute-start.13 = (f32[2,4,2,64,256]{4,3,2,1,0:T(8,128)S(1)}, f32[2,4,2,64,256]{4,3,2,1,0:T(8,128)S(1)}, u32[]{:S(2)}, u32[]{:S(2)}) collective-permute-start(f32[2,4,2,64,256]{4,3,2,1,0:T(8,128)S(1)} %get-tuple-element.65), channel_id=1, source_target_pairs={{0,1},{1,2},{2,3},{3,4},{4,5},{5,6},{6,7},{8,9},{9,10},{10,11},{11... | collective-permute-start | bytes 3145736 | tf_op jit(solution)/shard_map/ppermute | solution.py:370
  73.1 22.5 %collective-permute-start.14 = (f32[2,4,2,64,256]{4,3,2,1,0:T(8,128)}, f32[2,4,2,64,256]{4,3,2,1,0:T(8,128)}, u32[]{:S(2)}, u32[]{:S(2)}) collective-permute-start(f32[2,4,2,64,256]{4,3,2,1,0:T(8,128)} %get-tuple-element.66), channel_id=1, source_target_pairs={{1,0},{2,1},{3,2},{4,3},{5,4},{6,5},{7,6},{9,8},{10,9},{11,10},{12... | collective-permute-start | bytes 3145736 | tf_op jit(solution)/shard_map/ppermute | solution.py:370
  76.8 13.9 %collective-permute-start.16 = (f32[4,2,64,256]{3,2,1,0:T(8,128)S(1)}, f32[4,2,64,256]{3,2,1,0:T(8,128)S(1)}, u32[]{:S(2)}, u32[]{:S(2)}) collective-permute-start(f32[4,2,64,256]{3,2,1,0:T(8,128)S(1)} %get-tuple-element.71.refs_6_.refs_19_), channel_id=1, source_target_pairs={{0,8},{8,0},{16,24},{24,16},{1,9},{9,1},{17,25},{25,17},{2,10},{10... | collective-permute-start | bytes 1572872 | tf_op jit(solution)/shard_map/ppermute | solution.py:319
  82.5 32.5 %collective-permute-start.6 = (f32[2,4,2,64,256]{4,3,2,1,0:T(8,128)}, f32[2,4,2,64,256]{4,3,2,1,0:T(8,128)}, u32[]{:S(2)}, u32[]{:S(2)}) collective-permute-start(f32[2,4,2,64,256]{4,3,2,1,0:T(8,128)} %get-tuple-element.59), channel_id=1, source_target_pairs={{0,1},{1,2},{2,3},{3,4},{4,5},{5,6},{6,7},{8,9},{9,10},{10,11},{11... | collective-permute-start | bytes 3145736 | tf_op jit(solution)/shard_map/ppermute | solution.py:370
  84.4 0.8 copy-start.17
  85.2 29.8 %collective-permute-start.7 = (f32[2,4,2,64,256]{4,3,2,1,0:T(8,128)}, f32[2,4,2,64,256]{4,3,2,1,0:T(8,128)}, u32[]{:S(2)}, u32[]{:S(2)}) collective-permute-start(f32[2,4,2,64,256]{4,3,2,1,0:T(8,128)} %get-tuple-element.60), channel_id=1, source_target_pairs={{1,0},{2,1},{3,2},{4,3},{5,4},{6,5},{7,6},{9,8},{10,9},{11,10},{12... | collective-permute-start | bytes 3145736 | tf_op jit(solution)/shard_map/ppermute | solution.py:370
  90.7 0.8 copy-start.19
  91.5 23.5 %collective-permute-start.15 = (f32[4,2,64,256]{3,2,1,0:T(8,128)}, f32[4,2,64,256]{3,2,1,0:T(8,128)}, u32[]{:S(2)}, u32[]{:S(2)}) collective-permute-start(f32[4,2,64,256]{3,2,1,0:T(8,128)} %collective-permute-done.3.refs_3_.refs_12_), channel_id=1, source_target_pairs={{0,16},{8,24},{16,0},{24,8},{1,17},{9,25},{17,1},{25,9},{2,18},{10... | collective-permute-start | bytes 1572872 | tf_op jit(solution)/shard_map/ppermute | solution.py:319
  93.0 1.1 copy-start.25
  94.1 20.9 %collective-permute-start.17 = (f32[4,2,64,256]{3,2,1,0:T(8,128)}, f32[4,2,64,256]{3,2,1,0:T(8,128)}, u32[]{:S(2)}, u32[]{:S(2)}) collective-permute-start(f32[4,2,64,256]{3,2,1,0:T(8,128)} %collective-permute-done.5.refs_7_.refs_21_), channel_id=1, source_target_pairs={{0,8},{8,0},{16,24},{24,16},{1,9},{9,1},{17,25},{25,17},{2,10},{10... | collective-permute-start | bytes 1572872 | tf_op jit(solution)/shard_map/ppermute | solution.py:319
  95.6 1.1 copy-start.3
  96.7 1.1 copy-start.5
  97.8 1.1 copy-start.7
  98.9 1.1 copy-start.10
  100.0 1.1 copy-start.12
  101.2 1.2 copy-start.22
  102.4 1.2 copy-start.24
  103.6 1.2 copy-start.26
  104.8 10.2 %copy-start.18 = (f32[4,2,64,256]{3,2,1,0:T(8,128)S(1)}, f32[4,2,64,256]{3,2,1,0:T(8,128)}, u32[]{:S(2)}) copy-start(f32[4,2,64,256]{3,2,1,0:T(8,128)} %copy-done.17) | copy-start | bytes 1572868
  104.8 10.2 %copy-start.20 = (f32[4,2,64,256]{3,2,1,0:T(8,128)S(1)}, f32[4,2,64,256]{3,2,1,0:T(8,128)}, u32[]{:S(2)}) copy-start(f32[4,2,64,256]{3,2,1,0:T(8,128)} %copy-done.19) | copy-start | bytes 1572868
  104.8 31.0 %copy-start.8 = (f32[5,2,64,256]{3,2,1,0:T(8,128)S(1)}, f32[5,2,64,256]{3,2,1,0:T(8,128)}, u32[]{:S(2)}) copy-start(f32[5,2,64,256]{3,2,1,0:T(8,128)} %copy-done.6) | copy-start | bytes 1966084
  104.8 31.0 %copy-start.14 = (f32[4,2,64,256]{3,2,1,0:T(8,128)S(1)}, f32[4,2,64,256]{3,2,1,0:T(8,128)}, u32[]{:S(2)}) copy-start(f32[4,2,64,256]{3,2,1,0:T(8,128)} %copy-done.13) | copy-start | bytes 1572868
  104.9 31.0 %copy-start.16 = (f32[4,2,64,256]{3,2,1,0:T(8,128)S(1)}, f32[4,2,64,256]{3,2,1,0:T(8,128)}, u32[]{:S(2)}) copy-start(f32[4,2,64,256]{3,2,1,0:T(8,128)} %copy-done.15) | copy-start | bytes 1572868
  118.0 16.1 %collective-permute-start.18 = (f32[2,4,2,64,256]{4,3,2,1,0:T(8,128)S(1)}, f32[2,4,2,64,256]{4,3,2,1,0:T(8,128)S(1)}, u32[]{:S(2)}, u32[]{:S(2)}) collective-permute-start(f32[2,4,2,64,256]{4,3,2,1,0:T(8,128)S(1)} %get-tuple-element.73), channel_id=1, source_target_pairs={{0,1},{1,2},{2,3},{3,4},{4,5},{5,6},{6,7},{8,9},{9,10},{10,11},{11... | collective-permute-start | bytes 3145736 | tf_op jit(solution)/shard_map/ppermute | solution.py:370
  119.9 15.9 %collective-permute-start.19 = (f32[2,4,2,64,256]{4,3,2,1,0:T(8,128)S(1)}, f32[2,4,2,64,256]{4,3,2,1,0:T(8,128)S(1)}, u32[]{:S(2)}, u32[]{:S(2)}) collective-permute-start(f32[2,4,2,64,256]{4,3,2,1,0:T(8,128)S(1)} %get-tuple-element.74), channel_id=1, source_target_pairs={{1,0},{2,1},{3,2},{4,3},{5,4},{6,5},{7,6},{9,8},{10,9},{11,10},{12... | collective-permute-start | bytes 3145736 | tf_op jit(solution)/shard_map/ppermute | solution.py:370
  123.8 24.1 %collective-permute-start.23 = (f32[4,2,128,256]{3,2,1,0:T(8,128)S(1)}, f32[4,2,128,256]{3,2,1,0:T(8,128)S(1)}, u32[]{:S(2)}, u32[]{:S(2)}) collective-permute-start(f32[4,2,128,256]{3,2,1,0:T(8,128)S(1)} %get-tuple-element.81), channel_id=1, source_target_pairs={{0,16},{8,24},{16,0},{24,8},{1,17},{9,25},{17,1},{25,9},{2,18},{10... | collective-permute-start | bytes 3145736 | tf_op jit(solution)/shard_map/ppermute | solution.py:319
  124.3 24.1 %collective-permute-start.22 = (f32[4,2,128,256]{3,2,1,0:T(8,128)S(1)}, f32[4,2,128,256]{3,2,1,0:T(8,128)S(1)}, u32[]{:S(2)}, u32[]{:S(2)}) collective-permute-start(f32[4,2,128,256]{3,2,1,0:T(8,128)S(1)} %get-tuple-element.80), channel_id=1, source_target_pairs={{0,8},{8,0},{16,24},{24,16},{1,9},{9,1},{17,25},{25,17},{2,10},{10... | collective-permute-start | bytes 3145736 | tf_op jit(solution)/shard_map/ppermute | solution.py:319
  146.7 26.0 %collective-permute-start.21 = (f32[4,2,128,256]{3,2,1,0:T(8,128)S(1)}, f32[4,2,128,256]{3,2,1,0:T(8,128)S(1)}, u32[]{:S(2)}, u32[]{:S(2)}) collective-permute-start(f32[4,2,128,256]{3,2,1,0:T(8,128)S(1)} %get-tuple-element.79), channel_id=1, source_target_pairs={{0,16},{8,24},{16,0},{24,8},{1,17},{9,25},{17,1},{25,9},{2,18},{10... | collective-permute-start | bytes 3145736 | tf_op jit(solution)/shard_map/ppermute | solution.py:319
  147.3 25.8 %collective-permute-start.20 = (f32[4,2,128,256]{3,2,1,0:T(8,128)S(1)}, f32[4,2,128,256]{3,2,1,0:T(8,128)S(1)}, u32[]{:S(2)}, u32[]{:S(2)}) collective-permute-start(f32[4,2,128,256]{3,2,1,0:T(8,128)S(1)} %get-tuple-element.77), channel_id=1, source_target_pairs={{0,8},{8,0},{16,24},{24,16},{1,9},{9,1},{17,25},{25,17},{2,10},{10... | collective-permute-start | bytes 3145736 | tf_op jit(solution)/shard_map/ppermute | solution.py:319

commit v11 on v10

--- a/solution.py
+++ b/solution.py
@@ -13,12 +13,15 @@
 VMEM_LIMIT = 16 * 2**20
 HBM = pl.BlockSpec(memory_space=pl.ANY)
 VMEM = pl.BlockSpec(memory_space=pltpu.VMEM)
-SCALARS = pl.BlockSpec(memory_space=pltpu.SMEM)
 COST = 370000
 
 
 def cost(weight):
     return pl.CostEstimate(flops=0, bytes_accessed=weight * COST, transcendentals=0)
+
+
+def my_side(bit):
+    return jnp.where(jnp.bitwise_and(lax.axis_index("tm"), bit) > 0, 1, 0)
 
 
 def block_row(stream, side, row, depth, rows_x):
@@ -57,10 +60,9 @@
 def pick_kernel(chunk, depth, kinds, bits, step_ref, in_ref, *refs):
     outs, sems = refs[:-1], refs[-1]
     steps, planes, rows_x, _ = in_ref.shape
-    me = lax.axis_index("tm")
     jobs = []
     for place, (stream, other) in enumerate(kinds):
-        side = jnp.where(jnp.bitwise_and(me, bits[stream]) > 0, 1, 0)
+        side = my_side(bits[stream])
         side = 1 - side if other else side
         for at, row in enumerate(chunk_rows(stream, chunk, depth)):
             x = block_row(stream, side, row, depth, rows_x)
@@ -138,7 +140,7 @@
     return high, (value - high.astype(jnp.float32)).astype(jnp.bfloat16)
 
 
-def apply_kernel(chunk, depth, order, sides_ref, map_a_ref, map_b_ref, *refs):
+def apply_kernel(chunk, depth, order, bits, map_a_ref, map_b_ref, *refs):
     (early_low, early_high, late_low, late_high), raws = refs[:4], refs[4:-5]
     out_ref, gives, own, sems = refs[-5], refs[-4:-2], refs[-2], refs[-1]
     groups = sum(len(part) for part in order[0])
@@ -164,7 +166,7 @@
 
         for at, row in enumerate(own_rows(chunk, depth)):
             number = stream * len(own_rows(chunk, depth)) + at
-            x = block_row(stream, sides_ref[stream], row, depth, rows_x)
+            x = block_row(stream, my_side(bits[stream]), row, depth, rows_x)
             mids = [load(row, z) for z in range(planes)]
             for z, mid in enumerate(mids):
                 lane = lax.broadcasted_iota(jnp.int32, mid.shape, 1)
@@ -188,23 +190,23 @@
         store.wait()
 
 
-def apply(chunk, depth, order, sides, maps, early, late, raws, shape, result):
+def apply(chunk, depth, order, bits, maps, early, late, raws, shape, result):
     _, planes, _, rows_y = raws[0][0][0].shape
     high = len(own_rows(chunk, depth))
     half = shape[0]
     flat = [raw for stream in raws for arrays in stream for raw in arrays]
     first = [] if result is None else [result]
     give = jax.ShapeDtypeStruct((high, planes, half, rows_y), jnp.float32)
-    count = 3 + 4 + len(flat)
+    count = 2 + 4 + len(flat)
 
     def body(*refs):
         refs = refs[:count] + refs[count + len(first) :]
-        apply_kernel(chunk, depth, order, *refs)
+        apply_kernel(chunk, depth, order, bits, *refs)
 
     return pl.pallas_call(
         body,
         out_shape=[jax.ShapeDtypeStruct(shape, jnp.float32), give, give],
-        in_specs=[SCALARS] + [VMEM] * (count - 1) + [HBM] * len(first),
+        in_specs=[VMEM] * count + [HBM] * len(first),
         out_specs=[HBM, VMEM, VMEM],
         scratch_shapes=[
             pltpu.VMEM((2 * high, planes, half, rows_y), jnp.float32),
@@ -214,43 +216,43 @@
         compiler_params=pltpu.CompilerParams(vmem_limit_bytes=VMEM_LIMIT),
         cost_estimate=cost(10),
         name="apply",
-    )(sides, *maps, *early, *late, *flat, *first)
-
-
-def place_kernel(chunk, depth, sides_ref, got_a, got_b, _, out_ref, sems):
+    )(*maps, *early, *late, *flat, *first)
+
+
+def place_kernel(chunk, depth, bits, got_a, got_b, _, out_ref, sems):
     _, planes, rows_x, _ = out_ref.shape
     copies = []
     for stream, got in enumerate((got_a, got_b)):
         for at, row in enumerate(own_rows(chunk, depth)):
-            x = block_row(stream, 1 - sides_ref[stream], row, depth, rows_x)
+            x = block_row(stream, 1 - my_side(bits[stream]), row, depth, rows_x)
             for z in range(planes):
                 copies.append(pltpu.make_async_copy(got.at[at, z], out_ref.at[:, z, x], sems.at[len(copies)]))
     run(copies)
 
 
-def place(chunk, depth, sides, got, result):
+def place(chunk, depth, bits, got, result):
     planes = result.shape[1]
     return pl.pallas_call(
-        functools.partial(place_kernel, chunk, depth),
+        functools.partial(place_kernel, chunk, depth, bits),
         out_shape=jax.ShapeDtypeStruct(result.shape, jnp.float32),
-        in_specs=[SCALARS, VMEM, VMEM, HBM],
+        in_specs=[VMEM, VMEM, HBM],
         out_specs=HBM,
         scratch_shapes=[pltpu.SemaphoreType.DMA((2 * len(own_rows(chunk, depth)) * planes,))],
-        input_output_aliases={3: 0},
+        input_output_aliases={2: 0},
         compiler_params=pltpu.CompilerParams(vmem_limit_bytes=8 * 2**20),
         cost_estimate=cost(2),
         name="place",
-    )(sides, *got, result)
+    )(*got, result)
 
 
 def after(value, *others):
     return lax.optimization_barrier((value, *others))[0]
 
 
-def maps_kernel(bits, me_ref, ahead_ref, back_ref, eigen_ref, *outs):
+def maps_kernel(bits, ahead_ref, back_ref, eigen_ref, *outs):
     steps = ahead_ref.shape[1]
     local_steps = outs[0].shape[0] // 4
-    me = me_ref[0]
+    me = lax.axis_index("tm")
     real_part = 6.0 + eigen_ref[0:1, :]
     imag_part = eigen_ref[1:2, :]
     denom = real_part * real_part + imag_part * imag_part
@@ -291,18 +293,18 @@
                 out[place * half : (place + 1) * half, c * steps : (c + 1) * steps] = value
 
 
-def make_maps(forward_map, back_map, eigen_values, me, count, bits):
+def make_maps(forward_map, back_map, eigen_values, count, bits):
     steps = forward_map.shape[1]
     shape = jax.ShapeDtypeStruct((4 * steps // count, 6 * steps), jnp.bfloat16)
     return pl.pallas_call(
         functools.partial(maps_kernel, bits),
         out_shape=[shape, shape],
-        in_specs=[SCALARS] + [VMEM] * 3,
+        in_specs=[VMEM] * 3,
         out_specs=[VMEM] * 2,
         compiler_params=pltpu.CompilerParams(vmem_limit_bytes=VMEM_LIMIT),
         cost_estimate=cost(2),
         name="maps",
-    )(me.astype(jnp.int32).reshape(1), forward_map, back_map, eigen_values)
+    )(forward_map, back_map, eigen_values)
 
 
 def local(residual, step_ratio, forward_map, back_map, eigen_values):
@@ -311,8 +313,6 @@
     count = lax.axis_size("tm")
     bits = (1, count // 2)
     all_bits = [1 << k for k in range(count.bit_length() - 1)]
-    me = lax.axis_index("tm")
-    sides = jnp.stack([jnp.where(jnp.bitwise_and(me, b) > 0, 1, 0) for b in bits]).astype(jnp.int32)
     ratio = jnp.broadcast_to((step_ratio.astype(jnp.float32) / 8.0)[:, None], (local_steps, rows_y))
 
     def swap(data, bit):
@@ -338,7 +338,7 @@
     order = [[[m for m in masks if m in (0, b)], [m for m in masks if m not in (0, b)]] for b in bits]
     held = [[None] * CHUNKS for _ in range(2)]
 
-    maps = make_maps(forward_map, back_map, eigen_values, me, count, bits)
+    maps = make_maps(forward_map, back_map, eigen_values, count, bits)
     firsts = []
 
     def raw(chunk):
@@ -379,11 +379,11 @@
         early = beside(chunk, 0)
         late = beside(chunk, 1, *early, *(gives[-1] if gives else []))
         used = [held[s][max(chunk - 1, 0) : chunk + 1] for s in range(2)]
-        result, *give = apply(chunk, depth, order, sides, maps, early, late, used, shape, result)
+        result, *give = apply(chunk, depth, order, bits, maps, early, late, used, shape, result)
         gives.append(give)
         gots.append([swap_in_turn(give[s], bits[s], flight=1 + min(chunk, 1)) for s in range(2)])
     for chunk in range(CHUNKS):
-        result = place(chunk, depth, sides, gots[chunk], result)
+        result = place(chunk, depth, bits, gots[chunk], result)
     return result.reshape(2, local_steps, planes, rows_x, rows_y)
 
 

time: 177 us -> 162 us (0.915)
  local copies, waits for them, and re-layouts: 20.7 us -> 5.61 us
  waiting for transfers between devices: 66.5 us -> 73.6 us
  Pallas kernels: 47.5 us -> 41.1 us
    unnamed x62 -> x12, local copies, waits for them, and re-layouts: 20.7 us -> 5.61 us
    ppermute x16, waiting for transfers between devices: 55.5 us -> 63.6 us  [swap(): return lax.ppermute(data, 'tm', [(i, i ^ bit) for i in range(count)])]
    pallas_call x2, Pallas kernels: 21 us -> 16.7 us  [apply(): pl.pallas_call(body, out_shape=[jax.ShapeDtypeStruct(shape, jnp.float32),...]
  transfers between devices with their start and end apart: 24 -> 24, of which waited for: 11 -> 14; matrix products, arithmetic and copies ran while one was open for 0% -> 0% of each run, Pallas kernels for 22% -> 20%
where the time goes in v11:
time: 162 us
  waiting for transfers between devices  73.6 us (45%)
  Pallas kernels  41.1 us (25%)
  starting transfers between devices  41.1 us (25%)
  local copies, waits for them, and re-layouts  5.61 us (3%)
    ppermute x16, waiting for transfers between devices, swap(): return lax.ppermute(data, 'tm', [(i, i ^ bit) for i in range(count)])  63.6 us
    ppermute x16, starting transfers between devices, swap(): return lax.ppermute(data, 'tm', [(i, i ^ bit) for i in range(count)])  18.4 us
    pallas_call x2, Pallas kernels, apply(): pl.pallas_call(body, out_shape=[jax.ShapeDtypeStruct(shape, jnp.float32),...  16.7 us
    ppermute x4, starting transfers between devices, beside(): lax.ppermute(down, 'space', downward)  15 us
    pallas_call x4, Pallas kernels, edges(): pl.pallas_call(functools.partial(edge_kernel, chunk, depth, groups), out_...  12.1 us
    ppermute x4, waiting for transfers between devices, beside(): lax.ppermute(up, 'space', upward)  8.26 us
    ppermute x4, starting transfers between devices, beside(): lax.ppermute(up, 'space', upward)  7.68 us
    pallas_call x3, Pallas kernels, pick(): pl.pallas_call(functools.partial(pick_kernel, chunk, depth, kinds, bits),...  7.44 us
  transfers between devices with their start and end apart: 24, of which 14 were waited for; matrix products, arithmetic and copies ran while one was open for 0% of the time, Pallas kernels for 20%

profile of v11, /device:TPU:8, one launch (start us, length us, event | category | flops | bytes accessed | tf_op | source)
XLA Modules:
  0.0 161.7 jit_solution(17985791490910595528)
XLA Ops:
  0.0 3.8 %pick.4 = (f32[5,2,64,256]{3,2,1,0:T(8,128)}, f32[6,2,64,256]{3,2,1,0:T(8,128)}) custom-call(s32[1,64]{1,0:T(1,128)} %bitcast.2, f32[64,2,32,256]{3,2,1,0:T(8,128)} %in_ref.4), custom_call_target="tpu_custom_call" | custom-call | bytes 1850000 | tf_op jit(solution)/shard_map/pick/pallas_call | solution.py:88
  3.8 1.6 collective-permute-start.1
  5.4 1.5 collective-permute-start
  6.9 1.0 copy-done.2
  7.9 1.0 copy-done.3
  9.0 0.7 copy-done.5
  9.7 2.0 %maps.1 = (bf16[256,1536]{1,0:T(8,128)(2,1)S(1)}, bf16[256,1536]{1,0:T(8,128)(2,1)S(1)}) custom-call(f32[2,256,256]{2,1,0:T(8,128)S(1)} %copy-done.2, f32[2,256,256]{2,1,0:T(8,128)S(1)} %copy-done.3, f32[2,256]{1,0:T(2,128)S(1)} %copy-done.5), custom_call_target="tpu_custom_call" | custom-call | bytes 740000 | tf_op jit(solution)/shard_map/maps/pallas_call | solution.py:299
  11.7 10.1 %collective-permute-done.refs_1_.refs_7_ = f32[5,2,64,256]{3,2,1,0:T(8,128)S(1)} collective-permute-done((f32[5,2,64,256]{3,2,1,0:T(8,128)}, f32[5,2,64,256]{3,2,1,0:T(8,128)S(1)}, u32[]{:S(2)}, u32[]{:S(2)}) %collective-permute-start) | collective-permute-done | bytes 655392 | tf_op jit(solution)/shard_map/ppermute | solution.py:319
  21.8 1.6 collective-permute-done.1.refs_5_.refs_3_.refs_12_.refs_16_
  23.4 1.5 collective-permute-start.4
  24.9 1.5 collective-permute-start.2
  26.4 2.2 %copy-done = f32[64,2,32,256]{3,2,1,0:T(8,128)S(1)} copy-done((f32[64,2,32,256]{3,2,1,0:T(8,128)S(1)}, f32[64,2,32,256]{3,2,1,0:T(8,128)}, u32[]{:S(2)}) %copy-start) | copy-done | bytes 4194328
  28.6 0.7 copy-done.4
  29.2 1.5 pick.3
  30.7 3.0 %edges.5 = (f32[2,4,2,64,256]{4,3,2,1,0:T(8,128)S(1)}, f32[2,4,2,64,256]{4,3,2,1,0:T(8,128)S(1)}) custom-call(f32[5,2,64,256]{3,2,1,0:T(8,128)S(1)} %get-tuple-element.46.refs_0_.refs_6_, f32[5,2,64,256]{3,2,1,0:T(8,128)S(1)} %collective-permute-done.refs_1_.refs_7_, f32[6,2,64,256]{3,2,1,0:T(8,128)S(1)} %get-tuple-element.54.refs_4_.refs_2_.refs_10_.refs_14_, ...), custom_call_target="tpu_custom_call" | custom-call | bytes 1110000 | tf_op jit(solution)/shard_map/edges/pallas_call | solution.py:126
  33.8 1.9 %collective-permute-start.10 = (f32[2,4,2,64,256]{4,3,2,1,0:T(8,128)S(1)}, f32[2,4,2,64,256]{4,3,2,1,0:T(8,128)S(1)}, u32[]{:S(2)}, u32[]{:S(2)}) collective-permute-start(f32[2,4,2,64,256]{4,3,2,1,0:T(8,128)S(1)} %get-tuple-element.62), channel_id=1, source_target_pairs={{0,1},{1,2},{2,3},{3,4},{4,5},{5,6},{6,7},{8,9},{9,10},{10,11},{11... | collective-permute-start | bytes 3145736 | tf_op jit(solution)/shard_map/ppermute | solution.py:370
  35.7 3.6 %collective-permute-start.11 = (f32[2,4,2,64,256]{4,3,2,1,0:T(8,128)S(1)}, f32[2,4,2,64,256]{4,3,2,1,0:T(8,128)S(1)}, u32[]{:S(2)}, u32[]{:S(2)}) collective-permute-start(f32[2,4,2,64,256]{4,3,2,1,0:T(8,128)S(1)} %get-tuple-element.63), channel_id=1, source_target_pairs={{1,0},{2,1},{3,2},{4,3},{5,4},{6,5},{7,6},{9,8},{10,9},{11,10},{12... | collective-permute-start | bytes 3145736 | tf_op jit(solution)/shard_map/ppermute | solution.py:370
  39.4 0.6 collective-permute-start.12
  40.0 0.0 collective-permute-done.4.refs_1_.refs_9_
  40.0 0.5 collective-permute-start.8
  40.5 2.1 %pick.5 = (f32[4,2,64,256]{3,2,1,0:T(8,128)S(1)}, f32[4,2,64,256]{3,2,1,0:T(8,128)S(1)}, f32[4,2,64,256]{3,2,1,0:T(8,128)S(1)}, f32[4,2,64,256]{3,2,1,0:T(8,128)S(1)}) custom-call(s32[1,64]{1,0:T(1,128)S(1)} %bitcast.4, f32[64,2,32,256]{3,2,1,0:T(8,128)S(1)} %copy-done.1), custom_call_target="tpu_custom_call" | custom-call | bytes 1850000 | tf_op jit(solution)/shard_map/pick/pallas_call | solution.py:88
  42.6 1.3 collective-permute-done.2.refs_3_.refs_13_.refs_5_.refs_17_
  44.0 0.5 collective-permute-start.5
  44.5 13.1 %collective-permute-done.8.refs_0_.refs_8_ = f32[5,2,64,256]{3,2,1,0:T(8,128)S(1)} collective-permute-done((f32[5,2,64,256]{3,2,1,0:T(8,128)S(1)}, f32[5,2,64,256]{3,2,1,0:T(8,128)S(1)}, u32[]{:S(2)}, u32[]{:S(2)}) %collective-permute-start.8) | collective-permute-done | bytes 655392 | tf_op jit(solution)/shard_map/ppermute | solution.py:319
  57.6 1.5 collective-permute-start.3
  59.1 0.0 collective-permute-done.10.refs_2_
  59.1 0.0 collective-permute-done.11.refs_3_
  59.1 8.4 %collective-permute-done.5.refs_7_.refs_20_ = f32[4,2,64,256]{3,2,1,0:T(8,128)S(1)} collective-permute-done((f32[4,2,64,256]{3,2,1,0:T(8,128)S(1)}, f32[4,2,64,256]{3,2,1,0:T(8,128)S(1)}, u32[]{:S(2)}, u32[]{:S(2)}) %collective-permute-start.5) | collective-permute-done | bytes 524320 | tf_op jit(solution)/shard_map/ppermute | solution.py:319
  67.5 0.5 collective-permute-start.9
  68.0 0.0 collective-permute-done.12.refs_2_.refs_11_.refs_4_.refs_15_
  68.0 3.0 %edges.6 = (f32[2,4,2,64,256]{4,3,2,1,0:T(8,128)S(1)}, f32[2,4,2,64,256]{4,3,2,1,0:T(8,128)S(1)}) custom-call(f32[5,2,64,256]{3,2,1,0:T(8,128)S(1)} %collective-permute-done.8.refs_0_.refs_8_, f32[5,2,64,256]{3,2,1,0:T(8,128)S(1)} %collective-permute-done.4.refs_1_.refs_9_, f32[6,2,64,256]{3,2,1,0:T(8,128)S(1)} %collective-permute-done.12.refs_2_.refs_11_.refs_4_.refs_15_, ...), custom_call_target="tpu_custom_call" | custom-call | bytes 1110000 | tf_op jit(solution)/shard_map/edges/pallas_call | solution.py:126
  71.1 1.9 %collective-permute-start.13 = (f32[2,4,2,64,256]{4,3,2,1,0:T(8,128)S(1)}, f32[2,4,2,64,256]{4,3,2,1,0:T(8,128)S(1)}, u32[]{:S(2)}, u32[]{:S(2)}) collective-permute-start(f32[2,4,2,64,256]{4,3,2,1,0:T(8,128)S(1)} %get-tuple-element.65), channel_id=1, source_target_pairs={{0,1},{1,2},{2,3},{3,4},{4,5},{5,6},{6,7},{8,9},{9,10},{10,11},{11... | collective-permute-start | bytes 3145736 | tf_op jit(solution)/shard_map/ppermute | solution.py:370
  73.0 3.6 %collective-permute-start.14 = (f32[2,4,2,64,256]{4,3,2,1,0:T(8,128)S(1)}, f32[2,4,2,64,256]{4,3,2,1,0:T(8,128)S(1)}, u32[]{:S(2)}, u32[]{:S(2)}) collective-permute-start(f32[2,4,2,64,256]{4,3,2,1,0:T(8,128)S(1)} %get-tuple-element.66), channel_id=1, source_target_pairs={{1,0},{2,1},{3,2},{4,3},{5,4},{6,5},{7,6},{9,8},{10,9},{11,10},{12... | collective-permute-start | bytes 3145736 | tf_op jit(solution)/shard_map/ppermute | solution.py:370
  76.6 0.0 collective-permute-done.3.refs_3_.refs_11_
  76.7 1.6 collective-permute-start.16
  78.2 3.0 %edges.4 = (f32[2,4,2,64,256]{4,3,2,1,0:T(8,128)S(1)}, f32[2,4,2,64,256]{4,3,2,1,0:T(8,128)S(1)}) custom-call(f32[5,2,64,256]{3,2,1,0:T(8,128)S(1)} %get-tuple-element.46.refs_0_.refs_6_, f32[5,2,64,256]{3,2,1,0:T(8,128)S(1)} %collective-permute-done.refs_1_.refs_7_, f32[4,2,64,256]{3,2,1,0:T(8,128)S(1)} %get-tuple-element.61.refs_2_.refs_10_, ...), custom_call_target="tpu_custom_call" | custom-call | bytes 1110000 | tf_op jit(solution)/shard_map/edges/pallas_call | solution.py:126
  81.2 1.9 %collective-permute-start.6 = (f32[2,4,2,64,256]{4,3,2,1,0:T(8,128)S(1)}, f32[2,4,2,64,256]{4,3,2,1,0:T(8,128)S(1)}, u32[]{:S(2)}, u32[]{:S(2)}) collective-permute-start(f32[2,4,2,64,256]{4,3,2,1,0:T(8,128)S(1)} %get-tuple-element.59), channel_id=1, source_target_pairs={{0,1},{1,2},{2,3},{3,4},{4,5},{5,6},{6,7},{8,9},{9,10},{10,11},{11... | collective-permute-start | bytes 3145736 | tf_op jit(solution)/shard_map/ppermute | solution.py:370
  83.2 0.0 collective-permute-done.9.refs_2_.refs_12_
  83.2 3.8 %collective-permute-start.7 = (f32[2,4,2,64,256]{4,3,2,1,0:T(8,128)S(1)}, f32[2,4,2,64,256]{4,3,2,1,0:T(8,128)S(1)}, u32[]{:S(2)}, u32[]{:S(2)}) collective-permute-start(f32[2,4,2,64,256]{4,3,2,1,0:T(8,128)S(1)} %get-tuple-element.60), channel_id=1, source_target_pairs={{1,0},{2,1},{3,2},{4,3},{5,4},{6,5},{7,6},{9,8},{10,9},{11,10},{12... | collective-permute-start | bytes 3145736 | tf_op jit(solution)/shard_map/ppermute | solution.py:370
  87.0 3.5 %collective-permute-done.16.refs_6_.refs_19_ = f32[4,2,64,256]{3,2,1,0:T(8,128)S(1)} collective-permute-done((f32[4,2,64,256]{3,2,1,0:T(8,128)S(1)}, f32[4,2,64,256]{3,2,1,0:T(8,128)S(1)}, u32[]{:S(2)}, u32[]{:S(2)}) %collective-permute-start.16) | collective-permute-done | bytes 524320 | tf_op jit(solution)/shard_map/ppermute | solution.py:319
  90.5 1.5 collective-permute-start.15
  92.0 0.0 collective-permute-done.13.refs_4_
  92.0 1.5 collective-permute-start.17
  93.5 0.0 collective-permute-done.14.refs_5_
  93.5 8.3 %apply.2 = (f32[128,2,32,256]{3,2,1,0:T(8,128)}, f32[4,2,128,256]{3,2,1,0:T(8,128)S(1)}, f32[4,2,128,256]{3,2,1,0:T(8,128)S(1)}) custom-call(bf16[256,1536]{1,0:T(8,128)(2,1)S(1)} %get-tuple-element.44.refs_0_, bf16[256,1536]{1,0:T(8,128)(2,1)S(1)} %get-tuple-element.45.refs_1_, f32[2,4,2,64,256]{4,3,2,1,0:T(8,128)S(1)} %collective-permute-done.10.refs_2_, ...), custom_call_target="tpu_custom_call" | custom-call | bytes 3700000 | tf_op jit(solution)/shard_map/apply/pallas_call | solution.py:206
  101.9 0.0 collective-permute-done.7.refs_3_
  101.9 1.6 collective-permute-done.15.refs_3_.refs_13_
  103.4 1.2 collective-permute-done.17.refs_7_.refs_21_
  104.7 3.0 %edges.7 = (f32[2,4,2,64,256]{4,3,2,1,0:T(8,128)S(1)}, f32[2,4,2,64,256]{4,3,2,1,0:T(8,128)S(1)}) custom-call(f32[5,2,64,256]{3,2,1,0:T(8,128)S(1)} %collective-permute-done.8.refs_0_.refs_8_, f32[5,2,64,256]{3,2,1,0:T(8,128)S(1)} %collective-permute-done.4.refs_1_.refs_9_, f32[4,2,64,256]{3,2,1,0:T(8,128)S(1)} %collective-permute-done.9.refs_2_.refs_12_, ...), custom_call_target="tpu_custom_call" | custom-call | bytes 1110000 | tf_op jit(solution)/shard_map/edges/pallas_call | solution.py:126
  107.7 1.9 %collective-permute-start.18 = (f32[2,4,2,64,256]{4,3,2,1,0:T(8,128)S(1)}, f32[2,4,2,64,256]{4,3,2,1,0:T(8,128)S(1)}, u32[]{:S(2)}, u32[]{:S(2)}) collective-permute-start(f32[2,4,2,64,256]{4,3,2,1,0:T(8,128)S(1)} %get-tuple-element.73), channel_id=1, source_target_pairs={{0,1},{1,2},{2,3},{3,4},{4,5},{5,6},{6,7},{8,9},{9,10},{10,11},{11... | collective-permute-start | bytes 3145736 | tf_op jit(solution)/shard_map/ppermute | solution.py:370
  109.6 3.9 %collective-permute-start.19 = (f32[2,4,2,64,256]{4,3,2,1,0:T(8,128)S(1)}, f32[2,4,2,64,256]{4,3,2,1,0:T(8,128)S(1)}, u32[]{:S(2)}, u32[]{:S(2)}) collective-permute-start(f32[2,4,2,64,256]{4,3,2,1,0:T(8,128)S(1)} %get-tuple-element.74), channel_id=1, source_target_pairs={{1,0},{2,1},{3,2},{4,3},{5,4},{6,5},{7,6},{9,8},{10,9},{11,10},{12... | collective-permute-start | bytes 3145736 | tf_op jit(solution)/shard_map/ppermute | solution.py:370
  113.5 0.6 collective-permute-start.23
  114.1 1.5 collective-permute-start.22
  115.6 8.3 %collective-permute-done.18.refs_4_ = f32[2,4,2,64,256]{4,3,2,1,0:T(8,128)S(1)} collective-permute-done((f32[2,4,2,64,256]{4,3,2,1,0:T(8,128)S(1)}, f32[2,4,2,64,256]{4,3,2,1,0:T(8,128)S(1)}, u32[]{:S(2)}, u32[]{:S(2)}) %collective-permute-start.18) | collective-permute-done | bytes 1048608 | tf_op jit(solution)/shard_map/ppermute | solution.py:370
  123.8 1.8 %collective-permute-done.19.refs_5_ = f32[2,4,2,64,256]{4,3,2,1,0:T(8,128)S(1)} collective-permute-done((f32[2,4,2,64,256]{4,3,2,1,0:T(8,128)S(1)}, f32[2,4,2,64,256]{4,3,2,1,0:T(8,128)S(1)}, u32[]{:S(2)}, u32[]{:S(2)}) %collective-permute-start.19) | collective-permute-done | bytes 1048608 | tf_op jit(solution)/shard_map/ppermute | solution.py:370
  125.6 8.3 %apply.3 = (f32[128,2,32,256]{3,2,1,0:T(8,128)}, f32[4,2,128,256]{3,2,1,0:T(8,128)S(1)}, f32[4,2,128,256]{3,2,1,0:T(8,128)S(1)}) custom-call(bf16[256,1536]{1,0:T(8,128)(2,1)S(1)} %get-tuple-element.44.refs_0_, bf16[256,1536]{1,0:T(8,128)(2,1)S(1)} %get-tuple-element.45.refs_1_, ...), custom_call_target="tpu_custom_call", output_to_operand_aliasing={{0}: (22, {})} | custom-call | bytes 3700000 | tf_op jit(solution)/shard_map/apply/pallas_call | solution.py:206
  133.9 0.6 collective-permute-start.21
  134.5 1.5 collective-permute-start.20
  136.0 2.3 %collective-permute-done.23.got_b = f32[4,2,128,256]{3,2,1,0:T(8,128)S(1)} collective-permute-done((f32[4,2,128,256]{3,2,1,0:T(8,128)S(1)}, f32[4,2,128,256]{3,2,1,0:T(8,128)S(1)}, u32[]{:S(2)}, u32[]{:S(2)}) %collective-permute-start.23) | collective-permute-done | bytes 1048608 | tf_op jit(solution)/shard_map/ppermute | solution.py:319
  138.3 0.2 collective-permute-done.22.got_a
  138.6 1.4 place.2._
  140.0 19.9 %collective-permute-done.21.got_b = f32[4,2,128,256]{3,2,1,0:T(8,128)S(1)} collective-permute-done((f32[4,2,128,256]{3,2,1,0:T(8,128)S(1)}, f32[4,2,128,256]{3,2,1,0:T(8,128)S(1)}, u32[]{:S(2)}, u32[]{:S(2)}) %collective-permute-start.21) | collective-permute-done | bytes 1048608 | tf_op jit(solution)/shard_map/ppermute | solution.py:319
  159.9 0.2 collective-permute-done.20.got_a
  160.1 1.4 place.3
  (8 shorter events, 0.0 us)
Async XLA Ops:
  0.0 40.5 %copy-start.1 = (f32[64,2,32,256]{3,2,1,0:T(8,128)S(1)}, f32[64,2,32,256]{3,2,1,0:T(8,128)}, u32[]{:S(2)}) copy-start(f32[64,2,32,256]{3,2,1,0:T(8,128)} %in_ref.4) | copy-start | bytes 12582916
  3.8 19.6 %collective-permute-start.1 = (f32[6,2,64,256]{3,2,1,0:T(8,128)}, f32[6,2,64,256]{3,2,1,0:T(8,128)S(1)}, u32[]{:S(2)}, u32[]{:S(2)}) collective-permute-start(f32[6,2,64,256]{3,2,1,0:T(8,128)} %get-tuple-element.48), channel_id=1, source_target_pairs={{0,16},{8,24},{16,0},{24,8},{1,17},{9,25},{17,1},{25,9},{2,18},{10... | collective-permute-start | bytes 2359304 | tf_op jit(solution)/shard_map/ppermute | solution.py:319
  5.4 16.4 %collective-permute-start = (f32[5,2,64,256]{3,2,1,0:T(8,128)}, f32[5,2,64,256]{3,2,1,0:T(8,128)S(1)}, u32[]{:S(2)}, u32[]{:S(2)}) collective-permute-start(f32[5,2,64,256]{3,2,1,0:T(8,128)} %get-tuple-element.47), channel_id=1, source_target_pairs={{0,8},{8,0},{16,24},{24,16},{1,9},{9,1},{17,25},{25,17},{2,10},{10... | collective-permute-start | bytes 1966088 | tf_op jit(solution)/shard_map/ppermute | solution.py:319
  6.9 1.0 copy-start.2
  7.9 1.0 copy-start.3
  9.0 0.7 copy-start.5
  23.4 16.6 %collective-permute-start.4 = (f32[5,2,64,256]{3,2,1,0:T(8,128)S(1)}, f32[5,2,64,256]{3,2,1,0:T(8,128)S(1)}, u32[]{:S(2)}, u32[]{:S(2)}) collective-permute-start(f32[5,2,64,256]{3,2,1,0:T(8,128)S(1)} %collective-permute-done.refs_1_.refs_7_), channel_id=1, source_target_pairs={{0,16},{8,24},{16,0},{24,8},{1,17},{9,25},{17,1},{25,9},{2,18},{10... | collective-permute-start | bytes 1966088 | tf_op jit(solution)/shard_map/ppermute | solution.py:319
  24.9 19.1 %collective-permute-start.2 = (f32[6,2,64,256]{3,2,1,0:T(8,128)S(1)}, f32[6,2,64,256]{3,2,1,0:T(8,128)S(1)}, u32[]{:S(2)}, u32[]{:S(2)}) collective-permute-start(f32[6,2,64,256]{3,2,1,0:T(8,128)S(1)} %collective-permute-done.1.refs_5_.refs_3_.refs_12_.refs_16_), channel_id=1, source_target_pairs={{0,8},{8,0},{16,24},{24,16},{1,9},{9,1},{17,25},{25,17},{2,10},{10... | collective-permute-start | bytes 2359304 | tf_op jit(solution)/shard_map/ppermute | solution.py:319
  26.4 2.2 %copy-start = (f32[64,2,32,256]{3,2,1,0:T(8,128)S(1)}, f32[64,2,32,256]{3,2,1,0:T(8,128)}, u32[]{:S(2)}) copy-start(f32[64,2,32,256]{3,2,1,0:T(8,128)} %in_ref.4) | copy-start | bytes 12582916
  28.6 0.7 copy-start.4
  33.8 25.3 %collective-permute-start.10 = (f32[2,4,2,64,256]{4,3,2,1,0:T(8,128)S(1)}, f32[2,4,2,64,256]{4,3,2,1,0:T(8,128)S(1)}, u32[]{:S(2)}, u32[]{:S(2)}) collective-permute-start(f32[2,4,2,64,256]{4,3,2,1,0:T(8,128)S(1)} %get-tuple-element.62), channel_id=1, source_target_pairs={{0,1},{1,2},{2,3},{3,4},{4,5},{5,6},{6,7},{8,9},{9,10},{10,11},{11... | collective-permute-start | bytes 3145736 | tf_op jit(solution)/shard_map/ppermute | solution.py:370
  35.7 23.4 %collective-permute-start.11 = (f32[2,4,2,64,256]{4,3,2,1,0:T(8,128)S(1)}, f32[2,4,2,64,256]{4,3,2,1,0:T(8,128)S(1)}, u32[]{:S(2)}, u32[]{:S(2)}) collective-permute-start(f32[2,4,2,64,256]{4,3,2,1,0:T(8,128)S(1)} %get-tuple-element.63), channel_id=1, source_target_pairs={{1,0},{2,1},{3,2},{4,3},{5,4},{6,5},{7,6},{9,8},{10,9},{11,10},{12... | collective-permute-start | bytes 3145736 | tf_op jit(solution)/shard_map/ppermute | solution.py:370
  39.4 28.7 %collective-permute-start.12 = (f32[6,2,64,256]{3,2,1,0:T(8,128)S(1)}, f32[6,2,64,256]{3,2,1,0:T(8,128)S(1)}, u32[]{:S(2)}, u32[]{:S(2)}) collective-permute-start(f32[6,2,64,256]{3,2,1,0:T(8,128)S(1)} %get-tuple-element.54.refs_4_.refs_2_.refs_10_.refs_14_), channel_id=1, source_target_pairs={{0,8},{8,0},{16,24},{24,16},{1,9},{9,1},{17,25},{25,17},{2,10},{10... | collective-permute-start | bytes 2359304 | tf_op jit(solution)/shard_map/ppermute | solution.py:319
  40.0 17.6 %collective-permute-start.8 = (f32[5,2,64,256]{3,2,1,0:T(8,128)S(1)}, f32[5,2,64,256]{3,2,1,0:T(8,128)S(1)}, u32[]{:S(2)}, u32[]{:S(2)}) collective-permute-start(f32[5,2,64,256]{3,2,1,0:T(8,128)S(1)} %get-tuple-element.46.refs_0_.refs_6_), channel_id=1, source_target_pairs={{0,16},{8,24},{16,0},{24,8},{1,17},{9,25},{17,1},{25,9},{2,18},{10... | collective-permute-start | bytes 1966088 | tf_op jit(solution)/shard_map/ppermute | solution.py:319
  44.0 23.5 %collective-permute-start.5 = (f32[4,2,64,256]{3,2,1,0:T(8,128)S(1)}, f32[4,2,64,256]{3,2,1,0:T(8,128)S(1)}, u32[]{:S(2)}, u32[]{:S(2)}) collective-permute-start(f32[4,2,64,256]{3,2,1,0:T(8,128)S(1)} %get-tuple-element.58), channel_id=1, source_target_pairs={{0,16},{8,24},{16,0},{24,8},{1,17},{9,25},{17,1},{25,9},{2,18},{10... | collective-permute-start | bytes 1572872 | tf_op jit(solution)/shard_map/ppermute | solution.py:319
  57.6 19.0 %collective-permute-start.3 = (f32[4,2,64,256]{3,2,1,0:T(8,128)S(1)}, f32[4,2,64,256]{3,2,1,0:T(8,128)S(1)}, u32[]{:S(2)}, u32[]{:S(2)}) collective-permute-start(f32[4,2,64,256]{3,2,1,0:T(8,128)S(1)} %get-tuple-element.53), channel_id=1, source_target_pairs={{0,8},{8,0},{16,24},{24,16},{1,9},{9,1},{17,25},{25,17},{2,10},{10... | collective-permute-start | bytes 1572872 | tf_op jit(solution)/shard_map/ppermute | solution.py:319
  67.5 15.6 %collective-permute-start.9 = (f32[4,2,64,256]{3,2,1,0:T(8,128)S(1)}, f32[4,2,64,256]{3,2,1,0:T(8,128)S(1)}, u32[]{:S(2)}, u32[]{:S(2)}) collective-permute-start(f32[4,2,64,256]{3,2,1,0:T(8,128)S(1)} %get-tuple-element.61.refs_2_.refs_10_), channel_id=1, source_target_pairs={{0,16},{8,24},{16,0},{24,8},{1,17},{9,25},{17,1},{25,9},{2,18},{10... | collective-permute-start | bytes 1572872 | tf_op jit(solution)/shard_map/ppermute | solution.py:319
  71.1 21.0 %collective-permute-start.13 = (f32[2,4,2,64,256]{4,3,2,1,0:T(8,128)S(1)}, f32[2,4,2,64,256]{4,3,2,1,0:T(8,128)S(1)}, u32[]{:S(2)}, u32[]{:S(2)}) collective-permute-start(f32[2,4,2,64,256]{4,3,2,1,0:T(8,128)S(1)} %get-tuple-element.65), channel_id=1, source_target_pairs={{0,1},{1,2},{2,3},{3,4},{4,5},{5,6},{6,7},{8,9},{9,10},{10,11},{11... | collective-permute-start | bytes 3145736 | tf_op jit(solution)/shard_map/ppermute | solution.py:370
  73.0 20.5 %collective-permute-start.14 = (f32[2,4,2,64,256]{4,3,2,1,0:T(8,128)S(1)}, f32[2,4,2,64,256]{4,3,2,1,0:T(8,128)S(1)}, u32[]{:S(2)}, u32[]{:S(2)}) collective-permute-start(f32[2,4,2,64,256]{4,3,2,1,0:T(8,128)S(1)} %get-tuple-element.66), channel_id=1, source_target_pairs={{1,0},{2,1},{3,2},{4,3},{5,4},{6,5},{7,6},{9,8},{10,9},{11,10},{12... | collective-permute-start | bytes 3145736 | tf_op jit(solution)/shard_map/ppermute | solution.py:370
  76.7 13.9 %collective-permute-start.16 = (f32[4,2,64,256]{3,2,1,0:T(8,128)S(1)}, f32[4,2,64,256]{3,2,1,0:T(8,128)S(1)}, u32[]{:S(2)}, u32[]{:S(2)}) collective-permute-start(f32[4,2,64,256]{3,2,1,0:T(8,128)S(1)} %get-tuple-element.71.refs_6_.refs_18_), channel_id=1, source_target_pairs={{0,8},{8,0},{16,24},{24,16},{1,9},{9,1},{17,25},{25,17},{2,10},{10... | collective-permute-start | bytes 1572872 | tf_op jit(solution)/shard_map/ppermute | solution.py:319
  81.2 20.6 %collective-permute-start.6 = (f32[2,4,2,64,256]{4,3,2,1,0:T(8,128)S(1)}, f32[2,4,2,64,256]{4,3,2,1,0:T(8,128)S(1)}, u32[]{:S(2)}, u32[]{:S(2)}) collective-permute-start(f32[2,4,2,64,256]{4,3,2,1,0:T(8,128)S(1)} %get-tuple-element.59), channel_id=1, source_target_pairs={{0,1},{1,2},{2,3},{3,4},{4,5},{5,6},{6,7},{8,9},{9,10},{10,11},{11... | collective-permute-start | bytes 3145736 | tf_op jit(solution)/shard_map/ppermute | solution.py:370
  83.2 18.7 %collective-permute-start.7 = (f32[2,4,2,64,256]{4,3,2,1,0:T(8,128)S(1)}, f32[2,4,2,64,256]{4,3,2,1,0:T(8,128)S(1)}, u32[]{:S(2)}, u32[]{:S(2)}) collective-permute-start(f32[2,4,2,64,256]{4,3,2,1,0:T(8,128)S(1)} %get-tuple-element.60), channel_id=1, source_target_pairs={{1,0},{2,1},{3,2},{4,3},{5,4},{6,5},{7,6},{9,8},{10,9},{11,10},{12... | collective-permute-start | bytes 3145736 | tf_op jit(solution)/shard_map/ppermute | solution.py:370
  90.5 12.9 %collective-permute-start.15 = (f32[4,2,64,256]{3,2,1,0:T(8,128)S(1)}, f32[4,2,64,256]{3,2,1,0:T(8,128)S(1)}, u32[]{:S(2)}, u32[]{:S(2)}) collective-permute-start(f32[4,2,64,256]{3,2,1,0:T(8,128)S(1)} %collective-permute-done.3.refs_3_.refs_11_), channel_id=1, source_target_pairs={{0,16},{8,24},{16,0},{24,8},{1,17},{9,25},{17,1},{25,9},{2,18},{10... | collective-permute-start | bytes 1572872 | tf_op jit(solution)/shard_map/ppermute | solution.py:319
  92.0 12.6 %collective-permute-start.17 = (f32[4,2,64,256]{3,2,1,0:T(8,128)S(1)}, f32[4,2,64,256]{3,2,1,0:T(8,128)S(1)}, u32[]{:S(2)}, u32[]{:S(2)}) collective-permute-start(f32[4,2,64,256]{3,2,1,0:T(8,128)S(1)} %collective-permute-done.5.refs_7_.refs_20_), channel_id=1, source_target_pairs={{0,8},{8,0},{16,24},{24,16},{1,9},{9,1},{17,25},{25,17},{2,10},{10... | collective-permute-start | bytes 1572872 | tf_op jit(solution)/shard_map/ppermute | solution.py:319
  107.7 16.1 %collective-permute-start.18 = (f32[2,4,2,64,256]{4,3,2,1,0:T(8,128)S(1)}, f32[2,4,2,64,256]{4,3,2,1,0:T(8,128)S(1)}, u32[]{:S(2)}, u32[]{:S(2)}) collective-permute-start(f32[2,4,2,64,256]{4,3,2,1,0:T(8,128)S(1)} %get-tuple-element.73), channel_id=1, source_target_pairs={{0,1},{1,2},{2,3},{3,4},{4,5},{5,6},{6,7},{8,9},{9,10},{10,11},{11... | collective-permute-start | bytes 3145736 | tf_op jit(solution)/shard_map/ppermute | solution.py:370
  109.6 15.9 %collective-permute-start.19 = (f32[2,4,2,64,256]{4,3,2,1,0:T(8,128)S(1)}, f32[2,4,2,64,256]{4,3,2,1,0:T(8,128)S(1)}, u32[]{:S(2)}, u32[]{:S(2)}) collective-permute-start(f32[2,4,2,64,256]{4,3,2,1,0:T(8,128)S(1)} %get-tuple-element.74), channel_id=1, source_target_pairs={{1,0},{2,1},{3,2},{4,3},{5,4},{6,5},{7,6},{9,8},{10,9},{11,10},{12... | collective-permute-start | bytes 3145736 | tf_op jit(solution)/shard_map/ppermute | solution.py:370
  113.5 24.8 %collective-permute-start.23 = (f32[4,2,128,256]{3,2,1,0:T(8,128)S(1)}, f32[4,2,128,256]{3,2,1,0:T(8,128)S(1)}, u32[]{:S(2)}, u32[]{:S(2)}) collective-permute-start(f32[4,2,128,256]{3,2,1,0:T(8,128)S(1)} %get-tuple-element.81), channel_id=1, source_target_pairs={{0,16},{8,24},{16,0},{24,8},{1,17},{9,25},{17,1},{25,9},{2,18},{10... | collective-permute-start | bytes 3145736 | tf_op jit(solution)/shard_map/ppermute | solution.py:319
  114.1 24.5 %collective-permute-start.22 = (f32[4,2,128,256]{3,2,1,0:T(8,128)S(1)}, f32[4,2,128,256]{3,2,1,0:T(8,128)S(1)}, u32[]{:S(2)}, u32[]{:S(2)}) collective-permute-start(f32[4,2,128,256]{3,2,1,0:T(8,128)S(1)} %get-tuple-element.80), channel_id=1, source_target_pairs={{0,8},{8,0},{16,24},{24,16},{1,9},{9,1},{17,25},{25,17},{2,10},{10... | collective-permute-start | bytes 3145736 | tf_op jit(solution)/shard_map/ppermute | solution.py:319
  133.9 26.0 %collective-permute-start.21 = (f32[4,2,128,256]{3,2,1,0:T(8,128)S(1)}, f32[4,2,128,256]{3,2,1,0:T(8,128)S(1)}, u32[]{:S(2)}, u32[]{:S(2)}) collective-permute-start(f32[4,2,128,256]{3,2,1,0:T(8,128)S(1)} %get-tuple-element.79), channel_id=1, source_target_pairs={{0,16},{8,24},{16,0},{24,8},{1,17},{9,25},{17,1},{25,9},{2,18},{10... | collective-permute-start | bytes 3145736 | tf_op jit(solution)/shard_map/ppermute | solution.py:319
  134.5 25.6 %collective-permute-start.20 = (f32[4,2,128,256]{3,2,1,0:T(8,128)S(1)}, f32[4,2,128,256]{3,2,1,0:T(8,128)S(1)}, u32[]{:S(2)}, u32[]{:S(2)}) collective-permute-start(f32[4,2,128,256]{3,2,1,0:T(8,128)S(1)} %get-tuple-element.77), channel_id=1, source_target_pairs={{0,8},{8,0},{16,24},{24,16},{1,9},{9,1},{17,25},{25,17},{2,10},{10... | collective-permute-start | bytes 3145736 | tf_op jit(solution)/shard_map/ppermute | solution.py:319

commit v12 on v11

--- a/solution.py
+++ b/solution.py
@@ -99,10 +99,9 @@
 
 
 def edge_kernel(chunk, depth, groups, *refs):
-    raws, (up_ref, down_ref, sems) = refs[:-3], refs[-3:]
+    raws, (up_ref, down_ref) = refs[:-2], refs[-2:]
     planes = raws[0].shape[1]
     backs = 2 if chunk else 1
-    copies = []
     for stream in range(2):
         places = where_rows(stream, chunk, depth)
         for at, row in enumerate(own_rows(chunk, depth)):
@@ -110,11 +109,7 @@
             for group in range(groups):
                 raw = raws[(stream * backs + back - 2 + backs) * groups + group]
                 for z, out in ((planes - 1, up_ref), (0, down_ref)):
-                    copy = pltpu.make_async_copy(
-                        raw.at[index, z], out.at[stream, at, group], sems.at[len(copies)]
-                    )
-                    copies.append(copy)
-    run(copies)
+                    out[stream, at, group] = raw[index, z]
 
 
 def edges(chunk, depth, raws):
@@ -126,9 +121,8 @@
     return pl.pallas_call(
         functools.partial(edge_kernel, chunk, depth, groups),
         out_shape=[shape] * 2,
-        in_specs=[HBM] * len(flat),
+        in_specs=[VMEM] * len(flat),
         out_specs=[VMEM] * 2,
-        scratch_shapes=[pltpu.SemaphoreType.DMA((4 * high * groups,))],
         compiler_params=pltpu.CompilerParams(vmem_limit_bytes=8 * 2**20),
         cost_estimate=cost(3),
         name="edges",

time: 162 us -> 156 us (0.963)
  Pallas kernels: 41.1 us -> 29.5 us
  starting transfers between devices: 41.1 us -> 44 us
  waiting for transfers between devices: 73.6 us -> 76.1 us
    pallas_call x4, Pallas kernels: 12.1 us -> 0.55 us  [edges(): pl.pallas_call(functools.partial(edge_kernel, chunk, depth, groups), out_...]
    ppermute x16, waiting for transfers between devices: 63.6 us -> 67.1 us  [swap(): return lax.ppermute(data, 'tm', [(i, i ^ bit) for i in range(count)])]
    ppermute x16, starting transfers between devices: 18.4 us -> 21.4 us  [swap(): return lax.ppermute(data, 'tm', [(i, i ^ bit) for i in range(count)])]
  transfers between devices with their start and end apart: 24 -> 24, of which waited for: 14 -> 16; matrix products, arithmetic and copies ran while one was open for 0% -> 0% of each run, Pallas kernels for 20% -> 16%
where the time goes in v12:
time: 156 us
  waiting for transfers between devices  76.1 us (49%)
  starting transfers between devices  44 us (28%)
  Pallas kernels  29.5 us (19%)
  local copies, waits for them, and re-layouts  5.61 us (4%)
    ppermute x16, waiting for transfers between devices, swap(): return lax.ppermute(data, 'tm', [(i, i ^ bit) for i in range(count)])  67.1 us
    ppermute x16, starting transfers between devices, swap(): return lax.ppermute(data, 'tm', [(i, i ^ bit) for i in range(count)])  21.4 us
    pallas_call x2, Pallas kernels, apply(): pl.pallas_call(body, out_shape=[jax.ShapeDtypeStruct(shape, jnp.float32),...  16.6 us
    ppermute x4, starting transfers between devices, beside(): lax.ppermute(down, 'space', downward)  14.8 us
    ppermute x4, starting transfers between devices, beside(): lax.ppermute(up, 'space', upward)  7.68 us
    pallas_call x3, Pallas kernels, pick(): pl.pallas_call(functools.partial(pick_kernel, chunk, depth, kinds, bits),...  7.44 us
    ppermute x4, waiting for transfers between devices, beside(): lax.ppermute(up, 'space', upward)  7.25 us
    unnamed x12, local copies, waits for them, and re-layouts  5.61 us
  transfers between devices with their start and end apart: 24, of which 16 were waited for; matrix products, arithmetic and copies ran while one was open for 0% of the time, Pallas kernels for 16%

profile of v12, /device:TPU:8, one launch (start us, length us, event | category | flops | bytes accessed | tf_op | source)
XLA Modules:
  0.0 155.5 jit_solution(8952382599990441285)
XLA Ops:
  0.0 3.8 %pick.4 = (f32[5,2,64,256]{3,2,1,0:T(8,128)}, f32[6,2,64,256]{3,2,1,0:T(8,128)}) custom-call(s32[1,64]{1,0:T(1,128)} %bitcast.2, f32[64,2,32,256]{3,2,1,0:T(8,128)} %in_ref.4), custom_call_target="tpu_custom_call" | custom-call | bytes 1850000 | tf_op jit(solution)/shard_map/pick/pallas_call | solution.py:88
  3.8 1.6 %collective-permute-start.1 = (f32[6,2,64,256]{3,2,1,0:T(8,128)}, f32[6,2,64,256]{3,2,1,0:T(8,128)S(1)}, u32[]{:S(2)}, u32[]{:S(2)}) collective-permute-start(f32[6,2,64,256]{3,2,1,0:T(8,128)} %get-tuple-element.48), channel_id=1, source_target_pairs={{0,16},{8,24},{16,0},{24,8},{1,17},{9,25},{17,1},{25,9},{2,18},{10... | collective-permute-start | bytes 2359304 | tf_op jit(solution)/shard_map/ppermute | solution.py:313
  5.4 1.5 collective-permute-start
  6.9 1.0 copy-done.2
  7.9 1.0 copy-done.3
  9.0 0.7 copy-done.5
  9.7 2.0 %maps.1 = (bf16[256,1536]{1,0:T(8,128)(2,1)S(1)}, bf16[256,1536]{1,0:T(8,128)(2,1)S(1)}) custom-call(f32[2,256,256]{2,1,0:T(8,128)S(1)} %copy-done.2, f32[2,256,256]{2,1,0:T(8,128)S(1)} %copy-done.3, f32[2,256]{1,0:T(2,128)S(1)} %copy-done.5), custom_call_target="tpu_custom_call" | custom-call | bytes 740000 | tf_op jit(solution)/shard_map/maps/pallas_call | solution.py:293
  11.7 10.1 %collective-permute-done.refs_1_.refs_7_ = f32[5,2,64,256]{3,2,1,0:T(8,128)S(1)} collective-permute-done((f32[5,2,64,256]{3,2,1,0:T(8,128)}, f32[5,2,64,256]{3,2,1,0:T(8,128)S(1)}, u32[]{:S(2)}, u32[]{:S(2)}) %collective-permute-start) | collective-permute-done | bytes 655392 | tf_op jit(solution)/shard_map/ppermute | solution.py:313
  21.8 1.6 %collective-permute-done.1.refs_5_.refs_3_.refs_12_.refs_16_ = f32[6,2,64,256]{3,2,1,0:T(8,128)S(1)} collective-permute-done((f32[6,2,64,256]{3,2,1,0:T(8,128)}, f32[6,2,64,256]{3,2,1,0:T(8,128)S(1)}, u32[]{:S(2)}, u32[]{:S(2)}) %collective-permute-start.1) | collective-permute-done | bytes 786464 | tf_op jit(solution)/shard_map/ppermute | solution.py:313
  23.4 1.5 collective-permute-start.4
  24.9 1.5 collective-permute-start.2
  26.4 2.2 %copy-done = f32[64,2,32,256]{3,2,1,0:T(8,128)S(1)} copy-done((f32[64,2,32,256]{3,2,1,0:T(8,128)S(1)}, f32[64,2,32,256]{3,2,1,0:T(8,128)}, u32[]{:S(2)}) %copy-start) | copy-done | bytes 4194328
  28.6 0.7 copy-done.4
  29.2 1.5 pick.3
  30.7 0.1 edges.5
  30.9 1.9 %collective-permute-start.10 = (f32[2,4,2,64,256]{4,3,2,1,0:T(8,128)S(1)}, f32[2,4,2,64,256]{4,3,2,1,0:T(8,128)S(1)}, u32[]{:S(2)}, u32[]{:S(2)}) collective-permute-start(f32[2,4,2,64,256]{4,3,2,1,0:T(8,128)S(1)} %get-tuple-element.62), channel_id=1, source_target_pairs={{0,1},{1,2},{2,3},{3,4},{4,5},{5,6},{6,7},{8,9},{9,10},{10,11},{11... | collective-permute-start | bytes 3145736 | tf_op jit(solution)/shard_map/ppermute | solution.py:364
  32.8 3.6 %collective-permute-start.11 = (f32[2,4,2,64,256]{4,3,2,1,0:T(8,128)S(1)}, f32[2,4,2,64,256]{4,3,2,1,0:T(8,128)S(1)}, u32[]{:S(2)}, u32[]{:S(2)}) collective-permute-start(f32[2,4,2,64,256]{4,3,2,1,0:T(8,128)S(1)} %get-tuple-element.63), channel_id=1, source_target_pairs={{1,0},{2,1},{3,2},{4,3},{5,4},{6,5},{7,6},{9,8},{10,9},{11,10},{12... | collective-permute-start | bytes 3145736 | tf_op jit(solution)/shard_map/ppermute | solution.py:364
  36.5 0.6 collective-permute-start.12
  37.1 1.9 %collective-permute-done.4.refs_1_.refs_9_ = f32[5,2,64,256]{3,2,1,0:T(8,128)S(1)} collective-permute-done((f32[5,2,64,256]{3,2,1,0:T(8,128)S(1)}, f32[5,2,64,256]{3,2,1,0:T(8,128)S(1)}, u32[]{:S(2)}, u32[]{:S(2)}) %collective-permute-start.4) | collective-permute-done | bytes 655392 | tf_op jit(solution)/shard_map/ppermute | solution.py:313
  39.0 1.5 collective-permute-start.8
  40.5 2.1 %pick.5 = (f32[4,2,64,256]{3,2,1,0:T(8,128)S(1)}, f32[4,2,64,256]{3,2,1,0:T(8,128)S(1)}, f32[4,2,64,256]{3,2,1,0:T(8,128)S(1)}, f32[4,2,64,256]{3,2,1,0:T(8,128)S(1)}) custom-call(s32[1,64]{1,0:T(1,128)S(1)} %bitcast.4, f32[64,2,32,256]{3,2,1,0:T(8,128)S(1)} %copy-done.1), custom_call_target="tpu_custom_call" | custom-call | bytes 1850000 | tf_op jit(solution)/shard_map/pick/pallas_call | solution.py:88
  42.6 2.7 %collective-permute-done.2.refs_3_.refs_13_.refs_5_.refs_17_ = f32[6,2,64,256]{3,2,1,0:T(8,128)S(1)} collective-permute-done((f32[6,2,64,256]{3,2,1,0:T(8,128)S(1)}, f32[6,2,64,256]{3,2,1,0:T(8,128)S(1)}, u32[]{:S(2)}, u32[]{:S(2)}) %collective-permute-start.2) | collective-permute-done | bytes 786464 | tf_op jit(solution)/shard_map/ppermute | solution.py:313
  45.4 0.5 collective-permute-start.5
  45.9 10.8 %collective-permute-done.8.refs_0_.refs_8_ = f32[5,2,64,256]{3,2,1,0:T(8,128)S(1)} collective-permute-done((f32[5,2,64,256]{3,2,1,0:T(8,128)S(1)}, f32[5,2,64,256]{3,2,1,0:T(8,128)S(1)}, u32[]{:S(2)}, u32[]{:S(2)}) %collective-permute-start.8) | collective-permute-done | bytes 655392 | tf_op jit(solution)/shard_map/ppermute | solution.py:313
  56.6 1.5 collective-permute-start.3
  58.1 0.0 collective-permute-done.10.refs_2_
  58.1 0.0 collective-permute-done.11.refs_3_
  58.1 7.0 %collective-permute-done.5.refs_7_.refs_20_ = f32[4,2,64,256]{3,2,1,0:T(8,128)S(1)} collective-permute-done((f32[4,2,64,256]{3,2,1,0:T(8,128)S(1)}, f32[4,2,64,256]{3,2,1,0:T(8,128)S(1)}, u32[]{:S(2)}, u32[]{:S(2)}) %collective-permute-start.5) | collective-permute-done | bytes 524320 | tf_op jit(solution)/shard_map/ppermute | solution.py:313
  65.1 1.5 collective-permute-start.9
  66.6 0.0 collective-permute-done.12.refs_2_.refs_11_.refs_4_.refs_15_
  66.6 0.1 edges.6
  66.8 1.9 %collective-permute-start.13 = (f32[2,4,2,64,256]{4,3,2,1,0:T(8,128)S(1)}, f32[2,4,2,64,256]{4,3,2,1,0:T(8,128)S(1)}, u32[]{:S(2)}, u32[]{:S(2)}) collective-permute-start(f32[2,4,2,64,256]{4,3,2,1,0:T(8,128)S(1)} %get-tuple-element.65), channel_id=1, source_target_pairs={{0,1},{1,2},{2,3},{3,4},{4,5},{5,6},{6,7},{8,9},{9,10},{10,11},{11... | collective-permute-start | bytes 3145736 | tf_op jit(solution)/shard_map/ppermute | solution.py:364
  68.7 3.6 %collective-permute-start.14 = (f32[2,4,2,64,256]{4,3,2,1,0:T(8,128)S(1)}, f32[2,4,2,64,256]{4,3,2,1,0:T(8,128)S(1)}, u32[]{:S(2)}, u32[]{:S(2)}) collective-permute-start(f32[2,4,2,64,256]{4,3,2,1,0:T(8,128)S(1)} %get-tuple-element.66), channel_id=1, source_target_pairs={{1,0},{2,1},{3,2},{4,3},{5,4},{6,5},{7,6},{9,8},{10,9},{11,10},{12... | collective-permute-start | bytes 3145736 | tf_op jit(solution)/shard_map/ppermute | solution.py:364
  72.3 0.0 collective-permute-done.3.refs_3_.refs_11_
  72.4 1.6 %collective-permute-start.16 = (f32[4,2,64,256]{3,2,1,0:T(8,128)S(1)}, f32[4,2,64,256]{3,2,1,0:T(8,128)S(1)}, u32[]{:S(2)}, u32[]{:S(2)}) collective-permute-start(f32[4,2,64,256]{3,2,1,0:T(8,128)S(1)} %get-tuple-element.71.refs_6_.refs_18_), channel_id=1, source_target_pairs={{0,8},{8,0},{16,24},{24,16},{1,9},{9,1},{17,25},{25,17},{2,10},{10... | collective-permute-start | bytes 1572872 | tf_op jit(solution)/shard_map/ppermute | solution.py:313
  73.9 0.1 edges.4
  74.0 1.9 %collective-permute-start.6 = (f32[2,4,2,64,256]{4,3,2,1,0:T(8,128)S(1)}, f32[2,4,2,64,256]{4,3,2,1,0:T(8,128)S(1)}, u32[]{:S(2)}, u32[]{:S(2)}) collective-permute-start(f32[2,4,2,64,256]{4,3,2,1,0:T(8,128)S(1)} %get-tuple-element.59), channel_id=1, source_target_pairs={{0,1},{1,2},{2,3},{3,4},{4,5},{5,6},{6,7},{8,9},{9,10},{10,11},{11... | collective-permute-start | bytes 3145736 | tf_op jit(solution)/shard_map/ppermute | solution.py:364
  76.0 0.1 collective-permute-done.9.refs_2_.refs_12_
  76.1 3.7 %collective-permute-start.7 = (f32[2,4,2,64,256]{4,3,2,1,0:T(8,128)S(1)}, f32[2,4,2,64,256]{4,3,2,1,0:T(8,128)S(1)}, u32[]{:S(2)}, u32[]{:S(2)}) collective-permute-start(f32[2,4,2,64,256]{4,3,2,1,0:T(8,128)S(1)} %get-tuple-element.60), channel_id=1, source_target_pairs={{1,0},{2,1},{3,2},{4,3},{5,4},{6,5},{7,6},{9,8},{10,9},{11,10},{12... | collective-permute-start | bytes 3145736 | tf_op jit(solution)/shard_map/ppermute | solution.py:364
  79.8 6.4 %collective-permute-done.16.refs_6_.refs_19_ = f32[4,2,64,256]{3,2,1,0:T(8,128)S(1)} collective-permute-done((f32[4,2,64,256]{3,2,1,0:T(8,128)S(1)}, f32[4,2,64,256]{3,2,1,0:T(8,128)S(1)}, u32[]{:S(2)}, u32[]{:S(2)}) %collective-permute-start.16) | collective-permute-done | bytes 524320 | tf_op jit(solution)/shard_map/ppermute | solution.py:313
  86.2 0.5 collective-permute-start.15
  86.7 0.0 collective-permute-done.13.refs_4_
  86.7 1.5 collective-permute-start.17
  88.2 0.0 collective-permute-done.14.refs_5_
  88.2 8.3 %apply.2 = (f32[128,2,32,256]{3,2,1,0:T(8,128)}, f32[4,2,128,256]{3,2,1,0:T(8,128)S(1)}, f32[4,2,128,256]{3,2,1,0:T(8,128)S(1)}) custom-call(bf16[256,1536]{1,0:T(8,128)(2,1)S(1)} %get-tuple-element.44.refs_0_, bf16[256,1536]{1,0:T(8,128)(2,1)S(1)} %get-tuple-element.45.refs_1_, f32[2,4,2,64,256]{4,3,2,1,0:T(8,128)S(1)} %collective-permute-done.10.refs_2_, ...), custom_call_target="tpu_custom_call" | custom-call | bytes 3700000 | tf_op jit(solution)/shard_map/apply/pallas_call | solution.py:200
  96.5 0.0 collective-permute-done.6.refs_2_
  96.6 2.6 %collective-permute-done.15.refs_3_.refs_13_ = f32[4,2,64,256]{3,2,1,0:T(8,128)S(1)} collective-permute-done((f32[4,2,64,256]{3,2,1,0:T(8,128)S(1)}, f32[4,2,64,256]{3,2,1,0:T(8,128)S(1)}, u32[]{:S(2)}, u32[]{:S(2)}) %collective-permute-start.15) | collective-permute-done | bytes 524320 | tf_op jit(solution)/shard_map/ppermute | solution.py:313
  99.1 0.2 collective-permute-done.17.refs_7_.refs_21_
  99.4 0.1 edges.7
  99.5 1.9 %collective-permute-start.18 = (f32[2,4,2,64,256]{4,3,2,1,0:T(8,128)S(1)}, f32[2,4,2,64,256]{4,3,2,1,0:T(8,128)S(1)}, u32[]{:S(2)}, u32[]{:S(2)}) collective-permute-start(f32[2,4,2,64,256]{4,3,2,1,0:T(8,128)S(1)} %get-tuple-element.73), channel_id=1, source_target_pairs={{0,1},{1,2},{2,3},{3,4},{4,5},{5,6},{6,7},{8,9},{9,10},{10,11},{11... | collective-permute-start | bytes 3145736 | tf_op jit(solution)/shard_map/ppermute | solution.py:364
  101.4 3.9 %collective-permute-start.19 = (f32[2,4,2,64,256]{4,3,2,1,0:T(8,128)S(1)}, f32[2,4,2,64,256]{4,3,2,1,0:T(8,128)S(1)}, u32[]{:S(2)}, u32[]{:S(2)}) collective-permute-start(f32[2,4,2,64,256]{4,3,2,1,0:T(8,128)S(1)} %get-tuple-element.74), channel_id=1, source_target_pairs={{1,0},{2,1},{3,2},{4,3},{5,4},{6,5},{7,6},{9,8},{10,9},{11,10},{12... | collective-permute-start | bytes 3145736 | tf_op jit(solution)/shard_map/ppermute | solution.py:364
  105.3 1.6 %collective-permute-start.23 = (f32[4,2,128,256]{3,2,1,0:T(8,128)S(1)}, f32[4,2,128,256]{3,2,1,0:T(8,128)S(1)}, u32[]{:S(2)}, u32[]{:S(2)}) collective-permute-start(f32[4,2,128,256]{3,2,1,0:T(8,128)S(1)} %get-tuple-element.81), channel_id=1, source_target_pairs={{0,16},{8,24},{16,0},{24,8},{1,17},{9,25},{17,1},{25,9},{2,18},{10... | collective-permute-start | bytes 3145736 | tf_op jit(solution)/shard_map/ppermute | solution.py:313
  106.9 1.5 collective-permute-start.22
  108.4 7.2 %collective-permute-done.18.refs_4_ = f32[2,4,2,64,256]{4,3,2,1,0:T(8,128)S(1)} collective-permute-done((f32[2,4,2,64,256]{4,3,2,1,0:T(8,128)S(1)}, f32[2,4,2,64,256]{4,3,2,1,0:T(8,128)S(1)}, u32[]{:S(2)}, u32[]{:S(2)}) %collective-permute-start.18) | collective-permute-done | bytes 1048608 | tf_op jit(solution)/shard_map/ppermute | solution.py:364
  115.6 1.8 %collective-permute-done.19.refs_5_ = f32[2,4,2,64,256]{4,3,2,1,0:T(8,128)S(1)} collective-permute-done((f32[2,4,2,64,256]{4,3,2,1,0:T(8,128)S(1)}, f32[2,4,2,64,256]{4,3,2,1,0:T(8,128)S(1)}, u32[]{:S(2)}, u32[]{:S(2)}) %collective-permute-start.19) | collective-permute-done | bytes 1048608 | tf_op jit(solution)/shard_map/ppermute | solution.py:364
  117.4 8.3 %apply.3 = (f32[128,2,32,256]{3,2,1,0:T(8,128)}, f32[4,2,128,256]{3,2,1,0:T(8,128)S(1)}, f32[4,2,128,256]{3,2,1,0:T(8,128)S(1)}) custom-call(bf16[256,1536]{1,0:T(8,128)(2,1)S(1)} %get-tuple-element.44.refs_0_, bf16[256,1536]{1,0:T(8,128)(2,1)S(1)} %get-tuple-element.45.refs_1_, ...), custom_call_target="tpu_custom_call", output_to_operand_aliasing={{0}: (22, {})} | custom-call | bytes 3700000 | tf_op jit(solution)/shard_map/apply/pallas_call | solution.py:200
  125.7 1.6 %collective-permute-start.21 = (f32[4,2,128,256]{3,2,1,0:T(8,128)S(1)}, f32[4,2,128,256]{3,2,1,0:T(8,128)S(1)}, u32[]{:S(2)}, u32[]{:S(2)}) collective-permute-start(f32[4,2,128,256]{3,2,1,0:T(8,128)S(1)} %get-tuple-element.79), channel_id=1, source_target_pairs={{0,16},{8,24},{16,0},{24,8},{1,17},{9,25},{17,1},{25,9},{2,18},{10... | collective-permute-start | bytes 3145736 | tf_op jit(solution)/shard_map/ppermute | solution.py:313
  127.3 1.5 collective-permute-start.20
  128.8 1.6 %collective-permute-done.23.got_b = f32[4,2,128,256]{3,2,1,0:T(8,128)S(1)} collective-permute-done((f32[4,2,128,256]{3,2,1,0:T(8,128)S(1)}, f32[4,2,128,256]{3,2,1,0:T(8,128)S(1)}, u32[]{:S(2)}, u32[]{:S(2)}) %collective-permute-start.23) | collective-permute-done | bytes 1048608 | tf_op jit(solution)/shard_map/ppermute | solution.py:313
  130.4 1.2 collective-permute-done.22.got_a
  131.6 1.4 place.2._
  133.1 19.6 %collective-permute-done.21.got_b = f32[4,2,128,256]{3,2,1,0:T(8,128)S(1)} collective-permute-done((f32[4,2,128,256]{3,2,1,0:T(8,128)S(1)}, f32[4,2,128,256]{3,2,1,0:T(8,128)S(1)}, u32[]{:S(2)}, u32[]{:S(2)}) %collective-permute-start.21) | collective-permute-done | bytes 1048608 | tf_op jit(solution)/shard_map/ppermute | solution.py:313
  152.7 1.2 collective-permute-done.20.got_a
  153.9 1.4 place.3
  (8 shorter events, 0.0 us)
Async XLA Ops:
  0.0 40.5 %copy-start.1 = (f32[64,2,32,256]{3,2,1,0:T(8,128)S(1)}, f32[64,2,32,256]{3,2,1,0:T(8,128)}, u32[]{:S(2)}) copy-start(f32[64,2,32,256]{3,2,1,0:T(8,128)} %in_ref.4) | copy-start | bytes 12582916
  3.8 19.6 %collective-permute-start.1 = (f32[6,2,64,256]{3,2,1,0:T(8,128)}, f32[6,2,64,256]{3,2,1,0:T(8,128)S(1)}, u32[]{:S(2)}, u32[]{:S(2)}) collective-permute-start(f32[6,2,64,256]{3,2,1,0:T(8,128)} %get-tuple-element.48), channel_id=1, source_target_pairs={{0,16},{8,24},{16,0},{24,8},{1,17},{9,25},{17,1},{25,9},{2,18},{10... | collective-permute-start | bytes 2359304 | tf_op jit(solution)/shard_map/ppermute | solution.py:313
  5.4 16.4 %collective-permute-start = (f32[5,2,64,256]{3,2,1,0:T(8,128)}, f32[5,2,64,256]{3,2,1,0:T(8,128)S(1)}, u32[]{:S(2)}, u32[]{:S(2)}) collective-permute-start(f32[5,2,64,256]{3,2,1,0:T(8,128)} %get-tuple-element.47), channel_id=1, source_target_pairs={{0,8},{8,0},{16,24},{24,16},{1,9},{9,1},{17,25},{25,17},{2,10},{10... | collective-permute-start | bytes 1966088 | tf_op jit(solution)/shard_map/ppermute | solution.py:313
  6.9 1.0 copy-start.2
  7.9 1.0 copy-start.3
  9.0 0.7 copy-start.5
  23.4 15.6 %collective-permute-start.4 = (f32[5,2,64,256]{3,2,1,0:T(8,128)S(1)}, f32[5,2,64,256]{3,2,1,0:T(8,128)S(1)}, u32[]{:S(2)}, u32[]{:S(2)}) collective-permute-start(f32[5,2,64,256]{3,2,1,0:T(8,128)S(1)} %collective-permute-done.refs_1_.refs_7_), channel_id=1, source_target_pairs={{0,16},{8,24},{16,0},{24,8},{1,17},{9,25},{17,1},{25,9},{2,18},{10... | collective-permute-start | bytes 1966088 | tf_op jit(solution)/shard_map/ppermute | solution.py:313
  24.9 20.5 %collective-permute-start.2 = (f32[6,2,64,256]{3,2,1,0:T(8,128)S(1)}, f32[6,2,64,256]{3,2,1,0:T(8,128)S(1)}, u32[]{:S(2)}, u32[]{:S(2)}) collective-permute-start(f32[6,2,64,256]{3,2,1,0:T(8,128)S(1)} %collective-permute-done.1.refs_5_.refs_3_.refs_12_.refs_16_), channel_id=1, source_target_pairs={{0,8},{8,0},{16,24},{24,16},{1,9},{9,1},{17,25},{25,17},{2,10},{10... | collective-permute-start | bytes 2359304 | tf_op jit(solution)/shard_map/ppermute | solution.py:313
  26.4 2.2 %copy-start = (f32[64,2,32,256]{3,2,1,0:T(8,128)S(1)}, f32[64,2,32,256]{3,2,1,0:T(8,128)}, u32[]{:S(2)}) copy-start(f32[64,2,32,256]{3,2,1,0:T(8,128)} %in_ref.4) | copy-start | bytes 12582916
  28.6 0.7 copy-start.4
  30.9 27.3 %collective-permute-start.10 = (f32[2,4,2,64,256]{4,3,2,1,0:T(8,128)S(1)}, f32[2,4,2,64,256]{4,3,2,1,0:T(8,128)S(1)}, u32[]{:S(2)}, u32[]{:S(2)}) collective-permute-start(f32[2,4,2,64,256]{4,3,2,1,0:T(8,128)S(1)} %get-tuple-element.62), channel_id=1, source_target_pairs={{0,1},{1,2},{2,3},{3,4},{4,5},{5,6},{6,7},{8,9},{9,10},{10,11},{11... | collective-permute-start | bytes 3145736 | tf_op jit(solution)/shard_map/ppermute | solution.py:364
  32.8 25.3 %collective-permute-start.11 = (f32[2,4,2,64,256]{4,3,2,1,0:T(8,128)S(1)}, f32[2,4,2,64,256]{4,3,2,1,0:T(8,128)S(1)}, u32[]{:S(2)}, u32[]{:S(2)}) collective-permute-start(f32[2,4,2,64,256]{4,3,2,1,0:T(8,128)S(1)} %get-tuple-element.63), channel_id=1, source_target_pairs={{1,0},{2,1},{3,2},{4,3},{5,4},{6,5},{7,6},{9,8},{10,9},{11,10},{12... | collective-permute-start | bytes 3145736 | tf_op jit(solution)/shard_map/ppermute | solution.py:364
  36.5 30.2 %collective-permute-start.12 = (f32[6,2,64,256]{3,2,1,0:T(8,128)S(1)}, f32[6,2,64,256]{3,2,1,0:T(8,128)S(1)}, u32[]{:S(2)}, u32[]{:S(2)}) collective-permute-start(f32[6,2,64,256]{3,2,1,0:T(8,128)S(1)} %get-tuple-element.54.refs_4_.refs_2_.refs_10_.refs_14_), channel_id=1, source_target_pairs={{0,8},{8,0},{16,24},{24,16},{1,9},{9,1},{17,25},{25,17},{2,10},{10... | collective-permute-start | bytes 2359304 | tf_op jit(solution)/shard_map/ppermute | solution.py:313
  39.0 17.7 %collective-permute-start.8 = (f32[5,2,64,256]{3,2,1,0:T(8,128)S(1)}, f32[5,2,64,256]{3,2,1,0:T(8,128)S(1)}, u32[]{:S(2)}, u32[]{:S(2)}) collective-permute-start(f32[5,2,64,256]{3,2,1,0:T(8,128)S(1)} %get-tuple-element.46.refs_0_.refs_6_), channel_id=1, source_target_pairs={{0,16},{8,24},{16,0},{24,8},{1,17},{9,25},{17,1},{25,9},{2,18},{10... | collective-permute-start | bytes 1966088 | tf_op jit(solution)/shard_map/ppermute | solution.py:313
  45.4 19.7 %collective-permute-start.5 = (f32[4,2,64,256]{3,2,1,0:T(8,128)S(1)}, f32[4,2,64,256]{3,2,1,0:T(8,128)S(1)}, u32[]{:S(2)}, u32[]{:S(2)}) collective-permute-start(f32[4,2,64,256]{3,2,1,0:T(8,128)S(1)} %get-tuple-element.58), channel_id=1, source_target_pairs={{0,16},{8,24},{16,0},{24,8},{1,17},{9,25},{17,1},{25,9},{2,18},{10... | collective-permute-start | bytes 1572872 | tf_op jit(solution)/shard_map/ppermute | solution.py:313
  56.6 15.7 %collective-permute-start.3 = (f32[4,2,64,256]{3,2,1,0:T(8,128)S(1)}, f32[4,2,64,256]{3,2,1,0:T(8,128)S(1)}, u32[]{:S(2)}, u32[]{:S(2)}) collective-permute-start(f32[4,2,64,256]{3,2,1,0:T(8,128)S(1)} %get-tuple-element.53), channel_id=1, source_target_pairs={{0,8},{8,0},{16,24},{24,16},{1,9},{9,1},{17,25},{25,17},{2,10},{10... | collective-permute-start | bytes 1572872 | tf_op jit(solution)/shard_map/ppermute | solution.py:313
  65.1 11.0 %collective-permute-start.9 = (f32[4,2,64,256]{3,2,1,0:T(8,128)S(1)}, f32[4,2,64,256]{3,2,1,0:T(8,128)S(1)}, u32[]{:S(2)}, u32[]{:S(2)}) collective-permute-start(f32[4,2,64,256]{3,2,1,0:T(8,128)S(1)} %get-tuple-element.61.refs_2_.refs_10_), channel_id=1, source_target_pairs={{0,16},{8,24},{16,0},{24,8},{1,17},{9,25},{17,1},{25,9},{2,18},{10... | collective-permute-start | bytes 1572872 | tf_op jit(solution)/shard_map/ppermute | solution.py:313
  66.8 20.0 %collective-permute-start.13 = (f32[2,4,2,64,256]{4,3,2,1,0:T(8,128)S(1)}, f32[2,4,2,64,256]{4,3,2,1,0:T(8,128)S(1)}, u32[]{:S(2)}, u32[]{:S(2)}) collective-permute-start(f32[2,4,2,64,256]{4,3,2,1,0:T(8,128)S(1)} %get-tuple-element.65), channel_id=1, source_target_pairs={{0,1},{1,2},{2,3},{3,4},{4,5},{5,6},{6,7},{8,9},{9,10},{10,11},{11... | collective-permute-start | bytes 3145736 | tf_op jit(solution)/shard_map/ppermute | solution.py:364
  68.7 19.5 %collective-permute-start.14 = (f32[2,4,2,64,256]{4,3,2,1,0:T(8,128)S(1)}, f32[2,4,2,64,256]{4,3,2,1,0:T(8,128)S(1)}, u32[]{:S(2)}, u32[]{:S(2)}) collective-permute-start(f32[2,4,2,64,256]{4,3,2,1,0:T(8,128)S(1)} %get-tuple-element.66), channel_id=1, source_target_pairs={{1,0},{2,1},{3,2},{4,3},{5,4},{6,5},{7,6},{9,8},{10,9},{11,10},{12... | collective-permute-start | bytes 3145736 | tf_op jit(solution)/shard_map/ppermute | solution.py:364
  72.4 13.9 %collective-permute-start.16 = (f32[4,2,64,256]{3,2,1,0:T(8,128)S(1)}, f32[4,2,64,256]{3,2,1,0:T(8,128)S(1)}, u32[]{:S(2)}, u32[]{:S(2)}) collective-permute-start(f32[4,2,64,256]{3,2,1,0:T(8,128)S(1)} %get-tuple-element.71.refs_6_.refs_18_), channel_id=1, source_target_pairs={{0,8},{8,0},{16,24},{24,16},{1,9},{9,1},{17,25},{25,17},{2,10},{10... | collective-permute-start | bytes 1572872 | tf_op jit(solution)/shard_map/ppermute | solution.py:313
  74.0 22.5 %collective-permute-start.6 = (f32[2,4,2,64,256]{4,3,2,1,0:T(8,128)S(1)}, f32[2,4,2,64,256]{4,3,2,1,0:T(8,128)S(1)}, u32[]{:S(2)}, u32[]{:S(2)}) collective-permute-start(f32[2,4,2,64,256]{4,3,2,1,0:T(8,128)S(1)} %get-tuple-element.59), channel_id=1, source_target_pairs={{0,1},{1,2},{2,3},{3,4},{4,5},{5,6},{6,7},{8,9},{9,10},{10,11},{11... | collective-permute-start | bytes 3145736 | tf_op jit(solution)/shard_map/ppermute | solution.py:364
  76.1 20.4 %collective-permute-start.7 = (f32[2,4,2,64,256]{4,3,2,1,0:T(8,128)S(1)}, f32[2,4,2,64,256]{4,3,2,1,0:T(8,128)S(1)}, u32[]{:S(2)}, u32[]{:S(2)}) collective-permute-start(f32[2,4,2,64,256]{4,3,2,1,0:T(8,128)S(1)} %get-tuple-element.60), channel_id=1, source_target_pairs={{1,0},{2,1},{3,2},{4,3},{5,4},{6,5},{7,6},{9,8},{10,9},{11,10},{12... | collective-permute-start | bytes 3145736 | tf_op jit(solution)/shard_map/ppermute | solution.py:364
  86.2 12.9 %collective-permute-start.15 = (f32[4,2,64,256]{3,2,1,0:T(8,128)S(1)}, f32[4,2,64,256]{3,2,1,0:T(8,128)S(1)}, u32[]{:S(2)}, u32[]{:S(2)}) collective-permute-start(f32[4,2,64,256]{3,2,1,0:T(8,128)S(1)} %collective-permute-done.3.refs_3_.refs_11_), channel_id=1, source_target_pairs={{0,16},{8,24},{16,0},{24,8},{1,17},{9,25},{17,1},{25,9},{2,18},{10... | collective-permute-start | bytes 1572872 | tf_op jit(solution)/shard_map/ppermute | solution.py:313
  86.7 12.6 %collective-permute-start.17 = (f32[4,2,64,256]{3,2,1,0:T(8,128)S(1)}, f32[4,2,64,256]{3,2,1,0:T(8,128)S(1)}, u32[]{:S(2)}, u32[]{:S(2)}) collective-permute-start(f32[4,2,64,256]{3,2,1,0:T(8,128)S(1)} %collective-permute-done.5.refs_7_.refs_20_), channel_id=1, source_target_pairs={{0,8},{8,0},{16,24},{24,16},{1,9},{9,1},{17,25},{25,17},{2,10},{10... | collective-permute-start | bytes 1572872 | tf_op jit(solution)/shard_map/ppermute | solution.py:313
  99.5 16.1 %collective-permute-start.18 = (f32[2,4,2,64,256]{4,3,2,1,0:T(8,128)S(1)}, f32[2,4,2,64,256]{4,3,2,1,0:T(8,128)S(1)}, u32[]{:S(2)}, u32[]{:S(2)}) collective-permute-start(f32[2,4,2,64,256]{4,3,2,1,0:T(8,128)S(1)} %get-tuple-element.73), channel_id=1, source_target_pairs={{0,1},{1,2},{2,3},{3,4},{4,5},{5,6},{6,7},{8,9},{9,10},{10,11},{11... | collective-permute-start | bytes 3145736 | tf_op jit(solution)/shard_map/ppermute | solution.py:364
  101.4 15.9 %collective-permute-start.19 = (f32[2,4,2,64,256]{4,3,2,1,0:T(8,128)S(1)}, f32[2,4,2,64,256]{4,3,2,1,0:T(8,128)S(1)}, u32[]{:S(2)}, u32[]{:S(2)}) collective-permute-start(f32[2,4,2,64,256]{4,3,2,1,0:T(8,128)S(1)} %get-tuple-element.74), channel_id=1, source_target_pairs={{1,0},{2,1},{3,2},{4,3},{5,4},{6,5},{7,6},{9,8},{10,9},{11,10},{12... | collective-permute-start | bytes 3145736 | tf_op jit(solution)/shard_map/ppermute | solution.py:364
  105.3 25.1 %collective-permute-start.23 = (f32[4,2,128,256]{3,2,1,0:T(8,128)S(1)}, f32[4,2,128,256]{3,2,1,0:T(8,128)S(1)}, u32[]{:S(2)}, u32[]{:S(2)}) collective-permute-start(f32[4,2,128,256]{3,2,1,0:T(8,128)S(1)} %get-tuple-element.81), channel_id=1, source_target_pairs={{0,16},{8,24},{16,0},{24,8},{1,17},{9,25},{17,1},{25,9},{2,18},{10... | collective-permute-start | bytes 3145736 | tf_op jit(solution)/shard_map/ppermute | solution.py:313
  106.9 24.7 %collective-permute-start.22 = (f32[4,2,128,256]{3,2,1,0:T(8,128)S(1)}, f32[4,2,128,256]{3,2,1,0:T(8,128)S(1)}, u32[]{:S(2)}, u32[]{:S(2)}) collective-permute-start(f32[4,2,128,256]{3,2,1,0:T(8,128)S(1)} %get-tuple-element.80), channel_id=1, source_target_pairs={{0,8},{8,0},{16,24},{24,16},{1,9},{9,1},{17,25},{25,17},{2,10},{10... | collective-permute-start | bytes 3145736 | tf_op jit(solution)/shard_map/ppermute | solution.py:313
  125.7 26.9 %collective-permute-start.21 = (f32[4,2,128,256]{3,2,1,0:T(8,128)S(1)}, f32[4,2,128,256]{3,2,1,0:T(8,128)S(1)}, u32[]{:S(2)}, u32[]{:S(2)}) collective-permute-start(f32[4,2,128,256]{3,2,1,0:T(8,128)S(1)} %get-tuple-element.79), channel_id=1, source_target_pairs={{0,16},{8,24},{16,0},{24,8},{1,17},{9,25},{17,1},{25,9},{2,18},{10... | collective-permute-start | bytes 3145736 | tf_op jit(solution)/shard_map/ppermute | solution.py:313
  127.3 26.6 %collective-permute-start.20 = (f32[4,2,128,256]{3,2,1,0:T(8,128)S(1)}, f32[4,2,128,256]{3,2,1,0:T(8,128)S(1)}, u32[]{:S(2)}, u32[]{:S(2)}) collective-permute-start(f32[4,2,128,256]{3,2,1,0:T(8,128)S(1)} %get-tuple-element.77), channel_id=1, source_target_pairs={{0,8},{8,0},{16,24},{24,16},{1,9},{9,1},{17,25},{25,17},{2,10},{10... | collective-permute-start | bytes 3145736 | tf_op jit(solution)/shard_map/ppermute | solution.py:313
